TPU v7x, 32 devices: a whole 2x2x4 slice. The times are simulated.
32 devices in a mesh: seq: 8 (over z, x), chan: 4 (over y, core).
Axes of the slice: x: 2, y: 2, z: 4, core: 2. Of those that a mesh axis runs over, the one named last changes fastest.
Arguments:
- q_gate: bfloat16 [4096, 1024], P('seq', 'chan'), may hold values from -6 to 6
- k_gate: bfloat16 [4096, 1024], P('seq', 'chan'), may hold values from -6 to 6
- value: bfloat16 [4096, 1024], P('seq', 'chan'), may hold values from -6 to 6
- decay: float32 [16, 1024], P(None, 'chan'), may hold values from 6.1035156e-05 to 0.0333333333
- residue: float32 [16, 1024], P(None, 'chan'), may hold values from -1 to 1
- skip: float32 [1024], P('chan'), may hold values from -1 to 1
- out_weight: bfloat16 [1024, 1024], P(None, 'chan'), may hold values from -0.1875 to 0.1875
- out_bias: float32 [1024], P('chan'), may hold values from -3 to 3
Outputs:
- layer_out: bfloat16 [4096, 1024], P('seq', 'chan')
All inputs are finite; a program needn't handle non-finite values.
Results may differ from a plain program's by a relative error of at most 0.015.
Values may be sent and summed in bfloat16 or wider, within the bound.
No kernel may reach another device: no remote copies, remote signals or barrier semaphores. Data moves between devices by JAX's collectives and lax.ppermute only.
A program may use at most 64 MiB of HBM per device.

v0:
```python
import math

import jax
import jax.numpy as jnp
from jax import lax
from jax.sharding import PartitionSpec as P

precise = lax.Precision.HIGHEST


def shortened(shard):

    def short(part):
        return part.astype(jnp.bfloat16) if part.dtype == jnp.float32 else part

    return jax.tree.map(short, shard)


def inner_factor(length):
    factor = math.isqrt(length)
    while length % factor != 0:
        factor = factor - 1
    return factor


def phases(rows_count, cols_count, col_first, period, orient):
    row_index = lax.broadcasted_iota(jnp.int32, (rows_count, cols_count), 0)
    col_index = lax.broadcasted_iota(jnp.int32, (rows_count, cols_count), 1) + col_first
    phase_angle = (
        orient * 2.0 * math.pi / period * (row_index * col_index % period).astype(jnp.float32)
    )
    return (jnp.cos(phase_angle), jnp.sin(phase_angle))


def complex_block(cosine, sine_part):
    upper = jnp.concatenate([cosine, -sine_part], axis=1)
    lower = jnp.concatenate([sine_part, cosine], axis=1)
    return jnp.concatenate([upper, lower], axis=0)


def rotate(tensor, cosine, sine_part):
    real_part = tensor[:, 0]
    imag_part = tensor[:, 1]
    return jnp.stack(
        [real_part * cosine - imag_part * sine_part, real_part * sine_part + imag_part * cosine],
        axis=1,
    )


def complex_product(first_op, second_op):
    first_real, first_imag = (first_op[:, 0], first_op[:, 1])
    second_real, second_imag = (second_op[:, 0], second_op[:, 1])
    return jnp.stack(
        [
            first_real * second_real - first_imag * second_imag,
            first_real * second_imag + first_imag * second_real,
        ],
        axis=1,
    )


def first_section(tensor, matrix):
    lead_count, reim_count, size_one, size_two, chan_count = tensor.shape
    folded = tensor.reshape(lead_count, 2 * size_one, size_two * chan_count)
    combined = jnp.einsum("ab,kbx->kax", matrix, folded, precision=precise)
    return combined.reshape(lead_count, 2, matrix.shape[0] // 2, size_two, chan_count)


def second_section(tensor, matrix):
    size_two = matrix.shape[0] // 2
    coeffs = matrix.reshape(2, size_two, 2, size_two)
    return jnp.einsum("rbsj,ksajc->krabc", coeffs, tensor, precision=precise)


def spectral_conv(gated, decay, residue):
    seq_count = lax.axis_size("seq")
    seq_rank = lax.axis_index("seq")
    seg_len = gated.shape[0]
    channels = gated.shape[1]
    piece_len = seg_len // seq_count
    padded = 2 * seq_count * seg_len
    split_one = inner_factor(seg_len)
    split_two = seg_len // split_one
    columns = lax.all_to_all(
        gated.reshape(1, seg_len, channels), "seq", split_axis=1, concat_axis=0, tiled=True
    )
    front_cosine, front_sine = phases(2 * seq_count, seq_count, 0, 2 * seq_count, -1.0)
    front_coeffs = jnp.stack([front_cosine, front_sine], axis=1).reshape(4 * seq_count, seq_count)
    twist_cosine, twist_sine = phases(2 * seq_count, piece_len, seq_rank * piece_len, padded, -1.0)
    first_block = complex_block(*phases(split_one, split_one, 0, split_one, -1.0))
    second_block = complex_block(*phases(split_two, split_two, 0, split_two, -1.0))
    middle_cosine, middle_sine = phases(split_one, split_two, 0, seg_len, -1.0)

    def rows_forward(signal):
        combined = jnp.dot(
            front_coeffs, signal.reshape(seq_count, piece_len * channels), precision=precise
        )
        return rotate(
            combined.reshape(2 * seq_count, 2, piece_len, channels),
            twist_cosine[:, :, None],
            twist_sine[:, :, None],
        )

    def columns_forward(spread):
        sectioned = first_section(spread.reshape(2, 2, split_one, split_two, channels), first_block)
        sectioned = rotate(sectioned, middle_cosine[:, :, None], middle_sine[:, :, None])
        return second_section(sectioned, second_block)

    positions = (
        lax.broadcasted_iota(jnp.int32, (seq_count, piece_len), 0) * seg_len
        + seq_rank * piece_len
        + lax.broadcasted_iota(jnp.int32, (seq_count, piece_len), 1)
    ).astype(jnp.float32)[:, :, None]
    kernel = jnp.zeros((seq_count, piece_len, channels), jnp.float32)
    for order_index in range(decay.shape[0]):
        kernel = kernel + residue[order_index] * jnp.exp(-decay[order_index] * positions)
    spread, kernel_spread = (
        lax.all_to_all(
            rows_forward(columns.astype(jnp.float32)).astype(jnp.bfloat16),
            "seq",
            split_axis=0,
            concat_axis=2,
            tiled=True,
        ).astype(jnp.float32),
        lax.all_to_all(
            rows_forward(kernel).astype(jnp.bfloat16),
            "seq",
            split_axis=0,
            concat_axis=2,
            tiled=True,
        ).astype(jnp.float32),
    )
    spectrum = columns_forward(spread)
    response = columns_forward(kernel_spread)
    product = complex_product(spectrum, response)
    back_second = complex_block(*phases(split_two, split_two, 0, split_two, 1.0))
    back_first = complex_block(*phases(split_one, split_one, 0, split_one, 1.0))
    sectioned = second_section(product, back_second)
    sectioned = rotate(sectioned, middle_cosine[:, :, None], -middle_sine[:, :, None])
    sectioned = first_section(sectioned, back_first).reshape(2, 2, seg_len, channels)
    row_data = lax.all_to_all(
        shortened(sectioned), "seq", split_axis=2, concat_axis=0, tiled=True
    ).astype(sectioned.dtype)
    row_data = rotate(row_data, twist_cosine[:, :, None], -twist_sine[:, :, None])
    back_cosine, back_sine = phases(seq_count, 2 * seq_count, 0, 2 * seq_count, 1.0)
    back_coeffs = (jnp.stack([back_cosine, -back_sine], axis=2) / padded).reshape(
        seq_count, 4 * seq_count
    )
    convolved = jnp.dot(
        back_coeffs, row_data.reshape(4 * seq_count, piece_len * channels), precision=precise
    )
    convolved = lax.all_to_all(
        convolved.reshape(seq_count, piece_len, channels),
        "seq",
        split_axis=0,
        concat_axis=1,
        tiled=True,
    )
    return convolved.reshape(seg_len, channels)


def shards(q_gate, k_gate, value, decay, residue, skip, out_weight, out_bias):
    gated = (k_gate.astype(jnp.float32) * value.astype(jnp.float32)).astype(jnp.bfloat16)
    convolved = spectral_conv(gated, decay, residue)
    modulated = (
        q_gate.astype(jnp.float32) * (convolved + skip * gated.astype(jnp.float32))
    ).astype(jnp.bfloat16)
    projected = jnp.dot(
        lax.all_gather(modulated, "chan", axis=1, tiled=True),
        out_weight,
        preferred_element_type=jnp.float32,
    )
    return (projected + out_bias).astype(jnp.bfloat16)


def solution(mesh):
    return jax.shard_map(
        shards,
        mesh=mesh,
        in_specs=(
            P("seq", "chan"),
            P("seq", "chan"),
            P("seq", "chan"),
            P(None, "chan"),
            P(None, "chan"),
            P("chan"),
            P(None, "chan"),
            P("chan"),
        ),
        out_specs=P("seq", "chan"),
        check_vma=False,
    )
```

profile of v0, /device:TPU:0, one launch (start us, length us, event | category | flops | bytes accessed | tf_op | source)
XLA Modules:
  0.0 201.6 jit_solution(14413377606624419511)
XLA Ops:
  6.5 1.1 fusion.19
  7.7 0.4 copy.165
  8.1 0.5 broadcast.495
  8.6 2.2 %reduce.2 = bf16[512,256]{1,0:T(8,128)(2,1)S(1)} reduce(bf16[512,1,256]{2,1,0:T(2,128)(2,1)S(1)} %bitcast.292, bf16[]{:T(256)} %broadcast.495), dimensions={1}, to_apply=%bitcast.282.reduce_sub_computation | reduce | bytes 524290
  10.8 0.8 reshape.476
  11.6 7.3 %all-to-all-start = ((bf16[8,2,8192]{2,1,0:T(2,128)(2,1)}), bf16[8,2,8192]{2,1,0:T(2,128)(2,1)S(1)}, u32[]{:S(2)}, u32[]{:S(2)}) async-start(bf16[8,2,8192]{2,1,0:T(2,128)(2,1)} %reshape.476), calls=%async_computation | async-start | bytes 524288 | tf_op jit(solution)/shard_map/all_to_all | solution.py:84
  20.8 0.1 mul.1038
  20.9 1.5 multiply_add_fusion.5
  22.4 0.2 fusion.42
  22.7 1.8 fusion.58
  24.5 3.2 %all-to-all-done = bf16[8,2,8192]{2,1,0:T(2,128)(2,1)S(1)} async-done(((bf16[8,2,8192]{2,1,0:T(2,128)(2,1)}), bf16[8,2,8192]{2,1,0:T(2,128)(2,1)S(1)}, u32[]{:S(2)}, u32[]{:S(2)}) %all-to-all-start) | async-done | bytes 262176 | tf_op jit(solution)/shard_map/all_to_all | solution.py:84
  27.8 0.3 reshape.477
  28.1 1.5 bitcast_reduce_fusion
  29.6 0.1 reshape.450
  29.7 1.0 fusion.59
  30.7 1.4 subtract_convert_fusion.1
  32.1 0.1 pad_maximum_fusion.3
  32.3 1.3 copy.75
  33.6 3.6 %all-to-all-start.2 = ((bf16[16,2,64,256]{3,2,1,0:T(8,128)(2,1)}), bf16[16,2,64,256]{3,2,1,0:T(8,128)(2,1)S(1)}, u32[]{:S(2)}, u32[]{:S(2)}) async-start(bf16[16,2,64,256]{3,2,1,0:T(8,128)(2,1)} %copy.75), calls=%async_computation.2 | async-start | bytes 2097152 | tf_op jit(solution)/shard_map/all_to_all | solution.py:125
  37.2 0.1 pad_maximum_fusion.2
  37.3 1.3 copy.70
  38.6 24.2 %all-to-all-done.2 = bf16[16,2,64,256]{3,2,1,0:T(8,128)(2,1)S(1)} async-done(((bf16[16,2,64,256]{3,2,1,0:T(8,128)(2,1)}), bf16[16,2,64,256]{3,2,1,0:T(8,128)(2,1)S(1)}, u32[]{:S(2)}, u32[]{:S(2)}) %all-to-all-start.2) | async-done | bytes 1048608 | tf_op jit(solution)/shard_map/all_to_all | solution.py:125
  62.8 4.4 %all-to-all-start.1 = ((bf16[16,2,64,256]{3,2,1,0:T(8,128)(2,1)}), bf16[16,2,64,256]{3,2,1,0:T(8,128)(2,1)}, u32[]{:S(2)}, u32[]{:S(2)}) async-start(bf16[16,2,64,256]{3,2,1,0:T(8,128)(2,1)} %copy.70), calls=%async_computation.1 | async-start | bytes 2097152 | tf_op jit(solution)/shard_map/all_to_all | solution.py:118
  67.3 0.1 multiply_sine_fusion.1
  67.5 0.1 reshape.452
  67.6 0.1 fusion.57
  67.7 0.1 multiply_sine_fusion
  67.8 0.1 reshape.454
  68.3 0.1 copy.163
  68.4 0.5 reshape_reshape.8
  69.0 1.0 fusion.43
  70.0 0.6 copy.145
  70.7 21.8 %all-to-all-done.1 = bf16[16,2,64,256]{3,2,1,0:T(8,128)(2,1)} async-done(((bf16[16,2,64,256]{3,2,1,0:T(8,128)(2,1)}), bf16[16,2,64,256]{3,2,1,0:T(8,128)(2,1)}, u32[]{:S(2)}, u32[]{:S(2)}) %all-to-all-start.1) | async-done | bytes 1048608 | tf_op jit(solution)/shard_map/all_to_all | solution.py:118
  92.5 2.3 %copy.164 = bf16[8,2,2,64,256]{4,3,0,2,1:T(8,128)(2,1)} copy(bf16[8,2,2,64,256]{4,3,2,1,0:T(8,128)(2,1)} %bitcast.8) | data formatting | bytes 2097152 | tf_op jit(solution)/shard_map/all_to_all | solution.py:118
  94.7 2.3 %reshape_reshape.7 = bf16[2,32,8192]{2,1,0:T(8,128)(2,1)} reshape(bf16[2,2,8,64,256]{4,3,2,1,0:T(8,128)(2,1)} %bitcast.291) | data formatting | bytes 2097152 | tf_op jit(solution)/shard_map/reshape;reshape | solution.py:64
  97.1 2.3 %fusion.44 = f32[2,8192,32]{1,2,0:T(8,128)S(1)} fusion(bf16[2,32,8192]{2,1,0:T(8,128)(2,1)} %reshape_reshape.7, f32[16,16]{1,0:T(8,128)S(1)} %get-tuple-element.63, f32[16,16]{1,0:T(8,128)S(1)} %get-tuple-element.62, f32[16,16]{1,0:T(8,128)S(1)} %fusion.75), kind=kOutput, calls=%fused_computation.130 | convolution fusion | flops 201329664 | bytes 3148800 | tf_op jit(solution)/shard_map/ab,kbx->kax/dot_general | solution.py:65
  99.4 0.6 copy.112
  100.0 0.6 multiply_subtract_fusion.4
  100.7 2.0 fusion.15
  102.7 2.0 fusion.14
  104.7 0.6 multiply_subtract_fusion.2
  105.3 2.0 fusion.13
  107.4 0.3 multiply_subtract_fusion.1
  107.7 0.2 pad_maximum_fusion
  107.9 1.5 copy.81
  109.4 1.7 reshape.455
  111.2 2.9 %fusion = bf16[2,32,8192]{2,1,0:T(8,128)(2,1)} fusion(f32[2,32,8192]{2,1,0:T(8,128)S(1)} %reshape.455, f32[16,16]{1,0:T(8,128)S(1)} %get-tuple-element.71, f32[16,16]{1,0:T(8,128)S(1)} %get-tuple-element.70, f32[16,16]{1,0:T(8,128)S(1)} %fusion.76), kind=kOutput, calls=%fused_computation.1 | convolution fusion | flops 201853952 | bytes 3148800 | tf_op jit(solution)/shard_map/ab,kbx->kax/dot_general | solution.py:65
  114.1 1.6 convert_element_type.184
  115.7 2.1 %copy.82 = bf16[2,2,512,256]{3,1,0,2:T(2,128)(2,1)} copy(bf16[2,2,512,256]{3,2,1,0:T(8,128)(2,1)S(1)} %convert_element_type.184) | data formatting | bytes 2097152 | tf_op jit(solution)/shard_map/convert_element_type | solution.py:14
  117.7 3.6 %all-to-all-start.3 = ((bf16[2,2,512,256]{3,1,0,2:T(2,128)(2,1)}), bf16[2,2,512,256]{3,1,0,2:T(2,128)(2,1)S(1)}, u32[]{:S(2)}, u32[]{:S(2)}) async-start(bf16[2,2,512,256]{3,1,0,2:T(2,128)(2,1)} %copy.82), calls=%async_computation.3 | async-start | bytes 2097152 | tf_op jit(solution)/shard_map/all_to_all | solution.py:141
  121.5 25.6 %all-to-all-done.3 = bf16[2,2,512,256]{3,1,0,2:T(2,128)(2,1)S(1)} async-done(((bf16[2,2,512,256]{3,1,0,2:T(2,128)(2,1)}), bf16[2,2,512,256]{3,1,0,2:T(2,128)(2,1)S(1)}, u32[]{:S(2)}, u32[]{:S(2)}) %all-to-all-start.3) | async-done | bytes 1048608 | tf_op jit(solution)/shard_map/all_to_all | solution.py:141
  147.1 0.1 copy.83
  147.2 0.3 convert_bitcast_fusion
  147.5 3.0 %copy.84 = f32[8,2,2,64,256]{4,1,0,3,2:T(2,128)} copy(f32[8,2,2,64,256]{4,3,0,2,1:T(8,128)S(1)} %convert_bitcast_fusion) | data formatting | bytes 4194304 | tf_op jit(solution)/shard_map/convert_element_type | solution.py:143
  150.4 2.7 %reshape.458 = f32[16,2,64,256]{3,0,2,1:T(8,128)S(1)} reshape(f32[8,2,2,64,256]{4,1,0,3,2:T(2,128)} %copy.84) | data formatting | bytes 4194304 | tf_op jit(solution)/shard_map/convert_element_type | solution.py:143
  153.1 0.3 multiply_subtract_fusion
  153.5 0.2 pad_maximum_fusion.1
  153.6 1.2 copy.85
  154.9 2.2 %fusion.1 = f32[8,64,256]{2,0,1:T(8,128)S(1)} fusion(f32[8,32,1]{0,1,2:T(8,128)S(1)} %bitcast.299, f32[4,8,64,256]{3,2,1,0:T(8,128)S(1)} %bitcast.283), kind=kOutput, calls=%fused_computation.2 | convolution fusion | flops 50331648 | bytes 2622464 | tf_op jit(solution)/shard_map/dot_general | solution.py:149
  157.2 0.2 copy.88
  157.3 18.1 %all_to_all.57 = f32[8,64,256]{2,1,0:T(8,128)S(1)} all-to-all(f32[8,64,256]{2,1,0:T(8,128)S(1)} %copy.88), channel_id=1, replica_groups=mesh['seq'=8,'chan'=4] {'seq'}, dimensions={0} | all-to-all | bytes 1048576 | tf_op jit(solution)/shard_map/all_to_all | solution.py:152
  175.5 0.8 fusion.18
  176.3 16.1 %all-gather.2.cloned.1.call-done = bf16[512,1024]{1,0:T(8,128)(2,1)} async-done(((bf16[512,256]{1,0:T(8,128)(2,1)}), bf16[512,1024]{1,0:T(8,128)(2,1)}) %all-gather.2.cloned.1.call-update) | async-done | bytes 1048592 | tf_op jit(solution)/shard_map/all_gather | solution.py:169
  192.4 2.4 %fusion.16 = bf16[512,256]{1,0:T(8,128)(2,1)} fusion(bf16[512,1024]{1,0:T(8,128)(2,1)} %all-gather.2.cloned.1.call-done, bf16[1024,256]{1,0:T(8,128)(2,1)S(1)} %copy-done, f32[256]{0:T(256)S(1)} %copy-done.8), kind=kOutput, calls=%fused_computation.24 | convolution fusion | flops 268697600 | bytes 1836032 | tf_op jit(solution)/shard_map/dot_general | solution.py:168
  (102 shorter events, 2.3 us)
Async XLA Ops:
  6.5 185.9 %copy-start = (bf16[1024,256]{1,0:T(8,128)(2,1)S(1)}, bf16[1024,256]{1,0:T(8,128)(2,1)}, u32[]{:S(2)}) copy-start(bf16[1024,256]{1,0:T(8,128)(2,1)} %param.14) | copy-start | bytes 1572868
  6.5 12.3 %copy-start.5 = (f32[16,256]{1,0:T(8,128)S(1)}, f32[16,256]{1,0:T(8,128)}, u32[]{:S(2)}) copy-start(f32[16,256]{1,0:T(8,128)} %param.12) | copy-start | bytes 49156
  6.5 12.4 %copy-start.6 = (f32[16,256]{1,0:T(8,128)S(1)}, f32[16,256]{1,0:T(8,128)}, u32[]{:S(2)}) copy-start(f32[16,256]{1,0:T(8,128)} %param.11) | copy-start | bytes 49156
  11.6 16.2 %all-to-all-start = ((bf16[8,2,8192]{2,1,0:T(2,128)(2,1)}), bf16[8,2,8192]{2,1,0:T(2,128)(2,1)S(1)}, u32[]{:S(2)}, u32[]{:S(2)}) async-start(bf16[8,2,8192]{2,1,0:T(2,128)(2,1)} %reshape.476), calls=%async_computation | async-start | bytes 524288 | tf_op jit(solution)/shard_map/all_to_all | solution.py:84
  32.2 4.9 %copy-start.1 = (bf16[16,1,64,256]{3,0,2,1:T(8,128)(2,1)S(1)}, bf16[16,1,64,256]{3,0,2,1:T(8,128)(2,1)}, u32[]{:S(2)}) copy-start(bf16[16,1,64,256]{3,0,2,1:T(8,128)(2,1)} %get-tuple-element.10) | copy-start | bytes 1572868
  33.6 29.2 %all-to-all-start.2 = ((bf16[16,2,64,256]{3,2,1,0:T(8,128)(2,1)}), bf16[16,2,64,256]{3,2,1,0:T(8,128)(2,1)S(1)}, u32[]{:S(2)}, u32[]{:S(2)}) async-start(bf16[16,2,64,256]{3,2,1,0:T(8,128)(2,1)} %copy.75), calls=%async_computation.2 | async-start | bytes 2097152 | tf_op jit(solution)/shard_map/all_to_all | solution.py:125
  62.8 29.7 %all-to-all-start.1 = ((bf16[16,2,64,256]{3,2,1,0:T(8,128)(2,1)}), bf16[16,2,64,256]{3,2,1,0:T(8,128)(2,1)}, u32[]{:S(2)}, u32[]{:S(2)}) async-start(bf16[16,2,64,256]{3,2,1,0:T(8,128)(2,1)} %copy.70), calls=%async_computation.1 | async-start | bytes 2097152 | tf_op jit(solution)/shard_map/all_to_all | solution.py:118
  117.7 29.3 %all-to-all-start.3 = ((bf16[2,2,512,256]{3,1,0,2:T(2,128)(2,1)}), bf16[2,2,512,256]{3,1,0,2:T(2,128)(2,1)S(1)}, u32[]{:S(2)}, u32[]{:S(2)}) async-start(bf16[2,2,512,256]{3,1,0,2:T(2,128)(2,1)} %copy.82), calls=%async_computation.3 | async-start | bytes 2097152 | tf_op jit(solution)/shard_map/all_to_all | solution.py:141
  121.3 71.1 %all-gather.2.cloned.1.call-start = ((), (), s32[]{:S(2)}) async-start(), calls=%async_computation.5 | async-start | bytes 1310720 | tf_op jit(solution)/shard_map/all_gather | solution.py:169
  154.9 20.6 %copy-start.2 = (bf16[512,256]{1,0:T(8,128)(2,1)S(1)}, bf16[512,256]{1,0:T(8,128)(2,1)}, u32[]{:S(2)}) copy-start(bf16[512,256]{1,0:T(8,128)(2,1)} %param.10) | copy-start | bytes 786436
  154.9 20.6 %copy-start.3 = (bf16[512,256]{1,0:T(8,128)(2,1)S(1)}, bf16[512,256]{1,0:T(8,128)(2,1)}, u32[]{:S(2)}) copy-start(bf16[512,256]{1,0:T(8,128)(2,1)} %param.9) | copy-start | bytes 786436
  154.9 20.6 %copy-start.4 = (bf16[512,256]{1,0:T(8,128)(2,1)S(1)}, bf16[512,256]{1,0:T(8,128)(2,1)}, u32[]{:S(2)}) copy-start(bf16[512,256]{1,0:T(8,128)(2,1)} %param.8) | copy-start | bytes 786436
  154.9 20.6 %copy-start.7 = (f32[256]{0:T(256)S(1)}, f32[256]{0:T(256)}, u32[]{:S(2)}) copy-start(f32[256]{0:T(256)} %param.13) | copy-start | bytes 3076
  157.2 35.3 %copy-start.8 = (f32[256]{0:T(256)S(1)}, f32[256]{0:T(256)}, u32[]{:S(2)}) copy-start(f32[256]{0:T(256)} %param.15) | copy-start | bytes 3076
Sparse Core Ops, SparseCore 0:
  176.4 15.9 all-gather.1
where the time goes:
time: 202 us
  waiting for transfers between devices  90.9 us (45%)
  local copies, waits for them, and re-layouts  28.6 us (14%)
  matrix products  19.7 us (10%)
  starting transfers between devices  18.9 us (9%)
  blocking collectives  18.1 us (9%)
  between operations  14.4 us (7%)
  other arithmetic  11.1 us (5%)
    all_to_all x1, waiting for transfers between devices, spectral_conv(): lax.all_to_all(shortened(sectioned), 'seq', split_axis=2, concat_axis=0,...  25.6 us
    all_to_all x1, waiting for transfers between devices, spectral_conv(): lax.all_to_all(rows_forward(kernel).astype(jnp.bfloat16), 'seq', split_ax...  24.2 us
    all_to_all x1, waiting for transfers between devices, spectral_conv(): lax.all_to_all(rows_forward(columns.astype(jnp.float32)).astype(jnp.bfloa...  21.8 us
    all_to_all x1, blocking collectives, spectral_conv(): lax.all_to_all(convolved.reshape(seq_count, piece_len, channels), 'seq',...  18.1 us
    all_gather x1, waiting for transfers between devices, shards(): lax.all_gather(modulated, 'chan', axis=1, tiled=True)  16.1 us
    all_to_all x1, starting transfers between devices, spectral_conv(): lax.all_to_all(gated.reshape(1, seg_len, channels), 'seq', split_axis=1,...  7.25 us
    dot_general x3, matrix products, first_section(): combined = jnp.einsum('ab,kbx->kax', matrix, folded, precision=precise)  6.22 us
    dot_general x3, matrix products, second_section(): return jnp.einsum('rbsj,ksajc->krabc', coeffs, tensor, precision=precise)  6.04 us
  transfers between devices with their start and end apart: 5, of which 5 were waited for; matrix products, arithmetic and copies ran while one was open for 5% of the time, Pallas kernels for 0%

commit v1 on v0

v1 whole, which is shorter than its diff:
```python
import functools

import jax
import jax.numpy as jnp
from jax import lax
from jax.experimental import pallas as pl
from jax.experimental.pallas import tpu as pltpu
from jax.sharding import PartitionSpec as P

LANES = 128
SUBLANES = 8
STORES = 2
FOLD_COST = 3000000000
NEAR_COST = 3000000000
PART_COST = 1500000000
VMEM_LIMIT = 32 * 1024 * 1024


def row(ref, mode, part):
    return ref[mode : mode + 1, part * LANES : (part + 1) * LANES]


def full(value):
    return jnp.broadcast_to(value, (SUBLANES, LANES))


def tree_sum(terms):
    while len(terms) > 1:
        paired = [a + b for a, b in zip(terms[::2], terms[1::2])]
        terms = paired + ([terms[-1]] if len(terms) % 2 else [])
    return terms[0]


def lane_slice(part):
    return slice(part * LANES, (part + 1) * LANES)


def state_kernel(
    k_hbm, v_hbm, decay_hbm, residue_hbm, skip_hbm, bias_hbm,
    total_ref, chunk_ref, gated_ref, decay_ref, residue_ref, skip_ref, bias_ref,
    k_ref, v_ref, sems,
):
    modes = decay_hbm.shape[0]
    parts = gated_ref.shape[0]
    chunk_len = k_ref.shape[0] // SUBLANES
    pairs = [(decay_hbm, decay_ref)]
    for part in range(parts):
        lanes = pl.ds(part * LANES, LANES)
        pairs += [(k_hbm.at[:, lanes], k_ref.at[:, lanes]), (v_hbm.at[:, lanes], v_ref.at[:, lanes])]
    pairs += [(residue_hbm, residue_ref), (skip_hbm, skip_ref), (bias_hbm, bias_ref)]
    copies = [pltpu.make_async_copy(src, dst, sems.at[i]) for i, (src, dst) in enumerate(pairs)]
    for copy in copies:
        copy.start()
    copies[0].wait()
    later = (SUBLANES - 1 - lax.broadcasted_iota(jnp.int32, (SUBLANES, LANES), 0)) * chunk_len
    later = later.astype(jnp.float32)
    for part in range(parts):
        lanes = lane_slice(part)
        copies[1 + 2 * part].wait()
        copies[2 + 2 * part].wait()
        product = k_ref[:, lanes].astype(jnp.float32) * v_ref[:, lanes].astype(jnp.float32)
        gated_ref[part] = product.astype(jnp.bfloat16).astype(jnp.float32)
        factor = [full(jnp.exp(-row(decay_ref, n, part))) for n in range(modes)]

        def step(t, state):
            x = gated_ref[part, pl.ds(t, SUBLANES, stride=chunk_len), :]
            return tuple(f * h + x for f, h in zip(factor, state))

        zero = jnp.zeros((SUBLANES, LANES), jnp.float32)
        state = lax.fori_loop(0, chunk_len, step, (zero,) * modes, unroll=8)
        for n in range(modes):
            chunk_ref[n, :, lanes] = state[n]
            weight = jnp.exp(-row(decay_ref, n, part) * later)
            total_ref[n : n + 1, lanes] = jnp.sum(weight * state[n], axis=0, keepdims=True)
    for copy in copies[1 + 2 * parts :]:
        copy.wait()


def local_kernel(gated, decay_ref, residue_ref, skip_ref, chunk_ref, local_ref, short_ref):
    modes = decay_ref.shape[0]
    chunk_len = gated.shape[1] // SUBLANES
    index = lax.broadcasted_iota(jnp.int32, (SUBLANES, LANES), 0)
    for part in range(gated.shape[0]):
        lanes = lane_slice(part)
        factor, weight, start = [], [], []
        for n in range(modes):
            rate = row(decay_ref, n, part)
            prefix = chunk_ref[n, :, lanes]
            for shift in (1, 2, 4):
                moved = jnp.where(index >= shift, pltpu.roll(prefix, shift, 0), 0.0)
                prefix = prefix + jnp.exp(-rate * (shift * chunk_len)) * moved
            start.append(jnp.where(index >= 1, pltpu.roll(prefix, 1, 0), 0.0))
            factor.append(full(jnp.exp(-rate)))
            weight.append(full(row(residue_ref, n, part)))
        bypass = full(skip_ref[:, lanes])

        def step(t, state):
            rows = pl.ds(t, SUBLANES, stride=chunk_len)
            x = gated[part, rows, :]
            state = tuple(f * h + x for f, h in zip(factor, state))
            local_ref[part, rows, :] = tree_sum([w * h for w, h in zip(weight, state)] + [bypass * x])
            return state

        lax.fori_loop(0, chunk_len, step, tuple(start), unroll=4)
        short_ref[:, lanes] = local_ref[part].astype(short_ref.dtype)


def fold(rates, inner, total, received, stride, seg_len):
    place = lax.div(lax.axis_index("seq"), 2)
    radix = len(received) + 1
    spot = lax.rem(lax.div(place, stride), radix)
    offset = lax.rem(place, stride)

    def decayed(segments):
        return jnp.exp(-rates * (segments * 2 * seg_len).astype(jnp.float32))

    before = jnp.zeros_like(rates)
    whole = decayed((radix - 1 - spot) * stride) * total
    for i, block in enumerate(received):
        source = spot ^ (i + 1)
        past = source < spot
        gap = jnp.where(past, spot - 1 - source, 0) * stride
        before += jnp.where(past, decayed(gap) * block, 0.0)
        whole += decayed((radix - 1 - source) * stride) * block
    return inner + decayed(offset) * before, whole


def fold_kernel(stride, seg_len, rates_ref, total_ref, *rest):
    inner, rest = (rest[0][...], rest[1:]) if stride > 1 else (0.0, rest)
    received, (inner_out, total_out) = [ref[...] for ref in rest[:-2]], rest[-2:]
    inner_out[...], total_out[...] = fold(
        rates_ref[...], inner, total_ref[...], received, stride, seg_len
    )


def share_kernel(stride, seg_len, rates_ref, residue_ref, own_ref, total_ref, *rest):
    inner, rest = (rest[0][...], rest[1:]) if stride > 1 else (0.0, rest)
    received, (base_ref, extra_ref) = [ref[...] for ref in rest[:-2]], rest[-2:]
    modes = rates_ref.shape[0]
    rates = rates_ref[...]
    before, _ = fold(rates, inner, total_ref[...], received, stride, seg_len)
    before *= residue_ref[...]
    step = jnp.exp(-rates * float(seg_len))
    even = lax.rem(lax.axis_index("seq"), 2) == 0
    base_ref[:modes, :] = step * before
    base_ref[modes:, :] = rates
    extra_ref[...] = jnp.where(even, residue_ref[...] * own_ref[...] + step * step * before, before)


def carry_kernel(first, q_ref, local_ref, base_ref, extra_ref, out_ref):
    modes = extra_ref.shape[0]
    seg_len = q_ref.shape[0]
    block = 2 * SUBLANES
    ahead = (lax.broadcasted_iota(jnp.int32, (SUBLANES, LANES), 0) + 1).astype(jnp.float32)
    for index in range(out_ref.shape[1] // LANES):
        part = first + index
        lanes = lane_slice(part)
        factor, start = [], []
        for n in range(modes):
            rate = row(base_ref, modes + n, part)
            weight = row(base_ref, n, part) + row(extra_ref, n, part)
            start.append(weight * jnp.exp(-rate * ahead))
            factor.append(full(jnp.exp(-rate * SUBLANES)))

        def step(j, state):
            rows = pl.ds(pl.multiple_of(j * block, block), block)
            halves = []
            for _ in range(2):
                halves.append(tree_sum(list(state)))
                state = tuple(f * h for f, h in zip(factor, state))
            local = local_ref[part, rows, :] if len(local_ref.shape) == 3 else local_ref[rows, lanes]
            total = local.astype(jnp.float32) + jnp.concatenate(halves, axis=0)
            out_ref[rows, lane_slice(index)] = (q_ref[rows, lanes].astype(jnp.float32) * total).astype(out_ref.dtype)
            return state

        lax.fori_loop(0, seg_len // block, step, tuple(start), unroll=4)


def project(blocks, weight_ref):
    total = None
    for rank, parts in blocks:
        depth = weight_ref.shape[0] // lax.axis_size("chan")
        offset = pl.multiple_of(rank * depth, depth)
        for block in parts:
            rows = pl.ds(offset, block.shape[1])
            term = jnp.dot(block[...], weight_ref[rows, :], preferred_element_type=jnp.float32)
            total = term if total is None else total + term
            offset = pl.multiple_of(offset + block.shape[1], block.shape[1])
    return total


def near_kernel(weight_ref, bias_ref, *rest):
    blocks, out_ref = rest[:-1], rest[-1]
    rank = lax.axis_index("chan")
    parts = len(blocks) // 3
    blocks = [(rank ^ bit, blocks[i * parts : (i + 1) * parts]) for i, bit in enumerate((0, 2, 3))]
    out_ref[...] = project(blocks, weight_ref) + bias_ref[...]


def last_kernel(near_ref, weight_ref, *rest):
    pair, (out_hbm, out_ref, sems) = rest[:-3], rest[-3:]
    rank = lax.axis_index("chan")
    pieces = sems.shape[0]
    size = out_ref.shape[0] // pieces
    copies = []
    for i in range(pieces):
        rows = pl.ds(i * size, size)
        total = near_ref[rows, :] + project([(rank ^ 1, [ref.at[rows, :] for ref in pair])], weight_ref)
        out_ref[rows, :] = total.astype(out_ref.dtype)
        copies.append(pltpu.make_async_copy(out_ref.at[rows], out_hbm.at[rows], sems.at[i]))
        copies[-1].start()
    for copy in copies:
        copy.wait()


def call(kernel, out, *args, cost=0, scratch=(), ins=pltpu.VMEM, outs=pltpu.VMEM):
    return pl.pallas_call(
        kernel,
        out_shape=out,
        in_specs=[pl.BlockSpec(memory_space=ins)] * len(args),
        out_specs=jax.tree.map(lambda _: pl.BlockSpec(memory_space=outs), out),
        scratch_shapes=list(scratch),
        compiler_params=pltpu.CompilerParams(vmem_limit_bytes=VMEM_LIMIT),
        cost_estimate=pl.CostEstimate(flops=cost, bytes_accessed=0, transcendentals=0),
    )(*args)


def struct(shape, dtype=jnp.float32):
    return jax.ShapeDtypeStruct(shape, dtype)


def swapped(value, bit):
    count = lax.axis_size("chan")
    return lax.ppermute(value, "chan", [(r, r ^ bit) for r in range(count)])


def beside(value, step):
    count = lax.axis_size("seq")
    return lax.ppermute(value, "seq", [(r, r ^ step) for r in range(count)])


def corner(value, step, bit):
    count, width = lax.axis_size("seq"), lax.axis_size("chan")
    pairs = [(r * width + c, (r ^ step) * width + (c ^ bit)) for r in range(count) for c in range(width)]
    return lax.ppermute(value, ("seq", "chan"), pairs)


def carry_shares(total, decay, residue, seg_len, also):
    count = lax.axis_size("seq") // 2
    shape = struct(total.shape)
    own, inner, stride = total, (), 1
    while True:
        radix = min(4, count // stride)
        received = [beside(total, 2 * stride * step) for step in range(1, radix)]
        if stride * radix == count:
            break
        kernel = functools.partial(fold_kernel, stride, seg_len)
        *inner, total = call(kernel, [shape, shape], decay, total, *inner, *received)
        stride *= radix
    received, also = lax.optimization_barrier((received, also))
    kernel = functools.partial(share_kernel, stride, seg_len)
    outs = [struct((2 * total.shape[0], total.shape[1])), shape]
    base, extra = call(kernel, outs, decay, residue, own, total, *inner, *received, cost=FOLD_COST)
    return base, extra, also


def shards(q_gate, k_gate, value, decay, residue, skip, out_weight, out_bias):
    seg_len, channels = value.shape
    modes = decay.shape[0]
    cols = out_weight.shape[1]
    parts = channels // LANES
    tall = pltpu.VMEM((seg_len, channels), jnp.bfloat16)
    short = struct((seg_len, channels), jnp.bfloat16)
    q_across = swapped(q_gate, 2)
    inputs = (k_gate, value, decay, residue, skip.reshape(1, -1), out_bias.reshape(1, -1))
    total, chunks, gated, decay, residue, skip, bias = call(
        state_kernel,
        [
            struct((modes, channels)),
            struct((modes, SUBLANES, channels)),
            struct((parts, seg_len, LANES)),
            struct((modes, channels)),
            struct((modes, channels)),
            struct((1, channels)),
            struct((1, cols)),
        ],
        *(pltpu.with_memory_space_constraint(x, pltpu.HBM) for x in inputs),
        scratch=[tall, tall, pltpu.SemaphoreType.DMA((2 * parts + 4,))],
        ins=pltpu.HBM,
    )
    local, local_short = call(
        local_kernel, [struct((parts, seg_len, LANES)), short], gated, decay, residue, skip, chunks
    )
    local_across = swapped(local_short, 2)
    base, extra, q_across = carry_shares(total, decay, residue, seg_len, q_across)
    extra_corner = corner(extra, 1, 2)
    extra_beside = beside(extra, 1)
    base_across = swapped(base, 2)
    half = struct((seg_len, LANES), jnp.bfloat16)
    across = [
        call(
            functools.partial(carry_kernel, part), half, q_across, local_across, base_across, extra_corner,
            cost=PART_COST,
        )
        for part in range(parts)
    ]
    diagonal = [swapped(block, 1) for block in across]
    (extra_beside, *across) = lax.optimization_barrier((extra_beside, *across))
    own = [
        call(functools.partial(carry_kernel, part), half, q_gate, local, base, extra_beside, cost=PART_COST)
        for part in range(parts)
    ]
    pair = [swapped(block, 1) for block in own]
    near = call(near_kernel, struct((seg_len, cols)), out_weight, bias, *own, *across, *diagonal, cost=NEAR_COST)
    return call(
        last_kernel, struct((seg_len, cols), jnp.bfloat16), near, out_weight, *pair,
        scratch=[pltpu.VMEM((seg_len, cols), jnp.bfloat16), pltpu.SemaphoreType.DMA((STORES,))],
        outs=pltpu.HBM,
    )


def solution(mesh):
    return jax.shard_map(
        shards,
        mesh=mesh,
        in_specs=(
            P("seq", "chan"),
            P("seq", "chan"),
            P("seq", "chan"),
            P(None, "chan"),
            P(None, "chan"),
            P("chan"),
            P(None, "chan"),
            P("chan"),
        ),
        out_specs=P("seq", "chan"),
        check_vma=False,
    )
```

time: 202 us -> 25.2 us (0.12)
  waiting for transfers between devices: 90.9 us -> 5.28 us
  local copies, waits for them, and re-layouts: 28.6 us -> 0.04 us
  matrix products: 19.7 us -> 0 us
  blocking collectives: 18.1 us -> 0 us
  between operations: 14.4 us -> 0.1 us
  other arithmetic: 11.1 us -> 0 us
  Pallas kernels: 0 us -> 6.9 us
  starting transfers between devices: 18.9 us -> 12.6 us
    all_to_all x4 -> x0, waiting for transfers between devices: 74.8 us -> none  [the longest x1 25.6 us: spectral_conv(): lax.all_to_all(shortened(sectioned), 'seq', split_axis=2, concat_axis=0,...]
    dot_general x10 -> x0, matrix products: 19.7 us -> none  [the longest x3 6.22 us: first_section(): combined = jnp.einsum('ab,kbx->kax', matrix, folded, precision=precise)]
    all_to_all x4 -> x0, starting transfers between devices: 18.8 us -> none  [the longest x1 7.25 us: spectral_conv(): lax.all_to_all(gated.reshape(1, seg_len, channels), 'seq', split_axis=1,...]
    all_to_all x1 -> x0, blocking collectives: 18.1 us -> none  [spectral_conv(): lax.all_to_all(convolved.reshape(seq_count, piece_len, channels), 'seq',...]
    all_gather x1 -> x0, waiting for transfers between devices: 16.1 us -> none  [shards(): lax.all_gather(modulated, 'chan', axis=1, tiled=True)]
    ppermute x0 -> x12, starting transfers between devices: none -> 12.6 us  [the longest x7 5.15 us: swapped(): return lax.ppermute(value, 'chan', [(r, r ^ bit) for r in range(count)])]
    convert_element_type x4 -> x0, local copies, waits for them, and re-layouts: 9.27 us -> none  [the longest x2 5.65 us: spectral_conv(): row_data = lax.all_to_all(shortened(sectioned), 'seq', split_axis=2, conc...]
    another operation x6 -> x0, local copies, waits for them, and re-layouts: 8.21 us -> none  [the longest x4 5.33 us: rotate(): jnp.stack([real_part * cosine - imag_part * sine_part, real_part * sine_p...]
  transfers between devices with their start and end apart: 5 -> 12, of which waited for: 5 -> 5; matrix products, arithmetic and copies ran while one was open for 5% -> 0% of each run, Pallas kernels for 0% -> 24%
where the time goes in v1:
time: 25.2 us; the launch traced here: 24.9 us
  starting transfers between devices  12.6 us (50%)
  Pallas kernels  6.9 us (27%)
  waiting for transfers between devices  5.28 us (21%)
    pallas_call x9, Pallas kernels, call(): pl.pallas_call(kernel, out_shape=out, in_specs=[pl.BlockSpec(memory_space...  6.9 us
    ppermute x7, starting transfers between devices, swapped(): return lax.ppermute(value, 'chan', [(r, r ^ bit) for r in range(count)])  5.15 us
    ppermute x4, starting transfers between devices, beside(): return lax.ppermute(value, 'seq', [(r, r ^ step) for r in range(count)])  4.99 us
    ppermute x4, waiting for transfers between devices, beside(): return lax.ppermute(value, 'seq', [(r, r ^ step) for r in range(count)])  3.24 us
    ppermute x1, starting transfers between devices, corner(): return lax.ppermute(value, ('seq', 'chan'), pairs)  2.45 us
    ppermute x1, waiting for transfers between devices, corner(): return lax.ppermute(value, ('seq', 'chan'), pairs)  1.11 us
    ppermute x7, waiting for transfers between devices, swapped(): return lax.ppermute(value, 'chan', [(r, r ^ bit) for r in range(count)])  0.94 us
  transfers between devices with their start and end apart: 12, of which 5 were waited for; matrix products, arithmetic and copies ran while one was open for 0% of the time, Pallas kernels for 24%

profile of v1, /device:TPU:0, one launch (start us, length us, event | category | flops | bytes accessed | tf_op | source)
XLA Modules:
  0.0 24.9 jit_solution(8055294847298040873)
XLA Ops:
  0.0 3.0 %collective-permute-start.3 = (bf16[512,256]{1,0:T(8,128)(2,1)}, bf16[512,256]{1,0:T(8,128)(2,1)S(1)}, u32[]{:S(2)}, u32[]{:S(2)}) collective-permute-start(bf16[512,256]{1,0:T(8,128)(2,1)} %q_ref.3), channel_id=1, source_target_pairs={{0,2},{1,3},{2,0},{3,1},{4,6},{5,7},{6,4},{7,5},{8,10},{9,11},{10,... | collective-permute-start | bytes 786440 | tf_op jit(solution)/shard_map/ppermute | solution.py:234
  3.0 2.0 %shard_map.82 = (f32[16,256]{1,0:T(8,128)S(1)}, f32[16,8,256]{2,1,0:T(8,128)S(1)}, f32[2,512,128]{2,1,0:T(8,128)S(1)}, f32[16,256]{1,0:T(8,128)S(1)}, f32[16,256...) custom-call(bf16[512,256]{1,0:T(8,128)(2,1)} %k_hbm.1, bf16[512,256]{1,0:T(8,128)(2,1)} %v_hbm.1, ...), custom_call_target="tpu_custom_call" | custom-call | tf_op jit(solution)/shard_map/pallas_call | solution.py:217
  5.0 1.6 %collective-permute-start = (f32[16,256]{1,0:T(8,128)S(1)}, f32[16,256]{1,0:T(8,128)S(1)}, u32[]{:S(2)}, u32[]{:S(2)}) collective-permute-start(f32[16,256]{1,0:T(8,128)S(1)} %get-tuple-element.30.own_ref.total_ref), channel_id=1, source_target_pairs={{0,8},{4,12},{8,0},{12,4},{16,24},{20,28},{24,16},{28,20},{1,9},{5... | collective-permute-start | bytes 49160 | tf_op jit(solution)/shard_map/ppermute | solution.py:239
  6.6 2.6 %collective-permute-start.1 = (f32[16,256]{1,0:T(8,128)S(1)}, f32[16,256]{1,0:T(8,128)S(1)}, u32[]{:S(2)}, u32[]{:S(2)}) collective-permute-start(f32[16,256]{1,0:T(8,128)S(1)} %get-tuple-element.30.own_ref.total_ref), channel_id=1, source_target_pairs={{0,16},{4,20},{8,24},{12,28},{16,0},{20,4},{24,8},{28,12},{1,17},{... | collective-permute-start | bytes 49160 | tf_op jit(solution)/shard_map/ppermute | solution.py:239
  9.2 0.2 collective-permute-start.2
  9.4 1.9 %shard_map.83 = (f32[2,512,128]{2,1,0:T(8,128)S(1)}, bf16[512,256]{1,0:T(8,128)(2,1)S(1)}) custom-call(f32[2,512,128]{2,1,0:T(8,128)S(1)} %get-tuple-element.24.gated, f32[16,256]{1,0:T(8,128)S(1)} %get-tuple-element.25.decay_ref.rates_ref, f32[16,256]{1,0:T(8,128)S(1)} %get-tuple-element.26.residue_ref, f32[1,256]{1,0:T(1,128)S(1)} %get-tuple-element.27.skip_ref, ...), custom_call_target="tpu_custom_call" | custom-call | tf_op jit(solution)/shard_map/pallas_call | solution.py:217
  11.3 0.4 %collective-permute-start.5 = (bf16[512,256]{1,0:T(8,128)(2,1)S(1)}, bf16[512,256]{1,0:T(8,128)(2,1)S(1)}, u32[]{:S(2)}, u32[]{:S(2)}) collective-permute-start(bf16[512,256]{1,0:T(8,128)(2,1)S(1)} %get-tuple-element.37), channel_id=1, source_target_pairs={{0,2},{1,3},{2,0},{3,1},{4,6},{5,7},{6,4},{7,5},{8,10},{9,11},{10,... | collective-permute-start | bytes 786440 | tf_op jit(solution)/shard_map/ppermute | solution.py:234
  11.7 0.0 collective-permute-done.rest_0_
  11.7 0.0 collective-permute-done.1.rest_1_
  11.7 3.1 %collective-permute-done.2.rest_2_ = f32[16,256]{1,0:T(8,128)S(1)} collective-permute-done((f32[16,256]{1,0:T(8,128)S(1)}, f32[16,256]{1,0:T(8,128)S(1)}, u32[]{:S(2)}, u32[]{:S(2)}) %collective-permute-start.2) | collective-permute-done | bytes 16416 | tf_op jit(solution)/shard_map/ppermute | solution.py:239
  14.8 0.0 collective-permute-done.3.q_ref
  14.8 0.6 %collective-permute-start.6 = (f32[32,256]{1,0:T(8,128)S(1)}, f32[32,256]{1,0:T(8,128)S(1)}, u32[]{:S(2)}, u32[]{:S(2)}) collective-permute-start(f32[32,256]{1,0:T(8,128)S(1)} %get-tuple-element.34.base_ref), channel_id=1, source_target_pairs={{0,2},{1,3},{2,0},{3,1},{4,6},{5,7},{6,4},{7,5},{8,10},{9,11},{10,... | collective-permute-start | bytes 98312 | tf_op jit(solution)/shard_map/ppermute | solution.py:234
  15.4 2.4 %collective-permute-start.7 = (f32[16,256]{1,0:T(8,128)S(1)}, f32[16,256]{1,0:T(8,128)S(1)}, u32[]{:S(2)}, u32[]{:S(2)}) collective-permute-start(f32[16,256]{1,0:T(8,128)S(1)} %get-tuple-element.35), channel_id=1, source_target_pairs={{0,6},{1,7},{2,4},{3,5},{4,2},{5,3},{6,0},{7,1},{8,14},{9,15},{10,... | collective-permute-start | bytes 49160 | tf_op jit(solution)/shard_map/ppermute | solution.py:245
  17.8 0.5 %collective-permute-start.4 = (f32[16,256]{1,0:T(8,128)S(1)}, f32[16,256]{1,0:T(8,128)S(1)}, u32[]{:S(2)}, u32[]{:S(2)}) collective-permute-start(f32[16,256]{1,0:T(8,128)S(1)} %get-tuple-element.35), channel_id=1, source_target_pairs={{0,4},{4,0},{8,12},{12,8},{16,20},{20,16},{24,28},{28,24},{1,5},{5... | collective-permute-start | bytes 49160 | tf_op jit(solution)/shard_map/ppermute | solution.py:239
  18.4 0.5 %collective-permute-done.5.local_ref = bf16[512,256]{1,0:T(8,128)(2,1)S(1)} collective-permute-done((bf16[512,256]{1,0:T(8,128)(2,1)S(1)}, bf16[512,256]{1,0:T(8,128)(2,1)S(1)}, u32[]{:S(2)}, u32[]{:S(2)}) %collective-permute-start.5) | collective-permute-done | bytes 262176 | tf_op jit(solution)/shard_map/ppermute | solution.py:234
  18.9 1.1 %collective-permute-done.7.extra_ref = f32[16,256]{1,0:T(8,128)S(1)} collective-permute-done((f32[16,256]{1,0:T(8,128)S(1)}, f32[16,256]{1,0:T(8,128)S(1)}, u32[]{:S(2)}, u32[]{:S(2)}) %collective-permute-start.7) | collective-permute-done | bytes 16416 | tf_op jit(solution)/shard_map/ppermute | solution.py:245
  20.0 0.0 collective-permute-done.6.base_ref
  20.0 0.4 %shard_map.85.rest_2_ = bf16[512,128]{1,0:T(8,128)(2,1)S(1)} custom-call(bf16[512,256]{1,0:T(8,128)(2,1)S(1)} %collective-permute-done.3.q_ref, bf16[512,256]{1,0:T(8,128)(2,1)S(1)} %collective-permute-done.5.local_ref, f32[32,256]{1,0:T(8,128)S(1)} %collective-permute-done.6.base_ref, f32[16,256]{1,0:T(8,128)S(1)} %collective-permute-done.7.extra_ref), custom_call_target="tpu_custom_call" | custom-call | flops 1500000000 | tf_op jit(solution)/shard_map/pallas_call | solution.py:217
  20.4 0.0 copy-start.1
  20.4 0.1 collective-permute-start.8
  20.5 0.4 %shard_map.86.rest_3_ = bf16[512,128]{1,0:T(8,128)(2,1)S(1)} custom-call(bf16[512,256]{1,0:T(8,128)(2,1)S(1)} %collective-permute-done.3.q_ref, bf16[512,256]{1,0:T(8,128)(2,1)S(1)} %collective-permute-done.5.local_ref, f32[32,256]{1,0:T(8,128)S(1)} %collective-permute-done.6.base_ref, f32[16,256]{1,0:T(8,128)S(1)} %collective-permute-done.7.extra_ref), custom_call_target="tpu_custom_call" | custom-call | flops 1500000000 | tf_op jit(solution)/shard_map/pallas_call | solution.py:217
  20.8 0.6 %collective-permute-start.9 = (bf16[512,128]{1,0:T(8,128)(2,1)S(1)}, bf16[512,128]{1,0:T(8,128)(2,1)S(1)}, u32[]{:S(2)}, u32[]{:S(2)}) collective-permute-start(bf16[512,128]{1,0:T(8,128)(2,1)S(1)} %shard_map.86.rest_3_), channel_id=1, source_target_pairs={{0,1},{1,0},{2,3},{3,2},{4,5},{5,4},{6,7},{7,6},{8,9},{9,8},{10,11... | collective-permute-start | bytes 393224 | tf_op jit(solution)/shard_map/ppermute | solution.py:234
  21.4 0.2 collective-permute-done.4.extra_ref
  21.6 0.0 copy-done.1
  21.6 0.4 %shard_map.87.rest_0_ = bf16[512,128]{1,0:T(8,128)(2,1)S(1)} custom-call(bf16[512,256]{1,0:T(8,128)(2,1)S(1)} %copy-done.1, f32[2,512,128]{2,1,0:T(8,128)S(1)} %get-tuple-element.29.local_ref, f32[32,256]{1,0:T(8,128)S(1)} %get-tuple-element.34.base_ref, f32[16,256]{1,0:T(8,128)S(1)} %collective-permute-done.4.extra_ref), custom_call_target="tpu_custom_call" | custom-call | flops 1500000000 | tf_op jit(solution)/shard_map/pallas_call | solution.py:217
  21.9 0.0 copy-start
  21.9 0.1 collective-permute-start.10
  22.0 0.4 %shard_map.88.rest_1_ = bf16[512,128]{1,0:T(8,128)(2,1)S(1)} custom-call(bf16[512,256]{1,0:T(8,128)(2,1)S(1)} %copy-done.1, f32[2,512,128]{2,1,0:T(8,128)S(1)} %get-tuple-element.29.local_ref, f32[32,256]{1,0:T(8,128)S(1)} %get-tuple-element.34.base_ref, f32[16,256]{1,0:T(8,128)S(1)} %collective-permute-done.4.extra_ref), custom_call_target="tpu_custom_call" | custom-call | flops 1500000000 | tf_op jit(solution)/shard_map/pallas_call | solution.py:217
  22.4 0.6 %collective-permute-start.11 = (bf16[512,128]{1,0:T(8,128)(2,1)S(1)}, bf16[512,128]{1,0:T(8,128)(2,1)S(1)}, u32[]{:S(2)}, u32[]{:S(2)}) collective-permute-start(bf16[512,128]{1,0:T(8,128)(2,1)S(1)} %shard_map.88.rest_1_), channel_id=1, source_target_pairs={{0,1},{1,0},{2,3},{3,2},{4,5},{5,4},{6,7},{7,6},{8,9},{9,8},{10,11... | collective-permute-start | bytes 393224 | tf_op jit(solution)/shard_map/ppermute | solution.py:234
  22.9 0.0 collective-permute-done.8.rest_4_
  22.9 0.0 collective-permute-done.9.rest_5_
  22.9 0.0 copy-done
  23.0 0.6 %shard_map.89.near_ref = f32[512,256]{1,0:T(8,128)S(1)} custom-call(bf16[1024,256]{1,0:T(8,128)(2,1)S(1)} %copy-done, f32[1,256]{1,0:T(1,128)S(1)} %get-tuple-element.23.bias_ref, bf16[512,128]{1,0:T(8,128)(2,1)S(1)} %shard_map.87.rest_0_, bf16[512,128]{1,0:T(8,128)(2,1)S(1)} %shard_map.88.rest_1_, bf16[512,128]{1,0:T(8,128)(2,1)S(1)} %shard_map.85.rest_2_, ...), custom_call_target="tpu_custom_call" | custom-call | flops 3000000000 | tf_op jit(solution)/shard_map/pallas_call | solution.py:217
  23.5 0.0 collective-permute-done.10.rest_0_
  23.5 0.4 %collective-permute-done.11.rest_1_ = bf16[512,128]{1,0:T(8,128)(2,1)S(1)} collective-permute-done((bf16[512,128]{1,0:T(8,128)(2,1)S(1)}, bf16[512,128]{1,0:T(8,128)(2,1)S(1)}, u32[]{:S(2)}, u32[]{:S(2)}) %collective-permute-start.11) | collective-permute-done | bytes 131104 | tf_op jit(solution)/shard_map/ppermute | solution.py:234
  23.9 1.0 %shard_map.90 = bf16[512,256]{1,0:T(8,128)(2,1)} custom-call(f32[512,256]{1,0:T(8,128)S(1)} %shard_map.89.near_ref, bf16[1024,256]{1,0:T(8,128)(2,1)S(1)} %copy-done, bf16[512,128]{1,0:T(8,128)(2,1)S(1)} %collective-permute-done.10.rest_0_, bf16[512,128]{1,0:T(8,128)(2,1)S(1)} %collective-permute-done.11.rest_1_), custom_call_target="tpu_custom_call" | custom-call | tf_op jit(solution)/shard_map/pallas_call | solution.py:217
  (1 shorter events, 0.0 us)
Async XLA Ops:
  0.0 14.8 %collective-permute-start.3 = (bf16[512,256]{1,0:T(8,128)(2,1)}, bf16[512,256]{1,0:T(8,128)(2,1)S(1)}, u32[]{:S(2)}, u32[]{:S(2)}) collective-permute-start(bf16[512,256]{1,0:T(8,128)(2,1)} %q_ref.3), channel_id=1, source_target_pairs={{0,2},{1,3},{2,0},{3,1},{4,6},{5,7},{6,4},{7,5},{8,10},{9,11},{10,... | collective-permute-start | bytes 786440 | tf_op jit(solution)/shard_map/ppermute | solution.py:234
  5.0 6.7 %collective-permute-start = (f32[16,256]{1,0:T(8,128)S(1)}, f32[16,256]{1,0:T(8,128)S(1)}, u32[]{:S(2)}, u32[]{:S(2)}) collective-permute-start(f32[16,256]{1,0:T(8,128)S(1)} %get-tuple-element.30.own_ref.total_ref), channel_id=1, source_target_pairs={{0,8},{4,12},{8,0},{12,4},{16,24},{20,28},{24,16},{28,20},{1,9},{5... | collective-permute-start | bytes 49160 | tf_op jit(solution)/shard_map/ppermute | solution.py:239
  6.6 5.1 %collective-permute-start.1 = (f32[16,256]{1,0:T(8,128)S(1)}, f32[16,256]{1,0:T(8,128)S(1)}, u32[]{:S(2)}, u32[]{:S(2)}) collective-permute-start(f32[16,256]{1,0:T(8,128)S(1)} %get-tuple-element.30.own_ref.total_ref), channel_id=1, source_target_pairs={{0,16},{4,20},{8,24},{12,28},{16,0},{20,4},{24,8},{28,12},{1,17},{... | collective-permute-start | bytes 49160 | tf_op jit(solution)/shard_map/ppermute | solution.py:239
  9.2 5.5 %collective-permute-start.2 = (f32[16,256]{1,0:T(8,128)S(1)}, f32[16,256]{1,0:T(8,128)S(1)}, u32[]{:S(2)}, u32[]{:S(2)}) collective-permute-start(f32[16,256]{1,0:T(8,128)S(1)} %get-tuple-element.30.own_ref.total_ref), channel_id=1, source_target_pairs={{0,24},{4,28},{8,16},{12,20},{16,8},{20,12},{24,0},{28,4},{1,25},{... | collective-permute-start | bytes 49160 | tf_op jit(solution)/shard_map/ppermute | solution.py:239
  11.3 7.6 %collective-permute-start.5 = (bf16[512,256]{1,0:T(8,128)(2,1)S(1)}, bf16[512,256]{1,0:T(8,128)(2,1)S(1)}, u32[]{:S(2)}, u32[]{:S(2)}) collective-permute-start(bf16[512,256]{1,0:T(8,128)(2,1)S(1)} %get-tuple-element.37), channel_id=1, source_target_pairs={{0,2},{1,3},{2,0},{3,1},{4,6},{5,7},{6,4},{7,5},{8,10},{9,11},{10,... | collective-permute-start | bytes 786440 | tf_op jit(solution)/shard_map/ppermute | solution.py:234
  14.8 5.2 %collective-permute-start.6 = (f32[32,256]{1,0:T(8,128)S(1)}, f32[32,256]{1,0:T(8,128)S(1)}, u32[]{:S(2)}, u32[]{:S(2)}) collective-permute-start(f32[32,256]{1,0:T(8,128)S(1)} %get-tuple-element.34.base_ref), channel_id=1, source_target_pairs={{0,2},{1,3},{2,0},{3,1},{4,6},{5,7},{6,4},{7,5},{8,10},{9,11},{10,... | collective-permute-start | bytes 98312 | tf_op jit(solution)/shard_map/ppermute | solution.py:234
  15.4 4.6 %collective-permute-start.7 = (f32[16,256]{1,0:T(8,128)S(1)}, f32[16,256]{1,0:T(8,128)S(1)}, u32[]{:S(2)}, u32[]{:S(2)}) collective-permute-start(f32[16,256]{1,0:T(8,128)S(1)} %get-tuple-element.35), channel_id=1, source_target_pairs={{0,6},{1,7},{2,4},{3,5},{4,2},{5,3},{6,0},{7,1},{8,14},{9,15},{10,... | collective-permute-start | bytes 49160 | tf_op jit(solution)/shard_map/ppermute | solution.py:245
  17.8 3.7 %collective-permute-start.4 = (f32[16,256]{1,0:T(8,128)S(1)}, f32[16,256]{1,0:T(8,128)S(1)}, u32[]{:S(2)}, u32[]{:S(2)}) collective-permute-start(f32[16,256]{1,0:T(8,128)S(1)} %get-tuple-element.35), channel_id=1, source_target_pairs={{0,4},{4,0},{8,12},{12,8},{16,20},{20,16},{24,28},{28,24},{1,5},{5... | collective-permute-start | bytes 49160 | tf_op jit(solution)/shard_map/ppermute | solution.py:239
  20.4 1.2 %copy-start.1 = (bf16[512,256]{1,0:T(8,128)(2,1)S(1)}, bf16[512,256]{1,0:T(8,128)(2,1)}, u32[]{:S(2)}) copy-start(bf16[512,256]{1,0:T(8,128)(2,1)} %q_ref.3) | copy-start | bytes 786436
  20.4 2.5 %collective-permute-start.8 = (bf16[512,128]{1,0:T(8,128)(2,1)S(1)}, bf16[512,128]{1,0:T(8,128)(2,1)S(1)}, u32[]{:S(2)}, u32[]{:S(2)}) collective-permute-start(bf16[512,128]{1,0:T(8,128)(2,1)S(1)} %shard_map.85.rest_2_), channel_id=1, source_target_pairs={{0,1},{1,0},{2,3},{3,2},{4,5},{5,4},{6,7},{7,6},{8,9},{9,8},{10,11... | collective-permute-start | bytes 393224 | tf_op jit(solution)/shard_map/ppermute | solution.py:234
  20.8 2.1 %collective-permute-start.9 = (bf16[512,128]{1,0:T(8,128)(2,1)S(1)}, bf16[512,128]{1,0:T(8,128)(2,1)S(1)}, u32[]{:S(2)}, u32[]{:S(2)}) collective-permute-start(bf16[512,128]{1,0:T(8,128)(2,1)S(1)} %shard_map.86.rest_3_), channel_id=1, source_target_pairs={{0,1},{1,0},{2,3},{3,2},{4,5},{5,4},{6,7},{7,6},{8,9},{9,8},{10,11... | collective-permute-start | bytes 393224 | tf_op jit(solution)/shard_map/ppermute | solution.py:234
  21.9 1.0 %copy-start = (bf16[1024,256]{1,0:T(8,128)(2,1)S(1)}, bf16[1024,256]{1,0:T(8,128)(2,1)}, u32[]{:S(2)}) copy-start(bf16[1024,256]{1,0:T(8,128)(2,1)} %weight_ref.3) | copy-start | bytes 1572868
  21.9 1.6 %collective-permute-start.10 = (bf16[512,128]{1,0:T(8,128)(2,1)S(1)}, bf16[512,128]{1,0:T(8,128)(2,1)S(1)}, u32[]{:S(2)}, u32[]{:S(2)}) collective-permute-start(bf16[512,128]{1,0:T(8,128)(2,1)S(1)} %shard_map.87.rest_0_), channel_id=1, source_target_pairs={{0,1},{1,0},{2,3},{3,2},{4,5},{5,4},{6,7},{7,6},{8,9},{9,8},{10,11... | collective-permute-start | bytes 393224 | tf_op jit(solution)/shard_map/ppermute | solution.py:234
  22.4 1.5 %collective-permute-start.11 = (bf16[512,128]{1,0:T(8,128)(2,1)S(1)}, bf16[512,128]{1,0:T(8,128)(2,1)S(1)}, u32[]{:S(2)}, u32[]{:S(2)}) collective-permute-start(bf16[512,128]{1,0:T(8,128)(2,1)S(1)} %shard_map.88.rest_1_), channel_id=1, source_target_pairs={{0,1},{1,0},{2,3},{3,2},{4,5},{5,4},{6,7},{7,6},{8,9},{9,8},{10,11... | collective-permute-start | bytes 393224 | tf_op jit(solution)/shard_map/ppermute | solution.py:234

commit v2 on v1

--- a/solution.py
+++ b/solution.py
@@ -10,9 +10,10 @@
 LANES = 128
 SUBLANES = 8
 STORES = 2
-FOLD_COST = 3000000000
-NEAR_COST = 3000000000
-PART_COST = 1500000000
+FOLD_COST = 1000000000
+TREE_COST = 3000000000
+PIECES = 3
+PART_COST = 4000000000
 VMEM_LIMIT = 32 * 1024 * 1024
 
 
@@ -102,54 +103,56 @@
             return state
 
         lax.fori_loop(0, chunk_len, step, tuple(start), unroll=4)
-        short_ref[:, lanes] = local_ref[part].astype(short_ref.dtype)
-
-
-def fold(rates, inner, total, received, stride, seg_len):
-    place = lax.div(lax.axis_index("seq"), 2)
-    radix = len(received) + 1
-    spot = lax.rem(lax.div(place, stride), radix)
-    offset = lax.rem(place, stride)
-
-    def decayed(segments):
-        return jnp.exp(-rates * (segments * 2 * seg_len).astype(jnp.float32))
-
-    before = jnp.zeros_like(rates)
-    whole = decayed((radix - 1 - spot) * stride) * total
+        short_ref[: local_ref.shape[1], lanes] = local_ref[part].astype(short_ref.dtype)
+    left = decay_ref[...]
+    for first in range(local_ref.shape[1], short_ref.shape[0], modes):
+        piece = left.astype(short_ref.dtype)
+        short_ref[first : first + modes, :] = piece
+        left = left - piece.astype(jnp.float32)
+
+
+def tree_step(rates, before, received, seg_len):
+    reach = len(received)
+    spot = lax.rem(lax.div(lax.axis_index("seq"), 2), 2 * reach)
     for i, block in enumerate(received):
-        source = spot ^ (i + 1)
-        past = source < spot
-        gap = jnp.where(past, spot - 1 - source, 0) * stride
-        before += jnp.where(past, decayed(gap) * block, 0.0)
-        whole += decayed((radix - 1 - source) * stride) * block
-    return inner + decayed(offset) * before, whole
-
-
-def fold_kernel(stride, seg_len, rates_ref, total_ref, *rest):
-    inner, rest = (rest[0][...], rest[1:]) if stride > 1 else (0.0, rest)
-    received, (inner_out, total_out) = [ref[...] for ref in rest[:-2]], rest[-2:]
-    inner_out[...], total_out[...] = fold(
-        rates_ref[...], inner, total_ref[...], received, stride, seg_len
-    )
-
-
-def share_kernel(stride, seg_len, rates_ref, residue_ref, own_ref, total_ref, *rest):
-    inner, rest = (rest[0][...], rest[1:]) if stride > 1 else (0.0, rest)
+        weight = jnp.exp(-rates * float(2 * seg_len * i))
+        before = before + jnp.where(spot == reach + i, weight * block, 0.0)
+    return before
+
+
+def fold_kernel(seg_len, rates_ref, own_ref, *rest):
+    received, (before_ref, total_ref) = [ref[...] for ref in rest[:-2]], rest[-2:]
+    before, received = (received[0], received[1:]) if len(received) > 1 else (0.0, received)
+    rates = rates_ref[...]
+    before = tree_step(rates, before, received, seg_len)
+    before_ref[...] = before
+    total_ref[...] = own_ref[...] + jnp.exp(-rates * float(2 * seg_len)) * before
+
+
+def share_kernel(seg_len, rates_ref, residue_ref, own_ref, before_ref, *rest):
     received, (base_ref, extra_ref) = [ref[...] for ref in rest[:-2]], rest[-2:]
-    modes = rates_ref.shape[0]
-    rates = rates_ref[...]
-    before, _ = fold(rates, inner, total_ref[...], received, stride, seg_len)
-    before *= residue_ref[...]
+    rates, residue = rates_ref[...], residue_ref[...]
+    before = residue * tree_step(rates, before_ref[...], received, seg_len)
     step = jnp.exp(-rates * float(seg_len))
     even = lax.rem(lax.axis_index("seq"), 2) == 0
-    base_ref[:modes, :] = step * before
-    base_ref[modes:, :] = rates
-    extra_ref[...] = jnp.where(even, residue_ref[...] * own_ref[...] + step * step * before, before)
-
-
-def carry_kernel(first, q_ref, local_ref, base_ref, extra_ref, out_ref):
+    base_ref[...] = step * before
+    extra_ref[...] = jnp.where(even, residue * own_ref[...] + step * step * before, before)
+
+
+def read_rates(rates_ref, modes):
+    if rates_ref.shape[0] == modes:
+        return rates_ref[...]
+    count = rates_ref.shape[0] // modes
+    pieces = [rates_ref[i * modes : (i + 1) * modes, :].astype(jnp.float32) for i in range(count)]
+    return (pieces[2] + pieces[1]) + pieces[0]
+
+
+def carry_kernel(first, q_ref, local_ref, rates_ref, base_ref, extra_ref, out_ref):
     modes = extra_ref.shape[0]
     seg_len = q_ref.shape[0]
+    if rates_ref is None:
+        rates_ref = local_ref.at[pl.ds(seg_len, PIECES * modes), :]
+    rates = read_rates(rates_ref, modes)
     block = 2 * SUBLANES
     ahead = (lax.broadcasted_iota(jnp.int32, (SUBLANES, LANES), 0) + 1).astype(jnp.float32)
     for index in range(out_ref.shape[1] // LANES):
@@ -157,7 +160,7 @@
         lanes = lane_slice(part)
         factor, start = [], []
         for n in range(modes):
-            rate = row(base_ref, modes + n, part)
+            rate = rates[n : n + 1, lanes]
             weight = row(base_ref, n, part) + row(extra_ref, n, part)
             start.append(weight * jnp.exp(-rate * ahead))
             factor.append(full(jnp.exp(-rate * SUBLANES)))
@@ -174,6 +177,10 @@
             return state
 
         lax.fori_loop(0, seg_len // block, step, tuple(start), unroll=4)
+
+
+def across_kernel(first, q_ref, local_ref, base_ref, extra_ref, out_ref):
+    carry_kernel(first, q_ref, local_ref, None, base_ref, extra_ref, out_ref)
 
 
 def project(blocks, weight_ref):
@@ -189,23 +196,22 @@
     return total
 
 
-def near_kernel(weight_ref, bias_ref, *rest):
-    blocks, out_ref = rest[:-1], rest[-1]
+def near_kernel(weight_ref, bias_ref, own_ref, pair_ref, *rest):
+    across, out_ref = rest[:-1], rest[-1]
     rank = lax.axis_index("chan")
-    parts = len(blocks) // 3
-    blocks = [(rank ^ bit, blocks[i * parts : (i + 1) * parts]) for i, bit in enumerate((0, 2, 3))]
+    blocks = [(rank, [own_ref]), (rank ^ 1, [pair_ref]), (rank ^ 2, across)]
     out_ref[...] = project(blocks, weight_ref) + bias_ref[...]
 
 
 def last_kernel(near_ref, weight_ref, *rest):
-    pair, (out_hbm, out_ref, sems) = rest[:-3], rest[-3:]
+    diagonal, (out_hbm, out_ref, sems) = rest[:-3], rest[-3:]
     rank = lax.axis_index("chan")
     pieces = sems.shape[0]
     size = out_ref.shape[0] // pieces
     copies = []
     for i in range(pieces):
         rows = pl.ds(i * size, size)
-        total = near_ref[rows, :] + project([(rank ^ 1, [ref.at[rows, :] for ref in pair])], weight_ref)
+        total = near_ref[rows, :] + project([(rank ^ 3, [ref.at[rows, :] for ref in diagonal])], weight_ref)
         out_ref[rows, :] = total.astype(out_ref.dtype)
         copies.append(pltpu.make_async_copy(out_ref.at[rows], out_hbm.at[rows], sems.at[i]))
         copies[-1].start()
@@ -234,9 +240,22 @@
     return lax.ppermute(value, "chan", [(r, r ^ bit) for r in range(count)])
 
 
-def beside(value, step):
+def beside(value):
     count = lax.axis_size("seq")
-    return lax.ppermute(value, "seq", [(r, r ^ step) for r in range(count)])
+    return lax.ppermute(value, "seq", [(r, r ^ 1) for r in range(count)])
+
+
+def tree_sends(value, reach):
+    count = lax.axis_size("seq")
+    received = []
+    for i in reversed(range(reach)):
+        target = list(range(count))
+        for r in range(count):
+            if r // 2 % (2 * reach) == reach - 1:
+                other = r + 2 * (i + 1)
+                target[r], target[other] = other, r
+        received.append(lax.ppermute(value, "seq", list(enumerate(target))))
+    return received[::-1]
 
 
 def corner(value, step, bit):
@@ -245,22 +264,21 @@
     return lax.ppermute(value, ("seq", "chan"), pairs)
 
 
-def carry_shares(total, decay, residue, seg_len, also):
+def carry_shares(own, decay, residue, seg_len, also):
     count = lax.axis_size("seq") // 2
-    shape = struct(total.shape)
-    own, inner, stride = total, (), 1
-    while True:
-        radix = min(4, count // stride)
-        received = [beside(total, 2 * stride * step) for step in range(1, radix)]
-        if stride * radix == count:
-            break
-        kernel = functools.partial(fold_kernel, stride, seg_len)
-        *inner, total = call(kernel, [shape, shape], decay, total, *inner, *received)
-        stride *= radix
-    received, also = lax.optimization_barrier((received, also))
-    kernel = functools.partial(share_kernel, stride, seg_len)
-    outs = [struct((2 * total.shape[0], total.shape[1])), shape]
-    base, extra = call(kernel, outs, decay, residue, own, total, *inner, *received, cost=FOLD_COST)
+    shape = struct(own.shape)
+    total, before, reach = own, (), 1
+    while 2 * reach < count:
+        received = tree_sends(total, reach)
+        before, total = call(
+            functools.partial(fold_kernel, seg_len), [shape, shape], decay, own, *before, *received, cost=TREE_COST
+        )
+        before, reach = (before,), 2 * reach
+    received, also = lax.optimization_barrier((tree_sends(total, reach), also))
+    base, extra = call(
+        functools.partial(share_kernel, seg_len), [shape, shape], decay, residue, own, *before, *received,
+        cost=FOLD_COST,
+    )
     return base, extra, also
 
 
@@ -271,6 +289,7 @@
     parts = channels // LANES
     tall = pltpu.VMEM((seg_len, channels), jnp.bfloat16)
     short = struct((seg_len, channels), jnp.bfloat16)
+    taller = struct((seg_len + PIECES * modes, channels), jnp.bfloat16)
     q_across = swapped(q_gate, 2)
     inputs = (k_gate, value, decay, residue, skip.reshape(1, -1), out_bias.reshape(1, -1))
     total, chunks, gated, decay, residue, skip, bias = call(
@@ -289,31 +308,27 @@
         ins=pltpu.HBM,
     )
     local, local_short = call(
-        local_kernel, [struct((parts, seg_len, LANES)), short], gated, decay, residue, skip, chunks
+        local_kernel, [struct((parts, seg_len, LANES)), taller], gated, decay, residue, skip, chunks
     )
     local_across = swapped(local_short, 2)
     base, extra, q_across = carry_shares(total, decay, residue, seg_len, q_across)
+    extra_beside = beside(extra)
     extra_corner = corner(extra, 1, 2)
-    extra_beside = beside(extra, 1)
     base_across = swapped(base, 2)
+    own = call(functools.partial(carry_kernel, 0), short, q_gate, local, decay, base, extra_beside)
+    pair = swapped(own, 1)
     half = struct((seg_len, LANES), jnp.bfloat16)
     across = [
         call(
-            functools.partial(carry_kernel, part), half, q_across, local_across, base_across, extra_corner,
+            functools.partial(across_kernel, part), half, q_across, local_across, base_across, extra_corner,
             cost=PART_COST,
         )
         for part in range(parts)
     ]
     diagonal = [swapped(block, 1) for block in across]
-    (extra_beside, *across) = lax.optimization_barrier((extra_beside, *across))
-    own = [
-        call(functools.partial(carry_kernel, part), half, q_gate, local, base, extra_beside, cost=PART_COST)
-        for part in range(parts)
-    ]
-    pair = [swapped(block, 1) for block in own]
-    near = call(near_kernel, struct((seg_len, cols)), out_weight, bias, *own, *across, *diagonal, cost=NEAR_COST)
+    near = call(near_kernel, struct((seg_len, cols)), out_weight, bias, own, pair, *across)
     return call(
-        last_kernel, struct((seg_len, cols), jnp.bfloat16), near, out_weight, *pair,
+        last_kernel, struct((seg_len, cols), jnp.bfloat16), near, out_weight, *diagonal,
         scratch=[pltpu.VMEM((seg_len, cols), jnp.bfloat16), pltpu.SemaphoreType.DMA((STORES,))],
         outs=pltpu.HBM,
     )

time: 25.2 us -> 29.6 us (1.17)
  the two profiles are of different devices: /device:TPU:0 before, /device:TPU:9 now
where the time goes in v2:
time: 29.6 us; the launch traced here: 29.4 us
  starting transfers between devices  18 us (61%)
  Pallas kernels  6.92 us (23%)
  waiting for transfers between devices  4.33 us (15%)
    ppermute x6, starting transfers between devices, swapped(): return lax.ppermute(value, 'chan', [(r, r ^ bit) for r in range(count)])  10.1 us
    pallas_call x9, Pallas kernels, call(): pl.pallas_call(kernel, out_shape=out, in_specs=[pl.BlockSpec(memory_space...  6.92 us
    ppermute x3, starting transfers between devices, tree_sends(): received.append(lax.ppermute(value, 'seq', list(enumerate(target))))  6.41 us
    ppermute x3, waiting for transfers between devices, tree_sends(): received.append(lax.ppermute(value, 'seq', list(enumerate(target))))  3.45 us
    ppermute x1, starting transfers between devices, beside(): return lax.ppermute(value, 'seq', [(r, r ^ 1) for r in range(count)])  1.28 us
    ppermute x6, waiting for transfers between devices, swapped(): return lax.ppermute(value, 'chan', [(r, r ^ bit) for r in range(count)])  0.87 us
  transfers between devices with their start and end apart: 11, of which 3 were waited for; matrix products, arithmetic and copies ran while one was open for 0% of the time, Pallas kernels for 13%

profile of v2, /device:TPU:9, one launch (start us, length us, event | category | flops | bytes accessed | tf_op | source)
XLA Modules:
  0.0 29.4 jit_solution(5260231073341124686)
XLA Ops:
  0.0 0.0 copy-start.1
  0.0 2.1 %shard_map.82 = (f32[16,256]{1,0:T(8,128)S(1)}, f32[16,8,256]{2,1,0:T(8,128)S(1)}, f32[2,512,128]{2,1,0:T(8,128)S(1)}, f32[16,256]{1,0:T(8,128)S(1)}, f32[16,256...) custom-call(bf16[512,256]{1,0:T(8,128)(2,1)} %k_hbm.1, bf16[512,256]{1,0:T(8,128)(2,1)} %v_hbm.1, ...), custom_call_target="tpu_custom_call" | custom-call | tf_op jit(solution)/shard_map/pallas_call | solution.py:223
  2.1 0.1 collective-permute-start
  2.1 0.0 copy-done.1
  2.2 1.4 %collective-permute-start.3 = (bf16[512,256]{1,0:T(8,128)(2,1)S(1)}, bf16[512,256]{1,0:T(8,128)(2,1)S(1)}, u32[]{:S(2)}, u32[]{:S(2)}) collective-permute-start(bf16[512,256]{1,0:T(8,128)(2,1)S(1)} %copy-done.1), channel_id=1, source_target_pairs={{0,2},{1,3},{2,0},{3,1},{4,6},{5,7},{6,4},{7,5},{8,10},{9,11},{10,... | collective-permute-start | bytes 786440 | tf_op jit(solution)/shard_map/ppermute | solution.py:240
  3.5 1.9 %shard_map.83 = (f32[2,512,128]{2,1,0:T(8,128)S(1)}, bf16[560,256]{1,0:T(8,128)(2,1)S(1)}) custom-call(f32[2,512,128]{2,1,0:T(8,128)S(1)} %get-tuple-element.22.gated, f32[16,256]{1,0:T(8,128)S(1)} %get-tuple-element.23.decay_ref.rates_ref, f32[16,256]{1,0:T(8,128)S(1)} %get-tuple-element.24.residue_ref, f32[1,256]{1,0:T(1,128)S(1)} %get-tuple-element.25.skip_ref, ...), custom_call_target="tpu_custom_call" | custom-call | tf_op jit(solution)/shard_map/pallas_call | solution.py:223
  5.4 0.2 collective-permute-start.6
  5.6 0.0 collective-permute-done.rest_0_
  5.7 4.4 %collective-permute-start.1 = (f32[16,256]{1,0:T(8,128)S(1)}, f32[16,256]{1,0:T(8,128)S(1)}, u32[]{:S(2)}, u32[]{:S(2)}) collective-permute-start(f32[16,256]{1,0:T(8,128)S(1)} %get-tuple-element.30), channel_id=1, source_target_pairs={{0,0},{4,4},{8,16},{12,20},{16,8},{20,12},{24,24},{28,28},{1,1},{5... | collective-permute-start | bytes 49160 | tf_op jit(solution)/shard_map/ppermute | solution.py:257
  10.1 1.9 %collective-permute-start.2 = (f32[16,256]{1,0:T(8,128)S(1)}, f32[16,256]{1,0:T(8,128)S(1)}, u32[]{:S(2)}, u32[]{:S(2)}) collective-permute-start(f32[16,256]{1,0:T(8,128)S(1)} %get-tuple-element.30), channel_id=1, source_target_pairs={{0,0},{4,4},{8,24},{12,28},{16,16},{20,20},{24,8},{28,12},{1,1},{5... | collective-permute-start | bytes 49160 | tf_op jit(solution)/shard_map/ppermute | solution.py:257
  12.0 0.0 collective-permute-done.1.rest_0_
  12.0 3.4 %collective-permute-done.2.rest_1_ = f32[16,256]{1,0:T(8,128)S(1)} collective-permute-done((f32[16,256]{1,0:T(8,128)S(1)}, f32[16,256]{1,0:T(8,128)S(1)}, u32[]{:S(2)}, u32[]{:S(2)}) %collective-permute-start.2) | collective-permute-done | bytes 16416 | tf_op jit(solution)/shard_map/ppermute | solution.py:257
  15.5 0.0 collective-permute-done.3.q_ref
  15.5 1.3 %collective-permute-start.4 = (f32[16,256]{1,0:T(8,128)S(1)}, f32[16,256]{1,0:T(8,128)S(1)}, u32[]{:S(2)}, u32[]{:S(2)}) collective-permute-start(f32[16,256]{1,0:T(8,128)S(1)} %get-tuple-element.34), channel_id=1, source_target_pairs={{0,4},{4,0},{8,12},{12,8},{16,20},{20,16},{24,28},{28,24},{1,5},{5... | collective-permute-start | bytes 49160 | tf_op jit(solution)/shard_map/ppermute | solution.py:245
  16.8 1.2 %collective-permute-start.7 = (f32[16,256]{1,0:T(8,128)S(1)}, f32[16,256]{1,0:T(8,128)S(1)}, u32[]{:S(2)}, u32[]{:S(2)}) collective-permute-start(f32[16,256]{1,0:T(8,128)S(1)} %get-tuple-element.33.base_ref), channel_id=1, source_target_pairs={{0,2},{1,3},{2,0},{3,1},{4,6},{5,7},{6,4},{7,5},{8,10},{9,11},{10,... | collective-permute-start | bytes 49160 | tf_op jit(solution)/shard_map/ppermute | solution.py:240
  18.0 0.2 collective-permute-start.8
  18.2 0.0 collective-permute-done.4.extra_ref
  18.2 0.8 %shard_map.86.own_ref = bf16[512,256]{1,0:T(8,128)(2,1)S(1)} custom-call(bf16[512,256]{1,0:T(8,128)(2,1)S(1)} %copy-done.1, f32[2,512,128]{2,1,0:T(8,128)S(1)} %get-tuple-element.27.local_ref, f32[16,256]{1,0:T(8,128)S(1)} %get-tuple-element.23.decay_ref.rates_ref, f32[16,256]{1,0:T(8,128)S(1)} %get-tuple-element.33.base_ref, ...), custom_call_target="tpu_custom_call" | custom-call | tf_op jit(solution)/shard_map/pallas_call | solution.py:223
  19.0 4.1 %collective-permute-start.5 = (bf16[512,256]{1,0:T(8,128)(2,1)S(1)}, bf16[512,256]{1,0:T(8,128)(2,1)S(1)}, u32[]{:S(2)}, u32[]{:S(2)}) collective-permute-start(bf16[512,256]{1,0:T(8,128)(2,1)S(1)} %shard_map.86.own_ref), channel_id=1, source_target_pairs={{0,1},{1,0},{2,3},{3,2},{4,5},{5,4},{6,7},{7,6},{8,9},{9,8},{10,11... | collective-permute-start | bytes 786440 | tf_op jit(solution)/shard_map/ppermute | solution.py:240
  23.1 0.0 collective-permute-done.7.base_ref
  23.1 0.0 collective-permute-done.8.extra_ref
  23.1 0.0 collective-permute-done.6.local_ref
  23.1 0.4 %shard_map.87.rest_0_ = bf16[512,128]{1,0:T(8,128)(2,1)S(1)} custom-call(bf16[512,256]{1,0:T(8,128)(2,1)S(1)} %collective-permute-done.3.q_ref, bf16[560,256]{1,0:T(8,128)(2,1)S(1)} %collective-permute-done.6.local_ref, f32[16,256]{1,0:T(8,128)S(1)} %collective-permute-done.7.base_ref, f32[16,256]{1,0:T(8,128)S(1)} %collective-permute-done.8.extra_ref), custom_call_target="tpu_custom_call" | custom-call | flops 4000000000 | tf_op jit(solution)/shard_map/pallas_call | solution.py:223
  23.5 0.0 copy-start
  23.5 3.1 %collective-permute-start.9 = (bf16[512,128]{1,0:T(8,128)(2,1)S(1)}, bf16[512,128]{1,0:T(8,128)(2,1)S(1)}, u32[]{:S(2)}, u32[]{:S(2)}) collective-permute-start(bf16[512,128]{1,0:T(8,128)(2,1)S(1)} %shard_map.87.rest_0_), channel_id=1, source_target_pairs={{0,1},{1,0},{2,3},{3,2},{4,5},{5,4},{6,7},{7,6},{8,9},{9,8},{10,11... | collective-permute-start | bytes 393224 | tf_op jit(solution)/shard_map/ppermute | solution.py:240
  26.6 0.4 %shard_map.88.rest_1_ = bf16[512,128]{1,0:T(8,128)(2,1)S(1)} custom-call(bf16[512,256]{1,0:T(8,128)(2,1)S(1)} %collective-permute-done.3.q_ref, bf16[560,256]{1,0:T(8,128)(2,1)S(1)} %collective-permute-done.6.local_ref, f32[16,256]{1,0:T(8,128)S(1)} %collective-permute-done.7.base_ref, f32[16,256]{1,0:T(8,128)S(1)} %collective-permute-done.8.extra_ref), custom_call_target="tpu_custom_call" | custom-call | flops 4000000000 | tf_op jit(solution)/shard_map/pallas_call | solution.py:223
  27.0 0.1 collective-permute-start.10
  27.1 0.0 collective-permute-done.5.pair_ref
  27.1 0.0 copy-done
  27.1 0.4 %shard_map.89.near_ref = f32[512,256]{1,0:T(8,128)S(1)} custom-call(bf16[1024,256]{1,0:T(8,128)(2,1)S(1)} %copy-done, f32[1,256]{1,0:T(1,128)S(1)} %get-tuple-element.21.bias_ref, bf16[512,256]{1,0:T(8,128)(2,1)S(1)} %shard_map.86.own_ref, bf16[512,256]{1,0:T(8,128)(2,1)S(1)} %collective-permute-done.5.pair_ref, bf16[512,128]{1,0:T(8,128)(2,1)S(1)} %shard_map.87.rest_0_, ...), custom_call_target="tpu_custom_call" | custom-call | tf_op jit(solution)/shard_map/pallas_call | solution.py:223
  27.5 0.1 collective-permute-done.9.rest_0_
  27.6 0.8 %collective-permute-done.10.rest_1_ = bf16[512,128]{1,0:T(8,128)(2,1)S(1)} collective-permute-done((bf16[512,128]{1,0:T(8,128)(2,1)S(1)}, bf16[512,128]{1,0:T(8,128)(2,1)S(1)}, u32[]{:S(2)}, u32[]{:S(2)}) %collective-permute-start.10) | collective-permute-done | bytes 131104 | tf_op jit(solution)/shard_map/ppermute | solution.py:240
  28.4 1.0 %shard_map.90 = bf16[512,256]{1,0:T(8,128)(2,1)} custom-call(f32[512,256]{1,0:T(8,128)S(1)} %shard_map.89.near_ref, bf16[1024,256]{1,0:T(8,128)(2,1)S(1)} %copy-done, bf16[512,128]{1,0:T(8,128)(2,1)S(1)} %collective-permute-done.9.rest_0_, bf16[512,128]{1,0:T(8,128)(2,1)S(1)} %collective-permute-done.10.rest_1_), custom_call_target="tpu_custom_call" | custom-call | tf_op jit(solution)/shard_map/pallas_call | solution.py:223
  (2 shorter events, 0.0 us)
Async XLA Ops:
  0.0 2.1 %copy-start.1 = (bf16[512,256]{1,0:T(8,128)(2,1)S(1)}, bf16[512,256]{1,0:T(8,128)(2,1)}, u32[]{:S(2)}) copy-start(bf16[512,256]{1,0:T(8,128)(2,1)} %q_ref.1) | copy-start | bytes 786436
  2.1 3.6 %collective-permute-start = (f32[16,256]{1,0:T(8,128)S(1)}, f32[16,256]{1,0:T(8,128)S(1)}, u32[]{:S(2)}, u32[]{:S(2)}) collective-permute-start(f32[16,256]{1,0:T(8,128)S(1)} %get-tuple-element.28.own_ref), channel_id=1, source_target_pairs={{0,8},{4,12},{8,0},{12,4},{16,24},{20,28},{24,16},{28,20},{1,9},{5... | collective-permute-start | bytes 49160 | tf_op jit(solution)/shard_map/ppermute | solution.py:257
  2.2 13.3 %collective-permute-start.3 = (bf16[512,256]{1,0:T(8,128)(2,1)S(1)}, bf16[512,256]{1,0:T(8,128)(2,1)S(1)}, u32[]{:S(2)}, u32[]{:S(2)}) collective-permute-start(bf16[512,256]{1,0:T(8,128)(2,1)S(1)} %copy-done.1), channel_id=1, source_target_pairs={{0,2},{1,3},{2,0},{3,1},{4,6},{5,7},{6,4},{7,5},{8,10},{9,11},{10,... | collective-permute-start | bytes 786440 | tf_op jit(solution)/shard_map/ppermute | solution.py:240
  5.4 17.7 %collective-permute-start.6 = (bf16[560,256]{1,0:T(8,128)(2,1)S(1)}, bf16[560,256]{1,0:T(8,128)(2,1)S(1)}, u32[]{:S(2)}, u32[]{:S(2)}) collective-permute-start(bf16[560,256]{1,0:T(8,128)(2,1)S(1)} %get-tuple-element.36), channel_id=1, source_target_pairs={{0,2},{1,3},{2,0},{3,1},{4,6},{5,7},{6,4},{7,5},{8,10},{9,11},{10,... | collective-permute-start | bytes 860168 | tf_op jit(solution)/shard_map/ppermute | solution.py:240
  5.7 6.4 %collective-permute-start.1 = (f32[16,256]{1,0:T(8,128)S(1)}, f32[16,256]{1,0:T(8,128)S(1)}, u32[]{:S(2)}, u32[]{:S(2)}) collective-permute-start(f32[16,256]{1,0:T(8,128)S(1)} %get-tuple-element.30), channel_id=1, source_target_pairs={{0,0},{4,4},{8,16},{12,20},{16,8},{20,12},{24,24},{28,28},{1,1},{5... | collective-permute-start | bytes 49160 | tf_op jit(solution)/shard_map/ppermute | solution.py:257
  10.1 5.4 %collective-permute-start.2 = (f32[16,256]{1,0:T(8,128)S(1)}, f32[16,256]{1,0:T(8,128)S(1)}, u32[]{:S(2)}, u32[]{:S(2)}) collective-permute-start(f32[16,256]{1,0:T(8,128)S(1)} %get-tuple-element.30), channel_id=1, source_target_pairs={{0,0},{4,4},{8,24},{12,28},{16,16},{20,20},{24,8},{28,12},{1,1},{5... | collective-permute-start | bytes 49160 | tf_op jit(solution)/shard_map/ppermute | solution.py:257
  15.5 2.7 %collective-permute-start.4 = (f32[16,256]{1,0:T(8,128)S(1)}, f32[16,256]{1,0:T(8,128)S(1)}, u32[]{:S(2)}, u32[]{:S(2)}) collective-permute-start(f32[16,256]{1,0:T(8,128)S(1)} %get-tuple-element.34), channel_id=1, source_target_pairs={{0,4},{4,0},{8,12},{12,8},{16,20},{20,16},{24,28},{28,24},{1,5},{5... | collective-permute-start | bytes 49160 | tf_op jit(solution)/shard_map/ppermute | solution.py:245
  16.8 6.3 %collective-permute-start.7 = (f32[16,256]{1,0:T(8,128)S(1)}, f32[16,256]{1,0:T(8,128)S(1)}, u32[]{:S(2)}, u32[]{:S(2)}) collective-permute-start(f32[16,256]{1,0:T(8,128)S(1)} %get-tuple-element.33.base_ref), channel_id=1, source_target_pairs={{0,2},{1,3},{2,0},{3,1},{4,6},{5,7},{6,4},{7,5},{8,10},{9,11},{10,... | collective-permute-start | bytes 49160 | tf_op jit(solution)/shard_map/ppermute | solution.py:240
  18.0 5.1 %collective-permute-start.8 = (f32[16,256]{1,0:T(8,128)S(1)}, f32[16,256]{1,0:T(8,128)S(1)}, u32[]{:S(2)}, u32[]{:S(2)}) collective-permute-start(f32[16,256]{1,0:T(8,128)S(1)} %get-tuple-element.34), channel_id=1, source_target_pairs={{0,6},{1,7},{2,4},{3,5},{4,2},{5,3},{6,0},{7,1},{8,14},{9,15},{10,... | collective-permute-start | bytes 49160 | tf_op jit(solution)/shard_map/ppermute | solution.py:264
  19.0 8.0 %collective-permute-start.5 = (bf16[512,256]{1,0:T(8,128)(2,1)S(1)}, bf16[512,256]{1,0:T(8,128)(2,1)S(1)}, u32[]{:S(2)}, u32[]{:S(2)}) collective-permute-start(bf16[512,256]{1,0:T(8,128)(2,1)S(1)} %shard_map.86.own_ref), channel_id=1, source_target_pairs={{0,1},{1,0},{2,3},{3,2},{4,5},{5,4},{6,7},{7,6},{8,9},{9,8},{10,11... | collective-permute-start | bytes 786440 | tf_op jit(solution)/shard_map/ppermute | solution.py:240
  23.5 3.6 %copy-start = (bf16[1024,256]{1,0:T(8,128)(2,1)S(1)}, bf16[1024,256]{1,0:T(8,128)(2,1)}, u32[]{:S(2)}) copy-start(bf16[1024,256]{1,0:T(8,128)(2,1)} %weight_ref.3) | copy-start | bytes 1572868
  23.5 4.1 %collective-permute-start.9 = (bf16[512,128]{1,0:T(8,128)(2,1)S(1)}, bf16[512,128]{1,0:T(8,128)(2,1)S(1)}, u32[]{:S(2)}, u32[]{:S(2)}) collective-permute-start(bf16[512,128]{1,0:T(8,128)(2,1)S(1)} %shard_map.87.rest_0_), channel_id=1, source_target_pairs={{0,1},{1,0},{2,3},{3,2},{4,5},{5,4},{6,7},{7,6},{8,9},{9,8},{10,11... | collective-permute-start | bytes 393224 | tf_op jit(solution)/shard_map/ppermute | solution.py:240
  27.0 1.4 %collective-permute-start.10 = (bf16[512,128]{1,0:T(8,128)(2,1)S(1)}, bf16[512,128]{1,0:T(8,128)(2,1)S(1)}, u32[]{:S(2)}, u32[]{:S(2)}) collective-permute-start(bf16[512,128]{1,0:T(8,128)(2,1)S(1)} %shard_map.88.rest_1_), channel_id=1, source_target_pairs={{0,1},{1,0},{2,3},{3,2},{4,5},{5,4},{6,7},{7,6},{8,9},{9,8},{10,11... | collective-permute-start | bytes 393224 | tf_op jit(solution)/shard_map/ppermute | solution.py:240

commit v3 on v1

--- a/solution.py
+++ b/solution.py
@@ -11,8 +11,8 @@
 SUBLANES = 8
 STORES = 2
 FOLD_COST = 3000000000
-NEAR_COST = 3000000000
-PART_COST = 1500000000
+PIECES = 3
+PART_COST = 4000000000
 VMEM_LIMIT = 32 * 1024 * 1024
 
 
@@ -37,7 +37,7 @@
 
 def state_kernel(
     k_hbm, v_hbm, decay_hbm, residue_hbm, skip_hbm, bias_hbm,
-    total_ref, chunk_ref, gated_ref, decay_ref, residue_ref, skip_ref, bias_ref,
+    total_ref, chunk_ref, gated_ref, local_ref, short_ref, decay_ref, residue_ref, skip_ref, bias_ref,
     k_ref, v_ref, sems,
 ):
     modes = decay_hbm.shape[0]
@@ -75,8 +75,12 @@
     for copy in copies[1 + 2 * parts :]:
         copy.wait()
 
-
-def local_kernel(gated, decay_ref, residue_ref, skip_ref, chunk_ref, local_ref, short_ref):
+    @pl.when(runs_early())
+    def _():
+        convolve(gated_ref, decay_ref, residue_ref, skip_ref, chunk_ref, local_ref, short_ref)
+
+
+def convolve(gated, decay_ref, residue_ref, skip_ref, chunk_ref, local_ref, short_ref):
     modes = decay_ref.shape[0]
     chunk_len = gated.shape[1] // SUBLANES
     index = lax.broadcasted_iota(jnp.int32, (SUBLANES, LANES), 0)
@@ -102,7 +106,25 @@
             return state
 
         lax.fori_loop(0, chunk_len, step, tuple(start), unroll=4)
-        short_ref[:, lanes] = local_ref[part].astype(short_ref.dtype)
+        short_ref[: local_ref.shape[1], lanes] = local_ref[part].astype(short_ref.dtype)
+    left = decay_ref[...]
+    for first in range(local_ref.shape[1], short_ref.shape[0], modes):
+        piece = left.astype(short_ref.dtype)
+        short_ref[first : first + modes, :] = piece
+        left = left - piece.astype(jnp.float32)
+
+
+def runs_early():
+    count = lax.axis_size("seq")
+    return lax.axis_index("seq") < count - count // 4
+
+
+def local_kernel(gated, decay_ref, residue_ref, skip_ref, chunk_ref, local_in, short_in, local_ref, short_ref):
+    del local_in, short_in
+
+    @pl.when(jnp.logical_not(runs_early()))
+    def _():
+        convolve(gated, decay_ref, residue_ref, skip_ref, chunk_ref, local_ref, short_ref)
 
 
 def fold(rates, inner, total, received, stride, seg_len):
@@ -117,7 +139,7 @@
     before = jnp.zeros_like(rates)
     whole = decayed((radix - 1 - spot) * stride) * total
     for i, block in enumerate(received):
-        source = spot ^ (i + 1)
+        source = spot ^ (radix - 1 - i)
         past = source < spot
         gap = jnp.where(past, spot - 1 - source, 0) * stride
         before += jnp.where(past, decayed(gap) * block, 0.0)
@@ -136,20 +158,29 @@
 def share_kernel(stride, seg_len, rates_ref, residue_ref, own_ref, total_ref, *rest):
     inner, rest = (rest[0][...], rest[1:]) if stride > 1 else (0.0, rest)
     received, (base_ref, extra_ref) = [ref[...] for ref in rest[:-2]], rest[-2:]
-    modes = rates_ref.shape[0]
     rates = rates_ref[...]
     before, _ = fold(rates, inner, total_ref[...], received, stride, seg_len)
     before *= residue_ref[...]
     step = jnp.exp(-rates * float(seg_len))
     even = lax.rem(lax.axis_index("seq"), 2) == 0
-    base_ref[:modes, :] = step * before
-    base_ref[modes:, :] = rates
+    base_ref[...] = step * before
     extra_ref[...] = jnp.where(even, residue_ref[...] * own_ref[...] + step * step * before, before)
 
 
-def carry_kernel(first, q_ref, local_ref, base_ref, extra_ref, out_ref):
+def read_rates(rates_ref, modes):
+    if rates_ref.shape[0] == modes:
+        return rates_ref[...]
+    count = rates_ref.shape[0] // modes
+    pieces = [rates_ref[i * modes : (i + 1) * modes, :].astype(jnp.float32) for i in range(count)]
+    return (pieces[2] + pieces[1]) + pieces[0]
+
+
+def carry_kernel(first, q_ref, local_ref, rates_ref, base_ref, extra_ref, out_ref):
     modes = extra_ref.shape[0]
     seg_len = q_ref.shape[0]
+    if rates_ref is None:
+        rates_ref = local_ref.at[pl.ds(seg_len, PIECES * modes), :]
+    rates = read_rates(rates_ref, modes)
     block = 2 * SUBLANES
     ahead = (lax.broadcasted_iota(jnp.int32, (SUBLANES, LANES), 0) + 1).astype(jnp.float32)
     for index in range(out_ref.shape[1] // LANES):
@@ -157,7 +188,7 @@
         lanes = lane_slice(part)
         factor, start = [], []
         for n in range(modes):
-            rate = row(base_ref, modes + n, part)
+            rate = rates[n : n + 1, lanes]
             weight = row(base_ref, n, part) + row(extra_ref, n, part)
             start.append(weight * jnp.exp(-rate * ahead))
             factor.append(full(jnp.exp(-rate * SUBLANES)))
@@ -174,6 +205,10 @@
             return state
 
         lax.fori_loop(0, seg_len // block, step, tuple(start), unroll=4)
+
+
+def across_kernel(first, extra_ref, base_ref, q_ref, local_ref, out_ref):
+    carry_kernel(first, q_ref, local_ref, None, base_ref, extra_ref, out_ref)
 
 
 def project(blocks, weight_ref):
@@ -189,23 +224,22 @@
     return total
 
 
-def near_kernel(weight_ref, bias_ref, *rest):
-    blocks, out_ref = rest[:-1], rest[-1]
+def near_kernel(weight_ref, bias_ref, own_ref, pair_ref, *rest):
+    across, out_ref = rest[:-1], rest[-1]
     rank = lax.axis_index("chan")
-    parts = len(blocks) // 3
-    blocks = [(rank ^ bit, blocks[i * parts : (i + 1) * parts]) for i, bit in enumerate((0, 2, 3))]
+    blocks = [(rank, [own_ref]), (rank ^ 1, [pair_ref]), (rank ^ 2, across)]
     out_ref[...] = project(blocks, weight_ref) + bias_ref[...]
 
 
 def last_kernel(near_ref, weight_ref, *rest):
-    pair, (out_hbm, out_ref, sems) = rest[:-3], rest[-3:]
+    diagonal, (out_hbm, out_ref, sems) = rest[:-3], rest[-3:]
     rank = lax.axis_index("chan")
     pieces = sems.shape[0]
     size = out_ref.shape[0] // pieces
     copies = []
     for i in range(pieces):
         rows = pl.ds(i * size, size)
-        total = near_ref[rows, :] + project([(rank ^ 1, [ref.at[rows, :] for ref in pair])], weight_ref)
+        total = near_ref[rows, :] + project([(rank ^ 3, [ref.at[rows, :] for ref in diagonal])], weight_ref)
         out_ref[rows, :] = total.astype(out_ref.dtype)
         copies.append(pltpu.make_async_copy(out_ref.at[rows], out_hbm.at[rows], sems.at[i]))
         copies[-1].start()
@@ -213,13 +247,14 @@
         copy.wait()
 
 
-def call(kernel, out, *args, cost=0, scratch=(), ins=pltpu.VMEM, outs=pltpu.VMEM):
+def call(kernel, out, *args, cost=0, aliases=(), scratch=(), ins=pltpu.VMEM, outs=pltpu.VMEM):
     return pl.pallas_call(
         kernel,
         out_shape=out,
         in_specs=[pl.BlockSpec(memory_space=ins)] * len(args),
         out_specs=jax.tree.map(lambda _: pl.BlockSpec(memory_space=outs), out),
         scratch_shapes=list(scratch),
+        input_output_aliases=dict(aliases),
         compiler_params=pltpu.CompilerParams(vmem_limit_bytes=VMEM_LIMIT),
         cost_estimate=pl.CostEstimate(flops=cost, bytes_accessed=0, transcendentals=0),
     )(*args)
@@ -251,7 +286,7 @@
     own, inner, stride = total, (), 1
     while True:
         radix = min(4, count // stride)
-        received = [beside(total, 2 * stride * step) for step in range(1, radix)]
+        received = [beside(total, 2 * stride * step) for step in reversed(range(1, radix))]
         if stride * radix == count:
             break
         kernel = functools.partial(fold_kernel, stride, seg_len)
@@ -259,8 +294,7 @@
         stride *= radix
     received, also = lax.optimization_barrier((received, also))
     kernel = functools.partial(share_kernel, stride, seg_len)
-    outs = [struct((2 * total.shape[0], total.shape[1])), shape]
-    base, extra = call(kernel, outs, decay, residue, own, total, *inner, *received, cost=FOLD_COST)
+    base, extra = call(kernel, [shape, shape], decay, residue, own, total, *inner, *received, cost=FOLD_COST)
     return base, extra, also
 
 
@@ -271,14 +305,17 @@
     parts = channels // LANES
     tall = pltpu.VMEM((seg_len, channels), jnp.bfloat16)
     short = struct((seg_len, channels), jnp.bfloat16)
+    taller = struct((seg_len + PIECES * modes, channels), jnp.bfloat16)
     q_across = swapped(q_gate, 2)
     inputs = (k_gate, value, decay, residue, skip.reshape(1, -1), out_bias.reshape(1, -1))
-    total, chunks, gated, decay, residue, skip, bias = call(
+    total, chunks, gated, local, local_short, decay, residue, skip, bias = call(
         state_kernel,
         [
             struct((modes, channels)),
             struct((modes, SUBLANES, channels)),
             struct((parts, seg_len, LANES)),
+            struct((parts, seg_len, LANES)),
+            taller,
             struct((modes, channels)),
             struct((modes, channels)),
             struct((1, channels)),
@@ -289,31 +326,30 @@
         ins=pltpu.HBM,
     )
     local, local_short = call(
-        local_kernel, [struct((parts, seg_len, LANES)), short], gated, decay, residue, skip, chunks
+        local_kernel,
+        [struct((parts, seg_len, LANES)), taller],
+        gated, decay, residue, skip, chunks, local, local_short,
+        aliases={5: 0, 6: 1},
     )
     local_across = swapped(local_short, 2)
     base, extra, q_across = carry_shares(total, decay, residue, seg_len, q_across)
+    extra_beside = beside(extra, 1)
     extra_corner = corner(extra, 1, 2)
-    extra_beside = beside(extra, 1)
     base_across = swapped(base, 2)
+    own = call(functools.partial(carry_kernel, 0), short, q_gate, local, decay, base, extra_beside)
+    pair = swapped(own, 1)
     half = struct((seg_len, LANES), jnp.bfloat16)
     across = [
         call(
-            functools.partial(carry_kernel, part), half, q_across, local_across, base_across, extra_corner,
+            functools.partial(across_kernel, part), half, extra_corner, base_across, q_across, local_across,
             cost=PART_COST,
         )
         for part in range(parts)
     ]
     diagonal = [swapped(block, 1) for block in across]
-    (extra_beside, *across) = lax.optimization_barrier((extra_beside, *across))
-    own = [
-        call(functools.partial(carry_kernel, part), half, q_gate, local, base, extra_beside, cost=PART_COST)
-        for part in range(parts)
-    ]
-    pair = [swapped(block, 1) for block in own]
-    near = call(near_kernel, struct((seg_len, cols)), out_weight, bias, *own, *across, *diagonal, cost=NEAR_COST)
+    near = call(near_kernel, struct((seg_len, cols)), out_weight, bias, own, pair, *across)
     return call(
-        last_kernel, struct((seg_len, cols), jnp.bfloat16), near, out_weight, *pair,
+        last_kernel, struct((seg_len, cols), jnp.bfloat16), near, out_weight, *diagonal,
         scratch=[pltpu.VMEM((seg_len, cols), jnp.bfloat16), pltpu.SemaphoreType.DMA((STORES,))],
         outs=pltpu.HBM,
     )

time: 25.2 us -> 23.6 us (0.937)
  starting transfers between devices: 12.6 us -> 11.7 us
  waiting for transfers between devices: 5.28 us -> 4.68 us
    ppermute x1, starting transfers between devices: 2.45 us -> 0.48 us  [corner(): return lax.ppermute(value, ('seq', 'chan'), pairs)]
    ppermute x4, starting transfers between devices: 4.99 us -> 6.01 us  [beside(): return lax.ppermute(value, 'seq', [(r, r ^ step) for r in range(count)])]
    ppermute x4, waiting for transfers between devices: 3.24 us -> 2.63 us  [beside(): return lax.ppermute(value, 'seq', [(r, r ^ step) for r in range(count)])]
    ppermute x1, waiting for transfers between devices: 1.11 us -> 1.54 us  [corner(): return lax.ppermute(value, ('seq', 'chan'), pairs)]
    ppermute x7 -> x6, waiting for transfers between devices: 0.94 us -> 0.51 us  [swapped(): return lax.ppermute(value, 'chan', [(r, r ^ bit) for r in range(count)])]
    pallas_call x9 -> x8, Pallas kernels: 6.9 us -> 6.85 us  [call(): pl.pallas_call(kernel, out_shape=out, in_specs=[pl.BlockSpec(memory_space...]
    ppermute x7 -> x6, starting transfers between devices: 5.15 us -> 5.19 us  [swapped(): return lax.ppermute(value, 'chan', [(r, r ^ bit) for r in range(count)])]
  transfers between devices with their start and end apart: 12 -> 11, of which waited for: 5 -> 6; matrix products, arithmetic and copies ran while one was open for 0% -> 0% of each run, Pallas kernels for 24% -> 25%
where the time goes in v3:
time: 23.6 us; the launch traced here: 23.3 us
  starting transfers between devices  11.7 us (50%)
  Pallas kernels  6.85 us (29%)
  waiting for transfers between devices  4.68 us (20%)
    pallas_call x8, Pallas kernels, call(): pl.pallas_call(kernel, out_shape=out, in_specs=[pl.BlockSpec(memory_space...  6.85 us
    ppermute x4, starting transfers between devices, beside(): return lax.ppermute(value, 'seq', [(r, r ^ step) for r in range(count)])  6.01 us
    ppermute x6, starting transfers between devices, swapped(): return lax.ppermute(value, 'chan', [(r, r ^ bit) for r in range(count)])  5.19 us
    ppermute x4, waiting for transfers between devices, beside(): return lax.ppermute(value, 'seq', [(r, r ^ step) for r in range(count)])  2.63 us
    ppermute x1, waiting for transfers between devices, corner(): return lax.ppermute(value, ('seq', 'chan'), pairs)  1.54 us
    ppermute x6, waiting for transfers between devices, swapped(): return lax.ppermute(value, 'chan', [(r, r ^ bit) for r in range(count)])  0.51 us
    ppermute x1, starting transfers between devices, corner(): return lax.ppermute(value, ('seq', 'chan'), pairs)  0.48 us
  transfers between devices with their start and end apart: 11, of which 6 were waited for; matrix products, arithmetic and copies ran while one was open for 0% of the time, Pallas kernels for 25%

profile of v3, /device:TPU:0, one launch (start us, length us, event | category | flops | bytes accessed | tf_op | source)
XLA Modules:
  0.0 23.3 jit_solution(10476039477856423787)
XLA Ops:
  0.0 3.0 %collective-permute-start.3 = (bf16[512,256]{1,0:T(8,128)(2,1)}, bf16[512,256]{1,0:T(8,128)(2,1)S(1)}, u32[]{:S(2)}, u32[]{:S(2)}) collective-permute-start(bf16[512,256]{1,0:T(8,128)(2,1)} %q_ref.1), channel_id=1, source_target_pairs={{0,2},{1,3},{2,0},{3,1},{4,6},{5,7},{6,4},{7,5},{8,10},{9,11},{10,... | collective-permute-start | bytes 786440 | tf_op jit(solution)/shard_map/ppermute | solution.py:269
  3.0 3.9 %shard_map.82 = (f32[16,256]{1,0:T(8,128)S(1)}, f32[16,8,256]{2,1,0:T(8,128)S(1)}, f32[2,512,128]{2,1,0:T(8,128)S(1)}, f32[2,512,128]{2,1,0:T(8,128)S(1)}, bf16[...) custom-call(bf16[512,256]{1,0:T(8,128)(2,1)} %k_hbm.1, ...), custom_call_target="tpu_custom_call" | custom-call | tf_op jit(solution)/shard_map/pallas_call | solution.py:251
  6.9 1.8 %collective-permute-start = (f32[16,256]{1,0:T(8,128)S(1)}, f32[16,256]{1,0:T(8,128)S(1)}, u32[]{:S(2)}, u32[]{:S(2)}) collective-permute-start(f32[16,256]{1,0:T(8,128)S(1)} %get-tuple-element.31.own_ref.total_ref), channel_id=1, source_target_pairs={{0,24},{4,28},{8,16},{12,20},{16,8},{20,12},{24,0},{28,4},{1,25},{... | collective-permute-start | bytes 49160 | tf_op jit(solution)/shard_map/ppermute | solution.py:274
  8.7 1.3 %collective-permute-start.1 = (f32[16,256]{1,0:T(8,128)S(1)}, f32[16,256]{1,0:T(8,128)S(1)}, u32[]{:S(2)}, u32[]{:S(2)}) collective-permute-start(f32[16,256]{1,0:T(8,128)S(1)} %get-tuple-element.31.own_ref.total_ref), channel_id=1, source_target_pairs={{0,16},{4,20},{8,24},{12,28},{16,0},{20,4},{24,8},{28,12},{1,17},{... | collective-permute-start | bytes 49160 | tf_op jit(solution)/shard_map/ppermute | solution.py:274
  10.0 1.3 %collective-permute-start.2 = (f32[16,256]{1,0:T(8,128)S(1)}, f32[16,256]{1,0:T(8,128)S(1)}, u32[]{:S(2)}, u32[]{:S(2)}) collective-permute-start(f32[16,256]{1,0:T(8,128)S(1)} %get-tuple-element.31.own_ref.total_ref), channel_id=1, source_target_pairs={{0,8},{4,12},{8,0},{12,4},{16,24},{20,28},{24,16},{28,20},{1,9},{5... | collective-permute-start | bytes 49160 | tf_op jit(solution)/shard_map/ppermute | solution.py:274
  11.3 0.0 copy-start.1
  11.3 0.0 collective-permute-start.8
  11.3 1.3 %collective-permute-done.rest_0_ = f32[16,256]{1,0:T(8,128)S(1)} collective-permute-done((f32[16,256]{1,0:T(8,128)S(1)}, f32[16,256]{1,0:T(8,128)S(1)}, u32[]{:S(2)}, u32[]{:S(2)}) %collective-permute-start) | collective-permute-done | bytes 16416 | tf_op jit(solution)/shard_map/ppermute | solution.py:274
  12.7 0.6 %collective-permute-done.1.rest_1_ = f32[16,256]{1,0:T(8,128)S(1)} collective-permute-done((f32[16,256]{1,0:T(8,128)S(1)}, f32[16,256]{1,0:T(8,128)S(1)}, u32[]{:S(2)}, u32[]{:S(2)}) %collective-permute-start.1) | collective-permute-done | bytes 16416 | tf_op jit(solution)/shard_map/ppermute | solution.py:274
  13.3 0.4 %collective-permute-done.2.rest_2_ = f32[16,256]{1,0:T(8,128)S(1)} collective-permute-done((f32[16,256]{1,0:T(8,128)S(1)}, f32[16,256]{1,0:T(8,128)S(1)}, u32[]{:S(2)}, u32[]{:S(2)}) %collective-permute-start.2) | collective-permute-done | bytes 16416 | tf_op jit(solution)/shard_map/ppermute | solution.py:274
  13.7 0.0 collective-permute-done.3.q_ref
  13.8 1.6 %collective-permute-start.4 = (f32[16,256]{1,0:T(8,128)S(1)}, f32[16,256]{1,0:T(8,128)S(1)}, u32[]{:S(2)}, u32[]{:S(2)}) collective-permute-start(f32[16,256]{1,0:T(8,128)S(1)} %get-tuple-element.36), channel_id=1, source_target_pairs={{0,4},{4,0},{8,12},{12,8},{16,20},{20,16},{24,28},{28,24},{1,5},{5... | collective-permute-start | bytes 49160 | tf_op jit(solution)/shard_map/ppermute | solution.py:274
  15.3 0.5 %collective-permute-start.6 = (f32[16,256]{1,0:T(8,128)S(1)}, f32[16,256]{1,0:T(8,128)S(1)}, u32[]{:S(2)}, u32[]{:S(2)}) collective-permute-start(f32[16,256]{1,0:T(8,128)S(1)} %get-tuple-element.36), channel_id=1, source_target_pairs={{0,6},{1,7},{2,4},{3,5},{4,2},{5,3},{6,0},{7,1},{8,14},{9,15},{10,... | collective-permute-start | bytes 49160 | tf_op jit(solution)/shard_map/ppermute | solution.py:280
  15.8 1.5 %collective-permute-start.7 = (f32[16,256]{1,0:T(8,128)S(1)}, f32[16,256]{1,0:T(8,128)S(1)}, u32[]{:S(2)}, u32[]{:S(2)}) collective-permute-start(f32[16,256]{1,0:T(8,128)S(1)} %get-tuple-element.35.base_ref), channel_id=1, source_target_pairs={{0,2},{1,3},{2,0},{3,1},{4,6},{5,7},{6,4},{7,5},{8,10},{9,11},{10,... | collective-permute-start | bytes 49160 | tf_op jit(solution)/shard_map/ppermute | solution.py:269
  17.3 0.2 %collective-permute-done.4.extra_ref = f32[16,256]{1,0:T(8,128)S(1)} collective-permute-done((f32[16,256]{1,0:T(8,128)S(1)}, f32[16,256]{1,0:T(8,128)S(1)}, u32[]{:S(2)}, u32[]{:S(2)}) %collective-permute-start.4) | collective-permute-done | bytes 16416 | tf_op jit(solution)/shard_map/ppermute | solution.py:274
  17.6 0.0 copy-done.1
  17.6 0.8 %shard_map.85.own_ref = bf16[512,256]{1,0:T(8,128)(2,1)S(1)} custom-call(bf16[512,256]{1,0:T(8,128)(2,1)S(1)} %copy-done.1, f32[2,512,128]{2,1,0:T(8,128)S(1)} %get-tuple-element.30.local_ref, f32[16,256]{1,0:T(8,128)S(1)} %get-tuple-element.24.decay_ref.rates_ref, f32[16,256]{1,0:T(8,128)S(1)} %get-tuple-element.35.base_ref, ...), custom_call_target="tpu_custom_call" | custom-call | tf_op jit(solution)/shard_map/pallas_call | solution.py:251
  18.4 0.1 collective-permute-start.5
  18.4 1.5 %collective-permute-done.6.extra_ref = f32[16,256]{1,0:T(8,128)S(1)} collective-permute-done((f32[16,256]{1,0:T(8,128)S(1)}, f32[16,256]{1,0:T(8,128)S(1)}, u32[]{:S(2)}, u32[]{:S(2)}) %collective-permute-start.6) | collective-permute-done | bytes 16416 | tf_op jit(solution)/shard_map/ppermute | solution.py:280
  20.0 0.0 collective-permute-done.7.base_ref
  20.0 0.0 collective-permute-done.8.local_ref
  20.0 0.4 %shard_map.86.rest_0_ = bf16[512,128]{1,0:T(8,128)(2,1)S(1)} custom-call(f32[16,256]{1,0:T(8,128)S(1)} %collective-permute-done.6.extra_ref, f32[16,256]{1,0:T(8,128)S(1)} %collective-permute-done.7.base_ref, bf16[512,256]{1,0:T(8,128)(2,1)S(1)} %collective-permute-done.3.q_ref, bf16[560,256]{1,0:T(8,128)(2,1)S(1)} %collective-permute-done.8.local_ref), custom_call_target="tpu_custom_call" | custom-call | flops 4000000000 | tf_op jit(solution)/shard_map/pallas_call | solution.py:251
  20.3 0.0 copy-start
  20.3 0.1 collective-permute-start.9
  20.4 0.4 %shard_map.87.rest_1_ = bf16[512,128]{1,0:T(8,128)(2,1)S(1)} custom-call(f32[16,256]{1,0:T(8,128)S(1)} %collective-permute-done.6.extra_ref, f32[16,256]{1,0:T(8,128)S(1)} %collective-permute-done.7.base_ref, bf16[512,256]{1,0:T(8,128)(2,1)S(1)} %collective-permute-done.3.q_ref, bf16[560,256]{1,0:T(8,128)(2,1)S(1)} %collective-permute-done.8.local_ref), custom_call_target="tpu_custom_call" | custom-call | flops 4000000000 | tf_op jit(solution)/shard_map/pallas_call | solution.py:251
  20.8 0.6 %collective-permute-start.10 = (bf16[512,128]{1,0:T(8,128)(2,1)S(1)}, bf16[512,128]{1,0:T(8,128)(2,1)S(1)}, u32[]{:S(2)}, u32[]{:S(2)}) collective-permute-start(bf16[512,128]{1,0:T(8,128)(2,1)S(1)} %shard_map.87.rest_1_), channel_id=1, source_target_pairs={{0,1},{1,0},{2,3},{3,2},{4,5},{5,4},{6,7},{7,6},{8,9},{9,8},{10,11... | collective-permute-start | bytes 393224 | tf_op jit(solution)/shard_map/ppermute | solution.py:269
  21.3 0.0 collective-permute-done.5.pair_ref
  21.3 0.0 copy-done
  21.4 0.4 %shard_map.88.near_ref = f32[512,256]{1,0:T(8,128)S(1)} custom-call(bf16[1024,256]{1,0:T(8,128)(2,1)S(1)} %copy-done, f32[1,256]{1,0:T(1,128)S(1)} %get-tuple-element.22.bias_ref, bf16[512,256]{1,0:T(8,128)(2,1)S(1)} %shard_map.85.own_ref, bf16[512,256]{1,0:T(8,128)(2,1)S(1)} %collective-permute-done.5.pair_ref, bf16[512,128]{1,0:T(8,128)(2,1)S(1)} %shard_map.86.rest_0_, ...), custom_call_target="tpu_custom_call" | custom-call | tf_op jit(solution)/shard_map/pallas_call | solution.py:251
  21.8 0.0 collective-permute-done.9.rest_0_
  21.8 0.5 %collective-permute-done.10.rest_1_ = bf16[512,128]{1,0:T(8,128)(2,1)S(1)} collective-permute-done((bf16[512,128]{1,0:T(8,128)(2,1)S(1)}, bf16[512,128]{1,0:T(8,128)(2,1)S(1)}, u32[]{:S(2)}, u32[]{:S(2)}) %collective-permute-start.10) | collective-permute-done | bytes 131104 | tf_op jit(solution)/shard_map/ppermute | solution.py:269
  22.3 1.0 %shard_map.89 = bf16[512,256]{1,0:T(8,128)(2,1)} custom-call(f32[512,256]{1,0:T(8,128)S(1)} %shard_map.88.near_ref, bf16[1024,256]{1,0:T(8,128)(2,1)S(1)} %copy-done, bf16[512,128]{1,0:T(8,128)(2,1)S(1)} %collective-permute-done.9.rest_0_, bf16[512,128]{1,0:T(8,128)(2,1)S(1)} %collective-permute-done.10.rest_1_), custom_call_target="tpu_custom_call" | custom-call | tf_op jit(solution)/shard_map/pallas_call | solution.py:251
  (2 shorter events, 0.0 us)
Async XLA Ops:
  0.0 13.7 %collective-permute-start.3 = (bf16[512,256]{1,0:T(8,128)(2,1)}, bf16[512,256]{1,0:T(8,128)(2,1)S(1)}, u32[]{:S(2)}, u32[]{:S(2)}) collective-permute-start(bf16[512,256]{1,0:T(8,128)(2,1)} %q_ref.1), channel_id=1, source_target_pairs={{0,2},{1,3},{2,0},{3,1},{4,6},{5,7},{6,4},{7,5},{8,10},{9,11},{10,... | collective-permute-start | bytes 786440 | tf_op jit(solution)/shard_map/ppermute | solution.py:269
  6.9 5.8 %collective-permute-start = (f32[16,256]{1,0:T(8,128)S(1)}, f32[16,256]{1,0:T(8,128)S(1)}, u32[]{:S(2)}, u32[]{:S(2)}) collective-permute-start(f32[16,256]{1,0:T(8,128)S(1)} %get-tuple-element.31.own_ref.total_ref), channel_id=1, source_target_pairs={{0,24},{4,28},{8,16},{12,20},{16,8},{20,12},{24,0},{28,4},{1,25},{... | collective-permute-start | bytes 49160 | tf_op jit(solution)/shard_map/ppermute | solution.py:274
  8.7 4.6 %collective-permute-start.1 = (f32[16,256]{1,0:T(8,128)S(1)}, f32[16,256]{1,0:T(8,128)S(1)}, u32[]{:S(2)}, u32[]{:S(2)}) collective-permute-start(f32[16,256]{1,0:T(8,128)S(1)} %get-tuple-element.31.own_ref.total_ref), channel_id=1, source_target_pairs={{0,16},{4,20},{8,24},{12,28},{16,0},{20,4},{24,8},{28,12},{1,17},{... | collective-permute-start | bytes 49160 | tf_op jit(solution)/shard_map/ppermute | solution.py:274
  10.0 3.7 %collective-permute-start.2 = (f32[16,256]{1,0:T(8,128)S(1)}, f32[16,256]{1,0:T(8,128)S(1)}, u32[]{:S(2)}, u32[]{:S(2)}) collective-permute-start(f32[16,256]{1,0:T(8,128)S(1)} %get-tuple-element.31.own_ref.total_ref), channel_id=1, source_target_pairs={{0,8},{4,12},{8,0},{12,4},{16,24},{20,28},{24,16},{28,20},{1,9},{5... | collective-permute-start | bytes 49160 | tf_op jit(solution)/shard_map/ppermute | solution.py:274
  11.3 6.2 %copy-start.1 = (bf16[512,256]{1,0:T(8,128)(2,1)S(1)}, bf16[512,256]{1,0:T(8,128)(2,1)}, u32[]{:S(2)}) copy-start(bf16[512,256]{1,0:T(8,128)(2,1)} %q_ref.1) | copy-start | bytes 786436
  11.3 8.6 %collective-permute-start.8 = (bf16[560,256]{1,0:T(8,128)(2,1)S(1)}, bf16[560,256]{1,0:T(8,128)(2,1)S(1)}, u32[]{:S(2)}, u32[]{:S(2)}) collective-permute-start(bf16[560,256]{1,0:T(8,128)(2,1)S(1)} %get-tuple-element.38), channel_id=1, source_target_pairs={{0,2},{1,3},{2,0},{3,1},{4,6},{5,7},{6,4},{7,5},{8,10},{9,11},{10,... | collective-permute-start | bytes 860168 | tf_op jit(solution)/shard_map/ppermute | solution.py:269
  13.8 3.8 %collective-permute-start.4 = (f32[16,256]{1,0:T(8,128)S(1)}, f32[16,256]{1,0:T(8,128)S(1)}, u32[]{:S(2)}, u32[]{:S(2)}) collective-permute-start(f32[16,256]{1,0:T(8,128)S(1)} %get-tuple-element.36), channel_id=1, source_target_pairs={{0,4},{4,0},{8,12},{12,8},{16,20},{20,16},{24,28},{28,24},{1,5},{5... | collective-permute-start | bytes 49160 | tf_op jit(solution)/shard_map/ppermute | solution.py:274
  15.3 4.6 %collective-permute-start.6 = (f32[16,256]{1,0:T(8,128)S(1)}, f32[16,256]{1,0:T(8,128)S(1)}, u32[]{:S(2)}, u32[]{:S(2)}) collective-permute-start(f32[16,256]{1,0:T(8,128)S(1)} %get-tuple-element.36), channel_id=1, source_target_pairs={{0,6},{1,7},{2,4},{3,5},{4,2},{5,3},{6,0},{7,1},{8,14},{9,15},{10,... | collective-permute-start | bytes 49160 | tf_op jit(solution)/shard_map/ppermute | solution.py:280
  15.8 4.2 %collective-permute-start.7 = (f32[16,256]{1,0:T(8,128)S(1)}, f32[16,256]{1,0:T(8,128)S(1)}, u32[]{:S(2)}, u32[]{:S(2)}) collective-permute-start(f32[16,256]{1,0:T(8,128)S(1)} %get-tuple-element.35.base_ref), channel_id=1, source_target_pairs={{0,2},{1,3},{2,0},{3,1},{4,6},{5,7},{6,4},{7,5},{8,10},{9,11},{10,... | collective-permute-start | bytes 49160 | tf_op jit(solution)/shard_map/ppermute | solution.py:269
  18.4 3.0 %collective-permute-start.5 = (bf16[512,256]{1,0:T(8,128)(2,1)S(1)}, bf16[512,256]{1,0:T(8,128)(2,1)S(1)}, u32[]{:S(2)}, u32[]{:S(2)}) collective-permute-start(bf16[512,256]{1,0:T(8,128)(2,1)S(1)} %shard_map.85.own_ref), channel_id=1, source_target_pairs={{0,1},{1,0},{2,3},{3,2},{4,5},{5,4},{6,7},{7,6},{8,9},{9,8},{10,11... | collective-permute-start | bytes 786440 | tf_op jit(solution)/shard_map/ppermute | solution.py:269
  20.3 1.0 %copy-start = (bf16[1024,256]{1,0:T(8,128)(2,1)S(1)}, bf16[1024,256]{1,0:T(8,128)(2,1)}, u32[]{:S(2)}) copy-start(bf16[1024,256]{1,0:T(8,128)(2,1)} %weight_ref.3) | copy-start | bytes 1572868
  20.3 1.5 %collective-permute-start.9 = (bf16[512,128]{1,0:T(8,128)(2,1)S(1)}, bf16[512,128]{1,0:T(8,128)(2,1)S(1)}, u32[]{:S(2)}, u32[]{:S(2)}) collective-permute-start(bf16[512,128]{1,0:T(8,128)(2,1)S(1)} %shard_map.86.rest_0_), channel_id=1, source_target_pairs={{0,1},{1,0},{2,3},{3,2},{4,5},{5,4},{6,7},{7,6},{8,9},{9,8},{10,11... | collective-permute-start | bytes 393224 | tf_op jit(solution)/shard_map/ppermute | solution.py:269
  20.8 1.5 %collective-permute-start.10 = (bf16[512,128]{1,0:T(8,128)(2,1)S(1)}, bf16[512,128]{1,0:T(8,128)(2,1)S(1)}, u32[]{:S(2)}, u32[]{:S(2)}) collective-permute-start(bf16[512,128]{1,0:T(8,128)(2,1)S(1)} %shard_map.87.rest_1_), channel_id=1, source_target_pairs={{0,1},{1,0},{2,3},{3,2},{4,5},{5,4},{6,7},{7,6},{8,9},{9,8},{10,11... | collective-permute-start | bytes 393224 | tf_op jit(solution)/shard_map/ppermute | solution.py:269

commit v4 on v3

--- a/solution.py
+++ b/solution.py
@@ -10,8 +10,12 @@
 LANES = 128
 SUBLANES = 8
 STORES = 2
-FOLD_COST = 3000000000
+OWN_COST = 1000000000
+MORE_COST = 1000000000
+FOLD_COST = 500000000
 PIECES = 3
+INPUTS = 6
+KEPT = 6
 PART_COST = 4000000000
 VMEM_LIMIT = 32 * 1024 * 1024
 
@@ -35,9 +39,9 @@
     return slice(part * LANES, (part + 1) * LANES)
 
 
-def state_kernel(
+def summarize(
     k_hbm, v_hbm, decay_hbm, residue_hbm, skip_hbm, bias_hbm,
-    total_ref, chunk_ref, gated_ref, local_ref, short_ref, decay_ref, residue_ref, skip_ref, bias_ref,
+    total_ref, chunk_ref, gated_ref, decay_ref, residue_ref, skip_ref, bias_ref,
     k_ref, v_ref, sems,
 ):
     modes = decay_hbm.shape[0]
@@ -75,56 +79,73 @@
     for copy in copies[1 + 2 * parts :]:
         copy.wait()
 
-    @pl.when(runs_early())
+
+def is_last():
+    count = lax.axis_size("seq")
+    return lax.axis_index("seq") >= count - 2
+
+
+def state_kernel(*refs):
+    total_ref = refs[INPUTS]
+
+    @pl.when(jnp.logical_not(is_last()))
     def _():
-        convolve(gated_ref, decay_ref, residue_ref, skip_ref, chunk_ref, local_ref, short_ref)
-
-
-def convolve(gated, decay_ref, residue_ref, skip_ref, chunk_ref, local_ref, short_ref):
+        summarize(*refs)
+
+    @pl.when(is_last())
+    def _():
+        total_ref[...] = jnp.zeros_like(total_ref)
+
+
+def local_kernel(*refs):
+    inputs, rest = refs[:INPUTS], refs[INPUTS:]
+    total_in, rest = rest[0], rest[1 + KEPT :]
+    total_ref, kept, (local_ref, short_ref), scratch = rest[0], rest[1 : 1 + KEPT], rest[1 + KEPT : -3], rest[-3:]
+    chunk_ref, gated_ref, decay_ref, residue_ref, skip_ref, _ = kept
+
+    @pl.when(is_last())
+    def _():
+        summarize(*inputs, total_ref, *kept, *scratch)
+
+    @pl.when(jnp.logical_not(is_last()))
+    def _():
+        total_ref[...] = total_in[...]
+
+    convolve(0, gated_ref, decay_ref, residue_ref, skip_ref, chunk_ref, local_ref, short_ref)
+
+
+def convolve(part, gated, decay_ref, residue_ref, skip_ref, chunk_ref, local_ref, short_ref):
     modes = decay_ref.shape[0]
-    chunk_len = gated.shape[1] // SUBLANES
+    seg_len = gated.shape[1]
+    chunk_len = seg_len // SUBLANES
     index = lax.broadcasted_iota(jnp.int32, (SUBLANES, LANES), 0)
-    for part in range(gated.shape[0]):
-        lanes = lane_slice(part)
-        factor, weight, start = [], [], []
-        for n in range(modes):
-            rate = row(decay_ref, n, part)
-            prefix = chunk_ref[n, :, lanes]
-            for shift in (1, 2, 4):
-                moved = jnp.where(index >= shift, pltpu.roll(prefix, shift, 0), 0.0)
-                prefix = prefix + jnp.exp(-rate * (shift * chunk_len)) * moved
-            start.append(jnp.where(index >= 1, pltpu.roll(prefix, 1, 0), 0.0))
-            factor.append(full(jnp.exp(-rate)))
-            weight.append(full(row(residue_ref, n, part)))
-        bypass = full(skip_ref[:, lanes])
-
-        def step(t, state):
-            rows = pl.ds(t, SUBLANES, stride=chunk_len)
-            x = gated[part, rows, :]
-            state = tuple(f * h + x for f, h in zip(factor, state))
-            local_ref[part, rows, :] = tree_sum([w * h for w, h in zip(weight, state)] + [bypass * x])
-            return state
-
-        lax.fori_loop(0, chunk_len, step, tuple(start), unroll=4)
-        short_ref[: local_ref.shape[1], lanes] = local_ref[part].astype(short_ref.dtype)
-    left = decay_ref[...]
-    for first in range(local_ref.shape[1], short_ref.shape[0], modes):
+    lanes = lane_slice(part)
+    factor, weight, start = [], [], []
+    for n in range(modes):
+        rate = row(decay_ref, n, part)
+        prefix = chunk_ref[n, :, lanes]
+        for shift in (1, 2, 4):
+            moved = jnp.where(index >= shift, pltpu.roll(prefix, shift, 0), 0.0)
+            prefix = prefix + jnp.exp(-rate * (shift * chunk_len)) * moved
+        start.append(jnp.where(index >= 1, pltpu.roll(prefix, 1, 0), 0.0))
+        factor.append(full(jnp.exp(-rate)))
+        weight.append(full(row(residue_ref, n, part)))
+    bypass = full(skip_ref[:, lanes])
+
+    def step(t, state):
+        rows = pl.ds(t, SUBLANES, stride=chunk_len)
+        x = gated[part, rows, :]
+        state = tuple(f * h + x for f, h in zip(factor, state))
+        local_ref[rows, :] = tree_sum([w * h for w, h in zip(weight, state)] + [bypass * x])
+        return state
+
+    lax.fori_loop(0, chunk_len, step, tuple(start), unroll=4)
+    short_ref[:seg_len, :] = local_ref[...].astype(short_ref.dtype)
+    left = decay_ref[:, lanes]
+    for first in range(seg_len, short_ref.shape[0], modes):
         piece = left.astype(short_ref.dtype)
         short_ref[first : first + modes, :] = piece
         left = left - piece.astype(jnp.float32)
-
-
-def runs_early():
-    count = lax.axis_size("seq")
-    return lax.axis_index("seq") < count - count // 4
-
-
-def local_kernel(gated, decay_ref, residue_ref, skip_ref, chunk_ref, local_in, short_in, local_ref, short_ref):
-    del local_in, short_in
-
-    @pl.when(jnp.logical_not(runs_early()))
-    def _():
-        convolve(gated, decay_ref, residue_ref, skip_ref, chunk_ref, local_ref, short_ref)
 
 
 def fold(rates, inner, total, received, stride, seg_len):
@@ -167,48 +188,48 @@
     extra_ref[...] = jnp.where(even, residue_ref[...] * own_ref[...] + step * step * before, before)
 
 
-def read_rates(rates_ref, modes):
-    if rates_ref.shape[0] == modes:
-        return rates_ref[...]
-    count = rates_ref.shape[0] // modes
-    pieces = [rates_ref[i * modes : (i + 1) * modes, :].astype(jnp.float32) for i in range(count)]
-    return (pieces[2] + pieces[1]) + pieces[0]
-
-
-def carry_kernel(first, q_ref, local_ref, rates_ref, base_ref, extra_ref, out_ref):
-    modes = extra_ref.shape[0]
+def carry(q_ref, local_ref, rates, base_ref, extra_ref, out_ref, part, column):
+    modes = rates.shape[0]
     seg_len = q_ref.shape[0]
-    if rates_ref is None:
-        rates_ref = local_ref.at[pl.ds(seg_len, PIECES * modes), :]
-    rates = read_rates(rates_ref, modes)
     block = 2 * SUBLANES
     ahead = (lax.broadcasted_iota(jnp.int32, (SUBLANES, LANES), 0) + 1).astype(jnp.float32)
-    for index in range(out_ref.shape[1] // LANES):
-        part = first + index
-        lanes = lane_slice(part)
-        factor, start = [], []
-        for n in range(modes):
-            rate = rates[n : n + 1, lanes]
-            weight = row(base_ref, n, part) + row(extra_ref, n, part)
-            start.append(weight * jnp.exp(-rate * ahead))
-            factor.append(full(jnp.exp(-rate * SUBLANES)))
-
-        def step(j, state):
-            rows = pl.ds(pl.multiple_of(j * block, block), block)
-            halves = []
-            for _ in range(2):
-                halves.append(tree_sum(list(state)))
-                state = tuple(f * h for f, h in zip(factor, state))
-            local = local_ref[part, rows, :] if len(local_ref.shape) == 3 else local_ref[rows, lanes]
-            total = local.astype(jnp.float32) + jnp.concatenate(halves, axis=0)
-            out_ref[rows, lane_slice(index)] = (q_ref[rows, lanes].astype(jnp.float32) * total).astype(out_ref.dtype)
-            return state
-
-        lax.fori_loop(0, seg_len // block, step, tuple(start), unroll=4)
-
-
-def across_kernel(first, extra_ref, base_ref, q_ref, local_ref, out_ref):
-    carry_kernel(first, q_ref, local_ref, None, base_ref, extra_ref, out_ref)
+    lanes = lane_slice(part)
+    factor, start = [], []
+    for n in range(modes):
+        rate = rates[n : n + 1, :]
+        weight = row(base_ref, n, part) + row(extra_ref, n, part)
+        start.append(weight * jnp.exp(-rate * ahead))
+        factor.append(full(jnp.exp(-rate * SUBLANES)))
+
+    def step(j, state):
+        rows = pl.ds(pl.multiple_of(j * block, block), block)
+        halves = []
+        for _ in range(2):
+            halves.append(tree_sum(list(state)))
+            state = tuple(f * h for f, h in zip(factor, state))
+        total = local_ref[rows, :].astype(jnp.float32) + jnp.concatenate(halves, axis=0)
+        gate_rows = q_ref[rows, lanes].astype(jnp.float32)
+        out_ref[rows, lane_slice(column)] = (gate_rows * total).astype(out_ref.dtype)
+        return state
+
+    lax.fori_loop(0, seg_len // block, step, tuple(start), unroll=4)
+
+
+def own_kernel(q_ref, rates_ref, base_ref, extra_ref, *rest):
+    locals_in, out_ref = rest[:-1], rest[-1]
+    for part, local_ref in enumerate(locals_in):
+        carry(q_ref, local_ref, rates_ref[:, lane_slice(part)], base_ref, extra_ref, out_ref, part, part)
+
+
+def across_kernel(part, extra_ref, base_ref, q_ref, local_ref, out_ref):
+    modes = base_ref.shape[0]
+    seg_len = q_ref.shape[0]
+    pieces = [
+        local_ref[first : first + modes, :].astype(jnp.float32)
+        for first in range(seg_len, local_ref.shape[0], modes)
+    ]
+    rates = (pieces[2] + pieces[1]) + pieces[0]
+    carry(q_ref, local_ref, rates, base_ref, extra_ref, out_ref, part, 0)
 
 
 def project(blocks, weight_ref):
@@ -247,11 +268,12 @@
         copy.wait()
 
 
-def call(kernel, out, *args, cost=0, aliases=(), scratch=(), ins=pltpu.VMEM, outs=pltpu.VMEM):
+def call(kernel, out, *args, cost=0, aliases=(), scratch=(), hbm=0, outs=pltpu.VMEM):
+    spaces = [pltpu.HBM] * hbm + [pltpu.VMEM] * (len(args) - hbm)
     return pl.pallas_call(
         kernel,
         out_shape=out,
-        in_specs=[pl.BlockSpec(memory_space=ins)] * len(args),
+        in_specs=[pl.BlockSpec(memory_space=space) for space in spaces],
         out_specs=jax.tree.map(lambda _: pl.BlockSpec(memory_space=outs), out),
         scratch_shapes=list(scratch),
         input_output_aliases=dict(aliases),
@@ -280,10 +302,10 @@
     return lax.ppermute(value, ("seq", "chan"), pairs)
 
 
-def carry_shares(total, decay, residue, seg_len, also):
+def carry_shares(total, own, decay, residue, seg_len, also):
     count = lax.axis_size("seq") // 2
     shape = struct(total.shape)
-    own, inner, stride = total, (), 1
+    inner, stride = (), 1
     while True:
         radix = min(4, count // stride)
         received = [beside(total, 2 * stride * step) for step in reversed(range(1, radix))]
@@ -304,44 +326,44 @@
     cols = out_weight.shape[1]
     parts = channels // LANES
     tall = pltpu.VMEM((seg_len, channels), jnp.bfloat16)
-    short = struct((seg_len, channels), jnp.bfloat16)
-    taller = struct((seg_len + PIECES * modes, channels), jnp.bfloat16)
     q_across = swapped(q_gate, 2)
     inputs = (k_gate, value, decay, residue, skip.reshape(1, -1), out_bias.reshape(1, -1))
-    total, chunks, gated, local, local_short, decay, residue, skip, bias = call(
-        state_kernel,
-        [
-            struct((modes, channels)),
-            struct((modes, SUBLANES, channels)),
-            struct((parts, seg_len, LANES)),
-            struct((parts, seg_len, LANES)),
-            taller,
-            struct((modes, channels)),
-            struct((modes, channels)),
-            struct((1, channels)),
-            struct((1, cols)),
-        ],
-        *(pltpu.with_memory_space_constraint(x, pltpu.HBM) for x in inputs),
-        scratch=[tall, tall, pltpu.SemaphoreType.DMA((2 * parts + 4,))],
-        ins=pltpu.HBM,
+    inputs = [pltpu.with_memory_space_constraint(x, pltpu.HBM) for x in inputs]
+    tall = pltpu.VMEM((seg_len, channels), jnp.bfloat16)
+    scratch = [tall, tall, pltpu.SemaphoreType.DMA((2 * parts + 4,))]
+    few = struct((modes, channels))
+    kept = [
+        struct((modes, SUBLANES, channels)),
+        struct((parts, seg_len, LANES)),
+        few,
+        few,
+        struct((1, channels)),
+        struct((1, cols)),
+    ]
+    thin = [struct((seg_len, LANES)), struct((seg_len + PIECES * modes, LANES), jnp.bfloat16)]
+    total, *state = call(state_kernel, [few, *kept], *inputs, scratch=scratch, hbm=INPUTS)
+    own_total, *state, first_local, first_short = call(
+        local_kernel, [few, *kept, *thin], *inputs, total, *state,
+        scratch=scratch, hbm=INPUTS, aliases=[(INPUTS + 1 + i, 1 + i) for i in range(KEPT)],
     )
-    local, local_short = call(
-        local_kernel,
-        [struct((parts, seg_len, LANES)), taller],
-        gated, decay, residue, skip, chunks, local, local_short,
-        aliases={5: 0, 6: 1},
-    )
-    local_across = swapped(local_short, 2)
-    base, extra, q_across = carry_shares(total, decay, residue, seg_len, q_across)
-    extra_beside = beside(extra, 1)
+    chunks, gated, decay, residue, skip, bias = state
+    local, short = [first_local], [first_short]
+    for part in range(1, parts):
+        more = call(functools.partial(convolve, part), thin, gated, decay, residue, skip, chunks, cost=MORE_COST)
+        local.append(more[0])
+        short.append(more[1])
+    local_across = [swapped(block, 2) for block in short]
+    base, extra, q_across = carry_shares(total, own_total, decay, residue, seg_len, q_across)
+    extra_beside, local_across[0] = lax.optimization_barrier((beside(extra, 1), local_across[0]))
     extra_corner = corner(extra, 1, 2)
     base_across = swapped(base, 2)
-    own = call(functools.partial(carry_kernel, 0), short, q_gate, local, decay, base, extra_beside)
+    whole = struct((seg_len, channels), jnp.bfloat16)
+    own = call(own_kernel, whole, q_gate, decay, base, extra_beside, *local, cost=OWN_COST)
     pair = swapped(own, 1)
     half = struct((seg_len, LANES), jnp.bfloat16)
     across = [
         call(
-            functools.partial(across_kernel, part), half, extra_corner, base_across, q_across, local_across,
+            functools.partial(across_kernel, part), half, extra_corner, base_across, q_across, local_across[part],
             cost=PART_COST,
         )
         for part in range(parts)

time: 23.6 us -> 23.5 us (level)
  waiting for transfers between devices: 4.68 us -> 2.29 us
  starting transfers between devices: 11.7 us -> 13.8 us
    ppermute x6 -> x7, starting transfers between devices: 5.19 us -> 7.79 us  [swapped(): return lax.ppermute(value, 'chan', [(r, r ^ bit) for r in range(count)])]
    ppermute x4, waiting for transfers between devices: 2.63 us -> 0.25 us  [beside(): return lax.ppermute(value, 'seq', [(r, r ^ step) for r in range(count)])]
    ppermute x1, starting transfers between devices: 0.48 us -> 0.02 us  [corner(): return lax.ppermute(value, ('seq', 'chan'), pairs)]
    pallas_call x8 -> x9, Pallas kernels: 6.85 us -> 6.92 us  [call(): pl.pallas_call(kernel, out_shape=out, in_specs=[pl.BlockSpec(memory_space...]
    ppermute x6 -> x7, waiting for transfers between devices: 0.51 us -> 0.52 us  [swapped(): return lax.ppermute(value, 'chan', [(r, r ^ bit) for r in range(count)])]
  transfers between devices with their start and end apart: 11 -> 12, of which waited for: 6 -> 3; matrix products, arithmetic and copies ran while one was open for 0% -> 0% of each run, Pallas kernels for 25% -> 26%
where the time goes in v4:
time: 23.5 us; the launch traced here: 23.2 us
  starting transfers between devices  13.8 us (59%)
  Pallas kernels  6.92 us (29%)
  waiting for transfers between devices  2.29 us (10%)
    ppermute x7, starting transfers between devices, swapped(): return lax.ppermute(value, 'chan', [(r, r ^ bit) for r in range(count)])  7.79 us
    pallas_call x9, Pallas kernels, call(): pl.pallas_call(kernel, out_shape=out, in_specs=[pl.BlockSpec(memory_space...  6.92 us
    ppermute x4, starting transfers between devices, beside(): return lax.ppermute(value, 'seq', [(r, r ^ step) for r in range(count)])  6.01 us
    ppermute x1, waiting for transfers between devices, corner(): return lax.ppermute(value, ('seq', 'chan'), pairs)  1.51 us
    ppermute x7, waiting for transfers between devices, swapped(): return lax.ppermute(value, 'chan', [(r, r ^ bit) for r in range(count)])  0.52 us
  transfers between devices with their start and end apart: 12, of which 3 were waited for; matrix products, arithmetic and copies ran while one was open for 0% of the time, Pallas kernels for 26%

profile of v4, /device:TPU:0, one launch (start us, length us, event | category | flops | bytes accessed | tf_op | source)
XLA Modules:
  0.0 23.2 jit_solution(2089556610795501688)
XLA Ops:
  0.0 3.0 %collective-permute-start.3 = (bf16[512,256]{1,0:T(8,128)(2,1)}, bf16[512,256]{1,0:T(8,128)(2,1)S(1)}, u32[]{:S(2)}, u32[]{:S(2)}) collective-permute-start(bf16[512,256]{1,0:T(8,128)(2,1)} %q_ref.1), channel_id=1, source_target_pairs={{0,2},{1,3},{2,0},{3,1},{4,6},{5,7},{6,4},{7,5},{8,10},{9,11},{10,... | collective-permute-start | bytes 786440 | tf_op jit(solution)/shard_map/ppermute | solution.py:291
  3.0 2.0 %shard_map.82 = (f32[16,256]{1,0:T(8,128)S(1)}, f32[16,8,256]{2,1,0:T(8,128)S(1)}, f32[2,512,128]{2,1,0:T(8,128)S(1)}, f32[16,256]{1,0:T(8,128)S(1)}, f32[16,256...) custom-call(bf16[512,256]{1,0:T(8,128)(2,1)} %refs_0_.3, bf16[512,256]{1,0:T(8,128)(2,1)} %refs_1_.3, ...), custom_call_target="tpu_custom_call" | custom-call | tf_op jit(solution)/shard_map/pallas_call | solution.py:273
  5.0 1.7 %collective-permute-start = (f32[16,256]{1,0:T(8,128)S(1)}, f32[16,256]{1,0:T(8,128)S(1)}, u32[]{:S(2)}, u32[]{:S(2)}) collective-permute-start(f32[16,256]{1,0:T(8,128)S(1)} %get-tuple-element.31.refs_6_.total_ref), channel_id=1, source_target_pairs={{0,24},{4,28},{8,16},{12,20},{16,8},{20,12},{24,0},{28,4},{1,25},{... | collective-permute-start | bytes 49160 | tf_op jit(solution)/shard_map/ppermute | solution.py:296
  6.7 1.4 %collective-permute-start.1 = (f32[16,256]{1,0:T(8,128)S(1)}, f32[16,256]{1,0:T(8,128)S(1)}, u32[]{:S(2)}, u32[]{:S(2)}) collective-permute-start(f32[16,256]{1,0:T(8,128)S(1)} %get-tuple-element.31.refs_6_.total_ref), channel_id=1, source_target_pairs={{0,16},{4,20},{8,24},{12,28},{16,0},{20,4},{24,8},{28,12},{1,17},{... | collective-permute-start | bytes 49160 | tf_op jit(solution)/shard_map/ppermute | solution.py:296
  8.1 1.3 %collective-permute-start.2 = (f32[16,256]{1,0:T(8,128)S(1)}, f32[16,256]{1,0:T(8,128)S(1)}, u32[]{:S(2)}, u32[]{:S(2)}) collective-permute-start(f32[16,256]{1,0:T(8,128)S(1)} %get-tuple-element.31.refs_6_.total_ref), channel_id=1, source_target_pairs={{0,8},{4,12},{8,0},{12,4},{16,24},{20,28},{24,16},{28,20},{1,9},{5... | collective-permute-start | bytes 49160 | tf_op jit(solution)/shard_map/ppermute | solution.py:296
  9.4 1.0 %shard_map.83 = (f32[16,256]{1,0:T(8,128)S(1)}, f32[16,8,256]{2,1,0:T(8,128)S(1)}, f32[2,512,128]{2,1,0:T(8,128)S(1)}, f32[16,256]{1,0:T(8,128)S(1)}, f32[16,256...) custom-call(bf16[512,256]{1,0:T(8,128)(2,1)} %refs_0_.3, ...), custom_call_target="tpu_custom_call", output_to_operand_aliasing={{1}: (7, {}), {2}: (8, {}), {3}: (9, {}), {4}: (10, {}), {5... | custom-call | tf_op jit(solution)/shard_map/pallas_call | solution.py:273
  10.4 0.1 collective-permute-start.5
  10.5 0.9 %shard_map.85 = (f32[512,128]{1,0:T(8,128)S(1)}, bf16[560,128]{1,0:T(8,128)(2,1)S(1)}) custom-call(f32[2,512,128]{2,1,0:T(8,128)S(1)} %get-tuple-element.50.gated, f32[16,256]{1,0:T(8,128)S(1)} %get-tuple-element.39.rates_ref.decay_ref, f32[16,256]{1,0:T(8,128)S(1)} %get-tuple-element.40.residue_ref, f32[1,256]{1,0:T(1,128)S(1)} %get-tuple-element.51.skip_ref, ...), custom_call_target="tpu_custom_call" | custom-call | flops 1000000000 | tf_op jit(solution)/shard_map/pallas_call | solution.py:273
  11.5 0.0 collective-permute-done.rest_0_
  11.5 2.1 %collective-permute-start.9 = (bf16[560,128]{1,0:T(8,128)(2,1)S(1)}, bf16[560,128]{1,0:T(8,128)(2,1)S(1)}, u32[]{:S(2)}, u32[]{:S(2)}) collective-permute-start(bf16[560,128]{1,0:T(8,128)(2,1)S(1)} %get-tuple-element.56), channel_id=1, source_target_pairs={{0,2},{1,3},{2,0},{3,1},{4,6},{5,7},{6,4},{7,5},{8,10},{9,11},{10,... | collective-permute-start | bytes 430088 | tf_op jit(solution)/shard_map/ppermute | solution.py:291
  13.6 0.0 collective-permute-done.1.rest_1_
  13.6 0.0 collective-permute-done.2.rest_2_
  13.6 0.0 collective-permute-done.3.q_ref
  13.6 0.0 copy-start.1
  13.6 1.6 %collective-permute-start.4 = (f32[16,256]{1,0:T(8,128)S(1)}, f32[16,256]{1,0:T(8,128)S(1)}, u32[]{:S(2)}, u32[]{:S(2)}) collective-permute-start(f32[16,256]{1,0:T(8,128)S(1)} %get-tuple-element.46), channel_id=1, source_target_pairs={{0,4},{4,0},{8,12},{12,8},{16,20},{20,16},{24,28},{28,24},{1,5},{5... | collective-permute-start | bytes 49160 | tf_op jit(solution)/shard_map/ppermute | solution.py:296
  15.2 0.0 collective-permute-start.7
  15.2 2.0 %collective-permute-start.8 = (f32[16,256]{1,0:T(8,128)S(1)}, f32[16,256]{1,0:T(8,128)S(1)}, u32[]{:S(2)}, u32[]{:S(2)}) collective-permute-start(f32[16,256]{1,0:T(8,128)S(1)} %get-tuple-element.45.base_ref), channel_id=1, source_target_pairs={{0,2},{1,3},{2,0},{3,1},{4,6},{5,7},{6,4},{7,5},{8,10},{9,11},{10,... | collective-permute-start | bytes 49160 | tf_op jit(solution)/shard_map/ppermute | solution.py:291
  17.2 0.0 collective-permute-done.5.local_ref
  17.2 0.2 %collective-permute-done.4.extra_ref = f32[16,256]{1,0:T(8,128)S(1)} collective-permute-done((f32[16,256]{1,0:T(8,128)S(1)}, f32[16,256]{1,0:T(8,128)S(1)}, u32[]{:S(2)}, u32[]{:S(2)}) %collective-permute-start.4) | collective-permute-done | bytes 16416 | tf_op jit(solution)/shard_map/ppermute | solution.py:296
  17.4 0.0 copy-done.1
  17.4 0.8 %shard_map.86.own_ref = bf16[512,256]{1,0:T(8,128)(2,1)S(1)} custom-call(bf16[512,256]{1,0:T(8,128)(2,1)S(1)} %copy-done.1, f32[16,256]{1,0:T(8,128)S(1)} %get-tuple-element.39.rates_ref.decay_ref, f32[16,256]{1,0:T(8,128)S(1)} %get-tuple-element.45.base_ref, f32[16,256]{1,0:T(8,128)S(1)} %collective-permute-done.4.extra_ref, ...), custom_call_target="tpu_custom_call" | custom-call | flops 1000000000 | tf_op jit(solution)/shard_map/pallas_call | solution.py:273
  18.2 0.1 collective-permute-start.6
  18.3 0.0 collective-permute-done.9.local_ref
  18.3 1.5 %collective-permute-done.7.extra_ref = f32[16,256]{1,0:T(8,128)S(1)} collective-permute-done((f32[16,256]{1,0:T(8,128)S(1)}, f32[16,256]{1,0:T(8,128)S(1)}, u32[]{:S(2)}, u32[]{:S(2)}) %collective-permute-start.7) | collective-permute-done | bytes 16416 | tf_op jit(solution)/shard_map/ppermute | solution.py:302
  19.8 0.0 collective-permute-done.8.base_ref
  19.8 0.4 %shard_map.88.rest_1_ = bf16[512,128]{1,0:T(8,128)(2,1)S(1)} custom-call(f32[16,256]{1,0:T(8,128)S(1)} %collective-permute-done.7.extra_ref, f32[16,256]{1,0:T(8,128)S(1)} %collective-permute-done.8.base_ref, bf16[512,256]{1,0:T(8,128)(2,1)S(1)} %collective-permute-done.3.q_ref, bf16[560,128]{1,0:T(8,128)(2,1)S(1)} %collective-permute-done.9.local_ref), custom_call_target="tpu_custom_call" | custom-call | flops 4000000000 | tf_op jit(solution)/shard_map/pallas_call | solution.py:273
  20.2 0.0 copy-start
  20.2 0.1 collective-permute-start.11
  20.3 0.4 %shard_map.87.rest_0_ = bf16[512,128]{1,0:T(8,128)(2,1)S(1)} custom-call(f32[16,256]{1,0:T(8,128)S(1)} %collective-permute-done.7.extra_ref, f32[16,256]{1,0:T(8,128)S(1)} %collective-permute-done.8.base_ref, bf16[512,256]{1,0:T(8,128)(2,1)S(1)} %collective-permute-done.3.q_ref, bf16[560,128]{1,0:T(8,128)(2,1)S(1)} %collective-permute-done.5.local_ref), custom_call_target="tpu_custom_call" | custom-call | flops 4000000000 | tf_op jit(solution)/shard_map/pallas_call | solution.py:273
  20.7 0.6 %collective-permute-start.10 = (bf16[512,128]{1,0:T(8,128)(2,1)S(1)}, bf16[512,128]{1,0:T(8,128)(2,1)S(1)}, u32[]{:S(2)}, u32[]{:S(2)}) collective-permute-start(bf16[512,128]{1,0:T(8,128)(2,1)S(1)} %shard_map.87.rest_0_), channel_id=1, source_target_pairs={{0,1},{1,0},{2,3},{3,2},{4,5},{5,4},{6,7},{7,6},{8,9},{9,8},{10,11... | collective-permute-start | bytes 393224 | tf_op jit(solution)/shard_map/ppermute | solution.py:291
  21.2 0.0 collective-permute-done.6.pair_ref
  21.2 0.0 copy-done
  21.2 0.4 %shard_map.89.near_ref = f32[512,256]{1,0:T(8,128)S(1)} custom-call(bf16[1024,256]{1,0:T(8,128)(2,1)S(1)} %copy-done, f32[1,256]{1,0:T(1,128)S(1)} %get-tuple-element.38.bias_ref, bf16[512,256]{1,0:T(8,128)(2,1)S(1)} %shard_map.86.own_ref, bf16[512,256]{1,0:T(8,128)(2,1)S(1)} %collective-permute-done.6.pair_ref, bf16[512,128]{1,0:T(8,128)(2,1)S(1)} %shard_map.87.rest_0_, ...), custom_call_target="tpu_custom_call" | custom-call | tf_op jit(solution)/shard_map/pallas_call | solution.py:273
  21.7 0.0 collective-permute-done.11.rest_1_
  21.7 0.5 %collective-permute-done.10.rest_0_ = bf16[512,128]{1,0:T(8,128)(2,1)S(1)} collective-permute-done((bf16[512,128]{1,0:T(8,128)(2,1)S(1)}, bf16[512,128]{1,0:T(8,128)(2,1)S(1)}, u32[]{:S(2)}, u32[]{:S(2)}) %collective-permute-start.10) | collective-permute-done | bytes 131104 | tf_op jit(solution)/shard_map/ppermute | solution.py:291
  22.2 1.0 %shard_map.90 = bf16[512,256]{1,0:T(8,128)(2,1)} custom-call(f32[512,256]{1,0:T(8,128)S(1)} %shard_map.89.near_ref, bf16[1024,256]{1,0:T(8,128)(2,1)S(1)} %copy-done, bf16[512,128]{1,0:T(8,128)(2,1)S(1)} %collective-permute-done.10.rest_0_, bf16[512,128]{1,0:T(8,128)(2,1)S(1)} %collective-permute-done.11.rest_1_), custom_call_target="tpu_custom_call" | custom-call | tf_op jit(solution)/shard_map/pallas_call | solution.py:273
  (1 shorter events, 0.0 us)
Async XLA Ops:
  0.0 13.6 %collective-permute-start.3 = (bf16[512,256]{1,0:T(8,128)(2,1)}, bf16[512,256]{1,0:T(8,128)(2,1)S(1)}, u32[]{:S(2)}, u32[]{:S(2)}) collective-permute-start(bf16[512,256]{1,0:T(8,128)(2,1)} %q_ref.1), channel_id=1, source_target_pairs={{0,2},{1,3},{2,0},{3,1},{4,6},{5,7},{6,4},{7,5},{8,10},{9,11},{10,... | collective-permute-start | bytes 786440 | tf_op jit(solution)/shard_map/ppermute | solution.py:291
  5.0 6.5 %collective-permute-start = (f32[16,256]{1,0:T(8,128)S(1)}, f32[16,256]{1,0:T(8,128)S(1)}, u32[]{:S(2)}, u32[]{:S(2)}) collective-permute-start(f32[16,256]{1,0:T(8,128)S(1)} %get-tuple-element.31.refs_6_.total_ref), channel_id=1, source_target_pairs={{0,24},{4,28},{8,16},{12,20},{16,8},{20,12},{24,0},{28,4},{1,25},{... | collective-permute-start | bytes 49160 | tf_op jit(solution)/shard_map/ppermute | solution.py:296
  6.7 6.8 %collective-permute-start.1 = (f32[16,256]{1,0:T(8,128)S(1)}, f32[16,256]{1,0:T(8,128)S(1)}, u32[]{:S(2)}, u32[]{:S(2)}) collective-permute-start(f32[16,256]{1,0:T(8,128)S(1)} %get-tuple-element.31.refs_6_.total_ref), channel_id=1, source_target_pairs={{0,16},{4,20},{8,24},{12,28},{16,0},{20,4},{24,8},{28,12},{1,17},{... | collective-permute-start | bytes 49160 | tf_op jit(solution)/shard_map/ppermute | solution.py:296
  8.1 5.5 %collective-permute-start.2 = (f32[16,256]{1,0:T(8,128)S(1)}, f32[16,256]{1,0:T(8,128)S(1)}, u32[]{:S(2)}, u32[]{:S(2)}) collective-permute-start(f32[16,256]{1,0:T(8,128)S(1)} %get-tuple-element.31.refs_6_.total_ref), channel_id=1, source_target_pairs={{0,8},{4,12},{8,0},{12,4},{16,24},{20,28},{24,16},{28,20},{1,9},{5... | collective-permute-start | bytes 49160 | tf_op jit(solution)/shard_map/ppermute | solution.py:296
  10.4 6.7 %collective-permute-start.5 = (bf16[560,128]{1,0:T(8,128)(2,1)S(1)}, bf16[560,128]{1,0:T(8,128)(2,1)S(1)}, u32[]{:S(2)}, u32[]{:S(2)}) collective-permute-start(bf16[560,128]{1,0:T(8,128)(2,1)S(1)} %get-tuple-element.47), channel_id=1, source_target_pairs={{0,2},{1,3},{2,0},{3,1},{4,6},{5,7},{6,4},{7,5},{8,10},{9,11},{10,... | collective-permute-start | bytes 430088 | tf_op jit(solution)/shard_map/ppermute | solution.py:291
  11.5 6.8 %collective-permute-start.9 = (bf16[560,128]{1,0:T(8,128)(2,1)S(1)}, bf16[560,128]{1,0:T(8,128)(2,1)S(1)}, u32[]{:S(2)}, u32[]{:S(2)}) collective-permute-start(bf16[560,128]{1,0:T(8,128)(2,1)S(1)} %get-tuple-element.56), channel_id=1, source_target_pairs={{0,2},{1,3},{2,0},{3,1},{4,6},{5,7},{6,4},{7,5},{8,10},{9,11},{10,... | collective-permute-start | bytes 430088 | tf_op jit(solution)/shard_map/ppermute | solution.py:291
  13.6 3.9 %copy-start.1 = (bf16[512,256]{1,0:T(8,128)(2,1)S(1)}, bf16[512,256]{1,0:T(8,128)(2,1)}, u32[]{:S(2)}) copy-start(bf16[512,256]{1,0:T(8,128)(2,1)} %q_ref.1) | copy-start | bytes 786436
  13.6 3.8 %collective-permute-start.4 = (f32[16,256]{1,0:T(8,128)S(1)}, f32[16,256]{1,0:T(8,128)S(1)}, u32[]{:S(2)}, u32[]{:S(2)}) collective-permute-start(f32[16,256]{1,0:T(8,128)S(1)} %get-tuple-element.46), channel_id=1, source_target_pairs={{0,4},{4,0},{8,12},{12,8},{16,20},{20,16},{24,28},{28,24},{1,5},{5... | collective-permute-start | bytes 49160 | tf_op jit(solution)/shard_map/ppermute | solution.py:296
  15.2 4.6 %collective-permute-start.7 = (f32[16,256]{1,0:T(8,128)S(1)}, f32[16,256]{1,0:T(8,128)S(1)}, u32[]{:S(2)}, u32[]{:S(2)}) collective-permute-start(f32[16,256]{1,0:T(8,128)S(1)} %get-tuple-element.46), channel_id=1, source_target_pairs={{0,6},{1,7},{2,4},{3,5},{4,2},{5,3},{6,0},{7,1},{8,14},{9,15},{10,... | collective-permute-start | bytes 49160 | tf_op jit(solution)/shard_map/ppermute | solution.py:302
  15.2 4.6 %collective-permute-start.8 = (f32[16,256]{1,0:T(8,128)S(1)}, f32[16,256]{1,0:T(8,128)S(1)}, u32[]{:S(2)}, u32[]{:S(2)}) collective-permute-start(f32[16,256]{1,0:T(8,128)S(1)} %get-tuple-element.45.base_ref), channel_id=1, source_target_pairs={{0,2},{1,3},{2,0},{3,1},{4,6},{5,7},{6,4},{7,5},{8,10},{9,11},{10,... | collective-permute-start | bytes 49160 | tf_op jit(solution)/shard_map/ppermute | solution.py:291
  18.2 3.0 %collective-permute-start.6 = (bf16[512,256]{1,0:T(8,128)(2,1)S(1)}, bf16[512,256]{1,0:T(8,128)(2,1)S(1)}, u32[]{:S(2)}, u32[]{:S(2)}) collective-permute-start(bf16[512,256]{1,0:T(8,128)(2,1)S(1)} %shard_map.86.own_ref), channel_id=1, source_target_pairs={{0,1},{1,0},{2,3},{3,2},{4,5},{5,4},{6,7},{7,6},{8,9},{9,8},{10,11... | collective-permute-start | bytes 786440 | tf_op jit(solution)/shard_map/ppermute | solution.py:291
  20.2 1.0 %copy-start = (bf16[1024,256]{1,0:T(8,128)(2,1)S(1)}, bf16[1024,256]{1,0:T(8,128)(2,1)}, u32[]{:S(2)}) copy-start(bf16[1024,256]{1,0:T(8,128)(2,1)} %weight_ref.3) | copy-start | bytes 1572868
  20.2 1.5 %collective-permute-start.11 = (bf16[512,128]{1,0:T(8,128)(2,1)S(1)}, bf16[512,128]{1,0:T(8,128)(2,1)S(1)}, u32[]{:S(2)}, u32[]{:S(2)}) collective-permute-start(bf16[512,128]{1,0:T(8,128)(2,1)S(1)} %shard_map.88.rest_1_), channel_id=1, source_target_pairs={{0,1},{1,0},{2,3},{3,2},{4,5},{5,4},{6,7},{7,6},{8,9},{9,8},{10,11... | collective-permute-start | bytes 393224 | tf_op jit(solution)/shard_map/ppermute | solution.py:291
  20.7 1.5 %collective-permute-start.10 = (bf16[512,128]{1,0:T(8,128)(2,1)S(1)}, bf16[512,128]{1,0:T(8,128)(2,1)S(1)}, u32[]{:S(2)}, u32[]{:S(2)}) collective-permute-start(bf16[512,128]{1,0:T(8,128)(2,1)S(1)} %shard_map.87.rest_0_), channel_id=1, source_target_pairs={{0,1},{1,0},{2,3},{3,2},{4,5},{5,4},{6,7},{7,6},{8,9},{9,8},{10,11... | collective-permute-start | bytes 393224 | tf_op jit(solution)/shard_map/ppermute | solution.py:291

commit v5 on v4

--- a/solution.py
+++ b/solution.py
@@ -9,14 +9,13 @@
 
 LANES = 128
 SUBLANES = 8
-STORES = 2
-OWN_COST = 1000000000
-MORE_COST = 1000000000
-FOLD_COST = 500000000
+STORES = 4
+OWN_COST = 0
+FOLD_COST = 3000000000
 PIECES = 3
 INPUTS = 6
 KEPT = 6
-PART_COST = 4000000000
+PART_COST = 0
 VMEM_LIMIT = 32 * 1024 * 1024
 
 
@@ -100,7 +99,7 @@
 def local_kernel(*refs):
     inputs, rest = refs[:INPUTS], refs[INPUTS:]
     total_in, rest = rest[0], rest[1 + KEPT :]
-    total_ref, kept, (local_ref, short_ref), scratch = rest[0], rest[1 : 1 + KEPT], rest[1 + KEPT : -3], rest[-3:]
+    total_ref, kept, (*locals_out, short_ref), scratch = rest[0], rest[1 : 1 + KEPT], rest[1 + KEPT : -3], rest[-3:]
     chunk_ref, gated_ref, decay_ref, residue_ref, skip_ref, _ = kept
 
     @pl.when(is_last())
@@ -111,7 +110,8 @@
     def _():
         total_ref[...] = total_in[...]
 
-    convolve(0, gated_ref, decay_ref, residue_ref, skip_ref, chunk_ref, local_ref, short_ref)
+    for part, local_ref in enumerate(locals_out):
+        convolve(part, gated_ref, decay_ref, residue_ref, skip_ref, chunk_ref, local_ref, short_ref)
 
 
 def convolve(part, gated, decay_ref, residue_ref, skip_ref, chunk_ref, local_ref, short_ref):
@@ -140,11 +140,11 @@
         return state
 
     lax.fori_loop(0, chunk_len, step, tuple(start), unroll=4)
-    short_ref[:seg_len, :] = local_ref[...].astype(short_ref.dtype)
+    short_ref[:seg_len, lanes] = local_ref[...].astype(short_ref.dtype)
     left = decay_ref[:, lanes]
     for first in range(seg_len, short_ref.shape[0], modes):
         piece = left.astype(short_ref.dtype)
-        short_ref[first : first + modes, :] = piece
+        short_ref[first : first + modes, lanes] = piece
         left = left - piece.astype(jnp.float32)
 
 
@@ -221,7 +221,7 @@
         carry(q_ref, local_ref, rates_ref[:, lane_slice(part)], base_ref, extra_ref, out_ref, part, part)
 
 
-def across_kernel(part, extra_ref, base_ref, q_ref, local_ref, out_ref):
+def across_kernel(extra_ref, base_ref, q_ref, local_ref, out_ref):
     modes = base_ref.shape[0]
     seg_len = q_ref.shape[0]
     pieces = [
@@ -229,7 +229,9 @@
         for first in range(seg_len, local_ref.shape[0], modes)
     ]
     rates = (pieces[2] + pieces[1]) + pieces[0]
-    carry(q_ref, local_ref, rates, base_ref, extra_ref, out_ref, part, 0)
+    for part in range(q_ref.shape[1] // LANES):
+        lanes = lane_slice(part)
+        carry(q_ref, local_ref.at[:, lanes], rates[:, lanes], base_ref, extra_ref, out_ref, part, part)
 
 
 def project(blocks, weight_ref):
@@ -340,38 +342,29 @@
         struct((1, channels)),
         struct((1, cols)),
     ]
-    thin = [struct((seg_len, LANES)), struct((seg_len + PIECES * modes, LANES), jnp.bfloat16)]
+    thin = struct((seg_len, LANES))
+    short = struct((seg_len + PIECES * modes, channels), jnp.bfloat16)
     total, *state = call(state_kernel, [few, *kept], *inputs, scratch=scratch, hbm=INPUTS)
-    own_total, *state, first_local, first_short = call(
-        local_kernel, [few, *kept, *thin], *inputs, total, *state,
+    own_total, *state = call(
+        local_kernel, [few, *kept, *[thin] * parts, short], *inputs, total, *state,
         scratch=scratch, hbm=INPUTS, aliases=[(INPUTS + 1 + i, 1 + i) for i in range(KEPT)],
     )
-    chunks, gated, decay, residue, skip, bias = state
-    local, short = [first_local], [first_short]
-    for part in range(1, parts):
-        more = call(functools.partial(convolve, part), thin, gated, decay, residue, skip, chunks, cost=MORE_COST)
-        local.append(more[0])
-        short.append(more[1])
-    local_across = [swapped(block, 2) for block in short]
+    _, _, decay, residue, _, bias, *local, local_short = state
+    local_across = swapped(local_short, 2)
     base, extra, q_across = carry_shares(total, own_total, decay, residue, seg_len, q_across)
-    extra_beside, local_across[0] = lax.optimization_barrier((beside(extra, 1), local_across[0]))
+    extra_beside = beside(extra, 1)
     extra_corner = corner(extra, 1, 2)
     base_across = swapped(base, 2)
     whole = struct((seg_len, channels), jnp.bfloat16)
     own = call(own_kernel, whole, q_gate, decay, base, extra_beside, *local, cost=OWN_COST)
     pair = swapped(own, 1)
-    half = struct((seg_len, LANES), jnp.bfloat16)
-    across = [
-        call(
-            functools.partial(across_kernel, part), half, extra_corner, base_across, q_across, local_across[part],
-            cost=PART_COST,
-        )
-        for part in range(parts)
-    ]
-    diagonal = [swapped(block, 1) for block in across]
-    near = call(near_kernel, struct((seg_len, cols)), out_weight, bias, own, pair, *across)
+    across = call(
+        across_kernel, whole, extra_corner, base_across, q_across, local_across, cost=PART_COST
+    )
+    diagonal = swapped(across, 1)
+    near = call(near_kernel, struct((seg_len, cols)), out_weight, bias, own, pair, across)
     return call(
-        last_kernel, struct((seg_len, cols), jnp.bfloat16), near, out_weight, *diagonal,
+        last_kernel, struct((seg_len, cols), jnp.bfloat16), near, out_weight, diagonal,
         scratch=[pltpu.VMEM((seg_len, cols), jnp.bfloat16), pltpu.SemaphoreType.DMA((STORES,))],
         outs=pltpu.HBM,
     )

time: 23.5 us -> 23.2 us (0.987)
  starting transfers between devices: 13.8 us -> 11.2 us
  waiting for transfers between devices: 2.29 us -> 4.76 us
    ppermute x7 -> x5, starting transfers between devices: 7.79 us -> 3.51 us  [swapped(): return lax.ppermute(value, 'chan', [(r, r ^ bit) for r in range(count)])]
    ppermute x7 -> x5, waiting for transfers between devices: 0.52 us -> 2.38 us  [swapped(): return lax.ppermute(value, 'chan', [(r, r ^ bit) for r in range(count)])]
    ppermute x1, starting transfers between devices: 0.02 us -> 1.49 us  [corner(): return lax.ppermute(value, ('seq', 'chan'), pairs)]
    ppermute x4, waiting for transfers between devices: 0.25 us -> 0.58 us  [beside(): return lax.ppermute(value, 'seq', [(r, r ^ step) for r in range(count)])]
    ppermute x1, waiting for transfers between devices: 1.51 us -> 1.81 us  [corner(): return lax.ppermute(value, ('seq', 'chan'), pairs)]
    pallas_call x9 -> x7, Pallas kernels: 6.92 us -> 6.87 us  [call(): pl.pallas_call(kernel, out_shape=out, in_specs=[pl.BlockSpec(memory_space...]
  transfers between devices with their start and end apart: 12 -> 10, of which waited for: 3 -> 5; matrix products, arithmetic and copies ran while one was open for 0% -> 0% of each run, Pallas kernels for 26% -> 26%
where the time goes in v5:
time: 23.2 us; the launch traced here: 22.9 us
  starting transfers between devices  11.2 us (48%)
  Pallas kernels  6.87 us (30%)
  waiting for transfers between devices  4.76 us (21%)
    pallas_call x7, Pallas kernels, call(): pl.pallas_call(kernel, out_shape=out, in_specs=[pl.BlockSpec(memory_space...  6.87 us
    ppermute x4, starting transfers between devices, beside(): return lax.ppermute(value, 'seq', [(r, r ^ step) for r in range(count)])  6.19 us
    ppermute x5, starting transfers between devices, swapped(): return lax.ppermute(value, 'chan', [(r, r ^ bit) for r in range(count)])  3.51 us
    ppermute x5, waiting for transfers between devices, swapped(): return lax.ppermute(value, 'chan', [(r, r ^ bit) for r in range(count)])  2.38 us
    ppermute x1, waiting for transfers between devices, corner(): return lax.ppermute(value, ('seq', 'chan'), pairs)  1.81 us
    ppermute x1, starting transfers between devices, corner(): return lax.ppermute(value, ('seq', 'chan'), pairs)  1.49 us
    ppermute x4, waiting for transfers between devices, beside(): return lax.ppermute(value, 'seq', [(r, r ^ step) for r in range(count)])  0.58 us
  transfers between devices with their start and end apart: 10, of which 5 were waited for; matrix products, arithmetic and copies ran while one was open for 0% of the time, Pallas kernels for 26%

profile of v5, /device:TPU:0, one launch (start us, length us, event | category | flops | bytes accessed | tf_op | source)
XLA Modules:
  0.0 22.9 jit_solution(13037567412466613505)
XLA Ops:
  0.0 3.0 %collective-permute-start.3 = (bf16[512,256]{1,0:T(8,128)(2,1)}, bf16[512,256]{1,0:T(8,128)(2,1)S(1)}, u32[]{:S(2)}, u32[]{:S(2)}) collective-permute-start(bf16[512,256]{1,0:T(8,128)(2,1)} %q_ref.1), channel_id=1, source_target_pairs={{0,2},{1,3},{2,0},{3,1},{4,6},{5,7},{6,4},{7,5},{8,10},{9,11},{10,... | collective-permute-start | bytes 786440 | tf_op jit(solution)/shard_map/ppermute | solution.py:293
  3.0 2.0 %shard_map.82 = (f32[16,256]{1,0:T(8,128)S(1)}, f32[16,8,256]{2,1,0:T(8,128)S(1)}, f32[2,512,128]{2,1,0:T(8,128)S(1)}, f32[16,256]{1,0:T(8,128)S(1)}, f32[16,256...) custom-call(bf16[512,256]{1,0:T(8,128)(2,1)} %refs_0_.3, bf16[512,256]{1,0:T(8,128)(2,1)} %refs_1_.3, ...), custom_call_target="tpu_custom_call" | custom-call | tf_op jit(solution)/shard_map/pallas_call | solution.py:275
  5.0 1.7 %collective-permute-start = (f32[16,256]{1,0:T(8,128)S(1)}, f32[16,256]{1,0:T(8,128)S(1)}, u32[]{:S(2)}, u32[]{:S(2)}) collective-permute-start(f32[16,256]{1,0:T(8,128)S(1)} %get-tuple-element.25.refs_6_.total_ref), channel_id=1, source_target_pairs={{0,24},{4,28},{8,16},{12,20},{16,8},{20,12},{24,0},{28,4},{1,25},{... | collective-permute-start | bytes 49160 | tf_op jit(solution)/shard_map/ppermute | solution.py:298
  6.7 1.4 %collective-permute-start.1 = (f32[16,256]{1,0:T(8,128)S(1)}, f32[16,256]{1,0:T(8,128)S(1)}, u32[]{:S(2)}, u32[]{:S(2)}) collective-permute-start(f32[16,256]{1,0:T(8,128)S(1)} %get-tuple-element.25.refs_6_.total_ref), channel_id=1, source_target_pairs={{0,16},{4,20},{8,24},{12,28},{16,0},{20,4},{24,8},{28,12},{1,17},{... | collective-permute-start | bytes 49160 | tf_op jit(solution)/shard_map/ppermute | solution.py:298
  8.1 1.3 %collective-permute-start.2 = (f32[16,256]{1,0:T(8,128)S(1)}, f32[16,256]{1,0:T(8,128)S(1)}, u32[]{:S(2)}, u32[]{:S(2)}) collective-permute-start(f32[16,256]{1,0:T(8,128)S(1)} %get-tuple-element.25.refs_6_.total_ref), channel_id=1, source_target_pairs={{0,8},{4,12},{8,0},{12,4},{16,24},{20,28},{24,16},{28,20},{1,9},{5... | collective-permute-start | bytes 49160 | tf_op jit(solution)/shard_map/ppermute | solution.py:298
  9.4 2.0 %shard_map.83 = (f32[16,256]{1,0:T(8,128)S(1)}, f32[16,8,256]{2,1,0:T(8,128)S(1)}, f32[2,512,128]{2,1,0:T(8,128)S(1)}, f32[16,256]{1,0:T(8,128)S(1)}, f32[16,256...) custom-call(bf16[512,256]{1,0:T(8,128)(2,1)} %refs_0_.3, ...), custom_call_target="tpu_custom_call", output_to_operand_aliasing={{1}: (7, {}), {2}: (8, {}), {3}: (9, {}), {4}: (10, {}), {5... | custom-call | tf_op jit(solution)/shard_map/pallas_call | solution.py:275
  11.4 0.1 collective-permute-start.8
  11.5 0.0 collective-permute-done.rest_0_
  11.5 0.0 collective-permute-done.1.rest_1_
  11.5 0.3 %collective-permute-done.2.rest_2_ = f32[16,256]{1,0:T(8,128)S(1)} collective-permute-done((f32[16,256]{1,0:T(8,128)S(1)}, f32[16,256]{1,0:T(8,128)S(1)}, u32[]{:S(2)}, u32[]{:S(2)}) %collective-permute-start.2) | collective-permute-done | bytes 16416 | tf_op jit(solution)/shard_map/ppermute | solution.py:298
  11.8 0.0 collective-permute-done.3.q_ref
  11.8 0.0 copy-start.1
  11.9 1.7 %collective-permute-start.4 = (f32[16,256]{1,0:T(8,128)S(1)}, f32[16,256]{1,0:T(8,128)S(1)}, u32[]{:S(2)}, u32[]{:S(2)}) collective-permute-start(f32[16,256]{1,0:T(8,128)S(1)} %get-tuple-element.40), channel_id=1, source_target_pairs={{0,4},{4,0},{8,12},{12,8},{16,20},{20,16},{24,28},{28,24},{1,5},{5... | collective-permute-start | bytes 49160 | tf_op jit(solution)/shard_map/ppermute | solution.py:298
  13.6 1.5 %collective-permute-start.6 = (f32[16,256]{1,0:T(8,128)S(1)}, f32[16,256]{1,0:T(8,128)S(1)}, u32[]{:S(2)}, u32[]{:S(2)}) collective-permute-start(f32[16,256]{1,0:T(8,128)S(1)} %get-tuple-element.40), channel_id=1, source_target_pairs={{0,6},{1,7},{2,4},{3,5},{4,2},{5,3},{6,0},{7,1},{8,14},{9,15},{10,... | collective-permute-start | bytes 49160 | tf_op jit(solution)/shard_map/ppermute | solution.py:304
  15.1 0.3 %collective-permute-start.7 = (f32[16,256]{1,0:T(8,128)S(1)}, f32[16,256]{1,0:T(8,128)S(1)}, u32[]{:S(2)}, u32[]{:S(2)}) collective-permute-start(f32[16,256]{1,0:T(8,128)S(1)} %get-tuple-element.39.base_ref), channel_id=1, source_target_pairs={{0,2},{1,3},{2,0},{3,1},{4,6},{5,7},{6,4},{7,5},{8,10},{9,11},{10,... | collective-permute-start | bytes 49160 | tf_op jit(solution)/shard_map/ppermute | solution.py:293
  15.4 0.2 %collective-permute-done.4.extra_ref = f32[16,256]{1,0:T(8,128)S(1)} collective-permute-done((f32[16,256]{1,0:T(8,128)S(1)}, f32[16,256]{1,0:T(8,128)S(1)}, u32[]{:S(2)}, u32[]{:S(2)}) %collective-permute-start.4) | collective-permute-done | bytes 16416 | tf_op jit(solution)/shard_map/ppermute | solution.py:298
  15.7 0.0 copy-done.1
  15.7 0.8 %shard_map.85.own_ref = bf16[512,256]{1,0:T(8,128)(2,1)S(1)} custom-call(bf16[512,256]{1,0:T(8,128)(2,1)S(1)} %copy-done.1, f32[16,256]{1,0:T(8,128)S(1)} %get-tuple-element.33.rates_ref, f32[16,256]{1,0:T(8,128)S(1)} %get-tuple-element.39.base_ref, f32[16,256]{1,0:T(8,128)S(1)} %collective-permute-done.4.extra_ref, ...), custom_call_target="tpu_custom_call" | custom-call | tf_op jit(solution)/shard_map/pallas_call | solution.py:275
  16.5 0.0 copy-start
  16.5 0.1 collective-permute-start.5
  16.6 1.8 %collective-permute-done.6.extra_ref = f32[16,256]{1,0:T(8,128)S(1)} collective-permute-done((f32[16,256]{1,0:T(8,128)S(1)}, f32[16,256]{1,0:T(8,128)S(1)}, u32[]{:S(2)}, u32[]{:S(2)}) %collective-permute-start.6) | collective-permute-done | bytes 16416 | tf_op jit(solution)/shard_map/ppermute | solution.py:304
  18.4 1.3 %collective-permute-done.7.base_ref = f32[16,256]{1,0:T(8,128)S(1)} collective-permute-done((f32[16,256]{1,0:T(8,128)S(1)}, f32[16,256]{1,0:T(8,128)S(1)}, u32[]{:S(2)}, u32[]{:S(2)}) %collective-permute-start.7) | collective-permute-done | bytes 16416 | tf_op jit(solution)/shard_map/ppermute | solution.py:293
  19.6 0.0 collective-permute-done.8.local_ref
  19.6 0.8 %shard_map.86.rest_0_ = bf16[512,256]{1,0:T(8,128)(2,1)S(1)} custom-call(f32[16,256]{1,0:T(8,128)S(1)} %collective-permute-done.6.extra_ref, f32[16,256]{1,0:T(8,128)S(1)} %collective-permute-done.7.base_ref, bf16[512,256]{1,0:T(8,128)(2,1)S(1)} %collective-permute-done.3.q_ref, bf16[560,256]{1,0:T(8,128)(2,1)S(1)} %collective-permute-done.8.local_ref), custom_call_target="tpu_custom_call" | custom-call | tf_op jit(solution)/shard_map/pallas_call | solution.py:275
  20.4 0.1 collective-permute-start.9
  20.5 0.0 collective-permute-done.5.pair_ref
  20.5 0.0 copy-done
  20.5 0.4 %shard_map.87.near_ref = f32[512,256]{1,0:T(8,128)S(1)} custom-call(bf16[1024,256]{1,0:T(8,128)(2,1)S(1)} %copy-done, f32[1,256]{1,0:T(1,128)S(1)} %get-tuple-element.32.bias_ref, bf16[512,256]{1,0:T(8,128)(2,1)S(1)} %shard_map.85.own_ref, bf16[512,256]{1,0:T(8,128)(2,1)S(1)} %collective-permute-done.5.pair_ref, bf16[512,256]{1,0:T(8,128)(2,1)S(1)} %shard_map.86.rest_0_), custom_call_target="tpu_custom_call" | custom-call | tf_op jit(solution)/shard_map/pallas_call | solution.py:275
  20.9 1.1 %collective-permute-done.9.rest_0_ = bf16[512,256]{1,0:T(8,128)(2,1)S(1)} collective-permute-done((bf16[512,256]{1,0:T(8,128)(2,1)S(1)}, bf16[512,256]{1,0:T(8,128)(2,1)S(1)}, u32[]{:S(2)}, u32[]{:S(2)}) %collective-permute-start.9) | collective-permute-done | bytes 262176 | tf_op jit(solution)/shard_map/ppermute | solution.py:293
  22.0 0.9 %shard_map.88 = bf16[512,256]{1,0:T(8,128)(2,1)} custom-call(f32[512,256]{1,0:T(8,128)S(1)} %shard_map.87.near_ref, bf16[1024,256]{1,0:T(8,128)(2,1)S(1)} %copy-done, bf16[512,256]{1,0:T(8,128)(2,1)S(1)} %collective-permute-done.9.rest_0_), custom_call_target="tpu_custom_call" | custom-call | tf_op jit(solution)/shard_map/pallas_call | solution.py:275
  (1 shorter events, 0.0 us)
Async XLA Ops:
  0.0 11.8 %collective-permute-start.3 = (bf16[512,256]{1,0:T(8,128)(2,1)}, bf16[512,256]{1,0:T(8,128)(2,1)S(1)}, u32[]{:S(2)}, u32[]{:S(2)}) collective-permute-start(bf16[512,256]{1,0:T(8,128)(2,1)} %q_ref.1), channel_id=1, source_target_pairs={{0,2},{1,3},{2,0},{3,1},{4,6},{5,7},{6,4},{7,5},{8,10},{9,11},{10,... | collective-permute-start | bytes 786440 | tf_op jit(solution)/shard_map/ppermute | solution.py:293
  5.0 6.5 %collective-permute-start = (f32[16,256]{1,0:T(8,128)S(1)}, f32[16,256]{1,0:T(8,128)S(1)}, u32[]{:S(2)}, u32[]{:S(2)}) collective-permute-start(f32[16,256]{1,0:T(8,128)S(1)} %get-tuple-element.25.refs_6_.total_ref), channel_id=1, source_target_pairs={{0,24},{4,28},{8,16},{12,20},{16,8},{20,12},{24,0},{28,4},{1,25},{... | collective-permute-start | bytes 49160 | tf_op jit(solution)/shard_map/ppermute | solution.py:298
  6.7 4.8 %collective-permute-start.1 = (f32[16,256]{1,0:T(8,128)S(1)}, f32[16,256]{1,0:T(8,128)S(1)}, u32[]{:S(2)}, u32[]{:S(2)}) collective-permute-start(f32[16,256]{1,0:T(8,128)S(1)} %get-tuple-element.25.refs_6_.total_ref), channel_id=1, source_target_pairs={{0,16},{4,20},{8,24},{12,28},{16,0},{20,4},{24,8},{28,12},{1,17},{... | collective-permute-start | bytes 49160 | tf_op jit(solution)/shard_map/ppermute | solution.py:298
  8.1 3.7 %collective-permute-start.2 = (f32[16,256]{1,0:T(8,128)S(1)}, f32[16,256]{1,0:T(8,128)S(1)}, u32[]{:S(2)}, u32[]{:S(2)}) collective-permute-start(f32[16,256]{1,0:T(8,128)S(1)} %get-tuple-element.25.refs_6_.total_ref), channel_id=1, source_target_pairs={{0,8},{4,12},{8,0},{12,4},{16,24},{20,28},{24,16},{28,20},{1,9},{5... | collective-permute-start | bytes 49160 | tf_op jit(solution)/shard_map/ppermute | solution.py:298
  11.4 8.2 %collective-permute-start.8 = (bf16[560,256]{1,0:T(8,128)(2,1)S(1)}, bf16[560,256]{1,0:T(8,128)(2,1)S(1)}, u32[]{:S(2)}, u32[]{:S(2)}) collective-permute-start(bf16[560,256]{1,0:T(8,128)(2,1)S(1)} %get-tuple-element.44), channel_id=1, source_target_pairs={{0,2},{1,3},{2,0},{3,1},{4,6},{5,7},{6,4},{7,5},{8,10},{9,11},{10,... | collective-permute-start | bytes 860168 | tf_op jit(solution)/shard_map/ppermute | solution.py:293
  11.8 3.9 %copy-start.1 = (bf16[512,256]{1,0:T(8,128)(2,1)S(1)}, bf16[512,256]{1,0:T(8,128)(2,1)}, u32[]{:S(2)}) copy-start(bf16[512,256]{1,0:T(8,128)(2,1)} %q_ref.1) | copy-start | bytes 786436
  11.9 3.8 %collective-permute-start.4 = (f32[16,256]{1,0:T(8,128)S(1)}, f32[16,256]{1,0:T(8,128)S(1)}, u32[]{:S(2)}, u32[]{:S(2)}) collective-permute-start(f32[16,256]{1,0:T(8,128)S(1)} %get-tuple-element.40), channel_id=1, source_target_pairs={{0,4},{4,0},{8,12},{12,8},{16,20},{20,16},{24,28},{28,24},{1,5},{5... | collective-permute-start | bytes 49160 | tf_op jit(solution)/shard_map/ppermute | solution.py:298
  13.6 4.7 %collective-permute-start.6 = (f32[16,256]{1,0:T(8,128)S(1)}, f32[16,256]{1,0:T(8,128)S(1)}, u32[]{:S(2)}, u32[]{:S(2)}) collective-permute-start(f32[16,256]{1,0:T(8,128)S(1)} %get-tuple-element.40), channel_id=1, source_target_pairs={{0,6},{1,7},{2,4},{3,5},{4,2},{5,3},{6,0},{7,1},{8,14},{9,15},{10,... | collective-permute-start | bytes 49160 | tf_op jit(solution)/shard_map/ppermute | solution.py:304
  15.1 4.5 %collective-permute-start.7 = (f32[16,256]{1,0:T(8,128)S(1)}, f32[16,256]{1,0:T(8,128)S(1)}, u32[]{:S(2)}, u32[]{:S(2)}) collective-permute-start(f32[16,256]{1,0:T(8,128)S(1)} %get-tuple-element.39.base_ref), channel_id=1, source_target_pairs={{0,2},{1,3},{2,0},{3,1},{4,6},{5,7},{6,4},{7,5},{8,10},{9,11},{10,... | collective-permute-start | bytes 49160 | tf_op jit(solution)/shard_map/ppermute | solution.py:293
  16.5 4.0 %copy-start = (bf16[1024,256]{1,0:T(8,128)(2,1)S(1)}, bf16[1024,256]{1,0:T(8,128)(2,1)}, u32[]{:S(2)}) copy-start(bf16[1024,256]{1,0:T(8,128)(2,1)} %weight_ref.3) | copy-start | bytes 1572868
  16.5 4.0 %collective-permute-start.5 = (bf16[512,256]{1,0:T(8,128)(2,1)S(1)}, bf16[512,256]{1,0:T(8,128)(2,1)S(1)}, u32[]{:S(2)}, u32[]{:S(2)}) collective-permute-start(bf16[512,256]{1,0:T(8,128)(2,1)S(1)} %shard_map.85.own_ref), channel_id=1, source_target_pairs={{0,1},{1,0},{2,3},{3,2},{4,5},{5,4},{6,7},{7,6},{8,9},{9,8},{10,11... | collective-permute-start | bytes 786440 | tf_op jit(solution)/shard_map/ppermute | solution.py:293
  20.4 1.6 %collective-permute-start.9 = (bf16[512,256]{1,0:T(8,128)(2,1)S(1)}, bf16[512,256]{1,0:T(8,128)(2,1)S(1)}, u32[]{:S(2)}, u32[]{:S(2)}) collective-permute-start(bf16[512,256]{1,0:T(8,128)(2,1)S(1)} %shard_map.86.rest_0_), channel_id=1, source_target_pairs={{0,1},{1,0},{2,3},{3,2},{4,5},{5,4},{6,7},{7,6},{8,9},{9,8},{10,11... | collective-permute-start | bytes 786440 | tf_op jit(solution)/shard_map/ppermute | solution.py:293

commit v6 on v5

--- a/solution.py
+++ b/solution.py
@@ -13,6 +13,7 @@
 OWN_COST = 0
 FOLD_COST = 3000000000
 PIECES = 3
+ROUTES = {2: [(1, 0)], 4: [(3, 2, 1, 0), (2, 0, 3, 1), (1, 3, 0, 2)]}
 INPUTS = 6
 KEPT = 6
 PART_COST = 0
@@ -148,6 +149,13 @@
         left = left - piece.astype(jnp.float32)
 
 
+def lookup(spot, table):
+    found = table[0]
+    for i, entry in enumerate(table[1:]):
+        found = jnp.where(spot == i + 1, entry, found)
+    return found
+
+
 def fold(rates, inner, total, received, stride, seg_len):
     place = lax.div(lax.axis_index("seq"), 2)
     radix = len(received) + 1
@@ -159,8 +167,8 @@
 
     before = jnp.zeros_like(rates)
     whole = decayed((radix - 1 - spot) * stride) * total
-    for i, block in enumerate(received):
-        source = spot ^ (radix - 1 - i)
+    for route, block in zip(ROUTES[radix], received):
+        source = lookup(spot, [route.index(i) for i in range(radix)])
         past = source < spot
         gap = jnp.where(past, spot - 1 - source, 0) * stride
         before += jnp.where(past, decayed(gap) * block, 0.0)
@@ -293,9 +301,19 @@
     return lax.ppermute(value, "chan", [(r, r ^ bit) for r in range(count)])
 
 
-def beside(value, step):
+def beside(value):
     count = lax.axis_size("seq")
-    return lax.ppermute(value, "seq", [(r, r ^ step) for r in range(count)])
+    return lax.ppermute(value, "seq", [(r, r ^ 1) for r in range(count)])
+
+
+def along(value, stride, route):
+    count, radix = lax.axis_size("seq"), len(route)
+
+    def target(r):
+        spot = r // stride % radix
+        return r + (route[spot] - spot) * stride
+
+    return lax.ppermute(value, "seq", [(r, target(r)) for r in range(count)])
 
 
 def corner(value, step, bit):
@@ -310,7 +328,7 @@
     inner, stride = (), 1
     while True:
         radix = min(4, count // stride)
-        received = [beside(total, 2 * stride * step) for step in reversed(range(1, radix))]
+        received = [along(total, 2 * stride, route) for route in ROUTES[radix]]
         if stride * radix == count:
             break
         kernel = functools.partial(fold_kernel, stride, seg_len)
@@ -352,7 +370,7 @@
     _, _, decay, residue, _, bias, *local, local_short = state
     local_across = swapped(local_short, 2)
     base, extra, q_across = carry_shares(total, own_total, decay, residue, seg_len, q_across)
-    extra_beside = beside(extra, 1)
+    extra_beside = beside(extra)
     extra_corner = corner(extra, 1, 2)
     base_across = swapped(base, 2)
     whole = struct((seg_len, channels), jnp.bfloat16)

time: 23.2 us -> 22.6 us (0.974)
  waiting for transfers between devices: 4.76 us -> 4.34 us
    ppermute x5, starting transfers between devices: 3.51 us -> 5.2 us  [swapped(): return lax.ppermute(value, 'chan', [(r, r ^ bit) for r in range(count)])]
    ppermute x5, waiting for transfers between devices: 2.38 us -> 1.12 us  [swapped(): return lax.ppermute(value, 'chan', [(r, r ^ bit) for r in range(count)])]
    ppermute x4, waiting for transfers between devices: 0.58 us -> 1.7 us  [the longest x3 1.45 us: along(): return lax.ppermute(value, 'seq', [(r, target(r)) for r in range(count)])]
    ppermute x1, starting transfers between devices: 1.49 us -> 0.48 us  [corner(): return lax.ppermute(value, ('seq', 'chan'), pairs)]
    ppermute x4, starting transfers between devices: 6.19 us -> 5.31 us  [the longest x3 3.75 us: along(): return lax.ppermute(value, 'seq', [(r, target(r)) for r in range(count)])]
    ppermute x1, waiting for transfers between devices: 1.81 us -> 1.52 us  [corner(): return lax.ppermute(value, ('seq', 'chan'), pairs)]
  transfers between devices with their start and end apart: 10 -> 10, of which waited for: 5 -> 4; matrix products, arithmetic and copies ran while one was open for 0% -> 0% of each run, Pallas kernels for 26% -> 27%
where the time goes in v6:
time: 22.6 us; the launch traced here: 22.3 us
  starting transfers between devices  11 us (49%)
  Pallas kernels  6.88 us (30%)
  waiting for transfers between devices  4.34 us (19%)
    pallas_call x7, Pallas kernels, call(): pl.pallas_call(kernel, out_shape=out, in_specs=[pl.BlockSpec(memory_space...  6.88 us
    ppermute x5, starting transfers between devices, swapped(): return lax.ppermute(value, 'chan', [(r, r ^ bit) for r in range(count)])  5.2 us
    ppermute x3, starting transfers between devices, along(): return lax.ppermute(value, 'seq', [(r, target(r)) for r in range(count)])  3.75 us
    ppermute x1, starting transfers between devices, beside(): return lax.ppermute(value, 'seq', [(r, r ^ 1) for r in range(count)])  1.56 us
    ppermute x1, waiting for transfers between devices, corner(): return lax.ppermute(value, ('seq', 'chan'), pairs)  1.52 us
    ppermute x3, waiting for transfers between devices, along(): return lax.ppermute(value, 'seq', [(r, target(r)) for r in range(count)])  1.45 us
    ppermute x5, waiting for transfers between devices, swapped(): return lax.ppermute(value, 'chan', [(r, r ^ bit) for r in range(count)])  1.12 us
    ppermute x1, starting transfers between devices, corner(): return lax.ppermute(value, ('seq', 'chan'), pairs)  0.48 us
  transfers between devices with their start and end apart: 10, of which 4 were waited for; matrix products, arithmetic and copies ran while one was open for 0% of the time, Pallas kernels for 27%

profile of v6, /device:TPU:0, one launch (start us, length us, event | category | flops | bytes accessed | tf_op | source)
XLA Modules:
  0.0 22.3 jit_solution(11145416321860758900)
XLA Ops:
  0.0 3.0 %collective-permute-start.3 = (bf16[512,256]{1,0:T(8,128)(2,1)}, bf16[512,256]{1,0:T(8,128)(2,1)S(1)}, u32[]{:S(2)}, u32[]{:S(2)}) collective-permute-start(bf16[512,256]{1,0:T(8,128)(2,1)} %q_ref.1), channel_id=1, source_target_pairs={{0,2},{1,3},{2,0},{3,1},{4,6},{5,7},{6,4},{7,5},{8,10},{9,11},{10,... | collective-permute-start | bytes 786440 | tf_op jit(solution)/shard_map/ppermute | solution.py:301
  3.0 2.0 %shard_map.82 = (f32[16,256]{1,0:T(8,128)S(1)}, f32[16,8,256]{2,1,0:T(8,128)S(1)}, f32[2,512,128]{2,1,0:T(8,128)S(1)}, f32[16,256]{1,0:T(8,128)S(1)}, f32[16,256...) custom-call(bf16[512,256]{1,0:T(8,128)(2,1)} %refs_0_.3, bf16[512,256]{1,0:T(8,128)(2,1)} %refs_1_.3, ...), custom_call_target="tpu_custom_call" | custom-call | tf_op jit(solution)/shard_map/pallas_call | solution.py:283
  5.0 1.7 %collective-permute-start = (f32[16,256]{1,0:T(8,128)S(1)}, f32[16,256]{1,0:T(8,128)S(1)}, u32[]{:S(2)}, u32[]{:S(2)}) collective-permute-start(f32[16,256]{1,0:T(8,128)S(1)} %get-tuple-element.25.refs_6_.total_ref), channel_id=1, source_target_pairs={{0,24},{4,28},{8,16},{12,20},{16,8},{20,12},{24,0},{28,4},{1,25},{... | collective-permute-start | bytes 49160 | tf_op jit(solution)/shard_map/ppermute | solution.py:316
  6.7 1.4 %collective-permute-start.1 = (f32[16,256]{1,0:T(8,128)S(1)}, f32[16,256]{1,0:T(8,128)S(1)}, u32[]{:S(2)}, u32[]{:S(2)}) collective-permute-start(f32[16,256]{1,0:T(8,128)S(1)} %get-tuple-element.25.refs_6_.total_ref), channel_id=1, source_target_pairs={{0,16},{4,20},{8,0},{12,4},{16,24},{20,28},{24,8},{28,12},{1,17},{... | collective-permute-start | bytes 49160 | tf_op jit(solution)/shard_map/ppermute | solution.py:316
  8.1 0.6 %collective-permute-start.2 = (f32[16,256]{1,0:T(8,128)S(1)}, f32[16,256]{1,0:T(8,128)S(1)}, u32[]{:S(2)}, u32[]{:S(2)}) collective-permute-start(f32[16,256]{1,0:T(8,128)S(1)} %get-tuple-element.25.refs_6_.total_ref), channel_id=1, source_target_pairs={{0,8},{4,12},{8,24},{12,28},{16,0},{20,4},{24,16},{28,20},{1,9},{5... | collective-permute-start | bytes 49160 | tf_op jit(solution)/shard_map/ppermute | solution.py:316
  8.7 2.0 %shard_map.83 = (f32[16,256]{1,0:T(8,128)S(1)}, f32[16,8,256]{2,1,0:T(8,128)S(1)}, f32[2,512,128]{2,1,0:T(8,128)S(1)}, f32[16,256]{1,0:T(8,128)S(1)}, f32[16,256...) custom-call(bf16[512,256]{1,0:T(8,128)(2,1)} %refs_0_.3, ...), custom_call_target="tpu_custom_call", output_to_operand_aliasing={{1}: (7, {}), {2}: (8, {}), {3}: (9, {}), {4}: (10, {}), {5... | custom-call | tf_op jit(solution)/shard_map/pallas_call | solution.py:283
  10.7 0.6 %collective-permute-start.8 = (bf16[560,256]{1,0:T(8,128)(2,1)S(1)}, bf16[560,256]{1,0:T(8,128)(2,1)S(1)}, u32[]{:S(2)}, u32[]{:S(2)}) collective-permute-start(bf16[560,256]{1,0:T(8,128)(2,1)S(1)} %get-tuple-element.44), channel_id=1, source_target_pairs={{0,2},{1,3},{2,0},{3,1},{4,6},{5,7},{6,4},{7,5},{8,10},{9,11},{10,... | collective-permute-start | bytes 860168 | tf_op jit(solution)/shard_map/ppermute | solution.py:301
  11.3 0.0 collective-permute-done.rest_0_
  11.3 0.0 collective-permute-done.1.rest_1_
  11.3 1.4 %collective-permute-done.2.rest_2_ = f32[16,256]{1,0:T(8,128)S(1)} collective-permute-done((f32[16,256]{1,0:T(8,128)S(1)}, f32[16,256]{1,0:T(8,128)S(1)}, u32[]{:S(2)}, u32[]{:S(2)}) %collective-permute-start.2) | collective-permute-done | bytes 16416 | tf_op jit(solution)/shard_map/ppermute | solution.py:316
  12.7 0.0 collective-permute-done.3.q_ref
  12.7 0.0 copy-start.1
  12.8 1.6 %collective-permute-start.4 = (f32[16,256]{1,0:T(8,128)S(1)}, f32[16,256]{1,0:T(8,128)S(1)}, u32[]{:S(2)}, u32[]{:S(2)}) collective-permute-start(f32[16,256]{1,0:T(8,128)S(1)} %get-tuple-element.40), channel_id=1, source_target_pairs={{0,4},{4,0},{8,12},{12,8},{16,20},{20,16},{24,28},{28,24},{1,5},{5... | collective-permute-start | bytes 49160 | tf_op jit(solution)/shard_map/ppermute | solution.py:306
  14.3 0.5 %collective-permute-start.6 = (f32[16,256]{1,0:T(8,128)S(1)}, f32[16,256]{1,0:T(8,128)S(1)}, u32[]{:S(2)}, u32[]{:S(2)}) collective-permute-start(f32[16,256]{1,0:T(8,128)S(1)} %get-tuple-element.40), channel_id=1, source_target_pairs={{0,6},{1,7},{2,4},{3,5},{4,2},{5,3},{6,0},{7,1},{8,14},{9,15},{10,... | collective-permute-start | bytes 49160 | tf_op jit(solution)/shard_map/ppermute | solution.py:322
  14.8 1.5 %collective-permute-start.7 = (f32[16,256]{1,0:T(8,128)S(1)}, f32[16,256]{1,0:T(8,128)S(1)}, u32[]{:S(2)}, u32[]{:S(2)}) collective-permute-start(f32[16,256]{1,0:T(8,128)S(1)} %get-tuple-element.39.base_ref), channel_id=1, source_target_pairs={{0,2},{1,3},{2,0},{3,1},{4,6},{5,7},{6,4},{7,5},{8,10},{9,11},{10,... | collective-permute-start | bytes 49160 | tf_op jit(solution)/shard_map/ppermute | solution.py:301
  16.3 0.2 %collective-permute-done.4.extra_ref = f32[16,256]{1,0:T(8,128)S(1)} collective-permute-done((f32[16,256]{1,0:T(8,128)S(1)}, f32[16,256]{1,0:T(8,128)S(1)}, u32[]{:S(2)}, u32[]{:S(2)}) %collective-permute-start.4) | collective-permute-done | bytes 16416 | tf_op jit(solution)/shard_map/ppermute | solution.py:306
  16.6 0.0 copy-done.1
  16.6 0.8 %shard_map.85.own_ref = bf16[512,256]{1,0:T(8,128)(2,1)S(1)} custom-call(bf16[512,256]{1,0:T(8,128)(2,1)S(1)} %copy-done.1, f32[16,256]{1,0:T(8,128)S(1)} %get-tuple-element.33.rates_ref, f32[16,256]{1,0:T(8,128)S(1)} %get-tuple-element.39.base_ref, f32[16,256]{1,0:T(8,128)S(1)} %collective-permute-done.4.extra_ref, ...), custom_call_target="tpu_custom_call" | custom-call | tf_op jit(solution)/shard_map/pallas_call | solution.py:283
  17.4 0.0 copy-start
  17.4 0.1 collective-permute-start.5
  17.5 1.5 %collective-permute-done.6.extra_ref = f32[16,256]{1,0:T(8,128)S(1)} collective-permute-done((f32[16,256]{1,0:T(8,128)S(1)}, f32[16,256]{1,0:T(8,128)S(1)}, u32[]{:S(2)}, u32[]{:S(2)}) %collective-permute-start.6) | collective-permute-done | bytes 16416 | tf_op jit(solution)/shard_map/ppermute | solution.py:322
  19.0 0.0 collective-permute-done.7.base_ref
  19.0 0.0 collective-permute-done.8.local_ref
  19.0 0.8 %shard_map.86.rest_0_ = bf16[512,256]{1,0:T(8,128)(2,1)S(1)} custom-call(f32[16,256]{1,0:T(8,128)S(1)} %collective-permute-done.6.extra_ref, f32[16,256]{1,0:T(8,128)S(1)} %collective-permute-done.7.base_ref, bf16[512,256]{1,0:T(8,128)(2,1)S(1)} %collective-permute-done.3.q_ref, bf16[560,256]{1,0:T(8,128)(2,1)S(1)} %collective-permute-done.8.local_ref), custom_call_target="tpu_custom_call" | custom-call | tf_op jit(solution)/shard_map/pallas_call | solution.py:283
  19.8 0.1 collective-permute-start.9
  19.9 0.0 collective-permute-done.5.pair_ref
  19.9 0.0 copy-done
  19.9 0.4 %shard_map.87.near_ref = f32[512,256]{1,0:T(8,128)S(1)} custom-call(bf16[1024,256]{1,0:T(8,128)(2,1)S(1)} %copy-done, f32[1,256]{1,0:T(1,128)S(1)} %get-tuple-element.32.bias_ref, bf16[512,256]{1,0:T(8,128)(2,1)S(1)} %shard_map.85.own_ref, bf16[512,256]{1,0:T(8,128)(2,1)S(1)} %collective-permute-done.5.pair_ref, bf16[512,256]{1,0:T(8,128)(2,1)S(1)} %shard_map.86.rest_0_), custom_call_target="tpu_custom_call" | custom-call | tf_op jit(solution)/shard_map/pallas_call | solution.py:283
  20.3 1.1 %collective-permute-done.9.rest_0_ = bf16[512,256]{1,0:T(8,128)(2,1)S(1)} collective-permute-done((bf16[512,256]{1,0:T(8,128)(2,1)S(1)}, bf16[512,256]{1,0:T(8,128)(2,1)S(1)}, u32[]{:S(2)}, u32[]{:S(2)}) %collective-permute-start.9) | collective-permute-done | bytes 262176 | tf_op jit(solution)/shard_map/ppermute | solution.py:301
  21.4 0.9 %shard_map.88 = bf16[512,256]{1,0:T(8,128)(2,1)} custom-call(f32[512,256]{1,0:T(8,128)S(1)} %shard_map.87.near_ref, bf16[1024,256]{1,0:T(8,128)(2,1)S(1)} %copy-done, bf16[512,256]{1,0:T(8,128)(2,1)S(1)} %collective-permute-done.9.rest_0_), custom_call_target="tpu_custom_call" | custom-call | tf_op jit(solution)/shard_map/pallas_call | solution.py:283
  (1 shorter events, 0.0 us)
Async XLA Ops:
  0.0 12.7 %collective-permute-start.3 = (bf16[512,256]{1,0:T(8,128)(2,1)}, bf16[512,256]{1,0:T(8,128)(2,1)S(1)}, u32[]{:S(2)}, u32[]{:S(2)}) collective-permute-start(bf16[512,256]{1,0:T(8,128)(2,1)} %q_ref.1), channel_id=1, source_target_pairs={{0,2},{1,3},{2,0},{3,1},{4,6},{5,7},{6,4},{7,5},{8,10},{9,11},{10,... | collective-permute-start | bytes 786440 | tf_op jit(solution)/shard_map/ppermute | solution.py:301
  5.0 6.3 %collective-permute-start = (f32[16,256]{1,0:T(8,128)S(1)}, f32[16,256]{1,0:T(8,128)S(1)}, u32[]{:S(2)}, u32[]{:S(2)}) collective-permute-start(f32[16,256]{1,0:T(8,128)S(1)} %get-tuple-element.25.refs_6_.total_ref), channel_id=1, source_target_pairs={{0,24},{4,28},{8,16},{12,20},{16,8},{20,12},{24,0},{28,4},{1,25},{... | collective-permute-start | bytes 49160 | tf_op jit(solution)/shard_map/ppermute | solution.py:316
  6.7 4.6 %collective-permute-start.1 = (f32[16,256]{1,0:T(8,128)S(1)}, f32[16,256]{1,0:T(8,128)S(1)}, u32[]{:S(2)}, u32[]{:S(2)}) collective-permute-start(f32[16,256]{1,0:T(8,128)S(1)} %get-tuple-element.25.refs_6_.total_ref), channel_id=1, source_target_pairs={{0,16},{4,20},{8,0},{12,4},{16,24},{20,28},{24,8},{28,12},{1,17},{... | collective-permute-start | bytes 49160 | tf_op jit(solution)/shard_map/ppermute | solution.py:316
  8.1 4.6 %collective-permute-start.2 = (f32[16,256]{1,0:T(8,128)S(1)}, f32[16,256]{1,0:T(8,128)S(1)}, u32[]{:S(2)}, u32[]{:S(2)}) collective-permute-start(f32[16,256]{1,0:T(8,128)S(1)} %get-tuple-element.25.refs_6_.total_ref), channel_id=1, source_target_pairs={{0,8},{4,12},{8,24},{12,28},{16,0},{20,4},{24,16},{28,20},{1,9},{5... | collective-permute-start | bytes 49160 | tf_op jit(solution)/shard_map/ppermute | solution.py:316
  10.7 8.3 %collective-permute-start.8 = (bf16[560,256]{1,0:T(8,128)(2,1)S(1)}, bf16[560,256]{1,0:T(8,128)(2,1)S(1)}, u32[]{:S(2)}, u32[]{:S(2)}) collective-permute-start(bf16[560,256]{1,0:T(8,128)(2,1)S(1)} %get-tuple-element.44), channel_id=1, source_target_pairs={{0,2},{1,3},{2,0},{3,1},{4,6},{5,7},{6,4},{7,5},{8,10},{9,11},{10,... | collective-permute-start | bytes 860168 | tf_op jit(solution)/shard_map/ppermute | solution.py:301
  12.7 3.9 %copy-start.1 = (bf16[512,256]{1,0:T(8,128)(2,1)S(1)}, bf16[512,256]{1,0:T(8,128)(2,1)}, u32[]{:S(2)}) copy-start(bf16[512,256]{1,0:T(8,128)(2,1)} %q_ref.1) | copy-start | bytes 786436
  12.8 3.8 %collective-permute-start.4 = (f32[16,256]{1,0:T(8,128)S(1)}, f32[16,256]{1,0:T(8,128)S(1)}, u32[]{:S(2)}, u32[]{:S(2)}) collective-permute-start(f32[16,256]{1,0:T(8,128)S(1)} %get-tuple-element.40), channel_id=1, source_target_pairs={{0,4},{4,0},{8,12},{12,8},{16,20},{20,16},{24,28},{28,24},{1,5},{5... | collective-permute-start | bytes 49160 | tf_op jit(solution)/shard_map/ppermute | solution.py:306
  14.3 4.6 %collective-permute-start.6 = (f32[16,256]{1,0:T(8,128)S(1)}, f32[16,256]{1,0:T(8,128)S(1)}, u32[]{:S(2)}, u32[]{:S(2)}) collective-permute-start(f32[16,256]{1,0:T(8,128)S(1)} %get-tuple-element.40), channel_id=1, source_target_pairs={{0,6},{1,7},{2,4},{3,5},{4,2},{5,3},{6,0},{7,1},{8,14},{9,15},{10,... | collective-permute-start | bytes 49160 | tf_op jit(solution)/shard_map/ppermute | solution.py:322
  14.8 4.2 %collective-permute-start.7 = (f32[16,256]{1,0:T(8,128)S(1)}, f32[16,256]{1,0:T(8,128)S(1)}, u32[]{:S(2)}, u32[]{:S(2)}) collective-permute-start(f32[16,256]{1,0:T(8,128)S(1)} %get-tuple-element.39.base_ref), channel_id=1, source_target_pairs={{0,2},{1,3},{2,0},{3,1},{4,6},{5,7},{6,4},{7,5},{8,10},{9,11},{10,... | collective-permute-start | bytes 49160 | tf_op jit(solution)/shard_map/ppermute | solution.py:301
  17.4 2.5 %copy-start = (bf16[1024,256]{1,0:T(8,128)(2,1)S(1)}, bf16[1024,256]{1,0:T(8,128)(2,1)}, u32[]{:S(2)}) copy-start(bf16[1024,256]{1,0:T(8,128)(2,1)} %weight_ref.3) | copy-start | bytes 1572868
  17.4 2.5 %collective-permute-start.5 = (bf16[512,256]{1,0:T(8,128)(2,1)S(1)}, bf16[512,256]{1,0:T(8,128)(2,1)S(1)}, u32[]{:S(2)}, u32[]{:S(2)}) collective-permute-start(bf16[512,256]{1,0:T(8,128)(2,1)S(1)} %shard_map.85.own_ref), channel_id=1, source_target_pairs={{0,1},{1,0},{2,3},{3,2},{4,5},{5,4},{6,7},{7,6},{8,9},{9,8},{10,11... | collective-permute-start | bytes 786440 | tf_op jit(solution)/shard_map/ppermute | solution.py:301
  19.8 1.6 %collective-permute-start.9 = (bf16[512,256]{1,0:T(8,128)(2,1)S(1)}, bf16[512,256]{1,0:T(8,128)(2,1)S(1)}, u32[]{:S(2)}, u32[]{:S(2)}) collective-permute-start(bf16[512,256]{1,0:T(8,128)(2,1)S(1)} %shard_map.86.rest_0_), channel_id=1, source_target_pairs={{0,1},{1,0},{2,3},{3,2},{4,5},{5,4},{6,7},{7,6},{8,9},{9,8},{10,11... | collective-permute-start | bytes 786440 | tf_op jit(solution)/shard_map/ppermute | solution.py:301

commit v7 on v6

--- a/solution.py
+++ b/solution.py
@@ -13,9 +13,9 @@
 OWN_COST = 0
 FOLD_COST = 3000000000
 PIECES = 3
-ROUTES = {2: [(1, 0)], 4: [(3, 2, 1, 0), (2, 0, 3, 1), (1, 3, 0, 2)]}
+ROUTES = {2: [(1, 0)], 4: [(3, 2, 0, 1), (2, 3, 0, 1), (1, 0, 3, 2)]}
 INPUTS = 6
-KEPT = 6
+KEPT = 8
 PART_COST = 0
 VMEM_LIMIT = 32 * 1024 * 1024
 
@@ -26,13 +26,6 @@
 
 def full(value):
     return jnp.broadcast_to(value, (SUBLANES, LANES))
-
-
-def tree_sum(terms):
-    while len(terms) > 1:
-        paired = [a + b for a, b in zip(terms[::2], terms[1::2])]
-        terms = paired + ([terms[-1]] if len(terms) % 2 else [])
-    return terms[0]
 
 
 def lane_slice(part):
@@ -65,13 +58,15 @@
         product = k_ref[:, lanes].astype(jnp.float32) * v_ref[:, lanes].astype(jnp.float32)
         gated_ref[part] = product.astype(jnp.bfloat16).astype(jnp.float32)
         factor = [full(jnp.exp(-row(decay_ref, n, part))) for n in range(modes)]
+        square = [f * f for f in factor]
 
         def step(t, state):
-            x = gated_ref[part, pl.ds(t, SUBLANES, stride=chunk_len), :]
-            return tuple(f * h + x for f, h in zip(factor, state))
+            x = gated_ref[part, pl.ds(2 * t, SUBLANES, stride=chunk_len), :]
+            y = gated_ref[part, pl.ds(2 * t + 1, SUBLANES, stride=chunk_len), :]
+            return tuple(g * h + (f * x + y) for f, g, h in zip(factor, square, state))
 
         zero = jnp.zeros((SUBLANES, LANES), jnp.float32)
-        state = lax.fori_loop(0, chunk_len, step, (zero,) * modes, unroll=8)
+        state = lax.fori_loop(0, chunk_len // 2, step, (zero,) * modes, unroll=4)
         for n in range(modes):
             chunk_ref[n, :, lanes] = state[n]
             weight = jnp.exp(-row(decay_ref, n, part) * later)
@@ -85,43 +80,58 @@
     return lax.axis_index("seq") >= count - 2
 
 
+def is_first():
+    return lax.axis_index("seq") < 2
+
+
 def state_kernel(*refs):
-    total_ref = refs[INPUTS]
+    inputs, total_ref, kept = refs[:INPUTS], refs[INPUTS], refs[INPUTS + 1 : INPUTS + 1 + KEPT]
+    scratch, weights = refs[-4:-1], refs[-1]
+    state, (local_ref, short_ref) = kept[:-2], kept[-2:]
+    chunk_ref, gated_ref, decay_ref, residue_ref, skip_ref, _ = state
 
     @pl.when(jnp.logical_not(is_last()))
     def _():
-        summarize(*refs)
+        summarize(*inputs, total_ref, *state, *scratch)
 
     @pl.when(is_last())
     def _():
         total_ref[...] = jnp.zeros_like(total_ref)
 
+    @pl.when(is_first())
+    def _():
+        convolve(0, gated_ref, decay_ref, residue_ref, skip_ref, chunk_ref, local_ref, short_ref, weights)
+
 
 def local_kernel(*refs):
-    inputs, rest = refs[:INPUTS], refs[INPUTS:]
-    total_in, rest = rest[0], rest[1 + KEPT :]
-    total_ref, kept, (*locals_out, short_ref), scratch = rest[0], rest[1 : 1 + KEPT], rest[1 + KEPT : -3], rest[-3:]
-    chunk_ref, gated_ref, decay_ref, residue_ref, skip_ref, _ = kept
+    inputs, total_in, rest = refs[:INPUTS], refs[INPUTS], refs[INPUTS + 1 + KEPT :]
+    total_ref, kept, more, scratch, weights = rest[0], rest[1 : 1 + KEPT], rest[1 + KEPT : -4], rest[-4:-1], rest[-1]
+    state, (local_ref, short_ref) = kept[:-2], kept[-2:]
+    chunk_ref, gated_ref, decay_ref, residue_ref, skip_ref, _ = state
 
     @pl.when(is_last())
     def _():
-        summarize(*inputs, total_ref, *kept, *scratch)
+        summarize(*inputs, total_ref, *state, *scratch)
 
     @pl.when(jnp.logical_not(is_last()))
     def _():
         total_ref[...] = total_in[...]
 
-    for part, local_ref in enumerate(locals_out):
-        convolve(part, gated_ref, decay_ref, residue_ref, skip_ref, chunk_ref, local_ref, short_ref)
-
-
-def convolve(part, gated, decay_ref, residue_ref, skip_ref, chunk_ref, local_ref, short_ref):
+    @pl.when(jnp.logical_not(is_first()))
+    def _():
+        convolve(0, gated_ref, decay_ref, residue_ref, skip_ref, chunk_ref, local_ref, short_ref, weights)
+
+    for i, more_ref in enumerate(more):
+        convolve(i + 1, gated_ref, decay_ref, residue_ref, skip_ref, chunk_ref, more_ref, short_ref, weights)
+
+
+def convolve(part, gated, decay_ref, residue_ref, skip_ref, chunk_ref, local_ref, short_ref, weights):
     modes = decay_ref.shape[0]
     seg_len = gated.shape[1]
     chunk_len = seg_len // SUBLANES
     index = lax.broadcasted_iota(jnp.int32, (SUBLANES, LANES), 0)
     lanes = lane_slice(part)
-    factor, weight, start = [], [], []
+    factor, start = [], []
     for n in range(modes):
         rate = row(decay_ref, n, part)
         prefix = chunk_ref[n, :, lanes]
@@ -130,14 +140,18 @@
             prefix = prefix + jnp.exp(-rate * (shift * chunk_len)) * moved
         start.append(jnp.where(index >= 1, pltpu.roll(prefix, 1, 0), 0.0))
         factor.append(full(jnp.exp(-rate)))
-        weight.append(full(row(residue_ref, n, part)))
+        weights[n] = full(row(residue_ref, n, part))
     bypass = full(skip_ref[:, lanes])
 
     def step(t, state):
         rows = pl.ds(t, SUBLANES, stride=chunk_len)
         x = gated[part, rows, :]
         state = tuple(f * h + x for f, h in zip(factor, state))
-        local_ref[rows, :] = tree_sum([w * h for w, h in zip(weight, state)] + [bypass * x])
+        sums = [bypass * x] + [None] * 3
+        for n, h in enumerate(state):
+            term = weights[n] * h
+            sums[n % 4] = term if sums[n % 4] is None else sums[n % 4] + term
+        local_ref[rows, :] = (sums[0] + sums[1]) + (sums[2] + sums[3])
         return state
 
     lax.fori_loop(0, chunk_len, step, tuple(start), unroll=4)
@@ -213,7 +227,10 @@
         rows = pl.ds(pl.multiple_of(j * block, block), block)
         halves = []
         for _ in range(2):
-            halves.append(tree_sum(list(state)))
+            sums = list(state[:4])
+            for n, h in enumerate(state[4:]):
+                sums[n % 4] = sums[n % 4] + h
+            halves.append((sums[0] + sums[1]) + (sums[2] + sums[3]))
             state = tuple(f * h for f, h in zip(factor, state))
         total = local_ref[rows, :].astype(jnp.float32) + jnp.concatenate(halves, axis=0)
         gate_rows = q_ref[rows, lanes].astype(jnp.float32)
@@ -359,15 +376,18 @@
         few,
         struct((1, channels)),
         struct((1, cols)),
+        struct((seg_len, LANES)),
+        struct((seg_len + PIECES * modes, channels), jnp.bfloat16),
     ]
-    thin = struct((seg_len, LANES))
-    short = struct((seg_len + PIECES * modes, channels), jnp.bfloat16)
+    scratch += [pltpu.VMEM((modes, SUBLANES, LANES), jnp.float32)]
     total, *state = call(state_kernel, [few, *kept], *inputs, scratch=scratch, hbm=INPUTS)
+    more = [struct((seg_len, LANES))] * (parts - 1)
     own_total, *state = call(
-        local_kernel, [few, *kept, *[thin] * parts, short], *inputs, total, *state,
+        local_kernel, [few, *kept, *more], *inputs, total, *state,
         scratch=scratch, hbm=INPUTS, aliases=[(INPUTS + 1 + i, 1 + i) for i in range(KEPT)],
     )
-    _, _, decay, residue, _, bias, *local, local_short = state
+    _, _, decay, residue, _, bias, first_local, local_short, *more = state
+    local = [first_local, *more]
     local_across = swapped(local_short, 2)
     base, extra, q_across = carry_shares(total, own_total, decay, residue, seg_len, q_across)
     extra_beside = beside(extra)

time: 22.6 us -> 22.5 us (level)
    ppermute x5, starting transfers between devices: 5.2 us -> 5.66 us  [swapped(): return lax.ppermute(value, 'chan', [(r, r ^ bit) for r in range(count)])]
    ppermute x1, starting transfers between devices: 0.48 us -> 0.02 us  [corner(): return lax.ppermute(value, ('seq', 'chan'), pairs)]
  transfers between devices with their start and end apart: 10 -> 10, of which waited for: 4 -> 5; matrix products, arithmetic and copies ran while one was open for 0% -> 0% of each run, Pallas kernels for 27% -> 27%
where the time goes in v7:
time: 22.5 us; the launch traced here: 22.2 us
  starting transfers between devices  10.9 us (48%)
  Pallas kernels  6.84 us (30%)
  waiting for transfers between devices  4.41 us (20%)
    pallas_call x7, Pallas kernels, call(): pl.pallas_call(kernel, out_shape=out, in_specs=[pl.BlockSpec(memory_space...  6.84 us
    ppermute x5, starting transfers between devices, swapped(): return lax.ppermute(value, 'chan', [(r, r ^ bit) for r in range(count)])  5.66 us
    ppermute x3, starting transfers between devices, along(): return lax.ppermute(value, 'seq', [(r, target(r)) for r in range(count)])  3.64 us
    ppermute x1, starting transfers between devices, beside(): return lax.ppermute(value, 'seq', [(r, r ^ 1) for r in range(count)])  1.56 us
    ppermute x1, waiting for transfers between devices, corner(): return lax.ppermute(value, ('seq', 'chan'), pairs)  1.54 us
    ppermute x3, waiting for transfers between devices, along(): return lax.ppermute(value, 'seq', [(r, target(r)) for r in range(count)])  1.5 us
    ppermute x5, waiting for transfers between devices, swapped(): return lax.ppermute(value, 'chan', [(r, r ^ bit) for r in range(count)])  1.12 us
  transfers between devices with their start and end apart: 10, of which 5 were waited for; matrix products, arithmetic and copies ran while one was open for 0% of the time, Pallas kernels for 27%

profile of v7, /device:TPU:0, one launch (start us, length us, event | category | flops | bytes accessed | tf_op | source)
XLA Modules:
  0.0 22.2 jit_solution(6132935504035886268)
XLA Ops:
  0.0 3.0 %collective-permute-start.3 = (bf16[512,256]{1,0:T(8,128)(2,1)}, bf16[512,256]{1,0:T(8,128)(2,1)S(1)}, u32[]{:S(2)}, u32[]{:S(2)}) collective-permute-start(bf16[512,256]{1,0:T(8,128)(2,1)} %q_ref.1), channel_id=1, source_target_pairs={{0,2},{1,3},{2,0},{3,1},{4,6},{5,7},{6,4},{7,5},{8,10},{9,11},{10,... | collective-permute-start | bytes 786440 | tf_op jit(solution)/shard_map/ppermute | solution.py:318
  3.0 3.0 %shard_map.82 = (f32[16,256]{1,0:T(8,128)S(1)}, f32[16,8,256]{2,1,0:T(8,128)S(1)}, f32[2,512,128]{2,1,0:T(8,128)S(1)}, f32[16,256]{1,0:T(8,128)S(1)}, f32[16,256...) custom-call(bf16[512,256]{1,0:T(8,128)(2,1)} %refs_0_.3, ...), custom_call_target="tpu_custom_call" | custom-call | tf_op jit(solution)/shard_map/pallas_call | solution.py:300
  6.0 0.7 %collective-permute-start = (f32[16,256]{1,0:T(8,128)S(1)}, f32[16,256]{1,0:T(8,128)S(1)}, u32[]{:S(2)}, u32[]{:S(2)}) collective-permute-start(f32[16,256]{1,0:T(8,128)S(1)} %get-tuple-element.27.refs_6_.total_ref), channel_id=1, source_target_pairs={{0,24},{4,28},{8,16},{12,20},{16,0},{20,4},{24,8},{28,12},{1,25},{... | collective-permute-start | bytes 49160 | tf_op jit(solution)/shard_map/ppermute | solution.py:333
  6.7 2.2 %collective-permute-start.1 = (f32[16,256]{1,0:T(8,128)S(1)}, f32[16,256]{1,0:T(8,128)S(1)}, u32[]{:S(2)}, u32[]{:S(2)}) collective-permute-start(f32[16,256]{1,0:T(8,128)S(1)} %get-tuple-element.27.refs_6_.total_ref), channel_id=1, source_target_pairs={{0,16},{4,20},{8,24},{12,28},{16,0},{20,4},{24,8},{28,12},{1,17},{... | collective-permute-start | bytes 49160 | tf_op jit(solution)/shard_map/ppermute | solution.py:333
  9.0 0.7 %collective-permute-start.2 = (f32[16,256]{1,0:T(8,128)S(1)}, f32[16,256]{1,0:T(8,128)S(1)}, u32[]{:S(2)}, u32[]{:S(2)}) collective-permute-start(f32[16,256]{1,0:T(8,128)S(1)} %get-tuple-element.27.refs_6_.total_ref), channel_id=1, source_target_pairs={{0,8},{4,12},{8,0},{12,4},{16,24},{20,28},{24,16},{28,20},{1,9},{5... | collective-permute-start | bytes 49160 | tf_op jit(solution)/shard_map/ppermute | solution.py:333
  9.6 1.0 %shard_map.83 = (f32[16,256]{1,0:T(8,128)S(1)}, f32[16,8,256]{2,1,0:T(8,128)S(1)}, f32[2,512,128]{2,1,0:T(8,128)S(1)}, f32[16,256]{1,0:T(8,128)S(1)}, f32[16,256...) custom-call(bf16[512,256]{1,0:T(8,128)(2,1)} %refs_0_.3, ...), custom_call_target="tpu_custom_call", output_to_operand_aliasing={{1}: (7, {}), {2}: (8, {}), {3}: (9, {}), {4}: (10, {}), {5... | custom-call | tf_op jit(solution)/shard_map/pallas_call | solution.py:300
  10.6 0.6 %collective-permute-start.8 = (bf16[560,256]{1,0:T(8,128)(2,1)S(1)}, bf16[560,256]{1,0:T(8,128)(2,1)S(1)}, u32[]{:S(2)}, u32[]{:S(2)}) collective-permute-start(bf16[560,256]{1,0:T(8,128)(2,1)S(1)} %get-tuple-element.48), channel_id=1, source_target_pairs={{0,2},{1,3},{2,0},{3,1},{4,6},{5,7},{6,4},{7,5},{8,10},{9,11},{10,... | collective-permute-start | bytes 860168 | tf_op jit(solution)/shard_map/ppermute | solution.py:318
  11.2 0.0 collective-permute-done.rest_0_
  11.2 0.2 collective-permute-done.1.rest_1_
  11.3 1.4 %collective-permute-done.2.rest_2_ = f32[16,256]{1,0:T(8,128)S(1)} collective-permute-done((f32[16,256]{1,0:T(8,128)S(1)}, f32[16,256]{1,0:T(8,128)S(1)}, u32[]{:S(2)}, u32[]{:S(2)}) %collective-permute-start.2) | collective-permute-done | bytes 16416 | tf_op jit(solution)/shard_map/ppermute | solution.py:333
  12.7 0.0 collective-permute-done.3.q_ref
  12.7 0.0 copy-start.1
  12.7 1.6 %collective-permute-start.4 = (f32[16,256]{1,0:T(8,128)S(1)}, f32[16,256]{1,0:T(8,128)S(1)}, u32[]{:S(2)}, u32[]{:S(2)}) collective-permute-start(f32[16,256]{1,0:T(8,128)S(1)} %get-tuple-element.44), channel_id=1, source_target_pairs={{0,4},{4,0},{8,12},{12,8},{16,20},{20,16},{24,28},{28,24},{1,5},{5... | collective-permute-start | bytes 49160 | tf_op jit(solution)/shard_map/ppermute | solution.py:323
  14.3 0.0 collective-permute-start.6
  14.3 2.0 %collective-permute-start.7 = (f32[16,256]{1,0:T(8,128)S(1)}, f32[16,256]{1,0:T(8,128)S(1)}, u32[]{:S(2)}, u32[]{:S(2)}) collective-permute-start(f32[16,256]{1,0:T(8,128)S(1)} %get-tuple-element.43.base_ref), channel_id=1, source_target_pairs={{0,2},{1,3},{2,0},{3,1},{4,6},{5,7},{6,4},{7,5},{8,10},{9,11},{10,... | collective-permute-start | bytes 49160 | tf_op jit(solution)/shard_map/ppermute | solution.py:318
  16.3 0.2 %collective-permute-done.4.extra_ref = f32[16,256]{1,0:T(8,128)S(1)} collective-permute-done((f32[16,256]{1,0:T(8,128)S(1)}, f32[16,256]{1,0:T(8,128)S(1)}, u32[]{:S(2)}, u32[]{:S(2)}) %collective-permute-start.4) | collective-permute-done | bytes 16416 | tf_op jit(solution)/shard_map/ppermute | solution.py:323
  16.6 0.0 copy-done.1
  16.6 0.8 %shard_map.85.own_ref = bf16[512,256]{1,0:T(8,128)(2,1)S(1)} custom-call(bf16[512,256]{1,0:T(8,128)(2,1)S(1)} %copy-done.1, f32[16,256]{1,0:T(8,128)S(1)} %get-tuple-element.37.rates_ref, f32[16,256]{1,0:T(8,128)S(1)} %get-tuple-element.43.base_ref, f32[16,256]{1,0:T(8,128)S(1)} %collective-permute-done.4.extra_ref, ...), custom_call_target="tpu_custom_call" | custom-call | tf_op jit(solution)/shard_map/pallas_call | solution.py:300
  17.3 0.0 copy-start
  17.3 0.1 collective-permute-start.5
  17.4 1.5 %collective-permute-done.6.extra_ref = f32[16,256]{1,0:T(8,128)S(1)} collective-permute-done((f32[16,256]{1,0:T(8,128)S(1)}, f32[16,256]{1,0:T(8,128)S(1)}, u32[]{:S(2)}, u32[]{:S(2)}) %collective-permute-start.6) | collective-permute-done | bytes 16416 | tf_op jit(solution)/shard_map/ppermute | solution.py:339
  18.9 0.0 collective-permute-done.7.base_ref
  18.9 0.0 collective-permute-done.8.local_ref
  19.0 0.7 %shard_map.86.rest_0_ = bf16[512,256]{1,0:T(8,128)(2,1)S(1)} custom-call(f32[16,256]{1,0:T(8,128)S(1)} %collective-permute-done.6.extra_ref, f32[16,256]{1,0:T(8,128)S(1)} %collective-permute-done.7.base_ref, bf16[512,256]{1,0:T(8,128)(2,1)S(1)} %collective-permute-done.3.q_ref, bf16[560,256]{1,0:T(8,128)(2,1)S(1)} %collective-permute-done.8.local_ref), custom_call_target="tpu_custom_call" | custom-call | tf_op jit(solution)/shard_map/pallas_call | solution.py:300
  19.7 0.1 collective-permute-start.9
  19.8 0.0 collective-permute-done.5.pair_ref
  19.8 0.0 copy-done
  19.8 0.4 %shard_map.87.near_ref = f32[512,256]{1,0:T(8,128)S(1)} custom-call(bf16[1024,256]{1,0:T(8,128)(2,1)S(1)} %copy-done, f32[1,256]{1,0:T(1,128)S(1)} %get-tuple-element.36.bias_ref, bf16[512,256]{1,0:T(8,128)(2,1)S(1)} %shard_map.85.own_ref, bf16[512,256]{1,0:T(8,128)(2,1)S(1)} %collective-permute-done.5.pair_ref, bf16[512,256]{1,0:T(8,128)(2,1)S(1)} %shard_map.86.rest_0_), custom_call_target="tpu_custom_call" | custom-call | tf_op jit(solution)/shard_map/pallas_call | solution.py:300
  20.2 1.1 %collective-permute-done.9.rest_0_ = bf16[512,256]{1,0:T(8,128)(2,1)S(1)} collective-permute-done((bf16[512,256]{1,0:T(8,128)(2,1)S(1)}, bf16[512,256]{1,0:T(8,128)(2,1)S(1)}, u32[]{:S(2)}, u32[]{:S(2)}) %collective-permute-start.9) | collective-permute-done | bytes 262176 | tf_op jit(solution)/shard_map/ppermute | solution.py:318
  21.3 0.9 %shard_map.88 = bf16[512,256]{1,0:T(8,128)(2,1)} custom-call(f32[512,256]{1,0:T(8,128)S(1)} %shard_map.87.near_ref, bf16[1024,256]{1,0:T(8,128)(2,1)S(1)} %copy-done, bf16[512,256]{1,0:T(8,128)(2,1)S(1)} %collective-permute-done.9.rest_0_), custom_call_target="tpu_custom_call" | custom-call | tf_op jit(solution)/shard_map/pallas_call | solution.py:300
  (1 shorter events, 0.0 us)
Async XLA Ops:
  0.0 12.7 %collective-permute-start.3 = (bf16[512,256]{1,0:T(8,128)(2,1)}, bf16[512,256]{1,0:T(8,128)(2,1)S(1)}, u32[]{:S(2)}, u32[]{:S(2)}) collective-permute-start(bf16[512,256]{1,0:T(8,128)(2,1)} %q_ref.1), channel_id=1, source_target_pairs={{0,2},{1,3},{2,0},{3,1},{4,6},{5,7},{6,4},{7,5},{8,10},{9,11},{10,... | collective-permute-start | bytes 786440 | tf_op jit(solution)/shard_map/ppermute | solution.py:318
  6.0 5.2 %collective-permute-start = (f32[16,256]{1,0:T(8,128)S(1)}, f32[16,256]{1,0:T(8,128)S(1)}, u32[]{:S(2)}, u32[]{:S(2)}) collective-permute-start(f32[16,256]{1,0:T(8,128)S(1)} %get-tuple-element.27.refs_6_.total_ref), channel_id=1, source_target_pairs={{0,24},{4,28},{8,16},{12,20},{16,0},{20,4},{24,8},{28,12},{1,25},{... | collective-permute-start | bytes 49160 | tf_op jit(solution)/shard_map/ppermute | solution.py:333
  6.7 4.6 %collective-permute-start.1 = (f32[16,256]{1,0:T(8,128)S(1)}, f32[16,256]{1,0:T(8,128)S(1)}, u32[]{:S(2)}, u32[]{:S(2)}) collective-permute-start(f32[16,256]{1,0:T(8,128)S(1)} %get-tuple-element.27.refs_6_.total_ref), channel_id=1, source_target_pairs={{0,16},{4,20},{8,24},{12,28},{16,0},{20,4},{24,8},{28,12},{1,17},{... | collective-permute-start | bytes 49160 | tf_op jit(solution)/shard_map/ppermute | solution.py:333
  9.0 3.7 %collective-permute-start.2 = (f32[16,256]{1,0:T(8,128)S(1)}, f32[16,256]{1,0:T(8,128)S(1)}, u32[]{:S(2)}, u32[]{:S(2)}) collective-permute-start(f32[16,256]{1,0:T(8,128)S(1)} %get-tuple-element.27.refs_6_.total_ref), channel_id=1, source_target_pairs={{0,8},{4,12},{8,0},{12,4},{16,24},{20,28},{24,16},{28,20},{1,9},{5... | collective-permute-start | bytes 49160 | tf_op jit(solution)/shard_map/ppermute | solution.py:333
  10.6 8.3 %collective-permute-start.8 = (bf16[560,256]{1,0:T(8,128)(2,1)S(1)}, bf16[560,256]{1,0:T(8,128)(2,1)S(1)}, u32[]{:S(2)}, u32[]{:S(2)}) collective-permute-start(bf16[560,256]{1,0:T(8,128)(2,1)S(1)} %get-tuple-element.48), channel_id=1, source_target_pairs={{0,2},{1,3},{2,0},{3,1},{4,6},{5,7},{6,4},{7,5},{8,10},{9,11},{10,... | collective-permute-start | bytes 860168 | tf_op jit(solution)/shard_map/ppermute | solution.py:318
  12.7 3.9 %copy-start.1 = (bf16[512,256]{1,0:T(8,128)(2,1)S(1)}, bf16[512,256]{1,0:T(8,128)(2,1)}, u32[]{:S(2)}) copy-start(bf16[512,256]{1,0:T(8,128)(2,1)} %q_ref.1) | copy-start | bytes 786436
  12.7 3.8 %collective-permute-start.4 = (f32[16,256]{1,0:T(8,128)S(1)}, f32[16,256]{1,0:T(8,128)S(1)}, u32[]{:S(2)}, u32[]{:S(2)}) collective-permute-start(f32[16,256]{1,0:T(8,128)S(1)} %get-tuple-element.44), channel_id=1, source_target_pairs={{0,4},{4,0},{8,12},{12,8},{16,20},{20,16},{24,28},{28,24},{1,5},{5... | collective-permute-start | bytes 49160 | tf_op jit(solution)/shard_map/ppermute | solution.py:323
  14.3 4.6 %collective-permute-start.6 = (f32[16,256]{1,0:T(8,128)S(1)}, f32[16,256]{1,0:T(8,128)S(1)}, u32[]{:S(2)}, u32[]{:S(2)}) collective-permute-start(f32[16,256]{1,0:T(8,128)S(1)} %get-tuple-element.44), channel_id=1, source_target_pairs={{0,6},{1,7},{2,4},{3,5},{4,2},{5,3},{6,0},{7,1},{8,14},{9,15},{10,... | collective-permute-start | bytes 49160 | tf_op jit(solution)/shard_map/ppermute | solution.py:339
  14.3 4.6 %collective-permute-start.7 = (f32[16,256]{1,0:T(8,128)S(1)}, f32[16,256]{1,0:T(8,128)S(1)}, u32[]{:S(2)}, u32[]{:S(2)}) collective-permute-start(f32[16,256]{1,0:T(8,128)S(1)} %get-tuple-element.43.base_ref), channel_id=1, source_target_pairs={{0,2},{1,3},{2,0},{3,1},{4,6},{5,7},{6,4},{7,5},{8,10},{9,11},{10,... | collective-permute-start | bytes 49160 | tf_op jit(solution)/shard_map/ppermute | solution.py:318
  17.3 2.5 %copy-start = (bf16[1024,256]{1,0:T(8,128)(2,1)S(1)}, bf16[1024,256]{1,0:T(8,128)(2,1)}, u32[]{:S(2)}) copy-start(bf16[1024,256]{1,0:T(8,128)(2,1)} %weight_ref.3) | copy-start | bytes 1572868
  17.3 2.5 %collective-permute-start.5 = (bf16[512,256]{1,0:T(8,128)(2,1)S(1)}, bf16[512,256]{1,0:T(8,128)(2,1)S(1)}, u32[]{:S(2)}, u32[]{:S(2)}) collective-permute-start(bf16[512,256]{1,0:T(8,128)(2,1)S(1)} %shard_map.85.own_ref), channel_id=1, source_target_pairs={{0,1},{1,0},{2,3},{3,2},{4,5},{5,4},{6,7},{7,6},{8,9},{9,8},{10,11... | collective-permute-start | bytes 786440 | tf_op jit(solution)/shard_map/ppermute | solution.py:318
  19.7 1.6 %collective-permute-start.9 = (bf16[512,256]{1,0:T(8,128)(2,1)S(1)}, bf16[512,256]{1,0:T(8,128)(2,1)S(1)}, u32[]{:S(2)}, u32[]{:S(2)}) collective-permute-start(bf16[512,256]{1,0:T(8,128)(2,1)S(1)} %shard_map.86.rest_0_), channel_id=1, source_target_pairs={{0,1},{1,0},{2,3},{3,2},{4,5},{5,4},{6,7},{7,6},{8,9},{9,8},{10,11... | collective-permute-start | bytes 786440 | tf_op jit(solution)/shard_map/ppermute | solution.py:318

commit v8 on v7

--- a/solution.py
+++ b/solution.py
@@ -14,8 +14,7 @@
 FOLD_COST = 3000000000
 PIECES = 3
 ROUTES = {2: [(1, 0)], 4: [(3, 2, 0, 1), (2, 3, 0, 1), (1, 0, 3, 2)]}
-INPUTS = 6
-KEPT = 8
+FIRST_COST = 30000000000
 PART_COST = 0
 VMEM_LIMIT = 32 * 1024 * 1024
 
@@ -32,29 +31,13 @@
     return slice(part * LANES, (part + 1) * LANES)
 
 
-def summarize(
-    k_hbm, v_hbm, decay_hbm, residue_hbm, skip_hbm, bias_hbm,
-    total_ref, chunk_ref, gated_ref, decay_ref, residue_ref, skip_ref, bias_ref,
-    k_ref, v_ref, sems,
-):
-    modes = decay_hbm.shape[0]
-    parts = gated_ref.shape[0]
+def summarize(zero, k_ref, v_ref, decay_ref, total_ref, chunk_ref, gated_ref):
+    modes = decay_ref.shape[0]
     chunk_len = k_ref.shape[0] // SUBLANES
-    pairs = [(decay_hbm, decay_ref)]
-    for part in range(parts):
-        lanes = pl.ds(part * LANES, LANES)
-        pairs += [(k_hbm.at[:, lanes], k_ref.at[:, lanes]), (v_hbm.at[:, lanes], v_ref.at[:, lanes])]
-    pairs += [(residue_hbm, residue_ref), (skip_hbm, skip_ref), (bias_hbm, bias_ref)]
-    copies = [pltpu.make_async_copy(src, dst, sems.at[i]) for i, (src, dst) in enumerate(pairs)]
-    for copy in copies:
-        copy.start()
-    copies[0].wait()
     later = (SUBLANES - 1 - lax.broadcasted_iota(jnp.int32, (SUBLANES, LANES), 0)) * chunk_len
     later = later.astype(jnp.float32)
-    for part in range(parts):
+    for part in range(gated_ref.shape[0]):
         lanes = lane_slice(part)
-        copies[1 + 2 * part].wait()
-        copies[2 + 2 * part].wait()
         product = k_ref[:, lanes].astype(jnp.float32) * v_ref[:, lanes].astype(jnp.float32)
         gated_ref[part] = product.astype(jnp.bfloat16).astype(jnp.float32)
         factor = [full(jnp.exp(-row(decay_ref, n, part))) for n in range(modes)]
@@ -65,14 +48,11 @@
             y = gated_ref[part, pl.ds(2 * t + 1, SUBLANES, stride=chunk_len), :]
             return tuple(g * h + (f * x + y) for f, g, h in zip(factor, square, state))
 
-        zero = jnp.zeros((SUBLANES, LANES), jnp.float32)
         state = lax.fori_loop(0, chunk_len // 2, step, (zero,) * modes, unroll=4)
         for n in range(modes):
             chunk_ref[n, :, lanes] = state[n]
             weight = jnp.exp(-row(decay_ref, n, part) * later)
             total_ref[n : n + 1, lanes] = jnp.sum(weight * state[n], axis=0, keepdims=True)
-    for copy in copies[1 + 2 * parts :]:
-        copy.wait()
 
 
 def is_last():
@@ -84,15 +64,20 @@
     return lax.axis_index("seq") < 2
 
 
-def state_kernel(*refs):
-    inputs, total_ref, kept = refs[:INPUTS], refs[INPUTS], refs[INPUTS + 1 : INPUTS + 1 + KEPT]
-    scratch, weights = refs[-4:-1], refs[-1]
-    state, (local_ref, short_ref) = kept[:-2], kept[-2:]
-    chunk_ref, gated_ref, decay_ref, residue_ref, skip_ref, _ = state
-
+def first_kernel(out_ref):
+    out_ref[...] = jnp.zeros_like(out_ref)
+
+
+def state_kernel(
+    zero_ref, k_ref, v_ref, decay_ref, residue_ref, skip_hbm,
+    total_ref, chunk_ref, gated_ref, skip_ref, local_ref, short_ref, weights, sem,
+):
     @pl.when(jnp.logical_not(is_last()))
     def _():
-        summarize(*inputs, total_ref, *state, *scratch)
+        copy = pltpu.make_async_copy(skip_hbm, skip_ref, sem)
+        copy.start()
+        summarize(zero_ref[...], k_ref, v_ref, decay_ref, total_ref, chunk_ref, gated_ref)
+        copy.wait()
 
     @pl.when(is_last())
     def _():
@@ -103,26 +88,39 @@
         convolve(0, gated_ref, decay_ref, residue_ref, skip_ref, chunk_ref, local_ref, short_ref, weights)
 
 
-def local_kernel(*refs):
-    inputs, total_in, rest = refs[:INPUTS], refs[INPUTS], refs[INPUTS + 1 + KEPT :]
-    total_ref, kept, more, scratch, weights = rest[0], rest[1 : 1 + KEPT], rest[1 + KEPT : -4], rest[-4:-1], rest[-1]
-    state, (local_ref, short_ref) = kept[:-2], kept[-2:]
-    chunk_ref, gated_ref, decay_ref, residue_ref, skip_ref, _ = state
+def local_kernel(
+    zero_ref, k_ref, v_ref, decay_ref, residue_ref, skip_hbm,
+    total_in, chunk_in, gated_in, skip_in, local_in, short_in,
+    total_ref, short_ref, *rest,
+):
+    locals_out, (chunk_ref, gated_ref, skip_ref, weights, sem) = rest[:-5], rest[-5:]
+
+    def part_of(part, gated, skip, chunk):
+        convolve(part, gated, decay_ref, residue_ref, skip, chunk, locals_out[part], short_ref, weights)
 
     @pl.when(is_last())
     def _():
-        summarize(*inputs, total_ref, *state, *scratch)
+        copy = pltpu.make_async_copy(skip_hbm, skip_ref, sem)
+        copy.start()
+        summarize(zero_ref[...], k_ref, v_ref, decay_ref, total_ref, chunk_ref, gated_ref)
+        copy.wait()
+        for part in range(len(locals_out)):
+            part_of(part, gated_ref, skip_ref, chunk_ref)
 
     @pl.when(jnp.logical_not(is_last()))
     def _():
         total_ref[...] = total_in[...]
-
-    @pl.when(jnp.logical_not(is_first()))
-    def _():
-        convolve(0, gated_ref, decay_ref, residue_ref, skip_ref, chunk_ref, local_ref, short_ref, weights)
-
-    for i, more_ref in enumerate(more):
-        convolve(i + 1, gated_ref, decay_ref, residue_ref, skip_ref, chunk_ref, more_ref, short_ref, weights)
+        for part in range(1, len(locals_out)):
+            part_of(part, gated_in, skip_in, chunk_in)
+
+    @pl.when(is_first())
+    def _():
+        locals_out[0][...] = local_in[...]
+        short_ref[:, lane_slice(0)] = short_in[...]
+
+    @pl.when(jnp.logical_not(jnp.logical_or(is_first(), is_last())))
+    def _():
+        part_of(0, gated_in, skip_in, chunk_in)
 
 
 def convolve(part, gated, decay_ref, residue_ref, skip_ref, chunk_ref, local_ref, short_ref, weights):
@@ -155,11 +153,12 @@
         return state
 
     lax.fori_loop(0, chunk_len, step, tuple(start), unroll=4)
-    short_ref[:seg_len, lanes] = local_ref[...].astype(short_ref.dtype)
+    spot = lanes if short_ref.shape[1] > LANES else slice(None)
+    short_ref[:seg_len, spot] = local_ref[...].astype(short_ref.dtype)
     left = decay_ref[:, lanes]
     for first in range(seg_len, short_ref.shape[0], modes):
         piece = left.astype(short_ref.dtype)
-        short_ref[first : first + modes, lanes] = piece
+        short_ref[first : first + modes, spot] = piece
         left = left - piece.astype(jnp.float32)
 
 
@@ -295,15 +294,13 @@
         copy.wait()
 
 
-def call(kernel, out, *args, cost=0, aliases=(), scratch=(), hbm=0, outs=pltpu.VMEM):
-    spaces = [pltpu.HBM] * hbm + [pltpu.VMEM] * (len(args) - hbm)
+def call(kernel, out, *args, cost=0, scratch=(), hbm=(), outs=pltpu.VMEM):
     return pl.pallas_call(
         kernel,
         out_shape=out,
-        in_specs=[pl.BlockSpec(memory_space=space) for space in spaces],
+        in_specs=[pl.BlockSpec(memory_space=pltpu.HBM if i in hbm else pltpu.VMEM) for i in range(len(args))],
         out_specs=jax.tree.map(lambda _: pl.BlockSpec(memory_space=outs), out),
         scratch_shapes=list(scratch),
-        input_output_aliases=dict(aliases),
         compiler_params=pltpu.CompilerParams(vmem_limit_bytes=VMEM_LIMIT),
         cost_estimate=pl.CostEstimate(flops=cost, bytes_accessed=0, transcendentals=0),
     )(*args)
@@ -362,32 +359,28 @@
     modes = decay.shape[0]
     cols = out_weight.shape[1]
     parts = channels // LANES
-    tall = pltpu.VMEM((seg_len, channels), jnp.bfloat16)
+    bias = out_bias.reshape(1, -1)
+    zero = call(first_kernel, struct((SUBLANES, LANES)), cost=FIRST_COST)
     q_across = swapped(q_gate, 2)
-    inputs = (k_gate, value, decay, residue, skip.reshape(1, -1), out_bias.reshape(1, -1))
-    inputs = [pltpu.with_memory_space_constraint(x, pltpu.HBM) for x in inputs]
-    tall = pltpu.VMEM((seg_len, channels), jnp.bfloat16)
-    scratch = [tall, tall, pltpu.SemaphoreType.DMA((2 * parts + 4,))]
     few = struct((modes, channels))
-    kept = [
-        struct((modes, SUBLANES, channels)),
-        struct((parts, seg_len, LANES)),
-        few,
-        few,
-        struct((1, channels)),
-        struct((1, cols)),
-        struct((seg_len, LANES)),
-        struct((seg_len + PIECES * modes, channels), jnp.bfloat16),
-    ]
-    scratch += [pltpu.VMEM((modes, SUBLANES, LANES), jnp.float32)]
-    total, *state = call(state_kernel, [few, *kept], *inputs, scratch=scratch, hbm=INPUTS)
-    more = [struct((seg_len, LANES))] * (parts - 1)
-    own_total, *state = call(
-        local_kernel, [few, *kept, *more], *inputs, total, *state,
-        scratch=scratch, hbm=INPUTS, aliases=[(INPUTS + 1 + i, 1 + i) for i in range(KEPT)],
-    )
-    _, _, decay, residue, _, bias, first_local, local_short, *more = state
-    local = [first_local, *more]
+    chunks, gated, bypass = (modes, SUBLANES, channels), (parts, seg_len, LANES), (1, channels)
+    thin = struct((seg_len, LANES))
+    tall = seg_len + PIECES * modes
+    skip = pltpu.with_memory_space_constraint(skip.reshape(1, -1), pltpu.HBM)
+    inputs = (zero, k_gate, value, decay, residue, skip)
+    scratch = [pltpu.VMEM((modes, SUBLANES, LANES), jnp.float32), pltpu.SemaphoreType.DMA]
+    total, *state = call(
+        state_kernel,
+        [few, struct(chunks), struct(gated), struct(bypass), thin, struct((tall, LANES), jnp.bfloat16)],
+        *inputs,
+        scratch=scratch, hbm=(5,),
+    )
+    own_total, local_short, *local = call(
+        local_kernel,
+        [few, struct((tall, channels), jnp.bfloat16), *[thin] * parts],
+        *inputs, total, *state,
+        scratch=[pltpu.VMEM(shape, jnp.float32) for shape in (chunks, gated, bypass)] + scratch, hbm=(5,),
+    )
     local_across = swapped(local_short, 2)
     base, extra, q_across = carry_shares(total, own_total, decay, residue, seg_len, q_across)
     extra_beside = beside(extra)

time: 22.5 us -> 21.6 us (0.960)
  Pallas kernels: 6.84 us -> 5.8 us
  waiting for transfers between devices: 4.41 us -> 3.58 us
  local copies, waits for them, and re-layouts: 0.01 us -> 0.6 us
  starting transfers between devices: 10.9 us -> 11.4 us
    pallas_call x7 -> x8, Pallas kernels: 6.84 us -> 5.8 us  [call(): pl.pallas_call(kernel, out_shape=out, in_specs=[pl.BlockSpec(memory_space...]
    ppermute x1, starting transfers between devices: 0.02 us -> 0.91 us  [corner(): return lax.ppermute(value, ('seq', 'chan'), pairs)]
    unnamed x4 -> x14, local copies, waits for them, and re-layouts: 0.01 us -> 0.6 us
    ppermute x3, waiting for transfers between devices: 1.5 us -> 1.07 us  [along(): return lax.ppermute(value, 'seq', [(r, target(r)) for r in range(count)])]
    ppermute x5, waiting for transfers between devices: 1.12 us -> 0.72 us  [swapped(): return lax.ppermute(value, 'chan', [(r, r ^ bit) for r in range(count)])]
    ppermute x5, starting transfers between devices: 5.66 us -> 5.28 us  [swapped(): return lax.ppermute(value, 'chan', [(r, r ^ bit) for r in range(count)])]
  transfers between devices with their start and end apart: 10 -> 10, of which waited for: 5 -> 6; matrix products, arithmetic and copies ran while one was open for 0% -> 0% of each run, Pallas kernels for 27% -> 23%
where the time goes in v8:
time: 21.6 us; the launch traced here: 21.5 us
  starting transfers between devices  11.4 us (53%)
  Pallas kernels  5.8 us (27%)
  waiting for transfers between devices  3.58 us (17%)
  local copies, waits for them, and re-layouts  0.6 us (3%)
    pallas_call x8, Pallas kernels, call(): pl.pallas_call(kernel, out_shape=out, in_specs=[pl.BlockSpec(memory_space...  5.8 us
    ppermute x5, starting transfers between devices, swapped(): return lax.ppermute(value, 'chan', [(r, r ^ bit) for r in range(count)])  5.28 us
    ppermute x3, starting transfers between devices, along(): return lax.ppermute(value, 'seq', [(r, target(r)) for r in range(count)])  3.65 us
    ppermute x1, starting transfers between devices, beside(): return lax.ppermute(value, 'seq', [(r, r ^ 1) for r in range(count)])  1.56 us
    ppermute x1, waiting for transfers between devices, corner(): return lax.ppermute(value, ('seq', 'chan'), pairs)  1.54 us
    ppermute x3, waiting for transfers between devices, along(): return lax.ppermute(value, 'seq', [(r, target(r)) for r in range(count)])  1.07 us
    ppermute x1, starting transfers between devices, corner(): return lax.ppermute(value, ('seq', 'chan'), pairs)  0.91 us
    ppermute x5, waiting for transfers between devices, swapped(): return lax.ppermute(value, 'chan', [(r, r ^ bit) for r in range(count)])  0.72 us
  transfers between devices with their start and end apart: 10, of which 6 were waited for; matrix products, arithmetic and copies ran while one was open for 0% of the time, Pallas kernels for 23%

profile of v8, /device:TPU:0, one launch (start us, length us, event | category | flops | bytes accessed | tf_op | source)
XLA Modules:
  0.0 21.5 jit_solution(52247175555149992)
XLA Ops:
  0.0 0.0 copy-start.2
  0.0 0.0 copy-start.4
  0.0 0.0 copy-start.5
  0.0 0.0 copy-start.1
  0.0 3.0 %collective-permute-start.3 = (bf16[512,256]{1,0:T(8,128)(2,1)}, bf16[512,256]{1,0:T(8,128)(2,1)S(1)}, u32[]{:S(2)}, u32[]{:S(2)}) collective-permute-start(bf16[512,256]{1,0:T(8,128)(2,1)} %q_ref.1), channel_id=1, source_target_pairs={{0,2},{1,3},{2,0},{3,1},{4,6},{5,7},{6,4},{7,5},{8,10},{9,11},{10,... | collective-permute-start | bytes 786440 | tf_op jit(solution)/shard_map/ppermute | solution.py:315
  3.1 0.0 copy-done.2
  3.1 0.0 copy-done.4
  3.1 0.0 copy-done.5
  3.1 0.0 copy-done.1
  3.1 2.0 %shard_map.83 = (f32[16,256]{1,0:T(8,128)S(1)}, f32[16,8,256]{2,1,0:T(8,128)S(1)}, f32[2,512,128]{2,1,0:T(8,128)S(1)}, f32[1,256]{1,0:T(1,128)S(1)}, f32[512,128...) custom-call(f32[8,128]{1,0:T(8,128)S(1)} %shard_map.82.zero_ref, bf16[512,256]{1,0:T(8,128)(2,1)S(1)} %copy-done.1, ...), custom_call_target="tpu_custom_call" | custom-call | tf_op jit(solution)/shard_map/pallas_call | solution.py:298
  5.0 1.7 %collective-permute-start = (f32[16,256]{1,0:T(8,128)S(1)}, f32[16,256]{1,0:T(8,128)S(1)}, u32[]{:S(2)}, u32[]{:S(2)}) collective-permute-start(f32[16,256]{1,0:T(8,128)S(1)} %get-tuple-element.21.total_in.total_ref), channel_id=1, source_target_pairs={{0,24},{4,28},{8,16},{12,20},{16,0},{20,4},{24,8},{28,12},{1,25},{... | collective-permute-start | bytes 49160 | tf_op jit(solution)/shard_map/ppermute | solution.py:330
  6.8 1.2 %collective-permute-start.1 = (f32[16,256]{1,0:T(8,128)S(1)}, f32[16,256]{1,0:T(8,128)S(1)}, u32[]{:S(2)}, u32[]{:S(2)}) collective-permute-start(f32[16,256]{1,0:T(8,128)S(1)} %get-tuple-element.21.total_in.total_ref), channel_id=1, source_target_pairs={{0,16},{4,20},{8,24},{12,28},{16,0},{20,4},{24,8},{28,12},{1,17},{... | collective-permute-start | bytes 49160 | tf_op jit(solution)/shard_map/ppermute | solution.py:330
  8.0 0.7 %collective-permute-start.2 = (f32[16,256]{1,0:T(8,128)S(1)}, f32[16,256]{1,0:T(8,128)S(1)}, u32[]{:S(2)}, u32[]{:S(2)}) collective-permute-start(f32[16,256]{1,0:T(8,128)S(1)} %get-tuple-element.21.total_in.total_ref), channel_id=1, source_target_pairs={{0,8},{4,12},{8,0},{12,4},{16,24},{20,28},{24,16},{28,20},{1,9},{5... | collective-permute-start | bytes 49160 | tf_op jit(solution)/shard_map/ppermute | solution.py:330
  8.7 1.0 %shard_map.84 = (f32[16,256]{1,0:T(8,128)S(1)}, bf16[560,256]{1,0:T(8,128)(2,1)S(1)}, f32[512,128]{1,0:T(8,128)S(1)}, f32[512,128]{1,0:T(8,128)S(1)}) custom-call(f32[8,128]{1,0:T(8,128)S(1)} %shard_map.82.zero_ref, bf16[512,256]{1,0:T(8,128)(2,1)S(1)} %copy-done.1, bf16[512,256]{1,0:T(8,128)(2,1)S(1)} %copy-done.2, f32[16,256]{1,0:T(8,128)S(1)} %copy-done.4, ...), custom_call_target="tpu_custom_call" | custom-call | tf_op jit(solution)/shard_map/pallas_call | solution.py:298
  9.7 1.0 %collective-permute-start.8 = (bf16[560,256]{1,0:T(8,128)(2,1)S(1)}, bf16[560,256]{1,0:T(8,128)(2,1)S(1)}, u32[]{:S(2)}, u32[]{:S(2)}) collective-permute-start(bf16[560,256]{1,0:T(8,128)(2,1)S(1)} %get-tuple-element.36), channel_id=1, source_target_pairs={{0,2},{1,3},{2,0},{3,1},{4,6},{5,7},{6,4},{7,5},{8,10},{9,11},{10,... | collective-permute-start | bytes 860168 | tf_op jit(solution)/shard_map/ppermute | solution.py:315
  10.7 0.0 collective-permute-done.rest_0_
  10.7 0.9 %collective-permute-done.1.rest_1_ = f32[16,256]{1,0:T(8,128)S(1)} collective-permute-done((f32[16,256]{1,0:T(8,128)S(1)}, f32[16,256]{1,0:T(8,128)S(1)}, u32[]{:S(2)}, u32[]{:S(2)}) %collective-permute-start.1) | collective-permute-done | bytes 16416 | tf_op jit(solution)/shard_map/ppermute | solution.py:330
  11.6 0.2 collective-permute-done.2.rest_2_
  11.8 0.0 collective-permute-done.3.q_ref
  11.8 0.0 copy-start.3
  11.8 1.6 %collective-permute-start.4 = (f32[16,256]{1,0:T(8,128)S(1)}, f32[16,256]{1,0:T(8,128)S(1)}, u32[]{:S(2)}, u32[]{:S(2)}) collective-permute-start(f32[16,256]{1,0:T(8,128)S(1)} %get-tuple-element.32), channel_id=1, source_target_pairs={{0,4},{4,0},{8,12},{12,8},{16,20},{20,16},{24,28},{28,24},{1,5},{5... | collective-permute-start | bytes 49160 | tf_op jit(solution)/shard_map/ppermute | solution.py:320
  13.4 0.9 %collective-permute-start.6 = (f32[16,256]{1,0:T(8,128)S(1)}, f32[16,256]{1,0:T(8,128)S(1)}, u32[]{:S(2)}, u32[]{:S(2)}) collective-permute-start(f32[16,256]{1,0:T(8,128)S(1)} %get-tuple-element.32), channel_id=1, source_target_pairs={{0,6},{1,7},{2,4},{3,5},{4,2},{5,3},{6,0},{7,1},{8,14},{9,15},{10,... | collective-permute-start | bytes 49160 | tf_op jit(solution)/shard_map/ppermute | solution.py:336
  14.3 1.1 %collective-permute-start.7 = (f32[16,256]{1,0:T(8,128)S(1)}, f32[16,256]{1,0:T(8,128)S(1)}, u32[]{:S(2)}, u32[]{:S(2)}) collective-permute-start(f32[16,256]{1,0:T(8,128)S(1)} %get-tuple-element.31.base_ref), channel_id=1, source_target_pairs={{0,2},{1,3},{2,0},{3,1},{4,6},{5,7},{6,4},{7,5},{8,10},{9,11},{10,... | collective-permute-start | bytes 49160 | tf_op jit(solution)/shard_map/ppermute | solution.py:315
  15.4 0.2 %collective-permute-done.4.extra_ref = f32[16,256]{1,0:T(8,128)S(1)} collective-permute-done((f32[16,256]{1,0:T(8,128)S(1)}, f32[16,256]{1,0:T(8,128)S(1)}, u32[]{:S(2)}, u32[]{:S(2)}) %collective-permute-start.4) | collective-permute-done | bytes 16416 | tf_op jit(solution)/shard_map/ppermute | solution.py:320
  15.6 0.0 copy-done.3
  15.6 0.8 %shard_map.86.own_ref = bf16[512,256]{1,0:T(8,128)(2,1)S(1)} custom-call(bf16[512,256]{1,0:T(8,128)(2,1)S(1)} %copy-done.3, f32[16,256]{1,0:T(8,128)S(1)} %copy-done.4, f32[16,256]{1,0:T(8,128)S(1)} %get-tuple-element.31.base_ref, f32[16,256]{1,0:T(8,128)S(1)} %collective-permute-done.4.extra_ref, f32[512,128]{1,0:T(8,128)S(1)} %get-tuple-element.33.rest_0_, ...), custom_call_target="tpu_custom_call" | custom-call | tf_op jit(solution)/shard_map/pallas_call | solution.py:298
  16.4 0.0 copy-start
  16.4 0.1 collective-permute-start.5
  16.5 1.5 %collective-permute-done.6.extra_ref = f32[16,256]{1,0:T(8,128)S(1)} collective-permute-done((f32[16,256]{1,0:T(8,128)S(1)}, f32[16,256]{1,0:T(8,128)S(1)}, u32[]{:S(2)}, u32[]{:S(2)}) %collective-permute-start.6) | collective-permute-done | bytes 16416 | tf_op jit(solution)/shard_map/ppermute | solution.py:336
  18.0 0.2 collective-permute-done.7.base_ref
  18.2 0.0 collective-permute-done.8.local_ref
  18.2 0.7 %shard_map.87.rest_0_ = bf16[512,256]{1,0:T(8,128)(2,1)S(1)} custom-call(f32[16,256]{1,0:T(8,128)S(1)} %collective-permute-done.6.extra_ref, f32[16,256]{1,0:T(8,128)S(1)} %collective-permute-done.7.base_ref, bf16[512,256]{1,0:T(8,128)(2,1)S(1)} %collective-permute-done.3.q_ref, bf16[560,256]{1,0:T(8,128)(2,1)S(1)} %collective-permute-done.8.local_ref), custom_call_target="tpu_custom_call" | custom-call | tf_op jit(solution)/shard_map/pallas_call | solution.py:298
  18.9 0.0 copy-start.6
  19.0 0.1 collective-permute-start.9
  19.0 0.0 collective-permute-done.5.pair_ref
  19.0 0.0 copy-done
  19.1 0.6 %copy-done.6 = f32[256]{0:T(256)S(1)} copy-done((f32[256]{0:T(256)S(1)}, f32[256]{0:T(256)}, u32[]{:S(2)}) %copy-start.6) | copy-done | bytes 1048
  19.6 0.4 %shard_map.88.near_ref = f32[512,256]{1,0:T(8,128)S(1)} custom-call(bf16[1024,256]{1,0:T(8,128)(2,1)S(1)} %copy-done, f32[1,256]{1,0:T(1,128)S(1)} %bitcast.2, bf16[512,256]{1,0:T(8,128)(2,1)S(1)} %shard_map.86.own_ref, bf16[512,256]{1,0:T(8,128)(2,1)S(1)} %collective-permute-done.5.pair_ref, bf16[512,256]{1,0:T(8,128)(2,1)S(1)} %shard_map.87.rest_0_), custom_call_target="tpu_custom_call" | custom-call | tf_op jit(solution)/shard_map/pallas_call | solution.py:298
  20.0 0.6 %collective-permute-done.9.rest_0_ = bf16[512,256]{1,0:T(8,128)(2,1)S(1)} collective-permute-done((bf16[512,256]{1,0:T(8,128)(2,1)S(1)}, bf16[512,256]{1,0:T(8,128)(2,1)S(1)}, u32[]{:S(2)}, u32[]{:S(2)}) %collective-permute-start.9) | collective-permute-done | bytes 262176 | tf_op jit(solution)/shard_map/ppermute | solution.py:315
  20.6 0.9 %shard_map.89 = bf16[512,256]{1,0:T(8,128)(2,1)} custom-call(f32[512,256]{1,0:T(8,128)S(1)} %shard_map.88.near_ref, bf16[1024,256]{1,0:T(8,128)(2,1)S(1)} %copy-done, bf16[512,256]{1,0:T(8,128)(2,1)S(1)} %collective-permute-done.9.rest_0_), custom_call_target="tpu_custom_call" | custom-call | tf_op jit(solution)/shard_map/pallas_call | solution.py:298
  (2 shorter events, 0.0 us)
Async XLA Ops:
  0.0 3.1 %copy-start.2 = (bf16[512,256]{1,0:T(8,128)(2,1)S(1)}, bf16[512,256]{1,0:T(8,128)(2,1)}, u32[]{:S(2)}) copy-start(bf16[512,256]{1,0:T(8,128)(2,1)} %v_ref.3) | copy-start | bytes 786436
  0.0 3.1 %copy-start.4 = (f32[16,256]{1,0:T(8,128)S(1)}, f32[16,256]{1,0:T(8,128)}, u32[]{:S(2)}) copy-start(f32[16,256]{1,0:T(8,128)} %rates_ref.3) | copy-start | bytes 49156
  0.0 3.1 %copy-start.5 = (f32[16,256]{1,0:T(8,128)S(1)}, f32[16,256]{1,0:T(8,128)}, u32[]{:S(2)}) copy-start(f32[16,256]{1,0:T(8,128)} %residue_ref.5) | copy-start | bytes 49156
  0.0 3.1 %copy-start.1 = (bf16[512,256]{1,0:T(8,128)(2,1)S(1)}, bf16[512,256]{1,0:T(8,128)(2,1)}, u32[]{:S(2)}) copy-start(bf16[512,256]{1,0:T(8,128)(2,1)} %k_ref.3) | copy-start | bytes 786436
  0.0 11.8 %collective-permute-start.3 = (bf16[512,256]{1,0:T(8,128)(2,1)}, bf16[512,256]{1,0:T(8,128)(2,1)S(1)}, u32[]{:S(2)}, u32[]{:S(2)}) collective-permute-start(bf16[512,256]{1,0:T(8,128)(2,1)} %q_ref.1), channel_id=1, source_target_pairs={{0,2},{1,3},{2,0},{3,1},{4,6},{5,7},{6,4},{7,5},{8,10},{9,11},{10,... | collective-permute-start | bytes 786440 | tf_op jit(solution)/shard_map/ppermute | solution.py:315
  5.0 5.7 %collective-permute-start = (f32[16,256]{1,0:T(8,128)S(1)}, f32[16,256]{1,0:T(8,128)S(1)}, u32[]{:S(2)}, u32[]{:S(2)}) collective-permute-start(f32[16,256]{1,0:T(8,128)S(1)} %get-tuple-element.21.total_in.total_ref), channel_id=1, source_target_pairs={{0,24},{4,28},{8,16},{12,20},{16,0},{20,4},{24,8},{28,12},{1,25},{... | collective-permute-start | bytes 49160 | tf_op jit(solution)/shard_map/ppermute | solution.py:330
  6.8 4.8 %collective-permute-start.1 = (f32[16,256]{1,0:T(8,128)S(1)}, f32[16,256]{1,0:T(8,128)S(1)}, u32[]{:S(2)}, u32[]{:S(2)}) collective-permute-start(f32[16,256]{1,0:T(8,128)S(1)} %get-tuple-element.21.total_in.total_ref), channel_id=1, source_target_pairs={{0,16},{4,20},{8,24},{12,28},{16,0},{20,4},{24,8},{28,12},{1,17},{... | collective-permute-start | bytes 49160 | tf_op jit(solution)/shard_map/ppermute | solution.py:330
  8.0 3.7 %collective-permute-start.2 = (f32[16,256]{1,0:T(8,128)S(1)}, f32[16,256]{1,0:T(8,128)S(1)}, u32[]{:S(2)}, u32[]{:S(2)}) collective-permute-start(f32[16,256]{1,0:T(8,128)S(1)} %get-tuple-element.21.total_in.total_ref), channel_id=1, source_target_pairs={{0,8},{4,12},{8,0},{12,4},{16,24},{20,28},{24,16},{28,20},{1,9},{5... | collective-permute-start | bytes 49160 | tf_op jit(solution)/shard_map/ppermute | solution.py:330
  9.7 8.5 %collective-permute-start.8 = (bf16[560,256]{1,0:T(8,128)(2,1)S(1)}, bf16[560,256]{1,0:T(8,128)(2,1)S(1)}, u32[]{:S(2)}, u32[]{:S(2)}) collective-permute-start(bf16[560,256]{1,0:T(8,128)(2,1)S(1)} %get-tuple-element.36), channel_id=1, source_target_pairs={{0,2},{1,3},{2,0},{3,1},{4,6},{5,7},{6,4},{7,5},{8,10},{9,11},{10,... | collective-permute-start | bytes 860168 | tf_op jit(solution)/shard_map/ppermute | solution.py:315
  11.8 3.9 %copy-start.3 = (bf16[512,256]{1,0:T(8,128)(2,1)S(1)}, bf16[512,256]{1,0:T(8,128)(2,1)}, u32[]{:S(2)}) copy-start(bf16[512,256]{1,0:T(8,128)(2,1)} %q_ref.1) | copy-start | bytes 786436
  11.8 3.8 %collective-permute-start.4 = (f32[16,256]{1,0:T(8,128)S(1)}, f32[16,256]{1,0:T(8,128)S(1)}, u32[]{:S(2)}, u32[]{:S(2)}) collective-permute-start(f32[16,256]{1,0:T(8,128)S(1)} %get-tuple-element.32), channel_id=1, source_target_pairs={{0,4},{4,0},{8,12},{12,8},{16,20},{20,16},{24,28},{28,24},{1,5},{5... | collective-permute-start | bytes 49160 | tf_op jit(solution)/shard_map/ppermute | solution.py:320
  13.4 4.7 %collective-permute-start.6 = (f32[16,256]{1,0:T(8,128)S(1)}, f32[16,256]{1,0:T(8,128)S(1)}, u32[]{:S(2)}, u32[]{:S(2)}) collective-permute-start(f32[16,256]{1,0:T(8,128)S(1)} %get-tuple-element.32), channel_id=1, source_target_pairs={{0,6},{1,7},{2,4},{3,5},{4,2},{5,3},{6,0},{7,1},{8,14},{9,15},{10,... | collective-permute-start | bytes 49160 | tf_op jit(solution)/shard_map/ppermute | solution.py:336
  14.3 3.9 %collective-permute-start.7 = (f32[16,256]{1,0:T(8,128)S(1)}, f32[16,256]{1,0:T(8,128)S(1)}, u32[]{:S(2)}, u32[]{:S(2)}) collective-permute-start(f32[16,256]{1,0:T(8,128)S(1)} %get-tuple-element.31.base_ref), channel_id=1, source_target_pairs={{0,2},{1,3},{2,0},{3,1},{4,6},{5,7},{6,4},{7,5},{8,10},{9,11},{10,... | collective-permute-start | bytes 49160 | tf_op jit(solution)/shard_map/ppermute | solution.py:315
  16.4 2.7 %copy-start = (bf16[1024,256]{1,0:T(8,128)(2,1)S(1)}, bf16[1024,256]{1,0:T(8,128)(2,1)}, u32[]{:S(2)}) copy-start(bf16[1024,256]{1,0:T(8,128)(2,1)} %weight_ref.3) | copy-start | bytes 1572868
  16.4 2.6 %collective-permute-start.5 = (bf16[512,256]{1,0:T(8,128)(2,1)S(1)}, bf16[512,256]{1,0:T(8,128)(2,1)S(1)}, u32[]{:S(2)}, u32[]{:S(2)}) collective-permute-start(bf16[512,256]{1,0:T(8,128)(2,1)S(1)} %shard_map.86.own_ref), channel_id=1, source_target_pairs={{0,1},{1,0},{2,3},{3,2},{4,5},{5,4},{6,7},{7,6},{8,9},{9,8},{10,11... | collective-permute-start | bytes 786440 | tf_op jit(solution)/shard_map/ppermute | solution.py:315
  18.9 0.7 %copy-start.6 = (f32[256]{0:T(256)S(1)}, f32[256]{0:T(256)}, u32[]{:S(2)}) copy-start(f32[256]{0:T(256)} %param.15) | copy-start | bytes 3076
  19.0 1.6 %collective-permute-start.9 = (bf16[512,256]{1,0:T(8,128)(2,1)S(1)}, bf16[512,256]{1,0:T(8,128)(2,1)S(1)}, u32[]{:S(2)}, u32[]{:S(2)}) collective-permute-start(bf16[512,256]{1,0:T(8,128)(2,1)S(1)} %shard_map.87.rest_0_), channel_id=1, source_target_pairs={{0,1},{1,0},{2,3},{3,2},{4,5},{5,4},{6,7},{7,6},{8,9},{9,8},{10,11... | collective-permute-start | bytes 786440 | tf_op jit(solution)/shard_map/ppermute | solution.py:315

commit v9 on v8

--- a/solution.py
+++ b/solution.py
@@ -10,12 +10,14 @@
 LANES = 128
 SUBLANES = 8
 STORES = 4
-OWN_COST = 0
-FOLD_COST = 3000000000
-PIECES = 3
+OWN_COST = 3000000000
+FOLD_COST = 500000000
+PIECES = 2
 ROUTES = {2: [(1, 0)], 4: [(3, 2, 0, 1), (2, 3, 0, 1), (1, 0, 3, 2)]}
+MORE_COST = 1000000000
 FIRST_COST = 30000000000
-PART_COST = 0
+NEAR_COST = 3000000000
+PART_COST = 1000000000
 VMEM_LIMIT = 32 * 1024 * 1024
 
 
@@ -88,39 +90,44 @@
         convolve(0, gated_ref, decay_ref, residue_ref, skip_ref, chunk_ref, local_ref, short_ref, weights)
 
 
-def local_kernel(
+def first_part_kernel(
     zero_ref, k_ref, v_ref, decay_ref, residue_ref, skip_hbm,
     total_in, chunk_in, gated_in, skip_in, local_in, short_in,
-    total_ref, short_ref, *rest,
+    total_ref, chunk_ref, gated_ref, skip_ref, local_ref, short_ref, weights, sem,
 ):
-    locals_out, (chunk_ref, gated_ref, skip_ref, weights, sem) = rest[:-5], rest[-5:]
-
-    def part_of(part, gated, skip, chunk):
-        convolve(part, gated, decay_ref, residue_ref, skip, chunk, locals_out[part], short_ref, weights)
-
     @pl.when(is_last())
     def _():
         copy = pltpu.make_async_copy(skip_hbm, skip_ref, sem)
         copy.start()
         summarize(zero_ref[...], k_ref, v_ref, decay_ref, total_ref, chunk_ref, gated_ref)
         copy.wait()
-        for part in range(len(locals_out)):
-            part_of(part, gated_ref, skip_ref, chunk_ref)
+        convolve(0, gated_ref, decay_ref, residue_ref, skip_ref, chunk_ref, local_ref, short_ref, weights)
 
     @pl.when(jnp.logical_not(is_last()))
     def _():
         total_ref[...] = total_in[...]
-        for part in range(1, len(locals_out)):
-            part_of(part, gated_in, skip_in, chunk_in)
 
     @pl.when(is_first())
     def _():
-        locals_out[0][...] = local_in[...]
-        short_ref[:, lane_slice(0)] = short_in[...]
+        local_ref[...] = local_in[...]
+        short_ref[...] = short_in[...]
 
     @pl.when(jnp.logical_not(jnp.logical_or(is_first(), is_last())))
     def _():
-        part_of(0, gated_in, skip_in, chunk_in)
+        convolve(0, gated_in, decay_ref, residue_ref, skip_in, chunk_in, local_ref, short_ref, weights)
+
+
+def other_part_kernel(
+    part, decay_ref, residue_ref, chunk_in, gated_in, skip_in, chunk_last, gated_last, skip_last,
+    local_ref, short_ref, weights,
+):
+    @pl.when(is_last())
+    def _():
+        convolve(part, gated_last, decay_ref, residue_ref, skip_last, chunk_last, local_ref, short_ref, weights)
+
+    @pl.when(jnp.logical_not(is_last()))
+    def _():
+        convolve(part, gated_in, decay_ref, residue_ref, skip_in, chunk_in, local_ref, short_ref, weights)
 
 
 def convolve(part, gated, decay_ref, residue_ref, skip_ref, chunk_ref, local_ref, short_ref, weights):
@@ -153,12 +160,11 @@
         return state
 
     lax.fori_loop(0, chunk_len, step, tuple(start), unroll=4)
-    spot = lanes if short_ref.shape[1] > LANES else slice(None)
-    short_ref[:seg_len, spot] = local_ref[...].astype(short_ref.dtype)
+    short_ref[:seg_len, :] = local_ref[...].astype(short_ref.dtype)
     left = decay_ref[:, lanes]
     for first in range(seg_len, short_ref.shape[0], modes):
         piece = left.astype(short_ref.dtype)
-        short_ref[first : first + modes, spot] = piece
+        short_ref[first : first + modes, :] = piece
         left = left - piece.astype(jnp.float32)
 
 
@@ -245,17 +251,14 @@
         carry(q_ref, local_ref, rates_ref[:, lane_slice(part)], base_ref, extra_ref, out_ref, part, part)
 
 
-def across_kernel(extra_ref, base_ref, q_ref, local_ref, out_ref):
+def across_kernel(part, extra_ref, base_ref, q_ref, local_ref, out_ref):
     modes = base_ref.shape[0]
     seg_len = q_ref.shape[0]
-    pieces = [
+    rates = sum(
         local_ref[first : first + modes, :].astype(jnp.float32)
-        for first in range(seg_len, local_ref.shape[0], modes)
-    ]
-    rates = (pieces[2] + pieces[1]) + pieces[0]
-    for part in range(q_ref.shape[1] // LANES):
-        lanes = lane_slice(part)
-        carry(q_ref, local_ref.at[:, lanes], rates[:, lanes], base_ref, extra_ref, out_ref, part, part)
+        for first in reversed(range(seg_len, local_ref.shape[0], modes))
+    )
+    carry(q_ref, local_ref, rates, base_ref, extra_ref, out_ref, part, 0)
 
 
 def project(blocks, weight_ref):
@@ -271,22 +274,23 @@
     return total
 
 
-def near_kernel(weight_ref, bias_ref, own_ref, pair_ref, *rest):
-    across, out_ref = rest[:-1], rest[-1]
+def near_kernel(weight_ref, bias_ref, own_ref, *rest):
+    blocks, out_ref = rest[:-1], rest[-1]
+    parts = len(blocks) // 2
     rank = lax.axis_index("chan")
-    blocks = [(rank, [own_ref]), (rank ^ 1, [pair_ref]), (rank ^ 2, across)]
+    blocks = [(rank, [own_ref]), (rank ^ 2, blocks[:parts]), (rank ^ 3, blocks[parts:])]
     out_ref[...] = project(blocks, weight_ref) + bias_ref[...]
 
 
 def last_kernel(near_ref, weight_ref, *rest):
-    diagonal, (out_hbm, out_ref, sems) = rest[:-3], rest[-3:]
+    pair, (out_hbm, out_ref, sems) = rest[:-3], rest[-3:]
     rank = lax.axis_index("chan")
     pieces = sems.shape[0]
     size = out_ref.shape[0] // pieces
     copies = []
     for i in range(pieces):
         rows = pl.ds(i * size, size)
-        total = near_ref[rows, :] + project([(rank ^ 3, [ref.at[rows, :] for ref in diagonal])], weight_ref)
+        total = near_ref[rows, :] + project([(rank ^ 1, [ref.at[rows, :] for ref in pair])], weight_ref)
         out_ref[rows, :] = total.astype(out_ref.dtype)
         copies.append(pltpu.make_async_copy(out_ref.at[rows], out_hbm.at[rows], sems.at[i]))
         copies[-1].start()
@@ -369,33 +373,45 @@
     skip = pltpu.with_memory_space_constraint(skip.reshape(1, -1), pltpu.HBM)
     inputs = (zero, k_gate, value, decay, residue, skip)
     scratch = [pltpu.VMEM((modes, SUBLANES, LANES), jnp.float32), pltpu.SemaphoreType.DMA]
-    total, *state = call(
-        state_kernel,
-        [few, struct(chunks), struct(gated), struct(bypass), thin, struct((tall, LANES), jnp.bfloat16)],
-        *inputs,
-        scratch=scratch, hbm=(5,),
-    )
-    own_total, local_short, *local = call(
-        local_kernel,
-        [few, struct((tall, channels), jnp.bfloat16), *[thin] * parts],
-        *inputs, total, *state,
-        scratch=[pltpu.VMEM(shape, jnp.float32) for shape in (chunks, gated, bypass)] + scratch, hbm=(5,),
-    )
-    local_across = swapped(local_short, 2)
+    thin_short = struct((tall, LANES), jnp.bfloat16)
+    kept = [struct(chunks), struct(gated), struct(bypass)]
+    total, *state = call(state_kernel, [few, *kept, thin, thin_short], *inputs, scratch=scratch, hbm=(5,))
+    own_total, *last_state = call(
+        first_part_kernel, [few, *kept, thin, thin_short], *inputs, total, *state, scratch=scratch, hbm=(5,)
+    )
+    local, short = [last_state[3]], [last_state[4]]
+    for part in range(1, parts):
+        more = call(
+            functools.partial(other_part_kernel, part), [thin, thin_short],
+            decay, residue, *state[:3], *last_state[:3],
+            scratch=scratch[:1], cost=MORE_COST,
+        )
+        local.append(more[0])
+        short.append(more[1])
+    local_across = [swapped(block, 2) for block in short]
     base, extra, q_across = carry_shares(total, own_total, decay, residue, seg_len, q_across)
-    extra_beside = beside(extra)
     extra_corner = corner(extra, 1, 2)
     base_across = swapped(base, 2)
+    half = struct((seg_len, LANES), jnp.bfloat16)
+    across = []
+    for part in range(parts):
+        block = call(
+            functools.partial(across_kernel, part), half,
+            extra_corner, base_across, q_across, local_across[part],
+            cost=PART_COST,
+        )
+        block, extra_corner = lax.optimization_barrier((block, extra_corner))
+        across.append(block)
+    diagonal = [swapped(block, 1) for block in across]
+    extra_beside, *across = lax.optimization_barrier((beside(extra), *across))
     whole = struct((seg_len, channels), jnp.bfloat16)
     own = call(own_kernel, whole, q_gate, decay, base, extra_beside, *local, cost=OWN_COST)
     pair = swapped(own, 1)
-    across = call(
-        across_kernel, whole, extra_corner, base_across, q_across, local_across, cost=PART_COST
-    )
-    diagonal = swapped(across, 1)
-    near = call(near_kernel, struct((seg_len, cols)), out_weight, bias, own, pair, across)
+    near = call(
+        near_kernel, struct((seg_len, cols)), out_weight, bias, own, *across, *diagonal, cost=NEAR_COST
+    )
     return call(
-        last_kernel, struct((seg_len, cols), jnp.bfloat16), near, out_weight, diagonal,
+        last_kernel, struct((seg_len, cols), jnp.bfloat16), near, out_weight, pair,
         scratch=[pltpu.VMEM((seg_len, cols), jnp.bfloat16), pltpu.SemaphoreType.DMA((STORES,))],
         outs=pltpu.HBM,
     )

time: 21.6 us -> 22.4 us (1.037)
  starting transfers between devices: 11.4 us -> 13.1 us
  waiting for transfers between devices: 3.58 us -> 2.61 us
    ppermute x5 -> x7, starting transfers between devices: 5.28 us -> 7.02 us  [swapped(): return lax.ppermute(value, 'chan', [(r, r ^ bit) for r in range(count)])]
    ppermute x3, waiting for transfers between devices: 1.07 us -> 0.01 us  [along(): return lax.ppermute(value, 'seq', [(r, target(r)) for r in range(count)])]
    ppermute x1, starting transfers between devices: 1.56 us -> 0.51 us  [beside(): return lax.ppermute(value, 'seq', [(r, r ^ 1) for r in range(count)])]
    ppermute x1, starting transfers between devices: 0.91 us -> 1.94 us  [corner(): return lax.ppermute(value, ('seq', 'chan'), pairs)]
    ppermute x5 -> x7, waiting for transfers between devices: 0.72 us -> 1.34 us  [swapped(): return lax.ppermute(value, 'chan', [(r, r ^ bit) for r in range(count)])]
    ppermute x1, waiting for transfers between devices: 1.54 us -> 1.25 us  [corner(): return lax.ppermute(value, ('seq', 'chan'), pairs)]
    ppermute x1, waiting for transfers between devices: 0.25 us -> 0.01 us  [beside(): return lax.ppermute(value, 'seq', [(r, r ^ 1) for r in range(count)])]
    pallas_call x8 -> x10, Pallas kernels: 5.8 us -> 5.85 us  [call(): pl.pallas_call(kernel, out_shape=out, in_specs=[pl.BlockSpec(memory_space...]
  transfers between devices with their start and end apart: 10 -> 12, of which waited for: 6 -> 4; matrix products, arithmetic and copies ran while one was open for 0% -> 0% of each run, Pallas kernels for 23% -> 22%
where the time goes in v9:
time: 22.4 us; the launch traced here: 22.2 us
  starting transfers between devices  13.1 us (58%)
  Pallas kernels  5.85 us (26%)
  waiting for transfers between devices  2.61 us (12%)
  local copies, waits for them, and re-layouts  0.51 us (2%)
    ppermute x7, starting transfers between devices, swapped(): return lax.ppermute(value, 'chan', [(r, r ^ bit) for r in range(count)])  7.02 us
    pallas_call x10, Pallas kernels, call(): pl.pallas_call(kernel, out_shape=out, in_specs=[pl.BlockSpec(memory_space...  5.85 us
    ppermute x3, starting transfers between devices, along(): return lax.ppermute(value, 'seq', [(r, target(r)) for r in range(count)])  3.65 us
    ppermute x1, starting transfers between devices, corner(): return lax.ppermute(value, ('seq', 'chan'), pairs)  1.94 us
    ppermute x7, waiting for transfers between devices, swapped(): return lax.ppermute(value, 'chan', [(r, r ^ bit) for r in range(count)])  1.34 us
    ppermute x1, waiting for transfers between devices, corner(): return lax.ppermute(value, ('seq', 'chan'), pairs)  1.25 us
    ppermute x1, starting transfers between devices, beside(): return lax.ppermute(value, 'seq', [(r, r ^ 1) for r in range(count)])  0.51 us
    unnamed x14, local copies, waits for them, and re-layouts  0.51 us
  transfers between devices with their start and end apart: 12, of which 4 were waited for; matrix products, arithmetic and copies ran while one was open for 0% of the time, Pallas kernels for 22%

profile of v9, /device:TPU:0, one launch (start us, length us, event | category | flops | bytes accessed | tf_op | source)
XLA Modules:
  0.0 22.2 jit_solution(1941255925871879832)
XLA Ops:
  0.0 0.0 copy-start.1
  0.0 0.0 copy-start.4
  0.0 0.0 copy-start.3
  0.0 0.0 copy-start
  0.0 3.0 %collective-permute-start.3 = (bf16[512,256]{1,0:T(8,128)(2,1)}, bf16[512,256]{1,0:T(8,128)(2,1)S(1)}, u32[]{:S(2)}, u32[]{:S(2)}) collective-permute-start(bf16[512,256]{1,0:T(8,128)(2,1)} %q_ref.1), channel_id=1, source_target_pairs={{0,2},{1,3},{2,0},{3,1},{4,6},{5,7},{6,4},{7,5},{8,10},{9,11},{10,... | collective-permute-start | bytes 786440 | tf_op jit(solution)/shard_map/ppermute | solution.py:319
  3.1 0.0 copy-done.1
  3.1 0.0 copy-done.4
  3.1 0.0 copy-done.3
  3.1 0.0 copy-done
  3.1 2.0 %shard_map.83 = (f32[16,256]{1,0:T(8,128)S(1)}, f32[16,8,256]{2,1,0:T(8,128)S(1)}, f32[2,512,128]{2,1,0:T(8,128)S(1)}, f32[1,256]{1,0:T(1,128)S(1)}, f32[512,128...) custom-call(f32[8,128]{1,0:T(8,128)S(1)} %shard_map.82.zero_ref, bf16[512,256]{1,0:T(8,128)(2,1)S(1)} %copy-done, ...), custom_call_target="tpu_custom_call" | custom-call | tf_op jit(solution)/shard_map/pallas_call | solution.py:302
  5.0 1.7 %collective-permute-start = (f32[16,256]{1,0:T(8,128)S(1)}, f32[16,256]{1,0:T(8,128)S(1)}, u32[]{:S(2)}, u32[]{:S(2)}) collective-permute-start(f32[16,256]{1,0:T(8,128)S(1)} %get-tuple-element.31.total_in.total_ref), channel_id=1, source_target_pairs={{0,24},{4,28},{8,16},{12,20},{16,0},{20,4},{24,8},{28,12},{1,25},{... | collective-permute-start | bytes 49160 | tf_op jit(solution)/shard_map/ppermute | solution.py:334
  6.8 1.2 %collective-permute-start.1 = (f32[16,256]{1,0:T(8,128)S(1)}, f32[16,256]{1,0:T(8,128)S(1)}, u32[]{:S(2)}, u32[]{:S(2)}) collective-permute-start(f32[16,256]{1,0:T(8,128)S(1)} %get-tuple-element.31.total_in.total_ref), channel_id=1, source_target_pairs={{0,16},{4,20},{8,24},{12,28},{16,0},{20,4},{24,8},{28,12},{1,17},{... | collective-permute-start | bytes 49160 | tf_op jit(solution)/shard_map/ppermute | solution.py:334
  8.0 0.7 %collective-permute-start.2 = (f32[16,256]{1,0:T(8,128)S(1)}, f32[16,256]{1,0:T(8,128)S(1)}, u32[]{:S(2)}, u32[]{:S(2)}) collective-permute-start(f32[16,256]{1,0:T(8,128)S(1)} %get-tuple-element.31.total_in.total_ref), channel_id=1, source_target_pairs={{0,8},{4,12},{8,0},{12,4},{16,24},{20,28},{24,16},{28,20},{1,9},{5... | collective-permute-start | bytes 49160 | tf_op jit(solution)/shard_map/ppermute | solution.py:334
  8.7 1.0 %collective-permute-start.7 = (bf16[544,128]{1,0:T(8,128)(2,1)S(1)}, bf16[544,128]{1,0:T(8,128)(2,1)S(1)}, u32[]{:S(2)}, u32[]{:S(2)}) collective-permute-start(bf16[544,128]{1,0:T(8,128)(2,1)S(1)} %get-tuple-element.44), channel_id=1, source_target_pairs={{0,2},{1,3},{2,0},{3,1},{4,6},{5,7},{6,4},{7,5},{8,10},{9,11},{10,... | collective-permute-start | bytes 417800 | tf_op jit(solution)/shard_map/ppermute | solution.py:319
  9.7 0.9 %shard_map.87 = (f32[512,128]{1,0:T(8,128)S(1)}, bf16[544,128]{1,0:T(8,128)(2,1)S(1)}) custom-call(f32[16,256]{1,0:T(8,128)S(1)} %copy-done.4, f32[16,256]{1,0:T(8,128)S(1)} %copy-done.3, f32[16,8,256]{2,1,0:T(8,128)S(1)} %get-tuple-element.32.chunk_in, f32[2,512,128]{2,1,0:T(8,128)S(1)} %get-tuple-element.33.gated_in, ...), custom_call_target="tpu_custom_call" | custom-call | flops 1000000000 | tf_op jit(solution)/shard_map/pallas_call | solution.py:302
  10.6 0.0 collective-permute-done.rest_0_
  10.7 1.1 %collective-permute-start.8 = (bf16[544,128]{1,0:T(8,128)(2,1)S(1)}, bf16[544,128]{1,0:T(8,128)(2,1)S(1)}, u32[]{:S(2)}, u32[]{:S(2)}) collective-permute-start(bf16[544,128]{1,0:T(8,128)(2,1)S(1)} %get-tuple-element.50), channel_id=1, source_target_pairs={{0,2},{1,3},{2,0},{3,1},{4,6},{5,7},{6,4},{7,5},{8,10},{9,11},{10,... | collective-permute-start | bytes 417800 | tf_op jit(solution)/shard_map/ppermute | solution.py:319
  11.8 0.0 collective-permute-done.1.rest_1_
  11.8 0.0 collective-permute-done.2.rest_2_
  11.8 0.0 collective-permute-done.3.q_ref
  11.8 0.1 shard_map.85
  11.9 1.9 %collective-permute-start.5 = (f32[16,256]{1,0:T(8,128)S(1)}, f32[16,256]{1,0:T(8,128)S(1)}, u32[]{:S(2)}, u32[]{:S(2)}) collective-permute-start(f32[16,256]{1,0:T(8,128)S(1)} %get-tuple-element.42), channel_id=1, source_target_pairs={{0,6},{1,7},{2,4},{3,5},{4,2},{5,3},{6,0},{7,1},{8,14},{9,15},{10,... | collective-permute-start | bytes 49160 | tf_op jit(solution)/shard_map/ppermute | solution.py:340
  13.8 1.1 %collective-permute-start.6 = (f32[16,256]{1,0:T(8,128)S(1)}, f32[16,256]{1,0:T(8,128)S(1)}, u32[]{:S(2)}, u32[]{:S(2)}) collective-permute-start(f32[16,256]{1,0:T(8,128)S(1)} %get-tuple-element.41.base_ref), channel_id=1, source_target_pairs={{0,2},{1,3},{2,0},{3,1},{4,6},{5,7},{6,4},{7,5},{8,10},{9,11},{10,... | collective-permute-start | bytes 49160 | tf_op jit(solution)/shard_map/ppermute | solution.py:319
  14.9 0.5 %collective-permute-start.4 = (f32[16,256]{1,0:T(8,128)S(1)}, f32[16,256]{1,0:T(8,128)S(1)}, u32[]{:S(2)}, u32[]{:S(2)}) collective-permute-start(f32[16,256]{1,0:T(8,128)S(1)} %get-tuple-element.42), channel_id=1, source_target_pairs={{0,4},{4,0},{8,12},{12,8},{16,20},{20,16},{24,28},{28,24},{1,5},{5... | collective-permute-start | bytes 49160 | tf_op jit(solution)/shard_map/ppermute | solution.py:324
  15.4 0.0 collective-permute-done.7.local_ref
  15.4 1.3 %collective-permute-done.5.extra_ref = f32[16,256]{1,0:T(8,128)S(1)} collective-permute-done((f32[16,256]{1,0:T(8,128)S(1)}, f32[16,256]{1,0:T(8,128)S(1)}, u32[]{:S(2)}, u32[]{:S(2)}) %collective-permute-start.5) | collective-permute-done | bytes 16416 | tf_op jit(solution)/shard_map/ppermute | solution.py:340
  16.7 0.9 %collective-permute-done.6.base_ref = f32[16,256]{1,0:T(8,128)S(1)} collective-permute-done((f32[16,256]{1,0:T(8,128)S(1)}, f32[16,256]{1,0:T(8,128)S(1)}, u32[]{:S(2)}, u32[]{:S(2)}) %collective-permute-start.6) | collective-permute-done | bytes 16416 | tf_op jit(solution)/shard_map/ppermute | solution.py:319
  17.6 0.4 %shard_map.86.rest_0_ = bf16[512,128]{1,0:T(8,128)(2,1)S(1)} custom-call(f32[16,256]{1,0:T(8,128)S(1)} %collective-permute-done.5.extra_ref, f32[16,256]{1,0:T(8,128)S(1)} %collective-permute-done.6.base_ref, bf16[512,256]{1,0:T(8,128)(2,1)S(1)} %collective-permute-done.3.q_ref, bf16[544,128]{1,0:T(8,128)(2,1)S(1)} %collective-permute-done.7.local_ref), custom_call_target="tpu_custom_call" | custom-call | flops 1000000000 | tf_op jit(solution)/shard_map/pallas_call | solution.py:302
  17.9 0.0 copy-start.5
  17.9 0.0 collective-permute-done.8.local_ref
  17.9 0.4 %shard_map.88.rest_1_ = bf16[512,128]{1,0:T(8,128)(2,1)S(1)} custom-call(f32[16,256]{1,0:T(8,128)S(1)} %collective-permute-done.5.extra_ref, f32[16,256]{1,0:T(8,128)S(1)} %collective-permute-done.6.base_ref, bf16[512,256]{1,0:T(8,128)(2,1)S(1)} %collective-permute-done.3.q_ref, bf16[544,128]{1,0:T(8,128)(2,1)S(1)} %collective-permute-done.8.local_ref), custom_call_target="tpu_custom_call" | custom-call | flops 1000000000 | tf_op jit(solution)/shard_map/pallas_call | solution.py:302
  18.3 0.1 collective-permute-start.10
  18.4 0.5 %collective-permute-start.9 = (bf16[512,128]{1,0:T(8,128)(2,1)S(1)}, bf16[512,128]{1,0:T(8,128)(2,1)S(1)}, u32[]{:S(2)}, u32[]{:S(2)}) collective-permute-start(bf16[512,128]{1,0:T(8,128)(2,1)S(1)} %shard_map.86.rest_0_), channel_id=1, source_target_pairs={{0,1},{1,0},{2,3},{3,2},{4,5},{5,4},{6,7},{7,6},{8,9},{9,8},{10,11... | collective-permute-start | bytes 393224 | tf_op jit(solution)/shard_map/ppermute | solution.py:319
  18.9 0.0 collective-permute-done.4.extra_ref
  18.9 0.0 copy-done.5
  18.9 0.0 copy-start.2
  18.9 0.8 %shard_map.89.own_ref = bf16[512,256]{1,0:T(8,128)(2,1)S(1)} custom-call(bf16[512,256]{1,0:T(8,128)(2,1)S(1)} %copy-done.5, f32[16,256]{1,0:T(8,128)S(1)} %copy-done.4, f32[16,256]{1,0:T(8,128)S(1)} %get-tuple-element.41.base_ref, f32[16,256]{1,0:T(8,128)S(1)} %collective-permute-done.4.extra_ref, f32[512,128]{1,0:T(8,128)S(1)} %get-tuple-element.53.rest_0_, ...), custom_call_target="tpu_custom_call" | custom-call | flops 3000000000 | tf_op jit(solution)/shard_map/pallas_call | solution.py:302
  19.7 0.0 copy-start.6
  19.7 0.1 collective-permute-start.11
  19.8 0.0 collective-permute-done.10.rest_3_
  19.8 0.1 collective-permute-done.9.rest_2_
  19.9 0.0 copy-done.2
  19.9 0.5 %copy-done.6 = f32[256]{0:T(256)S(1)} copy-done((f32[256]{0:T(256)S(1)}, f32[256]{0:T(256)}, u32[]{:S(2)}) %copy-start.6) | copy-done | bytes 1048
  20.4 0.5 %shard_map.90.near_ref = f32[512,256]{1,0:T(8,128)S(1)} custom-call(bf16[1024,256]{1,0:T(8,128)(2,1)S(1)} %copy-done.2, f32[1,256]{1,0:T(1,128)S(1)} %bitcast.2, bf16[512,256]{1,0:T(8,128)(2,1)S(1)} %shard_map.89.own_ref, bf16[512,128]{1,0:T(8,128)(2,1)S(1)} %shard_map.86.rest_0_, bf16[512,128]{1,0:T(8,128)(2,1)S(1)} %shard_map.88.rest_1_, ...), custom_call_target="tpu_custom_call" | custom-call | flops 3000000000 | tf_op jit(solution)/shard_map/pallas_call | solution.py:302
  20.9 0.4 %collective-permute-done.11.rest_0_ = bf16[512,256]{1,0:T(8,128)(2,1)S(1)} collective-permute-done((bf16[512,256]{1,0:T(8,128)(2,1)S(1)}, bf16[512,256]{1,0:T(8,128)(2,1)S(1)}, u32[]{:S(2)}, u32[]{:S(2)}) %collective-permute-start.11) | collective-permute-done | bytes 262176 | tf_op jit(solution)/shard_map/ppermute | solution.py:319
  21.3 0.9 %shard_map.91 = bf16[512,256]{1,0:T(8,128)(2,1)} custom-call(f32[512,256]{1,0:T(8,128)S(1)} %shard_map.90.near_ref, bf16[1024,256]{1,0:T(8,128)(2,1)S(1)} %copy-done.2, bf16[512,256]{1,0:T(8,128)(2,1)S(1)} %collective-permute-done.11.rest_0_), custom_call_target="tpu_custom_call" | custom-call | tf_op jit(solution)/shard_map/pallas_call | solution.py:302
  (2 shorter events, 0.0 us)
Async XLA Ops:
  0.0 3.1 %copy-start.1 = (bf16[512,256]{1,0:T(8,128)(2,1)S(1)}, bf16[512,256]{1,0:T(8,128)(2,1)}, u32[]{:S(2)}) copy-start(bf16[512,256]{1,0:T(8,128)(2,1)} %v_ref.3) | copy-start | bytes 786436
  0.0 3.1 %copy-start.4 = (f32[16,256]{1,0:T(8,128)S(1)}, f32[16,256]{1,0:T(8,128)}, u32[]{:S(2)}) copy-start(f32[16,256]{1,0:T(8,128)} %rates_ref.3) | copy-start | bytes 49156
  0.0 3.1 %copy-start.3 = (f32[16,256]{1,0:T(8,128)S(1)}, f32[16,256]{1,0:T(8,128)}, u32[]{:S(2)}) copy-start(f32[16,256]{1,0:T(8,128)} %residue_ref.7) | copy-start | bytes 49156
  0.0 3.1 %copy-start = (bf16[512,256]{1,0:T(8,128)(2,1)S(1)}, bf16[512,256]{1,0:T(8,128)(2,1)}, u32[]{:S(2)}) copy-start(bf16[512,256]{1,0:T(8,128)(2,1)} %k_ref.3) | copy-start | bytes 786436
  0.0 11.8 %collective-permute-start.3 = (bf16[512,256]{1,0:T(8,128)(2,1)}, bf16[512,256]{1,0:T(8,128)(2,1)S(1)}, u32[]{:S(2)}, u32[]{:S(2)}) collective-permute-start(bf16[512,256]{1,0:T(8,128)(2,1)} %q_ref.1), channel_id=1, source_target_pairs={{0,2},{1,3},{2,0},{3,1},{4,6},{5,7},{6,4},{7,5},{8,10},{9,11},{10,... | collective-permute-start | bytes 786440 | tf_op jit(solution)/shard_map/ppermute | solution.py:319
  5.0 5.6 %collective-permute-start = (f32[16,256]{1,0:T(8,128)S(1)}, f32[16,256]{1,0:T(8,128)S(1)}, u32[]{:S(2)}, u32[]{:S(2)}) collective-permute-start(f32[16,256]{1,0:T(8,128)S(1)} %get-tuple-element.31.total_in.total_ref), channel_id=1, source_target_pairs={{0,24},{4,28},{8,16},{12,20},{16,0},{20,4},{24,8},{28,12},{1,25},{... | collective-permute-start | bytes 49160 | tf_op jit(solution)/shard_map/ppermute | solution.py:334
  6.8 5.0 %collective-permute-start.1 = (f32[16,256]{1,0:T(8,128)S(1)}, f32[16,256]{1,0:T(8,128)S(1)}, u32[]{:S(2)}, u32[]{:S(2)}) collective-permute-start(f32[16,256]{1,0:T(8,128)S(1)} %get-tuple-element.31.total_in.total_ref), channel_id=1, source_target_pairs={{0,16},{4,20},{8,24},{12,28},{16,0},{20,4},{24,8},{28,12},{1,17},{... | collective-permute-start | bytes 49160 | tf_op jit(solution)/shard_map/ppermute | solution.py:334
  8.0 3.8 %collective-permute-start.2 = (f32[16,256]{1,0:T(8,128)S(1)}, f32[16,256]{1,0:T(8,128)S(1)}, u32[]{:S(2)}, u32[]{:S(2)}) collective-permute-start(f32[16,256]{1,0:T(8,128)S(1)} %get-tuple-element.31.total_in.total_ref), channel_id=1, source_target_pairs={{0,8},{4,12},{8,0},{12,4},{16,24},{20,28},{24,16},{28,20},{1,9},{5... | collective-permute-start | bytes 49160 | tf_op jit(solution)/shard_map/ppermute | solution.py:334
  8.7 6.7 %collective-permute-start.7 = (bf16[544,128]{1,0:T(8,128)(2,1)S(1)}, bf16[544,128]{1,0:T(8,128)(2,1)S(1)}, u32[]{:S(2)}, u32[]{:S(2)}) collective-permute-start(bf16[544,128]{1,0:T(8,128)(2,1)S(1)} %get-tuple-element.44), channel_id=1, source_target_pairs={{0,2},{1,3},{2,0},{3,1},{4,6},{5,7},{6,4},{7,5},{8,10},{9,11},{10,... | collective-permute-start | bytes 417800 | tf_op jit(solution)/shard_map/ppermute | solution.py:319
  10.7 7.3 %collective-permute-start.8 = (bf16[544,128]{1,0:T(8,128)(2,1)S(1)}, bf16[544,128]{1,0:T(8,128)(2,1)S(1)}, u32[]{:S(2)}, u32[]{:S(2)}) collective-permute-start(bf16[544,128]{1,0:T(8,128)(2,1)S(1)} %get-tuple-element.50), channel_id=1, source_target_pairs={{0,2},{1,3},{2,0},{3,1},{4,6},{5,7},{6,4},{7,5},{8,10},{9,11},{10,... | collective-permute-start | bytes 417800 | tf_op jit(solution)/shard_map/ppermute | solution.py:319
  11.9 4.8 %collective-permute-start.5 = (f32[16,256]{1,0:T(8,128)S(1)}, f32[16,256]{1,0:T(8,128)S(1)}, u32[]{:S(2)}, u32[]{:S(2)}) collective-permute-start(f32[16,256]{1,0:T(8,128)S(1)} %get-tuple-element.42), channel_id=1, source_target_pairs={{0,6},{1,7},{2,4},{3,5},{4,2},{5,3},{6,0},{7,1},{8,14},{9,15},{10,... | collective-permute-start | bytes 49160 | tf_op jit(solution)/shard_map/ppermute | solution.py:340
  13.8 3.7 %collective-permute-start.6 = (f32[16,256]{1,0:T(8,128)S(1)}, f32[16,256]{1,0:T(8,128)S(1)}, u32[]{:S(2)}, u32[]{:S(2)}) collective-permute-start(f32[16,256]{1,0:T(8,128)S(1)} %get-tuple-element.41.base_ref), channel_id=1, source_target_pairs={{0,2},{1,3},{2,0},{3,1},{4,6},{5,7},{6,4},{7,5},{8,10},{9,11},{10,... | collective-permute-start | bytes 49160 | tf_op jit(solution)/shard_map/ppermute | solution.py:319
  14.9 4.0 %collective-permute-start.4 = (f32[16,256]{1,0:T(8,128)S(1)}, f32[16,256]{1,0:T(8,128)S(1)}, u32[]{:S(2)}, u32[]{:S(2)}) collective-permute-start(f32[16,256]{1,0:T(8,128)S(1)} %get-tuple-element.42), channel_id=1, source_target_pairs={{0,4},{4,0},{8,12},{12,8},{16,20},{20,16},{24,28},{28,24},{1,5},{5... | collective-permute-start | bytes 49160 | tf_op jit(solution)/shard_map/ppermute | solution.py:324
  17.9 1.0 %copy-start.5 = (bf16[512,256]{1,0:T(8,128)(2,1)S(1)}, bf16[512,256]{1,0:T(8,128)(2,1)}, u32[]{:S(2)}) copy-start(bf16[512,256]{1,0:T(8,128)(2,1)} %q_ref.1) | copy-start | bytes 786436
  18.3 1.5 %collective-permute-start.10 = (bf16[512,128]{1,0:T(8,128)(2,1)S(1)}, bf16[512,128]{1,0:T(8,128)(2,1)S(1)}, u32[]{:S(2)}, u32[]{:S(2)}) collective-permute-start(bf16[512,128]{1,0:T(8,128)(2,1)S(1)} %shard_map.88.rest_1_), channel_id=1, source_target_pairs={{0,1},{1,0},{2,3},{3,2},{4,5},{5,4},{6,7},{7,6},{8,9},{9,8},{10,11... | collective-permute-start | bytes 393224 | tf_op jit(solution)/shard_map/ppermute | solution.py:319
  18.4 1.5 %collective-permute-start.9 = (bf16[512,128]{1,0:T(8,128)(2,1)S(1)}, bf16[512,128]{1,0:T(8,128)(2,1)S(1)}, u32[]{:S(2)}, u32[]{:S(2)}) collective-permute-start(bf16[512,128]{1,0:T(8,128)(2,1)S(1)} %shard_map.86.rest_0_), channel_id=1, source_target_pairs={{0,1},{1,0},{2,3},{3,2},{4,5},{5,4},{6,7},{7,6},{8,9},{9,8},{10,11... | collective-permute-start | bytes 393224 | tf_op jit(solution)/shard_map/ppermute | solution.py:319
  18.9 1.0 %copy-start.2 = (bf16[1024,256]{1,0:T(8,128)(2,1)S(1)}, bf16[1024,256]{1,0:T(8,128)(2,1)}, u32[]{:S(2)}) copy-start(bf16[1024,256]{1,0:T(8,128)(2,1)} %weight_ref.3) | copy-start | bytes 1572868
  19.7 0.7 %copy-start.6 = (f32[256]{0:T(256)S(1)}, f32[256]{0:T(256)}, u32[]{:S(2)}) copy-start(f32[256]{0:T(256)} %param.15) | copy-start | bytes 3076
  19.7 1.6 %collective-permute-start.11 = (bf16[512,256]{1,0:T(8,128)(2,1)S(1)}, bf16[512,256]{1,0:T(8,128)(2,1)S(1)}, u32[]{:S(2)}, u32[]{:S(2)}) collective-permute-start(bf16[512,256]{1,0:T(8,128)(2,1)S(1)} %shard_map.89.own_ref), channel_id=1, source_target_pairs={{0,1},{1,0},{2,3},{3,2},{4,5},{5,4},{6,7},{7,6},{8,9},{9,8},{10,11... | collective-permute-start | bytes 786440 | tf_op jit(solution)/shard_map/ppermute | solution.py:319

commit v10 on v9

--- a/solution.py
+++ b/solution.py
@@ -10,14 +10,13 @@
 LANES = 128
 SUBLANES = 8
 STORES = 4
-OWN_COST = 3000000000
-FOLD_COST = 500000000
+OWN_COST = 1000000000
+FOLD_COST = 700000000
 PIECES = 2
 ROUTES = {2: [(1, 0)], 4: [(3, 2, 0, 1), (2, 3, 0, 1), (1, 0, 3, 2)]}
 MORE_COST = 1000000000
 FIRST_COST = 30000000000
-NEAR_COST = 3000000000
-PART_COST = 1000000000
+PART_COST = 0
 VMEM_LIMIT = 32 * 1024 * 1024
 
 
@@ -251,14 +250,16 @@
         carry(q_ref, local_ref, rates_ref[:, lane_slice(part)], base_ref, extra_ref, out_ref, part, part)
 
 
-def across_kernel(part, extra_ref, base_ref, q_ref, local_ref, out_ref):
+def across_kernel(extra_ref, base_ref, q_ref, *rest):
+    blocks, out_ref = rest[:-1], rest[-1]
     modes = base_ref.shape[0]
     seg_len = q_ref.shape[0]
-    rates = sum(
-        local_ref[first : first + modes, :].astype(jnp.float32)
-        for first in reversed(range(seg_len, local_ref.shape[0], modes))
-    )
-    carry(q_ref, local_ref, rates, base_ref, extra_ref, out_ref, part, 0)
+    for part, local_ref in enumerate(blocks):
+        rates = sum(
+            local_ref[first : first + modes, :].astype(jnp.float32)
+            for first in reversed(range(seg_len, local_ref.shape[0], modes))
+        )
+        carry(q_ref, local_ref, rates, base_ref, extra_ref, out_ref, part, part)
 
 
 def project(blocks, weight_ref):
@@ -274,23 +275,22 @@
     return total
 
 
-def near_kernel(weight_ref, bias_ref, own_ref, *rest):
-    blocks, out_ref = rest[:-1], rest[-1]
-    parts = len(blocks) // 2
+def near_kernel(weight_ref, bias_ref, own_ref, pair_ref, *rest):
+    across, out_ref = rest[:-1], rest[-1]
     rank = lax.axis_index("chan")
-    blocks = [(rank, [own_ref]), (rank ^ 2, blocks[:parts]), (rank ^ 3, blocks[parts:])]
+    blocks = [(rank, [own_ref]), (rank ^ 1, [pair_ref]), (rank ^ 2, across)]
     out_ref[...] = project(blocks, weight_ref) + bias_ref[...]
 
 
 def last_kernel(near_ref, weight_ref, *rest):
-    pair, (out_hbm, out_ref, sems) = rest[:-3], rest[-3:]
+    diagonal, (out_hbm, out_ref, sems) = rest[:-3], rest[-3:]
     rank = lax.axis_index("chan")
     pieces = sems.shape[0]
     size = out_ref.shape[0] // pieces
     copies = []
     for i in range(pieces):
         rows = pl.ds(i * size, size)
-        total = near_ref[rows, :] + project([(rank ^ 1, [ref.at[rows, :] for ref in pair])], weight_ref)
+        total = near_ref[rows, :] + project([(rank ^ 3, [ref.at[rows, :] for ref in diagonal])], weight_ref)
         out_ref[rows, :] = total.astype(out_ref.dtype)
         copies.append(pltpu.make_async_copy(out_ref.at[rows], out_hbm.at[rows], sems.at[i]))
         copies[-1].start()
@@ -390,28 +390,19 @@
         short.append(more[1])
     local_across = [swapped(block, 2) for block in short]
     base, extra, q_across = carry_shares(total, own_total, decay, residue, seg_len, q_across)
+    extra_beside, local_across[0] = lax.optimization_barrier((beside(extra), local_across[0]))
     extra_corner = corner(extra, 1, 2)
     base_across = swapped(base, 2)
-    half = struct((seg_len, LANES), jnp.bfloat16)
-    across = []
-    for part in range(parts):
-        block = call(
-            functools.partial(across_kernel, part), half,
-            extra_corner, base_across, q_across, local_across[part],
-            cost=PART_COST,
-        )
-        block, extra_corner = lax.optimization_barrier((block, extra_corner))
-        across.append(block)
-    diagonal = [swapped(block, 1) for block in across]
-    extra_beside, *across = lax.optimization_barrier((beside(extra), *across))
     whole = struct((seg_len, channels), jnp.bfloat16)
     own = call(own_kernel, whole, q_gate, decay, base, extra_beside, *local, cost=OWN_COST)
     pair = swapped(own, 1)
-    near = call(
-        near_kernel, struct((seg_len, cols)), out_weight, bias, own, *across, *diagonal, cost=NEAR_COST
+    across = call(
+        across_kernel, whole, extra_corner, base_across, q_across, *local_across, cost=PART_COST
     )
+    diagonal = swapped(across, 1)
+    near = call(near_kernel, struct((seg_len, cols)), out_weight, bias, own, pair, across)
     return call(
-        last_kernel, struct((seg_len, cols), jnp.bfloat16), near, out_weight, pair,
+        last_kernel, struct((seg_len, cols), jnp.bfloat16), near, out_weight, diagonal,
         scratch=[pltpu.VMEM((seg_len, cols), jnp.bfloat16), pltpu.SemaphoreType.DMA((STORES,))],
         outs=pltpu.HBM,
     )

time: 22.4 us -> 21.7 us (0.969)
  starting transfers between devices: 13.1 us -> 12.5 us
    ppermute x1, starting transfers between devices: 0.51 us -> 1.56 us  [beside(): return lax.ppermute(value, 'seq', [(r, r ^ 1) for r in range(count)])]
    ppermute x1, starting transfers between devices: 1.94 us -> 0.91 us  [corner(): return lax.ppermute(value, ('seq', 'chan'), pairs)]
    ppermute x7 -> x6, starting transfers between devices: 7.02 us -> 6.42 us  [swapped(): return lax.ppermute(value, 'chan', [(r, r ^ bit) for r in range(count)])]
    ppermute x7 -> x6, waiting for transfers between devices: 1.34 us -> 1 us  [swapped(): return lax.ppermute(value, 'chan', [(r, r ^ bit) for r in range(count)])]
    ppermute x1, waiting for transfers between devices: 0.01 us -> 0.25 us  [beside(): return lax.ppermute(value, 'seq', [(r, r ^ 1) for r in range(count)])]
    pallas_call x10 -> x9, Pallas kernels: 5.85 us -> 5.82 us  [call(): pl.pallas_call(kernel, out_shape=out, in_specs=[pl.BlockSpec(memory_space...]
  transfers between devices with their start and end apart: 12 -> 11, of which waited for: 4 -> 5; matrix products, arithmetic and copies ran while one was open for 0% -> 0% of each run, Pallas kernels for 22% -> 23%
where the time goes in v10:
time: 21.7 us; the launch traced here: 21.6 us
  starting transfers between devices  12.5 us (58%)
  Pallas kernels  5.82 us (27%)
  waiting for transfers between devices  2.49 us (11%)
  local copies, waits for them, and re-layouts  0.6 us (3%)
    ppermute x6, starting transfers between devices, swapped(): return lax.ppermute(value, 'chan', [(r, r ^ bit) for r in range(count)])  6.42 us
    pallas_call x9, Pallas kernels, call(): pl.pallas_call(kernel, out_shape=out, in_specs=[pl.BlockSpec(memory_space...  5.82 us
    ppermute x3, starting transfers between devices, along(): return lax.ppermute(value, 'seq', [(r, target(r)) for r in range(count)])  3.65 us
    ppermute x1, starting transfers between devices, beside(): return lax.ppermute(value, 'seq', [(r, r ^ 1) for r in range(count)])  1.56 us
    ppermute x1, waiting for transfers between devices, corner(): return lax.ppermute(value, ('seq', 'chan'), pairs)  1.24 us
    ppermute x6, waiting for transfers between devices, swapped(): return lax.ppermute(value, 'chan', [(r, r ^ bit) for r in range(count)])  1 us
    ppermute x1, starting transfers between devices, corner(): return lax.ppermute(value, ('seq', 'chan'), pairs)  0.91 us
    unnamed x14, local copies, waits for them, and re-layouts  0.6 us
  transfers between devices with their start and end apart: 11, of which 5 were waited for; matrix products, arithmetic and copies ran while one was open for 0% of the time, Pallas kernels for 23%

profile of v10, /device:TPU:0, one launch (start us, length us, event | category | flops | bytes accessed | tf_op | source)
XLA Modules:
  0.0 21.6 jit_solution(8382424760947372332)
XLA Ops:
  0.0 0.0 copy-start.2
  0.0 0.0 copy-start.4
  0.0 0.0 copy-start.3
  0.0 0.0 copy-start.1
  0.0 3.0 %collective-permute-start.3 = (bf16[512,256]{1,0:T(8,128)(2,1)}, bf16[512,256]{1,0:T(8,128)(2,1)S(1)}, u32[]{:S(2)}, u32[]{:S(2)}) collective-permute-start(bf16[512,256]{1,0:T(8,128)(2,1)} %q_ref.1), channel_id=1, source_target_pairs={{0,2},{1,3},{2,0},{3,1},{4,6},{5,7},{6,4},{7,5},{8,10},{9,11},{10,... | collective-permute-start | bytes 786440 | tf_op jit(solution)/shard_map/ppermute | solution.py:319
  3.1 0.0 copy-done.2
  3.1 0.0 copy-done.4
  3.1 0.0 copy-done.3
  3.1 0.0 copy-done.1
  3.1 2.0 %shard_map.83 = (f32[16,256]{1,0:T(8,128)S(1)}, f32[16,8,256]{2,1,0:T(8,128)S(1)}, f32[2,512,128]{2,1,0:T(8,128)S(1)}, f32[1,256]{1,0:T(1,128)S(1)}, f32[512,128...) custom-call(f32[8,128]{1,0:T(8,128)S(1)} %shard_map.82.zero_ref, bf16[512,256]{1,0:T(8,128)(2,1)S(1)} %copy-done.1, ...), custom_call_target="tpu_custom_call" | custom-call | tf_op jit(solution)/shard_map/pallas_call | solution.py:302
  5.0 1.7 %collective-permute-start = (f32[16,256]{1,0:T(8,128)S(1)}, f32[16,256]{1,0:T(8,128)S(1)}, u32[]{:S(2)}, u32[]{:S(2)}) collective-permute-start(f32[16,256]{1,0:T(8,128)S(1)} %get-tuple-element.27.total_in.total_ref), channel_id=1, source_target_pairs={{0,24},{4,28},{8,16},{12,20},{16,0},{20,4},{24,8},{28,12},{1,25},{... | collective-permute-start | bytes 49160 | tf_op jit(solution)/shard_map/ppermute | solution.py:334
  6.8 1.2 %collective-permute-start.1 = (f32[16,256]{1,0:T(8,128)S(1)}, f32[16,256]{1,0:T(8,128)S(1)}, u32[]{:S(2)}, u32[]{:S(2)}) collective-permute-start(f32[16,256]{1,0:T(8,128)S(1)} %get-tuple-element.27.total_in.total_ref), channel_id=1, source_target_pairs={{0,16},{4,20},{8,24},{12,28},{16,0},{20,4},{24,8},{28,12},{1,17},{... | collective-permute-start | bytes 49160 | tf_op jit(solution)/shard_map/ppermute | solution.py:334
  8.0 0.7 %collective-permute-start.2 = (f32[16,256]{1,0:T(8,128)S(1)}, f32[16,256]{1,0:T(8,128)S(1)}, u32[]{:S(2)}, u32[]{:S(2)}) collective-permute-start(f32[16,256]{1,0:T(8,128)S(1)} %get-tuple-element.27.total_in.total_ref), channel_id=1, source_target_pairs={{0,8},{4,12},{8,0},{12,4},{16,24},{20,28},{24,16},{28,20},{1,9},{5... | collective-permute-start | bytes 49160 | tf_op jit(solution)/shard_map/ppermute | solution.py:334
  8.7 1.0 %collective-permute-start.5 = (bf16[544,128]{1,0:T(8,128)(2,1)S(1)}, bf16[544,128]{1,0:T(8,128)(2,1)S(1)}, u32[]{:S(2)}, u32[]{:S(2)}) collective-permute-start(bf16[544,128]{1,0:T(8,128)(2,1)S(1)} %get-tuple-element.39), channel_id=1, source_target_pairs={{0,2},{1,3},{2,0},{3,1},{4,6},{5,7},{6,4},{7,5},{8,10},{9,11},{10,... | collective-permute-start | bytes 417800 | tf_op jit(solution)/shard_map/ppermute | solution.py:319
  9.7 0.9 %shard_map.86 = (f32[512,128]{1,0:T(8,128)S(1)}, bf16[544,128]{1,0:T(8,128)(2,1)S(1)}) custom-call(f32[16,256]{1,0:T(8,128)S(1)} %copy-done.4, f32[16,256]{1,0:T(8,128)S(1)} %copy-done.3, f32[16,8,256]{2,1,0:T(8,128)S(1)} %get-tuple-element.28.chunk_in, f32[2,512,128]{2,1,0:T(8,128)S(1)} %get-tuple-element.29.gated_in, ...), custom_call_target="tpu_custom_call" | custom-call | flops 1000000000 | tf_op jit(solution)/shard_map/pallas_call | solution.py:302
  10.6 0.0 collective-permute-done.rest_0_
  10.7 1.1 %collective-permute-start.9 = (bf16[544,128]{1,0:T(8,128)(2,1)S(1)}, bf16[544,128]{1,0:T(8,128)(2,1)S(1)}, u32[]{:S(2)}, u32[]{:S(2)}) collective-permute-start(bf16[544,128]{1,0:T(8,128)(2,1)S(1)} %get-tuple-element.48), channel_id=1, source_target_pairs={{0,2},{1,3},{2,0},{3,1},{4,6},{5,7},{6,4},{7,5},{8,10},{9,11},{10,... | collective-permute-start | bytes 417800 | tf_op jit(solution)/shard_map/ppermute | solution.py:319
  11.8 0.0 collective-permute-done.1.rest_1_
  11.8 0.0 collective-permute-done.2.rest_2_
  11.8 0.0 collective-permute-done.3.q_ref
  11.8 0.0 copy-start.6
  11.8 0.1 shard_map.85
  11.9 1.6 %collective-permute-start.4 = (f32[16,256]{1,0:T(8,128)S(1)}, f32[16,256]{1,0:T(8,128)S(1)}, u32[]{:S(2)}, u32[]{:S(2)}) collective-permute-start(f32[16,256]{1,0:T(8,128)S(1)} %get-tuple-element.38), channel_id=1, source_target_pairs={{0,4},{4,0},{8,12},{12,8},{16,20},{20,16},{24,28},{28,24},{1,5},{5... | collective-permute-start | bytes 49160 | tf_op jit(solution)/shard_map/ppermute | solution.py:324
  13.4 0.9 %collective-permute-start.7 = (f32[16,256]{1,0:T(8,128)S(1)}, f32[16,256]{1,0:T(8,128)S(1)}, u32[]{:S(2)}, u32[]{:S(2)}) collective-permute-start(f32[16,256]{1,0:T(8,128)S(1)} %get-tuple-element.38), channel_id=1, source_target_pairs={{0,6},{1,7},{2,4},{3,5},{4,2},{5,3},{6,0},{7,1},{8,14},{9,15},{10,... | collective-permute-start | bytes 49160 | tf_op jit(solution)/shard_map/ppermute | solution.py:340
  14.4 1.1 %collective-permute-start.8 = (f32[16,256]{1,0:T(8,128)S(1)}, f32[16,256]{1,0:T(8,128)S(1)}, u32[]{:S(2)}, u32[]{:S(2)}) collective-permute-start(f32[16,256]{1,0:T(8,128)S(1)} %get-tuple-element.37.base_ref), channel_id=1, source_target_pairs={{0,2},{1,3},{2,0},{3,1},{4,6},{5,7},{6,4},{7,5},{8,10},{9,11},{10,... | collective-permute-start | bytes 49160 | tf_op jit(solution)/shard_map/ppermute | solution.py:319
  15.4 0.0 collective-permute-done.5.rest_0_
  15.4 0.2 %collective-permute-done.4.extra_ref = f32[16,256]{1,0:T(8,128)S(1)} collective-permute-done((f32[16,256]{1,0:T(8,128)S(1)}, f32[16,256]{1,0:T(8,128)S(1)}, u32[]{:S(2)}, u32[]{:S(2)}) %collective-permute-start.4) | collective-permute-done | bytes 16416 | tf_op jit(solution)/shard_map/ppermute | solution.py:324
  15.7 0.0 copy-done.6
  15.7 0.8 %shard_map.87.own_ref = bf16[512,256]{1,0:T(8,128)(2,1)S(1)} custom-call(bf16[512,256]{1,0:T(8,128)(2,1)S(1)} %copy-done.6, f32[16,256]{1,0:T(8,128)S(1)} %copy-done.4, f32[16,256]{1,0:T(8,128)S(1)} %get-tuple-element.37.base_ref, f32[16,256]{1,0:T(8,128)S(1)} %collective-permute-done.4.extra_ref, f32[512,128]{1,0:T(8,128)S(1)} %get-tuple-element.41.rest_0_, ...), custom_call_target="tpu_custom_call" | custom-call | flops 1000000000 | tf_op jit(solution)/shard_map/pallas_call | solution.py:302
  16.5 0.0 copy-start
  16.5 0.1 collective-permute-start.6
  16.6 0.3 %collective-permute-done.9.rest_1_ = bf16[544,128]{1,0:T(8,128)(2,1)S(1)} collective-permute-done((bf16[544,128]{1,0:T(8,128)(2,1)S(1)}, bf16[544,128]{1,0:T(8,128)(2,1)S(1)}, u32[]{:S(2)}, u32[]{:S(2)}) %collective-permute-start.9) | collective-permute-done | bytes 139296 | tf_op jit(solution)/shard_map/ppermute | solution.py:319
  16.9 1.2 %collective-permute-done.7.extra_ref = f32[16,256]{1,0:T(8,128)S(1)} collective-permute-done((f32[16,256]{1,0:T(8,128)S(1)}, f32[16,256]{1,0:T(8,128)S(1)}, u32[]{:S(2)}, u32[]{:S(2)}) %collective-permute-start.7) | collective-permute-done | bytes 16416 | tf_op jit(solution)/shard_map/ppermute | solution.py:340
  18.1 0.2 collective-permute-done.8.base_ref
  18.3 0.8 %shard_map.88.rest_0_ = bf16[512,256]{1,0:T(8,128)(2,1)S(1)} custom-call(f32[16,256]{1,0:T(8,128)S(1)} %collective-permute-done.7.extra_ref, f32[16,256]{1,0:T(8,128)S(1)} %collective-permute-done.8.base_ref, bf16[512,256]{1,0:T(8,128)(2,1)S(1)} %collective-permute-done.3.q_ref, bf16[544,128]{1,0:T(8,128)(2,1)S(1)} %collective-permute-done.5.rest_0_, ...), custom_call_target="tpu_custom_call" | custom-call | tf_op jit(solution)/shard_map/pallas_call | solution.py:302
  19.0 0.0 copy-start.5
  19.1 0.1 collective-permute-start.10
  19.1 0.0 collective-permute-done.6.pair_ref
  19.1 0.0 copy-done
  19.2 0.6 %copy-done.5 = f32[256]{0:T(256)S(1)} copy-done((f32[256]{0:T(256)S(1)}, f32[256]{0:T(256)}, u32[]{:S(2)}) %copy-start.5) | copy-done | bytes 1048
  19.7 0.4 %shard_map.89.near_ref = f32[512,256]{1,0:T(8,128)S(1)} custom-call(bf16[1024,256]{1,0:T(8,128)(2,1)S(1)} %copy-done, f32[1,256]{1,0:T(1,128)S(1)} %bitcast.2, bf16[512,256]{1,0:T(8,128)(2,1)S(1)} %shard_map.87.own_ref, bf16[512,256]{1,0:T(8,128)(2,1)S(1)} %collective-permute-done.6.pair_ref, bf16[512,256]{1,0:T(8,128)(2,1)S(1)} %shard_map.88.rest_0_), custom_call_target="tpu_custom_call" | custom-call | tf_op jit(solution)/shard_map/pallas_call | solution.py:302
  20.1 0.5 %collective-permute-done.10.rest_0_ = bf16[512,256]{1,0:T(8,128)(2,1)S(1)} collective-permute-done((bf16[512,256]{1,0:T(8,128)(2,1)S(1)}, bf16[512,256]{1,0:T(8,128)(2,1)S(1)}, u32[]{:S(2)}, u32[]{:S(2)}) %collective-permute-start.10) | collective-permute-done | bytes 262176 | tf_op jit(solution)/shard_map/ppermute | solution.py:319
  20.7 0.9 %shard_map.90 = bf16[512,256]{1,0:T(8,128)(2,1)} custom-call(f32[512,256]{1,0:T(8,128)S(1)} %shard_map.89.near_ref, bf16[1024,256]{1,0:T(8,128)(2,1)S(1)} %copy-done, bf16[512,256]{1,0:T(8,128)(2,1)S(1)} %collective-permute-done.10.rest_0_), custom_call_target="tpu_custom_call" | custom-call | tf_op jit(solution)/shard_map/pallas_call | solution.py:302
  (2 shorter events, 0.0 us)
Async XLA Ops:
  0.0 3.1 %copy-start.2 = (bf16[512,256]{1,0:T(8,128)(2,1)S(1)}, bf16[512,256]{1,0:T(8,128)(2,1)}, u32[]{:S(2)}) copy-start(bf16[512,256]{1,0:T(8,128)(2,1)} %v_ref.3) | copy-start | bytes 786436
  0.0 3.1 %copy-start.4 = (f32[16,256]{1,0:T(8,128)S(1)}, f32[16,256]{1,0:T(8,128)}, u32[]{:S(2)}) copy-start(f32[16,256]{1,0:T(8,128)} %rates_ref.3) | copy-start | bytes 49156
  0.0 3.1 %copy-start.3 = (f32[16,256]{1,0:T(8,128)S(1)}, f32[16,256]{1,0:T(8,128)}, u32[]{:S(2)}) copy-start(f32[16,256]{1,0:T(8,128)} %residue_ref.7) | copy-start | bytes 49156
  0.0 3.1 %copy-start.1 = (bf16[512,256]{1,0:T(8,128)(2,1)S(1)}, bf16[512,256]{1,0:T(8,128)(2,1)}, u32[]{:S(2)}) copy-start(bf16[512,256]{1,0:T(8,128)(2,1)} %k_ref.3) | copy-start | bytes 786436
  0.0 11.8 %collective-permute-start.3 = (bf16[512,256]{1,0:T(8,128)(2,1)}, bf16[512,256]{1,0:T(8,128)(2,1)S(1)}, u32[]{:S(2)}, u32[]{:S(2)}) collective-permute-start(bf16[512,256]{1,0:T(8,128)(2,1)} %q_ref.1), channel_id=1, source_target_pairs={{0,2},{1,3},{2,0},{3,1},{4,6},{5,7},{6,4},{7,5},{8,10},{9,11},{10,... | collective-permute-start | bytes 786440 | tf_op jit(solution)/shard_map/ppermute | solution.py:319
  5.0 5.6 %collective-permute-start = (f32[16,256]{1,0:T(8,128)S(1)}, f32[16,256]{1,0:T(8,128)S(1)}, u32[]{:S(2)}, u32[]{:S(2)}) collective-permute-start(f32[16,256]{1,0:T(8,128)S(1)} %get-tuple-element.27.total_in.total_ref), channel_id=1, source_target_pairs={{0,24},{4,28},{8,16},{12,20},{16,0},{20,4},{24,8},{28,12},{1,25},{... | collective-permute-start | bytes 49160 | tf_op jit(solution)/shard_map/ppermute | solution.py:334
  6.8 5.0 %collective-permute-start.1 = (f32[16,256]{1,0:T(8,128)S(1)}, f32[16,256]{1,0:T(8,128)S(1)}, u32[]{:S(2)}, u32[]{:S(2)}) collective-permute-start(f32[16,256]{1,0:T(8,128)S(1)} %get-tuple-element.27.total_in.total_ref), channel_id=1, source_target_pairs={{0,16},{4,20},{8,24},{12,28},{16,0},{20,4},{24,8},{28,12},{1,17},{... | collective-permute-start | bytes 49160 | tf_op jit(solution)/shard_map/ppermute | solution.py:334
  8.0 3.8 %collective-permute-start.2 = (f32[16,256]{1,0:T(8,128)S(1)}, f32[16,256]{1,0:T(8,128)S(1)}, u32[]{:S(2)}, u32[]{:S(2)}) collective-permute-start(f32[16,256]{1,0:T(8,128)S(1)} %get-tuple-element.27.total_in.total_ref), channel_id=1, source_target_pairs={{0,8},{4,12},{8,0},{12,4},{16,24},{20,28},{24,16},{28,20},{1,9},{5... | collective-permute-start | bytes 49160 | tf_op jit(solution)/shard_map/ppermute | solution.py:334
  8.7 6.7 %collective-permute-start.5 = (bf16[544,128]{1,0:T(8,128)(2,1)S(1)}, bf16[544,128]{1,0:T(8,128)(2,1)S(1)}, u32[]{:S(2)}, u32[]{:S(2)}) collective-permute-start(bf16[544,128]{1,0:T(8,128)(2,1)S(1)} %get-tuple-element.39), channel_id=1, source_target_pairs={{0,2},{1,3},{2,0},{3,1},{4,6},{5,7},{6,4},{7,5},{8,10},{9,11},{10,... | collective-permute-start | bytes 417800 | tf_op jit(solution)/shard_map/ppermute | solution.py:319
  10.7 6.2 %collective-permute-start.9 = (bf16[544,128]{1,0:T(8,128)(2,1)S(1)}, bf16[544,128]{1,0:T(8,128)(2,1)S(1)}, u32[]{:S(2)}, u32[]{:S(2)}) collective-permute-start(bf16[544,128]{1,0:T(8,128)(2,1)S(1)} %get-tuple-element.48), channel_id=1, source_target_pairs={{0,2},{1,3},{2,0},{3,1},{4,6},{5,7},{6,4},{7,5},{8,10},{9,11},{10,... | collective-permute-start | bytes 417800 | tf_op jit(solution)/shard_map/ppermute | solution.py:319
  11.8 3.9 %copy-start.6 = (bf16[512,256]{1,0:T(8,128)(2,1)S(1)}, bf16[512,256]{1,0:T(8,128)(2,1)}, u32[]{:S(2)}) copy-start(bf16[512,256]{1,0:T(8,128)(2,1)} %q_ref.1) | copy-start | bytes 786436
  11.9 3.8 %collective-permute-start.4 = (f32[16,256]{1,0:T(8,128)S(1)}, f32[16,256]{1,0:T(8,128)S(1)}, u32[]{:S(2)}, u32[]{:S(2)}) collective-permute-start(f32[16,256]{1,0:T(8,128)S(1)} %get-tuple-element.38), channel_id=1, source_target_pairs={{0,4},{4,0},{8,12},{12,8},{16,20},{20,16},{24,28},{28,24},{1,5},{5... | collective-permute-start | bytes 49160 | tf_op jit(solution)/shard_map/ppermute | solution.py:324
  13.4 4.7 %collective-permute-start.7 = (f32[16,256]{1,0:T(8,128)S(1)}, f32[16,256]{1,0:T(8,128)S(1)}, u32[]{:S(2)}, u32[]{:S(2)}) collective-permute-start(f32[16,256]{1,0:T(8,128)S(1)} %get-tuple-element.38), channel_id=1, source_target_pairs={{0,6},{1,7},{2,4},{3,5},{4,2},{5,3},{6,0},{7,1},{8,14},{9,15},{10,... | collective-permute-start | bytes 49160 | tf_op jit(solution)/shard_map/ppermute | solution.py:340
  14.4 3.9 %collective-permute-start.8 = (f32[16,256]{1,0:T(8,128)S(1)}, f32[16,256]{1,0:T(8,128)S(1)}, u32[]{:S(2)}, u32[]{:S(2)}) collective-permute-start(f32[16,256]{1,0:T(8,128)S(1)} %get-tuple-element.37.base_ref), channel_id=1, source_target_pairs={{0,2},{1,3},{2,0},{3,1},{4,6},{5,7},{6,4},{7,5},{8,10},{9,11},{10,... | collective-permute-start | bytes 49160 | tf_op jit(solution)/shard_map/ppermute | solution.py:319
  16.5 2.7 %copy-start = (bf16[1024,256]{1,0:T(8,128)(2,1)S(1)}, bf16[1024,256]{1,0:T(8,128)(2,1)}, u32[]{:S(2)}) copy-start(bf16[1024,256]{1,0:T(8,128)(2,1)} %weight_ref.3) | copy-start | bytes 1572868
  16.5 2.6 %collective-permute-start.6 = (bf16[512,256]{1,0:T(8,128)(2,1)S(1)}, bf16[512,256]{1,0:T(8,128)(2,1)S(1)}, u32[]{:S(2)}, u32[]{:S(2)}) collective-permute-start(bf16[512,256]{1,0:T(8,128)(2,1)S(1)} %shard_map.87.own_ref), channel_id=1, source_target_pairs={{0,1},{1,0},{2,3},{3,2},{4,5},{5,4},{6,7},{7,6},{8,9},{9,8},{10,11... | collective-permute-start | bytes 786440 | tf_op jit(solution)/shard_map/ppermute | solution.py:319
  19.0 0.7 %copy-start.5 = (f32[256]{0:T(256)S(1)}, f32[256]{0:T(256)}, u32[]{:S(2)}) copy-start(f32[256]{0:T(256)} %param.15) | copy-start | bytes 3076
  19.1 1.6 %collective-permute-start.10 = (bf16[512,256]{1,0:T(8,128)(2,1)S(1)}, bf16[512,256]{1,0:T(8,128)(2,1)S(1)}, u32[]{:S(2)}, u32[]{:S(2)}) collective-permute-start(bf16[512,256]{1,0:T(8,128)(2,1)S(1)} %shard_map.88.rest_0_), channel_id=1, source_target_pairs={{0,1},{1,0},{2,3},{3,2},{4,5},{5,4},{6,7},{7,6},{8,9},{9,8},{10,11... | collective-permute-start | bytes 786440 | tf_op jit(solution)/shard_map/ppermute | solution.py:319

commit v11 on v8

--- a/solution.py
+++ b/solution.py
@@ -15,7 +15,8 @@
 PIECES = 3
 ROUTES = {2: [(1, 0)], 4: [(3, 2, 0, 1), (2, 3, 0, 1), (1, 0, 3, 2)]}
 FIRST_COST = 30000000000
-PART_COST = 0
+PART_COST = 1500000000
+NEAR_COST = 0
 VMEM_LIMIT = 32 * 1024 * 1024
 
 
@@ -209,11 +210,10 @@
     extra_ref[...] = jnp.where(even, residue_ref[...] * own_ref[...] + step * step * before, before)
 
 
-def carry(q_ref, local_ref, rates, base_ref, extra_ref, out_ref, part, column):
+def carry(q_ref, local_ref, rates, base_ref, extra_ref, out_ref, part, first_row=0):
     modes = rates.shape[0]
-    seg_len = q_ref.shape[0]
     block = 2 * SUBLANES
-    ahead = (lax.broadcasted_iota(jnp.int32, (SUBLANES, LANES), 0) + 1).astype(jnp.float32)
+    ahead = (lax.broadcasted_iota(jnp.int32, (SUBLANES, LANES), 0) + 1 + first_row).astype(jnp.float32)
     lanes = lane_slice(part)
     factor, start = [], []
     for n in range(modes):
@@ -223,7 +223,7 @@
         factor.append(full(jnp.exp(-rate * SUBLANES)))
 
     def step(j, state):
-        rows = pl.ds(pl.multiple_of(j * block, block), block)
+        rows = pl.ds(pl.multiple_of(j * block + first_row, block), block)
         halves = []
         for _ in range(2):
             sums = list(state[:4])
@@ -233,19 +233,20 @@
             state = tuple(f * h for f, h in zip(factor, state))
         total = local_ref[rows, :].astype(jnp.float32) + jnp.concatenate(halves, axis=0)
         gate_rows = q_ref[rows, lanes].astype(jnp.float32)
-        out_ref[rows, lane_slice(column)] = (gate_rows * total).astype(out_ref.dtype)
+        out_rows = pl.ds(pl.multiple_of(j * block, block), block)
+        out_ref[out_rows, lanes] = (gate_rows * total).astype(out_ref.dtype)
         return state
 
-    lax.fori_loop(0, seg_len // block, step, tuple(start), unroll=4)
+    lax.fori_loop(0, out_ref.shape[0] // block, step, tuple(start), unroll=4)
 
 
 def own_kernel(q_ref, rates_ref, base_ref, extra_ref, *rest):
     locals_in, out_ref = rest[:-1], rest[-1]
     for part, local_ref in enumerate(locals_in):
-        carry(q_ref, local_ref, rates_ref[:, lane_slice(part)], base_ref, extra_ref, out_ref, part, part)
-
-
-def across_kernel(extra_ref, base_ref, q_ref, local_ref, out_ref):
+        carry(q_ref, local_ref, rates_ref[:, lane_slice(part)], base_ref, extra_ref, out_ref, part)
+
+
+def across_kernel(first_row, extra_ref, base_ref, q_ref, local_ref, out_ref):
     modes = base_ref.shape[0]
     seg_len = q_ref.shape[0]
     pieces = [
@@ -255,7 +256,7 @@
     rates = (pieces[2] + pieces[1]) + pieces[0]
     for part in range(q_ref.shape[1] // LANES):
         lanes = lane_slice(part)
-        carry(q_ref, local_ref.at[:, lanes], rates[:, lanes], base_ref, extra_ref, out_ref, part, part)
+        carry(q_ref, local_ref.at[:, lanes], rates[:, lanes], base_ref, extra_ref, out_ref, part, first_row)
 
 
 def project(blocks, weight_ref):
@@ -274,19 +275,23 @@
 def near_kernel(weight_ref, bias_ref, own_ref, pair_ref, *rest):
     across, out_ref = rest[:-1], rest[-1]
     rank = lax.axis_index("chan")
-    blocks = [(rank, [own_ref]), (rank ^ 1, [pair_ref]), (rank ^ 2, across)]
-    out_ref[...] = project(blocks, weight_ref) + bias_ref[...]
+    first = 0
+    for across_ref in across:
+        rows = pl.ds(first, across_ref.shape[0])
+        blocks = [(rank, [own_ref.at[rows, :]]), (rank ^ 1, [pair_ref.at[rows, :]]), (rank ^ 2, [across_ref])]
+        out_ref[rows, :] = project(blocks, weight_ref) + bias_ref[...]
+        first += across_ref.shape[0]
 
 
 def last_kernel(near_ref, weight_ref, *rest):
     diagonal, (out_hbm, out_ref, sems) = rest[:-3], rest[-3:]
     rank = lax.axis_index("chan")
-    pieces = sems.shape[0]
-    size = out_ref.shape[0] // pieces
+    size = out_ref.shape[0] // sems.shape[0]
+    cuts = [ref.at[pl.ds(first, size), :] for ref in diagonal for first in range(0, ref.shape[0], size)]
     copies = []
-    for i in range(pieces):
+    for i, cut in enumerate(cuts):
         rows = pl.ds(i * size, size)
-        total = near_ref[rows, :] + project([(rank ^ 3, [ref.at[rows, :] for ref in diagonal])], weight_ref)
+        total = near_ref[rows, :] + project([(rank ^ 3, [cut])], weight_ref)
         out_ref[rows, :] = total.astype(out_ref.dtype)
         copies.append(pltpu.make_async_copy(out_ref.at[rows], out_hbm.at[rows], sems.at[i]))
         copies[-1].start()
@@ -389,13 +394,19 @@
     whole = struct((seg_len, channels), jnp.bfloat16)
     own = call(own_kernel, whole, q_gate, decay, base, extra_beside, *local, cost=OWN_COST)
     pair = swapped(own, 1)
-    across = call(
-        across_kernel, whole, extra_corner, base_across, q_across, local_across, cost=PART_COST
-    )
-    diagonal = swapped(across, 1)
-    near = call(near_kernel, struct((seg_len, cols)), out_weight, bias, own, pair, across)
+    early = seg_len - seg_len // STORES
+    across = [
+        call(
+            functools.partial(across_kernel, first), struct((count, channels), jnp.bfloat16),
+            extra_corner, base_across, q_across, local_across,
+            cost=PART_COST,
+        )
+        for first, count in ((0, early), (early, seg_len - early))
+    ]
+    diagonal = [swapped(block, 1) for block in across]
+    near = call(near_kernel, struct((seg_len, cols)), out_weight, bias, own, pair, *across, cost=NEAR_COST)
     return call(
-        last_kernel, struct((seg_len, cols), jnp.bfloat16), near, out_weight, diagonal,
+        last_kernel, struct((seg_len, cols), jnp.bfloat16), near, out_weight, *diagonal,
         scratch=[pltpu.VMEM((seg_len, cols), jnp.bfloat16), pltpu.SemaphoreType.DMA((STORES,))],
         outs=pltpu.HBM,
     )

time: 21.6 us -> 21.6 us (level)
  starting transfers between devices: 11.4 us -> 12 us
  local copies, waits for them, and re-layouts: 0.6 us -> 0.17 us
    ppermute x5 -> x6, starting transfers between devices: 5.28 us -> 5.84 us  [swapped(): return lax.ppermute(value, 'chan', [(r, r ^ bit) for r in range(count)])]
    unnamed x14, local copies, waits for them, and re-layouts: 0.6 us -> 0.17 us
    ppermute x5 -> x6, waiting for transfers between devices: 0.72 us -> 0.54 us  [swapped(): return lax.ppermute(value, 'chan', [(r, r ^ bit) for r in range(count)])]
    pallas_call x8 -> x9, Pallas kernels: 5.8 us -> 5.86 us  [call(): pl.pallas_call(kernel, out_shape=out, in_specs=[pl.BlockSpec(memory_space...]
  transfers between devices with their start and end apart: 10 -> 11, of which waited for: 6 -> 6; matrix products, arithmetic and copies ran while one was open for 0% -> 0% of each run, Pallas kernels for 23% -> 23%
where the time goes in v11:
time: 21.6 us; the launch traced here: 21.5 us
  starting transfers between devices  12 us (56%)
  Pallas kernels  5.86 us (27%)
  waiting for transfers between devices  3.41 us (16%)
    pallas_call x9, Pallas kernels, call(): pl.pallas_call(kernel, out_shape=out, in_specs=[pl.BlockSpec(memory_space...  5.86 us
    ppermute x6, starting transfers between devices, swapped(): return lax.ppermute(value, 'chan', [(r, r ^ bit) for r in range(count)])  5.84 us
    ppermute x3, starting transfers between devices, along(): return lax.ppermute(value, 'seq', [(r, target(r)) for r in range(count)])  3.65 us
    ppermute x1, starting transfers between devices, beside(): return lax.ppermute(value, 'seq', [(r, r ^ 1) for r in range(count)])  1.56 us
    ppermute x1, waiting for transfers between devices, corner(): return lax.ppermute(value, ('seq', 'chan'), pairs)  1.54 us
    ppermute x3, waiting for transfers between devices, along(): return lax.ppermute(value, 'seq', [(r, target(r)) for r in range(count)])  1.07 us
    ppermute x1, starting transfers between devices, corner(): return lax.ppermute(value, ('seq', 'chan'), pairs)  0.91 us
    ppermute x6, waiting for transfers between devices, swapped(): return lax.ppermute(value, 'chan', [(r, r ^ bit) for r in range(count)])  0.54 us
  transfers between devices with their start and end apart: 11, of which 6 were waited for; matrix products, arithmetic and copies ran while one was open for 0% of the time, Pallas kernels for 23%

profile of v11, /device:TPU:0, one launch (start us, length us, event | category | flops | bytes accessed | tf_op | source)
XLA Modules:
  0.0 21.5 jit_solution(9212125547568115075)
XLA Ops:
  0.0 0.0 copy-start.2
  0.0 0.0 copy-start.4
  0.0 0.0 copy-start.5
  0.0 0.0 copy-start.1
  0.0 3.0 %collective-permute-start.3 = (bf16[512,256]{1,0:T(8,128)(2,1)}, bf16[512,256]{1,0:T(8,128)(2,1)S(1)}, u32[]{:S(2)}, u32[]{:S(2)}) collective-permute-start(bf16[512,256]{1,0:T(8,128)(2,1)} %q_ref.1), channel_id=1, source_target_pairs={{0,2},{1,3},{2,0},{3,1},{4,6},{5,7},{6,4},{7,5},{8,10},{9,11},{10,... | collective-permute-start | bytes 786440 | tf_op jit(solution)/shard_map/ppermute | solution.py:320
  3.1 0.0 copy-done.2
  3.1 0.0 copy-done.4
  3.1 0.0 copy-done.5
  3.1 0.0 copy-done.1
  3.1 2.0 %shard_map.83 = (f32[16,256]{1,0:T(8,128)S(1)}, f32[16,8,256]{2,1,0:T(8,128)S(1)}, f32[2,512,128]{2,1,0:T(8,128)S(1)}, f32[1,256]{1,0:T(1,128)S(1)}, f32[512,128...) custom-call(f32[8,128]{1,0:T(8,128)S(1)} %shard_map.82.zero_ref, bf16[512,256]{1,0:T(8,128)(2,1)S(1)} %copy-done.1, ...), custom_call_target="tpu_custom_call" | custom-call | tf_op jit(solution)/shard_map/pallas_call | solution.py:303
  5.0 1.7 %collective-permute-start = (f32[16,256]{1,0:T(8,128)S(1)}, f32[16,256]{1,0:T(8,128)S(1)}, u32[]{:S(2)}, u32[]{:S(2)}) collective-permute-start(f32[16,256]{1,0:T(8,128)S(1)} %get-tuple-element.21.total_in.total_ref), channel_id=1, source_target_pairs={{0,24},{4,28},{8,16},{12,20},{16,0},{20,4},{24,8},{28,12},{1,25},{... | collective-permute-start | bytes 49160 | tf_op jit(solution)/shard_map/ppermute | solution.py:335
  6.8 1.2 %collective-permute-start.1 = (f32[16,256]{1,0:T(8,128)S(1)}, f32[16,256]{1,0:T(8,128)S(1)}, u32[]{:S(2)}, u32[]{:S(2)}) collective-permute-start(f32[16,256]{1,0:T(8,128)S(1)} %get-tuple-element.21.total_in.total_ref), channel_id=1, source_target_pairs={{0,16},{4,20},{8,24},{12,28},{16,0},{20,4},{24,8},{28,12},{1,17},{... | collective-permute-start | bytes 49160 | tf_op jit(solution)/shard_map/ppermute | solution.py:335
  8.0 0.7 %collective-permute-start.2 = (f32[16,256]{1,0:T(8,128)S(1)}, f32[16,256]{1,0:T(8,128)S(1)}, u32[]{:S(2)}, u32[]{:S(2)}) collective-permute-start(f32[16,256]{1,0:T(8,128)S(1)} %get-tuple-element.21.total_in.total_ref), channel_id=1, source_target_pairs={{0,8},{4,12},{8,0},{12,4},{16,24},{20,28},{24,16},{28,20},{1,9},{5... | collective-permute-start | bytes 49160 | tf_op jit(solution)/shard_map/ppermute | solution.py:335
  8.7 1.0 %shard_map.84 = (f32[16,256]{1,0:T(8,128)S(1)}, bf16[560,256]{1,0:T(8,128)(2,1)S(1)}, f32[512,128]{1,0:T(8,128)S(1)}, f32[512,128]{1,0:T(8,128)S(1)}) custom-call(f32[8,128]{1,0:T(8,128)S(1)} %shard_map.82.zero_ref, bf16[512,256]{1,0:T(8,128)(2,1)S(1)} %copy-done.1, bf16[512,256]{1,0:T(8,128)(2,1)S(1)} %copy-done.2, f32[16,256]{1,0:T(8,128)S(1)} %copy-done.4, ...), custom_call_target="tpu_custom_call" | custom-call | tf_op jit(solution)/shard_map/pallas_call | solution.py:303
  9.7 1.0 %collective-permute-start.8 = (bf16[560,256]{1,0:T(8,128)(2,1)S(1)}, bf16[560,256]{1,0:T(8,128)(2,1)S(1)}, u32[]{:S(2)}, u32[]{:S(2)}) collective-permute-start(bf16[560,256]{1,0:T(8,128)(2,1)S(1)} %get-tuple-element.36), channel_id=1, source_target_pairs={{0,2},{1,3},{2,0},{3,1},{4,6},{5,7},{6,4},{7,5},{8,10},{9,11},{10,... | collective-permute-start | bytes 860168 | tf_op jit(solution)/shard_map/ppermute | solution.py:320
  10.7 0.0 collective-permute-done.rest_0_
  10.7 0.9 %collective-permute-done.1.rest_1_ = f32[16,256]{1,0:T(8,128)S(1)} collective-permute-done((f32[16,256]{1,0:T(8,128)S(1)}, f32[16,256]{1,0:T(8,128)S(1)}, u32[]{:S(2)}, u32[]{:S(2)}) %collective-permute-start.1) | collective-permute-done | bytes 16416 | tf_op jit(solution)/shard_map/ppermute | solution.py:335
  11.6 0.2 collective-permute-done.2.rest_2_
  11.8 0.0 collective-permute-done.3.q_ref
  11.8 0.0 copy-start.3
  11.8 1.6 %collective-permute-start.4 = (f32[16,256]{1,0:T(8,128)S(1)}, f32[16,256]{1,0:T(8,128)S(1)}, u32[]{:S(2)}, u32[]{:S(2)}) collective-permute-start(f32[16,256]{1,0:T(8,128)S(1)} %get-tuple-element.32), channel_id=1, source_target_pairs={{0,4},{4,0},{8,12},{12,8},{16,20},{20,16},{24,28},{28,24},{1,5},{5... | collective-permute-start | bytes 49160 | tf_op jit(solution)/shard_map/ppermute | solution.py:325
  13.4 0.9 %collective-permute-start.6 = (f32[16,256]{1,0:T(8,128)S(1)}, f32[16,256]{1,0:T(8,128)S(1)}, u32[]{:S(2)}, u32[]{:S(2)}) collective-permute-start(f32[16,256]{1,0:T(8,128)S(1)} %get-tuple-element.32), channel_id=1, source_target_pairs={{0,6},{1,7},{2,4},{3,5},{4,2},{5,3},{6,0},{7,1},{8,14},{9,15},{10,... | collective-permute-start | bytes 49160 | tf_op jit(solution)/shard_map/ppermute | solution.py:341
  14.3 1.1 %collective-permute-start.7 = (f32[16,256]{1,0:T(8,128)S(1)}, f32[16,256]{1,0:T(8,128)S(1)}, u32[]{:S(2)}, u32[]{:S(2)}) collective-permute-start(f32[16,256]{1,0:T(8,128)S(1)} %get-tuple-element.31.base_ref), channel_id=1, source_target_pairs={{0,2},{1,3},{2,0},{3,1},{4,6},{5,7},{6,4},{7,5},{8,10},{9,11},{10,... | collective-permute-start | bytes 49160 | tf_op jit(solution)/shard_map/ppermute | solution.py:320
  15.4 0.2 %collective-permute-done.4.extra_ref = f32[16,256]{1,0:T(8,128)S(1)} collective-permute-done((f32[16,256]{1,0:T(8,128)S(1)}, f32[16,256]{1,0:T(8,128)S(1)}, u32[]{:S(2)}, u32[]{:S(2)}) %collective-permute-start.4) | collective-permute-done | bytes 16416 | tf_op jit(solution)/shard_map/ppermute | solution.py:325
  15.6 0.0 copy-done.3
  15.6 0.8 %shard_map.86.own_ref = bf16[512,256]{1,0:T(8,128)(2,1)S(1)} custom-call(bf16[512,256]{1,0:T(8,128)(2,1)S(1)} %copy-done.3, f32[16,256]{1,0:T(8,128)S(1)} %copy-done.4, f32[16,256]{1,0:T(8,128)S(1)} %get-tuple-element.31.base_ref, f32[16,256]{1,0:T(8,128)S(1)} %collective-permute-done.4.extra_ref, f32[512,128]{1,0:T(8,128)S(1)} %get-tuple-element.33.rest_0_, ...), custom_call_target="tpu_custom_call" | custom-call | tf_op jit(solution)/shard_map/pallas_call | solution.py:303
  16.4 0.1 collective-permute-start.5
  16.5 1.5 %collective-permute-done.6.extra_ref = f32[16,256]{1,0:T(8,128)S(1)} collective-permute-done((f32[16,256]{1,0:T(8,128)S(1)}, f32[16,256]{1,0:T(8,128)S(1)}, u32[]{:S(2)}, u32[]{:S(2)}) %collective-permute-start.6) | collective-permute-done | bytes 16416 | tf_op jit(solution)/shard_map/ppermute | solution.py:341
  18.0 0.2 collective-permute-done.7.base_ref
  18.2 0.0 collective-permute-done.8.local_ref
  18.2 0.6 %shard_map.87.rest_0_ = bf16[384,256]{1,0:T(8,128)(2,1)S(1)} custom-call(f32[16,256]{1,0:T(8,128)S(1)} %collective-permute-done.6.extra_ref, f32[16,256]{1,0:T(8,128)S(1)} %collective-permute-done.7.base_ref, bf16[512,256]{1,0:T(8,128)(2,1)S(1)} %collective-permute-done.3.q_ref, bf16[560,256]{1,0:T(8,128)(2,1)S(1)} %collective-permute-done.8.local_ref), custom_call_target="tpu_custom_call" | custom-call | flops 1500000000 | tf_op jit(solution)/shard_map/pallas_call | solution.py:303
  18.8 0.0 copy-start
  18.8 0.1 collective-permute-start.9
  18.9 0.2 %shard_map.88.rest_1_ = bf16[128,256]{1,0:T(8,128)(2,1)S(1)} custom-call(f32[16,256]{1,0:T(8,128)S(1)} %collective-permute-done.6.extra_ref, f32[16,256]{1,0:T(8,128)S(1)} %collective-permute-done.7.base_ref, bf16[512,256]{1,0:T(8,128)(2,1)S(1)} %collective-permute-done.3.q_ref, bf16[560,256]{1,0:T(8,128)(2,1)S(1)} %collective-permute-done.8.local_ref), custom_call_target="tpu_custom_call" | custom-call | flops 1500000000 | tf_op jit(solution)/shard_map/pallas_call | solution.py:303
  19.1 0.0 copy-start.6
  19.1 0.6 %collective-permute-start.10 = (bf16[128,256]{1,0:T(8,128)(2,1)S(1)}, bf16[128,256]{1,0:T(8,128)(2,1)S(1)}, u32[]{:S(2)}, u32[]{:S(2)}) collective-permute-start(bf16[128,256]{1,0:T(8,128)(2,1)S(1)} %shard_map.88.rest_1_), channel_id=1, source_target_pairs={{0,1},{1,0},{2,3},{3,2},{4,5},{5,4},{6,7},{7,6},{8,9},{9,8},{10,11... | collective-permute-start | bytes 196616 | tf_op jit(solution)/shard_map/ppermute | solution.py:320
  19.7 0.0 collective-permute-done.5.pair_ref
  19.7 0.1 copy-done
  19.8 0.0 copy-done.6
  19.8 0.4 %shard_map.89.near_ref = f32[512,256]{1,0:T(8,128)S(1)} custom-call(bf16[1024,256]{1,0:T(8,128)(2,1)S(1)} %copy-done, f32[1,256]{1,0:T(1,128)S(1)} %bitcast.2, bf16[512,256]{1,0:T(8,128)(2,1)S(1)} %shard_map.86.own_ref, bf16[512,256]{1,0:T(8,128)(2,1)S(1)} %collective-permute-done.5.pair_ref, bf16[384,256]{1,0:T(8,128)(2,1)S(1)} %shard_map.87.rest_0_, ...), custom_call_target="tpu_custom_call" | custom-call | tf_op jit(solution)/shard_map/pallas_call | solution.py:303
  20.2 0.4 %collective-permute-done.10.rest_1_ = bf16[128,256]{1,0:T(8,128)(2,1)S(1)} collective-permute-done((bf16[128,256]{1,0:T(8,128)(2,1)S(1)}, bf16[128,256]{1,0:T(8,128)(2,1)S(1)}, u32[]{:S(2)}, u32[]{:S(2)}) %collective-permute-start.10) | collective-permute-done | bytes 65568 | tf_op jit(solution)/shard_map/ppermute | solution.py:320
  20.6 0.0 collective-permute-done.9.rest_0_
  20.6 0.9 %shard_map.90 = bf16[512,256]{1,0:T(8,128)(2,1)} custom-call(f32[512,256]{1,0:T(8,128)S(1)} %shard_map.89.near_ref, bf16[1024,256]{1,0:T(8,128)(2,1)S(1)} %copy-done, bf16[384,256]{1,0:T(8,128)(2,1)S(1)} %collective-permute-done.9.rest_0_, bf16[128,256]{1,0:T(8,128)(2,1)S(1)} %collective-permute-done.10.rest_1_), custom_call_target="tpu_custom_call" | custom-call | tf_op jit(solution)/shard_map/pallas_call | solution.py:303
  (2 shorter events, 0.0 us)
Async XLA Ops:
  0.0 3.1 %copy-start.2 = (bf16[512,256]{1,0:T(8,128)(2,1)S(1)}, bf16[512,256]{1,0:T(8,128)(2,1)}, u32[]{:S(2)}) copy-start(bf16[512,256]{1,0:T(8,128)(2,1)} %v_ref.3) | copy-start | bytes 786436
  0.0 3.1 %copy-start.4 = (f32[16,256]{1,0:T(8,128)S(1)}, f32[16,256]{1,0:T(8,128)}, u32[]{:S(2)}) copy-start(f32[16,256]{1,0:T(8,128)} %rates_ref.3) | copy-start | bytes 49156
  0.0 3.1 %copy-start.5 = (f32[16,256]{1,0:T(8,128)S(1)}, f32[16,256]{1,0:T(8,128)}, u32[]{:S(2)}) copy-start(f32[16,256]{1,0:T(8,128)} %residue_ref.5) | copy-start | bytes 49156
  0.0 3.1 %copy-start.1 = (bf16[512,256]{1,0:T(8,128)(2,1)S(1)}, bf16[512,256]{1,0:T(8,128)(2,1)}, u32[]{:S(2)}) copy-start(bf16[512,256]{1,0:T(8,128)(2,1)} %k_ref.3) | copy-start | bytes 786436
  0.0 11.8 %collective-permute-start.3 = (bf16[512,256]{1,0:T(8,128)(2,1)}, bf16[512,256]{1,0:T(8,128)(2,1)S(1)}, u32[]{:S(2)}, u32[]{:S(2)}) collective-permute-start(bf16[512,256]{1,0:T(8,128)(2,1)} %q_ref.1), channel_id=1, source_target_pairs={{0,2},{1,3},{2,0},{3,1},{4,6},{5,7},{6,4},{7,5},{8,10},{9,11},{10,... | collective-permute-start | bytes 786440 | tf_op jit(solution)/shard_map/ppermute | solution.py:320
  5.0 5.7 %collective-permute-start = (f32[16,256]{1,0:T(8,128)S(1)}, f32[16,256]{1,0:T(8,128)S(1)}, u32[]{:S(2)}, u32[]{:S(2)}) collective-permute-start(f32[16,256]{1,0:T(8,128)S(1)} %get-tuple-element.21.total_in.total_ref), channel_id=1, source_target_pairs={{0,24},{4,28},{8,16},{12,20},{16,0},{20,4},{24,8},{28,12},{1,25},{... | collective-permute-start | bytes 49160 | tf_op jit(solution)/shard_map/ppermute | solution.py:335
  6.8 4.8 %collective-permute-start.1 = (f32[16,256]{1,0:T(8,128)S(1)}, f32[16,256]{1,0:T(8,128)S(1)}, u32[]{:S(2)}, u32[]{:S(2)}) collective-permute-start(f32[16,256]{1,0:T(8,128)S(1)} %get-tuple-element.21.total_in.total_ref), channel_id=1, source_target_pairs={{0,16},{4,20},{8,24},{12,28},{16,0},{20,4},{24,8},{28,12},{1,17},{... | collective-permute-start | bytes 49160 | tf_op jit(solution)/shard_map/ppermute | solution.py:335
  8.0 3.7 %collective-permute-start.2 = (f32[16,256]{1,0:T(8,128)S(1)}, f32[16,256]{1,0:T(8,128)S(1)}, u32[]{:S(2)}, u32[]{:S(2)}) collective-permute-start(f32[16,256]{1,0:T(8,128)S(1)} %get-tuple-element.21.total_in.total_ref), channel_id=1, source_target_pairs={{0,8},{4,12},{8,0},{12,4},{16,24},{20,28},{24,16},{28,20},{1,9},{5... | collective-permute-start | bytes 49160 | tf_op jit(solution)/shard_map/ppermute | solution.py:335
  9.7 8.5 %collective-permute-start.8 = (bf16[560,256]{1,0:T(8,128)(2,1)S(1)}, bf16[560,256]{1,0:T(8,128)(2,1)S(1)}, u32[]{:S(2)}, u32[]{:S(2)}) collective-permute-start(bf16[560,256]{1,0:T(8,128)(2,1)S(1)} %get-tuple-element.36), channel_id=1, source_target_pairs={{0,2},{1,3},{2,0},{3,1},{4,6},{5,7},{6,4},{7,5},{8,10},{9,11},{10,... | collective-permute-start | bytes 860168 | tf_op jit(solution)/shard_map/ppermute | solution.py:320
  11.8 3.9 %copy-start.3 = (bf16[512,256]{1,0:T(8,128)(2,1)S(1)}, bf16[512,256]{1,0:T(8,128)(2,1)}, u32[]{:S(2)}) copy-start(bf16[512,256]{1,0:T(8,128)(2,1)} %q_ref.1) | copy-start | bytes 786436
  11.8 3.8 %collective-permute-start.4 = (f32[16,256]{1,0:T(8,128)S(1)}, f32[16,256]{1,0:T(8,128)S(1)}, u32[]{:S(2)}, u32[]{:S(2)}) collective-permute-start(f32[16,256]{1,0:T(8,128)S(1)} %get-tuple-element.32), channel_id=1, source_target_pairs={{0,4},{4,0},{8,12},{12,8},{16,20},{20,16},{24,28},{28,24},{1,5},{5... | collective-permute-start | bytes 49160 | tf_op jit(solution)/shard_map/ppermute | solution.py:325
  13.4 4.7 %collective-permute-start.6 = (f32[16,256]{1,0:T(8,128)S(1)}, f32[16,256]{1,0:T(8,128)S(1)}, u32[]{:S(2)}, u32[]{:S(2)}) collective-permute-start(f32[16,256]{1,0:T(8,128)S(1)} %get-tuple-element.32), channel_id=1, source_target_pairs={{0,6},{1,7},{2,4},{3,5},{4,2},{5,3},{6,0},{7,1},{8,14},{9,15},{10,... | collective-permute-start | bytes 49160 | tf_op jit(solution)/shard_map/ppermute | solution.py:341
  14.3 3.9 %collective-permute-start.7 = (f32[16,256]{1,0:T(8,128)S(1)}, f32[16,256]{1,0:T(8,128)S(1)}, u32[]{:S(2)}, u32[]{:S(2)}) collective-permute-start(f32[16,256]{1,0:T(8,128)S(1)} %get-tuple-element.31.base_ref), channel_id=1, source_target_pairs={{0,2},{1,3},{2,0},{3,1},{4,6},{5,7},{6,4},{7,5},{8,10},{9,11},{10,... | collective-permute-start | bytes 49160 | tf_op jit(solution)/shard_map/ppermute | solution.py:320
  16.4 3.3 %collective-permute-start.5 = (bf16[512,256]{1,0:T(8,128)(2,1)S(1)}, bf16[512,256]{1,0:T(8,128)(2,1)S(1)}, u32[]{:S(2)}, u32[]{:S(2)}) collective-permute-start(bf16[512,256]{1,0:T(8,128)(2,1)S(1)} %shard_map.86.own_ref), channel_id=1, source_target_pairs={{0,1},{1,0},{2,3},{3,2},{4,5},{5,4},{6,7},{7,6},{8,9},{9,8},{10,11... | collective-permute-start | bytes 786440 | tf_op jit(solution)/shard_map/ppermute | solution.py:320
  18.8 1.0 %copy-start = (bf16[1024,256]{1,0:T(8,128)(2,1)S(1)}, bf16[1024,256]{1,0:T(8,128)(2,1)}, u32[]{:S(2)}) copy-start(bf16[1024,256]{1,0:T(8,128)(2,1)} %weight_ref.3) | copy-start | bytes 1572868
  18.8 1.8 %collective-permute-start.9 = (bf16[384,256]{1,0:T(8,128)(2,1)S(1)}, bf16[384,256]{1,0:T(8,128)(2,1)S(1)}, u32[]{:S(2)}, u32[]{:S(2)}) collective-permute-start(bf16[384,256]{1,0:T(8,128)(2,1)S(1)} %shard_map.87.rest_0_), channel_id=1, source_target_pairs={{0,1},{1,0},{2,3},{3,2},{4,5},{5,4},{6,7},{7,6},{8,9},{9,8},{10,11... | collective-permute-start | bytes 589832 | tf_op jit(solution)/shard_map/ppermute | solution.py:320
  19.1 0.7 %copy-start.6 = (f32[256]{0:T(256)S(1)}, f32[256]{0:T(256)}, u32[]{:S(2)}) copy-start(f32[256]{0:T(256)} %param.15) | copy-start | bytes 3076
  19.1 1.5 %collective-permute-start.10 = (bf16[128,256]{1,0:T(8,128)(2,1)S(1)}, bf16[128,256]{1,0:T(8,128)(2,1)S(1)}, u32[]{:S(2)}, u32[]{:S(2)}) collective-permute-start(bf16[128,256]{1,0:T(8,128)(2,1)S(1)} %shard_map.88.rest_1_), channel_id=1, source_target_pairs={{0,1},{1,0},{2,3},{3,2},{4,5},{5,4},{6,7},{7,6},{8,9},{9,8},{10,11... | collective-permute-start | bytes 196616 | tf_op jit(solution)/shard_map/ppermute | solution.py:320

commit v12 on v8

--- a/solution.py
+++ b/solution.py
@@ -12,7 +12,7 @@
 STORES = 4
 OWN_COST = 0
 FOLD_COST = 3000000000
-PIECES = 3
+PIECES = 2
 ROUTES = {2: [(1, 0)], 4: [(3, 2, 0, 1), (2, 3, 0, 1), (1, 0, 3, 2)]}
 FIRST_COST = 30000000000
 PART_COST = 0
@@ -252,7 +252,7 @@
         local_ref[first : first + modes, :].astype(jnp.float32)
         for first in range(seg_len, local_ref.shape[0], modes)
     ]
-    rates = (pieces[2] + pieces[1]) + pieces[0]
+    rates = pieces[1] + pieces[0]
     for part in range(q_ref.shape[1] // LANES):
         lanes = lane_slice(part)
         carry(q_ref, local_ref.at[:, lanes], rates[:, lanes], base_ref, extra_ref, out_ref, part, part)

time: 21.6 us -> 21.6 us (level)
  no operation moved by 1% of the time
where the time goes in v12:
time: 21.6 us; the launch traced here: 21.5 us
  starting transfers between devices  11.4 us (53%)
  Pallas kernels  5.77 us (27%)
  waiting for transfers between devices  3.59 us (17%)
  local copies, waits for them, and re-layouts  0.6 us (3%)
    pallas_call x8, Pallas kernels, call(): pl.pallas_call(kernel, out_shape=out, in_specs=[pl.BlockSpec(memory_space...  5.77 us
    ppermute x5, starting transfers between devices, swapped(): return lax.ppermute(value, 'chan', [(r, r ^ bit) for r in range(count)])  5.28 us
    ppermute x3, starting transfers between devices, along(): return lax.ppermute(value, 'seq', [(r, target(r)) for r in range(count)])  3.65 us
    ppermute x1, starting transfers between devices, beside(): return lax.ppermute(value, 'seq', [(r, r ^ 1) for r in range(count)])  1.56 us
    ppermute x1, waiting for transfers between devices, corner(): return lax.ppermute(value, ('seq', 'chan'), pairs)  1.55 us
    ppermute x3, waiting for transfers between devices, along(): return lax.ppermute(value, 'seq', [(r, target(r)) for r in range(count)])  1.07 us
    ppermute x1, starting transfers between devices, corner(): return lax.ppermute(value, ('seq', 'chan'), pairs)  0.91 us
    ppermute x5, waiting for transfers between devices, swapped(): return lax.ppermute(value, 'chan', [(r, r ^ bit) for r in range(count)])  0.72 us
  transfers between devices with their start and end apart: 10, of which 6 were waited for; matrix products, arithmetic and copies ran while one was open for 0% of the time, Pallas kernels for 23%

profile of v12, /device:TPU:0, one launch (start us, length us, event | category | flops | bytes accessed | tf_op | source)
XLA Modules:
  0.0 21.5 jit_solution(4400657938500530866)
XLA Ops:
  0.0 0.0 copy-start.2
  0.0 0.0 copy-start.4
  0.0 0.0 copy-start.5
  0.0 0.0 copy-start.1
  0.0 3.0 %collective-permute-start.3 = (bf16[512,256]{1,0:T(8,128)(2,1)}, bf16[512,256]{1,0:T(8,128)(2,1)S(1)}, u32[]{:S(2)}, u32[]{:S(2)}) collective-permute-start(bf16[512,256]{1,0:T(8,128)(2,1)} %q_ref.1), channel_id=1, source_target_pairs={{0,2},{1,3},{2,0},{3,1},{4,6},{5,7},{6,4},{7,5},{8,10},{9,11},{10,... | collective-permute-start | bytes 786440 | tf_op jit(solution)/shard_map/ppermute | solution.py:315
  3.1 0.0 copy-done.2
  3.1 0.0 copy-done.4
  3.1 0.0 copy-done.5
  3.1 0.0 copy-done.1
  3.1 1.9 %shard_map.83 = (f32[16,256]{1,0:T(8,128)S(1)}, f32[16,8,256]{2,1,0:T(8,128)S(1)}, f32[2,512,128]{2,1,0:T(8,128)S(1)}, f32[1,256]{1,0:T(1,128)S(1)}, f32[512,128...) custom-call(f32[8,128]{1,0:T(8,128)S(1)} %shard_map.82.zero_ref, bf16[512,256]{1,0:T(8,128)(2,1)S(1)} %copy-done.1, ...), custom_call_target="tpu_custom_call" | custom-call | tf_op jit(solution)/shard_map/pallas_call | solution.py:298
  5.0 1.7 %collective-permute-start = (f32[16,256]{1,0:T(8,128)S(1)}, f32[16,256]{1,0:T(8,128)S(1)}, u32[]{:S(2)}, u32[]{:S(2)}) collective-permute-start(f32[16,256]{1,0:T(8,128)S(1)} %get-tuple-element.21.total_in.total_ref), channel_id=1, source_target_pairs={{0,24},{4,28},{8,16},{12,20},{16,0},{20,4},{24,8},{28,12},{1,25},{... | collective-permute-start | bytes 49160 | tf_op jit(solution)/shard_map/ppermute | solution.py:330
  6.8 1.2 %collective-permute-start.1 = (f32[16,256]{1,0:T(8,128)S(1)}, f32[16,256]{1,0:T(8,128)S(1)}, u32[]{:S(2)}, u32[]{:S(2)}) collective-permute-start(f32[16,256]{1,0:T(8,128)S(1)} %get-tuple-element.21.total_in.total_ref), channel_id=1, source_target_pairs={{0,16},{4,20},{8,24},{12,28},{16,0},{20,4},{24,8},{28,12},{1,17},{... | collective-permute-start | bytes 49160 | tf_op jit(solution)/shard_map/ppermute | solution.py:330
  8.0 0.7 %collective-permute-start.2 = (f32[16,256]{1,0:T(8,128)S(1)}, f32[16,256]{1,0:T(8,128)S(1)}, u32[]{:S(2)}, u32[]{:S(2)}) collective-permute-start(f32[16,256]{1,0:T(8,128)S(1)} %get-tuple-element.21.total_in.total_ref), channel_id=1, source_target_pairs={{0,8},{4,12},{8,0},{12,4},{16,24},{20,28},{24,16},{28,20},{1,9},{5... | collective-permute-start | bytes 49160 | tf_op jit(solution)/shard_map/ppermute | solution.py:330
  8.7 1.0 %shard_map.84 = (f32[16,256]{1,0:T(8,128)S(1)}, bf16[544,256]{1,0:T(8,128)(2,1)S(1)}, f32[512,128]{1,0:T(8,128)S(1)}, f32[512,128]{1,0:T(8,128)S(1)}) custom-call(f32[8,128]{1,0:T(8,128)S(1)} %shard_map.82.zero_ref, bf16[512,256]{1,0:T(8,128)(2,1)S(1)} %copy-done.1, bf16[512,256]{1,0:T(8,128)(2,1)S(1)} %copy-done.2, f32[16,256]{1,0:T(8,128)S(1)} %copy-done.4, ...), custom_call_target="tpu_custom_call" | custom-call | tf_op jit(solution)/shard_map/pallas_call | solution.py:298
  9.7 1.0 %collective-permute-start.8 = (bf16[544,256]{1,0:T(8,128)(2,1)S(1)}, bf16[544,256]{1,0:T(8,128)(2,1)S(1)}, u32[]{:S(2)}, u32[]{:S(2)}) collective-permute-start(bf16[544,256]{1,0:T(8,128)(2,1)S(1)} %get-tuple-element.36), channel_id=1, source_target_pairs={{0,2},{1,3},{2,0},{3,1},{4,6},{5,7},{6,4},{7,5},{8,10},{9,11},{10,... | collective-permute-start | bytes 835592 | tf_op jit(solution)/shard_map/ppermute | solution.py:315
  10.7 0.0 collective-permute-done.rest_0_
  10.7 0.9 %collective-permute-done.1.rest_1_ = f32[16,256]{1,0:T(8,128)S(1)} collective-permute-done((f32[16,256]{1,0:T(8,128)S(1)}, f32[16,256]{1,0:T(8,128)S(1)}, u32[]{:S(2)}, u32[]{:S(2)}) %collective-permute-start.1) | collective-permute-done | bytes 16416 | tf_op jit(solution)/shard_map/ppermute | solution.py:330
  11.6 0.2 collective-permute-done.2.rest_2_
  11.8 0.0 collective-permute-done.3.q_ref
  11.8 0.0 copy-start.3
  11.8 1.6 %collective-permute-start.4 = (f32[16,256]{1,0:T(8,128)S(1)}, f32[16,256]{1,0:T(8,128)S(1)}, u32[]{:S(2)}, u32[]{:S(2)}) collective-permute-start(f32[16,256]{1,0:T(8,128)S(1)} %get-tuple-element.32), channel_id=1, source_target_pairs={{0,4},{4,0},{8,12},{12,8},{16,20},{20,16},{24,28},{28,24},{1,5},{5... | collective-permute-start | bytes 49160 | tf_op jit(solution)/shard_map/ppermute | solution.py:320
  13.4 0.9 %collective-permute-start.6 = (f32[16,256]{1,0:T(8,128)S(1)}, f32[16,256]{1,0:T(8,128)S(1)}, u32[]{:S(2)}, u32[]{:S(2)}) collective-permute-start(f32[16,256]{1,0:T(8,128)S(1)} %get-tuple-element.32), channel_id=1, source_target_pairs={{0,6},{1,7},{2,4},{3,5},{4,2},{5,3},{6,0},{7,1},{8,14},{9,15},{10,... | collective-permute-start | bytes 49160 | tf_op jit(solution)/shard_map/ppermute | solution.py:336
  14.3 1.1 %collective-permute-start.7 = (f32[16,256]{1,0:T(8,128)S(1)}, f32[16,256]{1,0:T(8,128)S(1)}, u32[]{:S(2)}, u32[]{:S(2)}) collective-permute-start(f32[16,256]{1,0:T(8,128)S(1)} %get-tuple-element.31.base_ref), channel_id=1, source_target_pairs={{0,2},{1,3},{2,0},{3,1},{4,6},{5,7},{6,4},{7,5},{8,10},{9,11},{10,... | collective-permute-start | bytes 49160 | tf_op jit(solution)/shard_map/ppermute | solution.py:315
  15.4 0.2 %collective-permute-done.4.extra_ref = f32[16,256]{1,0:T(8,128)S(1)} collective-permute-done((f32[16,256]{1,0:T(8,128)S(1)}, f32[16,256]{1,0:T(8,128)S(1)}, u32[]{:S(2)}, u32[]{:S(2)}) %collective-permute-start.4) | collective-permute-done | bytes 16416 | tf_op jit(solution)/shard_map/ppermute | solution.py:320
  15.6 0.0 copy-done.3
  15.6 0.8 %shard_map.86.own_ref = bf16[512,256]{1,0:T(8,128)(2,1)S(1)} custom-call(bf16[512,256]{1,0:T(8,128)(2,1)S(1)} %copy-done.3, f32[16,256]{1,0:T(8,128)S(1)} %copy-done.4, f32[16,256]{1,0:T(8,128)S(1)} %get-tuple-element.31.base_ref, f32[16,256]{1,0:T(8,128)S(1)} %collective-permute-done.4.extra_ref, f32[512,128]{1,0:T(8,128)S(1)} %get-tuple-element.33.rest_0_, ...), custom_call_target="tpu_custom_call" | custom-call | tf_op jit(solution)/shard_map/pallas_call | solution.py:298
  16.4 0.0 copy-start
  16.4 0.1 collective-permute-start.5
  16.5 1.5 %collective-permute-done.6.extra_ref = f32[16,256]{1,0:T(8,128)S(1)} collective-permute-done((f32[16,256]{1,0:T(8,128)S(1)}, f32[16,256]{1,0:T(8,128)S(1)}, u32[]{:S(2)}, u32[]{:S(2)}) %collective-permute-start.6) | collective-permute-done | bytes 16416 | tf_op jit(solution)/shard_map/ppermute | solution.py:336
  18.0 0.2 collective-permute-done.7.base_ref
  18.2 0.0 collective-permute-done.8.local_ref
  18.2 0.7 %shard_map.87.rest_0_ = bf16[512,256]{1,0:T(8,128)(2,1)S(1)} custom-call(f32[16,256]{1,0:T(8,128)S(1)} %collective-permute-done.6.extra_ref, f32[16,256]{1,0:T(8,128)S(1)} %collective-permute-done.7.base_ref, bf16[512,256]{1,0:T(8,128)(2,1)S(1)} %collective-permute-done.3.q_ref, bf16[544,256]{1,0:T(8,128)(2,1)S(1)} %collective-permute-done.8.local_ref), custom_call_target="tpu_custom_call" | custom-call | tf_op jit(solution)/shard_map/pallas_call | solution.py:298
  18.9 0.0 copy-start.6
  18.9 0.1 collective-permute-start.9
  19.0 0.0 collective-permute-done.5.pair_ref
  19.0 0.0 copy-done
  19.0 0.6 %copy-done.6 = f32[256]{0:T(256)S(1)} copy-done((f32[256]{0:T(256)S(1)}, f32[256]{0:T(256)}, u32[]{:S(2)}) %copy-start.6) | copy-done | bytes 1048
  19.6 0.4 %shard_map.88.near_ref = f32[512,256]{1,0:T(8,128)S(1)} custom-call(bf16[1024,256]{1,0:T(8,128)(2,1)S(1)} %copy-done, f32[1,256]{1,0:T(1,128)S(1)} %bitcast.2, bf16[512,256]{1,0:T(8,128)(2,1)S(1)} %shard_map.86.own_ref, bf16[512,256]{1,0:T(8,128)(2,1)S(1)} %collective-permute-done.5.pair_ref, bf16[512,256]{1,0:T(8,128)(2,1)S(1)} %shard_map.87.rest_0_), custom_call_target="tpu_custom_call" | custom-call | tf_op jit(solution)/shard_map/pallas_call | solution.py:298
  20.0 0.6 %collective-permute-done.9.rest_0_ = bf16[512,256]{1,0:T(8,128)(2,1)S(1)} collective-permute-done((bf16[512,256]{1,0:T(8,128)(2,1)S(1)}, bf16[512,256]{1,0:T(8,128)(2,1)S(1)}, u32[]{:S(2)}, u32[]{:S(2)}) %collective-permute-start.9) | collective-permute-done | bytes 262176 | tf_op jit(solution)/shard_map/ppermute | solution.py:315
  20.5 0.9 %shard_map.89 = bf16[512,256]{1,0:T(8,128)(2,1)} custom-call(f32[512,256]{1,0:T(8,128)S(1)} %shard_map.88.near_ref, bf16[1024,256]{1,0:T(8,128)(2,1)S(1)} %copy-done, bf16[512,256]{1,0:T(8,128)(2,1)S(1)} %collective-permute-done.9.rest_0_), custom_call_target="tpu_custom_call" | custom-call | tf_op jit(solution)/shard_map/pallas_call | solution.py:298
  (2 shorter events, 0.0 us)
Async XLA Ops:
  0.0 3.1 %copy-start.2 = (bf16[512,256]{1,0:T(8,128)(2,1)S(1)}, bf16[512,256]{1,0:T(8,128)(2,1)}, u32[]{:S(2)}) copy-start(bf16[512,256]{1,0:T(8,128)(2,1)} %v_ref.3) | copy-start | bytes 786436
  0.0 3.1 %copy-start.4 = (f32[16,256]{1,0:T(8,128)S(1)}, f32[16,256]{1,0:T(8,128)}, u32[]{:S(2)}) copy-start(f32[16,256]{1,0:T(8,128)} %rates_ref.3) | copy-start | bytes 49156
  0.0 3.1 %copy-start.5 = (f32[16,256]{1,0:T(8,128)S(1)}, f32[16,256]{1,0:T(8,128)}, u32[]{:S(2)}) copy-start(f32[16,256]{1,0:T(8,128)} %residue_ref.5) | copy-start | bytes 49156
  0.0 3.1 %copy-start.1 = (bf16[512,256]{1,0:T(8,128)(2,1)S(1)}, bf16[512,256]{1,0:T(8,128)(2,1)}, u32[]{:S(2)}) copy-start(bf16[512,256]{1,0:T(8,128)(2,1)} %k_ref.3) | copy-start | bytes 786436
  0.0 11.8 %collective-permute-start.3 = (bf16[512,256]{1,0:T(8,128)(2,1)}, bf16[512,256]{1,0:T(8,128)(2,1)S(1)}, u32[]{:S(2)}, u32[]{:S(2)}) collective-permute-start(bf16[512,256]{1,0:T(8,128)(2,1)} %q_ref.1), channel_id=1, source_target_pairs={{0,2},{1,3},{2,0},{3,1},{4,6},{5,7},{6,4},{7,5},{8,10},{9,11},{10,... | collective-permute-start | bytes 786440 | tf_op jit(solution)/shard_map/ppermute | solution.py:315
  5.0 5.7 %collective-permute-start = (f32[16,256]{1,0:T(8,128)S(1)}, f32[16,256]{1,0:T(8,128)S(1)}, u32[]{:S(2)}, u32[]{:S(2)}) collective-permute-start(f32[16,256]{1,0:T(8,128)S(1)} %get-tuple-element.21.total_in.total_ref), channel_id=1, source_target_pairs={{0,24},{4,28},{8,16},{12,20},{16,0},{20,4},{24,8},{28,12},{1,25},{... | collective-permute-start | bytes 49160 | tf_op jit(solution)/shard_map/ppermute | solution.py:330
  6.8 4.8 %collective-permute-start.1 = (f32[16,256]{1,0:T(8,128)S(1)}, f32[16,256]{1,0:T(8,128)S(1)}, u32[]{:S(2)}, u32[]{:S(2)}) collective-permute-start(f32[16,256]{1,0:T(8,128)S(1)} %get-tuple-element.21.total_in.total_ref), channel_id=1, source_target_pairs={{0,16},{4,20},{8,24},{12,28},{16,0},{20,4},{24,8},{28,12},{1,17},{... | collective-permute-start | bytes 49160 | tf_op jit(solution)/shard_map/ppermute | solution.py:330
  8.0 3.8 %collective-permute-start.2 = (f32[16,256]{1,0:T(8,128)S(1)}, f32[16,256]{1,0:T(8,128)S(1)}, u32[]{:S(2)}, u32[]{:S(2)}) collective-permute-start(f32[16,256]{1,0:T(8,128)S(1)} %get-tuple-element.21.total_in.total_ref), channel_id=1, source_target_pairs={{0,8},{4,12},{8,0},{12,4},{16,24},{20,28},{24,16},{28,20},{1,9},{5... | collective-permute-start | bytes 49160 | tf_op jit(solution)/shard_map/ppermute | solution.py:330
  9.7 8.5 %collective-permute-start.8 = (bf16[544,256]{1,0:T(8,128)(2,1)S(1)}, bf16[544,256]{1,0:T(8,128)(2,1)S(1)}, u32[]{:S(2)}, u32[]{:S(2)}) collective-permute-start(bf16[544,256]{1,0:T(8,128)(2,1)S(1)} %get-tuple-element.36), channel_id=1, source_target_pairs={{0,2},{1,3},{2,0},{3,1},{4,6},{5,7},{6,4},{7,5},{8,10},{9,11},{10,... | collective-permute-start | bytes 835592 | tf_op jit(solution)/shard_map/ppermute | solution.py:315
  11.8 3.9 %copy-start.3 = (bf16[512,256]{1,0:T(8,128)(2,1)S(1)}, bf16[512,256]{1,0:T(8,128)(2,1)}, u32[]{:S(2)}) copy-start(bf16[512,256]{1,0:T(8,128)(2,1)} %q_ref.1) | copy-start | bytes 786436
  11.8 3.8 %collective-permute-start.4 = (f32[16,256]{1,0:T(8,128)S(1)}, f32[16,256]{1,0:T(8,128)S(1)}, u32[]{:S(2)}, u32[]{:S(2)}) collective-permute-start(f32[16,256]{1,0:T(8,128)S(1)} %get-tuple-element.32), channel_id=1, source_target_pairs={{0,4},{4,0},{8,12},{12,8},{16,20},{20,16},{24,28},{28,24},{1,5},{5... | collective-permute-start | bytes 49160 | tf_op jit(solution)/shard_map/ppermute | solution.py:320
  13.4 4.7 %collective-permute-start.6 = (f32[16,256]{1,0:T(8,128)S(1)}, f32[16,256]{1,0:T(8,128)S(1)}, u32[]{:S(2)}, u32[]{:S(2)}) collective-permute-start(f32[16,256]{1,0:T(8,128)S(1)} %get-tuple-element.32), channel_id=1, source_target_pairs={{0,6},{1,7},{2,4},{3,5},{4,2},{5,3},{6,0},{7,1},{8,14},{9,15},{10,... | collective-permute-start | bytes 49160 | tf_op jit(solution)/shard_map/ppermute | solution.py:336
  14.3 3.9 %collective-permute-start.7 = (f32[16,256]{1,0:T(8,128)S(1)}, f32[16,256]{1,0:T(8,128)S(1)}, u32[]{:S(2)}, u32[]{:S(2)}) collective-permute-start(f32[16,256]{1,0:T(8,128)S(1)} %get-tuple-element.31.base_ref), channel_id=1, source_target_pairs={{0,2},{1,3},{2,0},{3,1},{4,6},{5,7},{6,4},{7,5},{8,10},{9,11},{10,... | collective-permute-start | bytes 49160 | tf_op jit(solution)/shard_map/ppermute | solution.py:315
  16.4 2.6 %copy-start = (bf16[1024,256]{1,0:T(8,128)(2,1)S(1)}, bf16[1024,256]{1,0:T(8,128)(2,1)}, u32[]{:S(2)}) copy-start(bf16[1024,256]{1,0:T(8,128)(2,1)} %weight_ref.3) | copy-start | bytes 1572868
  16.4 2.6 %collective-permute-start.5 = (bf16[512,256]{1,0:T(8,128)(2,1)S(1)}, bf16[512,256]{1,0:T(8,128)(2,1)S(1)}, u32[]{:S(2)}, u32[]{:S(2)}) collective-permute-start(bf16[512,256]{1,0:T(8,128)(2,1)S(1)} %shard_map.86.own_ref), channel_id=1, source_target_pairs={{0,1},{1,0},{2,3},{3,2},{4,5},{5,4},{6,7},{7,6},{8,9},{9,8},{10,11... | collective-permute-start | bytes 786440 | tf_op jit(solution)/shard_map/ppermute | solution.py:315
  18.9 0.7 %copy-start.6 = (f32[256]{0:T(256)S(1)}, f32[256]{0:T(256)}, u32[]{:S(2)}) copy-start(f32[256]{0:T(256)} %param.15) | copy-start | bytes 3076
  18.9 1.6 %collective-permute-start.9 = (bf16[512,256]{1,0:T(8,128)(2,1)S(1)}, bf16[512,256]{1,0:T(8,128)(2,1)S(1)}, u32[]{:S(2)}, u32[]{:S(2)}) collective-permute-start(bf16[512,256]{1,0:T(8,128)(2,1)S(1)} %shard_map.87.rest_0_), channel_id=1, source_target_pairs={{0,1},{1,0},{2,3},{3,2},{4,5},{5,4},{6,7},{7,6},{8,9},{9,8},{10,11... | collective-permute-start | bytes 786440 | tf_op jit(solution)/shard_map/ppermute | solution.py:315

commit v13 on v8

--- a/solution.py
+++ b/solution.py
@@ -9,7 +9,7 @@
 
 LANES = 128
 SUBLANES = 8
-STORES = 4
+STORES = 8
 OWN_COST = 0
 FOLD_COST = 3000000000
 PIECES = 3

time: 21.6 us -> 21.7 us (level)
  no operation moved by 1% of the time
where the time goes in v13:
time: 21.7 us; the launch traced here: 21.6 us
  starting transfers between devices  11.4 us (53%)
  Pallas kernels  5.86 us (27%)
  waiting for transfers between devices  3.58 us (16%)
  local copies, waits for them, and re-layouts  0.6 us (3%)
    pallas_call x8, Pallas kernels, call(): pl.pallas_call(kernel, out_shape=out, in_specs=[pl.BlockSpec(memory_space...  5.86 us
    ppermute x5, starting transfers between devices, swapped(): return lax.ppermute(value, 'chan', [(r, r ^ bit) for r in range(count)])  5.28 us
    ppermute x3, starting transfers between devices, along(): return lax.ppermute(value, 'seq', [(r, target(r)) for r in range(count)])  3.65 us
    ppermute x1, starting transfers between devices, beside(): return lax.ppermute(value, 'seq', [(r, r ^ 1) for r in range(count)])  1.56 us
    ppermute x1, waiting for transfers between devices, corner(): return lax.ppermute(value, ('seq', 'chan'), pairs)  1.54 us
    ppermute x3, waiting for transfers between devices, along(): return lax.ppermute(value, 'seq', [(r, target(r)) for r in range(count)])  1.07 us
    ppermute x1, starting transfers between devices, corner(): return lax.ppermute(value, ('seq', 'chan'), pairs)  0.91 us
    ppermute x5, waiting for transfers between devices, swapped(): return lax.ppermute(value, 'chan', [(r, r ^ bit) for r in range(count)])  0.72 us
  transfers between devices with their start and end apart: 10, of which 6 were waited for; matrix products, arithmetic and copies ran while one was open for 0% of the time, Pallas kernels for 23%

profile of v13, /device:TPU:0, one launch (start us, length us, event | category | flops | bytes accessed | tf_op | source)
XLA Modules:
  0.0 21.6 jit_solution(12014628495449258809)
XLA Ops:
  0.0 0.0 copy-start.2
  0.0 0.0 copy-start.4
  0.0 0.0 copy-start.5
  0.0 0.0 copy-start.1
  0.0 3.0 %collective-permute-start.3 = (bf16[512,256]{1,0:T(8,128)(2,1)}, bf16[512,256]{1,0:T(8,128)(2,1)S(1)}, u32[]{:S(2)}, u32[]{:S(2)}) collective-permute-start(bf16[512,256]{1,0:T(8,128)(2,1)} %q_ref.1), channel_id=1, source_target_pairs={{0,2},{1,3},{2,0},{3,1},{4,6},{5,7},{6,4},{7,5},{8,10},{9,11},{10,... | collective-permute-start | bytes 786440 | tf_op jit(solution)/shard_map/ppermute | solution.py:315
  3.1 0.0 copy-done.2
  3.1 0.0 copy-done.4
  3.1 0.0 copy-done.5
  3.1 0.0 copy-done.1
  3.1 2.0 %shard_map.83 = (f32[16,256]{1,0:T(8,128)S(1)}, f32[16,8,256]{2,1,0:T(8,128)S(1)}, f32[2,512,128]{2,1,0:T(8,128)S(1)}, f32[1,256]{1,0:T(1,128)S(1)}, f32[512,128...) custom-call(f32[8,128]{1,0:T(8,128)S(1)} %shard_map.82.zero_ref, bf16[512,256]{1,0:T(8,128)(2,1)S(1)} %copy-done.1, ...), custom_call_target="tpu_custom_call" | custom-call | tf_op jit(solution)/shard_map/pallas_call | solution.py:298
  5.0 1.7 %collective-permute-start = (f32[16,256]{1,0:T(8,128)S(1)}, f32[16,256]{1,0:T(8,128)S(1)}, u32[]{:S(2)}, u32[]{:S(2)}) collective-permute-start(f32[16,256]{1,0:T(8,128)S(1)} %get-tuple-element.21.total_in.total_ref), channel_id=1, source_target_pairs={{0,24},{4,28},{8,16},{12,20},{16,0},{20,4},{24,8},{28,12},{1,25},{... | collective-permute-start | bytes 49160 | tf_op jit(solution)/shard_map/ppermute | solution.py:330
  6.8 1.2 %collective-permute-start.1 = (f32[16,256]{1,0:T(8,128)S(1)}, f32[16,256]{1,0:T(8,128)S(1)}, u32[]{:S(2)}, u32[]{:S(2)}) collective-permute-start(f32[16,256]{1,0:T(8,128)S(1)} %get-tuple-element.21.total_in.total_ref), channel_id=1, source_target_pairs={{0,16},{4,20},{8,24},{12,28},{16,0},{20,4},{24,8},{28,12},{1,17},{... | collective-permute-start | bytes 49160 | tf_op jit(solution)/shard_map/ppermute | solution.py:330
  8.0 0.7 %collective-permute-start.2 = (f32[16,256]{1,0:T(8,128)S(1)}, f32[16,256]{1,0:T(8,128)S(1)}, u32[]{:S(2)}, u32[]{:S(2)}) collective-permute-start(f32[16,256]{1,0:T(8,128)S(1)} %get-tuple-element.21.total_in.total_ref), channel_id=1, source_target_pairs={{0,8},{4,12},{8,0},{12,4},{16,24},{20,28},{24,16},{28,20},{1,9},{5... | collective-permute-start | bytes 49160 | tf_op jit(solution)/shard_map/ppermute | solution.py:330
  8.7 1.0 %shard_map.84 = (f32[16,256]{1,0:T(8,128)S(1)}, bf16[560,256]{1,0:T(8,128)(2,1)S(1)}, f32[512,128]{1,0:T(8,128)S(1)}, f32[512,128]{1,0:T(8,128)S(1)}) custom-call(f32[8,128]{1,0:T(8,128)S(1)} %shard_map.82.zero_ref, bf16[512,256]{1,0:T(8,128)(2,1)S(1)} %copy-done.1, bf16[512,256]{1,0:T(8,128)(2,1)S(1)} %copy-done.2, f32[16,256]{1,0:T(8,128)S(1)} %copy-done.4, ...), custom_call_target="tpu_custom_call" | custom-call | tf_op jit(solution)/shard_map/pallas_call | solution.py:298
  9.7 1.0 %collective-permute-start.8 = (bf16[560,256]{1,0:T(8,128)(2,1)S(1)}, bf16[560,256]{1,0:T(8,128)(2,1)S(1)}, u32[]{:S(2)}, u32[]{:S(2)}) collective-permute-start(bf16[560,256]{1,0:T(8,128)(2,1)S(1)} %get-tuple-element.36), channel_id=1, source_target_pairs={{0,2},{1,3},{2,0},{3,1},{4,6},{5,7},{6,4},{7,5},{8,10},{9,11},{10,... | collective-permute-start | bytes 860168 | tf_op jit(solution)/shard_map/ppermute | solution.py:315
  10.7 0.0 collective-permute-done.rest_0_
  10.7 0.9 %collective-permute-done.1.rest_1_ = f32[16,256]{1,0:T(8,128)S(1)} collective-permute-done((f32[16,256]{1,0:T(8,128)S(1)}, f32[16,256]{1,0:T(8,128)S(1)}, u32[]{:S(2)}, u32[]{:S(2)}) %collective-permute-start.1) | collective-permute-done | bytes 16416 | tf_op jit(solution)/shard_map/ppermute | solution.py:330
  11.6 0.2 collective-permute-done.2.rest_2_
  11.8 0.0 collective-permute-done.3.q_ref
  11.8 0.0 copy-start.3
  11.8 1.6 %collective-permute-start.4 = (f32[16,256]{1,0:T(8,128)S(1)}, f32[16,256]{1,0:T(8,128)S(1)}, u32[]{:S(2)}, u32[]{:S(2)}) collective-permute-start(f32[16,256]{1,0:T(8,128)S(1)} %get-tuple-element.32), channel_id=1, source_target_pairs={{0,4},{4,0},{8,12},{12,8},{16,20},{20,16},{24,28},{28,24},{1,5},{5... | collective-permute-start | bytes 49160 | tf_op jit(solution)/shard_map/ppermute | solution.py:320
  13.4 0.9 %collective-permute-start.6 = (f32[16,256]{1,0:T(8,128)S(1)}, f32[16,256]{1,0:T(8,128)S(1)}, u32[]{:S(2)}, u32[]{:S(2)}) collective-permute-start(f32[16,256]{1,0:T(8,128)S(1)} %get-tuple-element.32), channel_id=1, source_target_pairs={{0,6},{1,7},{2,4},{3,5},{4,2},{5,3},{6,0},{7,1},{8,14},{9,15},{10,... | collective-permute-start | bytes 49160 | tf_op jit(solution)/shard_map/ppermute | solution.py:336
  14.3 1.1 %collective-permute-start.7 = (f32[16,256]{1,0:T(8,128)S(1)}, f32[16,256]{1,0:T(8,128)S(1)}, u32[]{:S(2)}, u32[]{:S(2)}) collective-permute-start(f32[16,256]{1,0:T(8,128)S(1)} %get-tuple-element.31.base_ref), channel_id=1, source_target_pairs={{0,2},{1,3},{2,0},{3,1},{4,6},{5,7},{6,4},{7,5},{8,10},{9,11},{10,... | collective-permute-start | bytes 49160 | tf_op jit(solution)/shard_map/ppermute | solution.py:315
  15.4 0.2 %collective-permute-done.4.extra_ref = f32[16,256]{1,0:T(8,128)S(1)} collective-permute-done((f32[16,256]{1,0:T(8,128)S(1)}, f32[16,256]{1,0:T(8,128)S(1)}, u32[]{:S(2)}, u32[]{:S(2)}) %collective-permute-start.4) | collective-permute-done | bytes 16416 | tf_op jit(solution)/shard_map/ppermute | solution.py:320
  15.6 0.0 copy-done.3
  15.6 0.8 %shard_map.86.own_ref = bf16[512,256]{1,0:T(8,128)(2,1)S(1)} custom-call(bf16[512,256]{1,0:T(8,128)(2,1)S(1)} %copy-done.3, f32[16,256]{1,0:T(8,128)S(1)} %copy-done.4, f32[16,256]{1,0:T(8,128)S(1)} %get-tuple-element.31.base_ref, f32[16,256]{1,0:T(8,128)S(1)} %collective-permute-done.4.extra_ref, f32[512,128]{1,0:T(8,128)S(1)} %get-tuple-element.33.rest_0_, ...), custom_call_target="tpu_custom_call" | custom-call | tf_op jit(solution)/shard_map/pallas_call | solution.py:298
  16.4 0.0 copy-start
  16.4 0.1 collective-permute-start.5
  16.5 1.5 %collective-permute-done.6.extra_ref = f32[16,256]{1,0:T(8,128)S(1)} collective-permute-done((f32[16,256]{1,0:T(8,128)S(1)}, f32[16,256]{1,0:T(8,128)S(1)}, u32[]{:S(2)}, u32[]{:S(2)}) %collective-permute-start.6) | collective-permute-done | bytes 16416 | tf_op jit(solution)/shard_map/ppermute | solution.py:336
  18.0 0.2 collective-permute-done.7.base_ref
  18.2 0.0 collective-permute-done.8.local_ref
  18.2 0.7 %shard_map.87.rest_0_ = bf16[512,256]{1,0:T(8,128)(2,1)S(1)} custom-call(f32[16,256]{1,0:T(8,128)S(1)} %collective-permute-done.6.extra_ref, f32[16,256]{1,0:T(8,128)S(1)} %collective-permute-done.7.base_ref, bf16[512,256]{1,0:T(8,128)(2,1)S(1)} %collective-permute-done.3.q_ref, bf16[560,256]{1,0:T(8,128)(2,1)S(1)} %collective-permute-done.8.local_ref), custom_call_target="tpu_custom_call" | custom-call | tf_op jit(solution)/shard_map/pallas_call | solution.py:298
  18.9 0.0 copy-start.6
  19.0 0.1 collective-permute-start.9
  19.0 0.0 collective-permute-done.5.pair_ref
  19.0 0.0 copy-done
  19.1 0.6 %copy-done.6 = f32[256]{0:T(256)S(1)} copy-done((f32[256]{0:T(256)S(1)}, f32[256]{0:T(256)}, u32[]{:S(2)}) %copy-start.6) | copy-done | bytes 1048
  19.6 0.4 %shard_map.88.near_ref = f32[512,256]{1,0:T(8,128)S(1)} custom-call(bf16[1024,256]{1,0:T(8,128)(2,1)S(1)} %copy-done, f32[1,256]{1,0:T(1,128)S(1)} %bitcast.2, bf16[512,256]{1,0:T(8,128)(2,1)S(1)} %shard_map.86.own_ref, bf16[512,256]{1,0:T(8,128)(2,1)S(1)} %collective-permute-done.5.pair_ref, bf16[512,256]{1,0:T(8,128)(2,1)S(1)} %shard_map.87.rest_0_), custom_call_target="tpu_custom_call" | custom-call | tf_op jit(solution)/shard_map/pallas_call | solution.py:298
  20.0 0.6 %collective-permute-done.9.rest_0_ = bf16[512,256]{1,0:T(8,128)(2,1)S(1)} collective-permute-done((bf16[512,256]{1,0:T(8,128)(2,1)S(1)}, bf16[512,256]{1,0:T(8,128)(2,1)S(1)}, u32[]{:S(2)}, u32[]{:S(2)}) %collective-permute-start.9) | collective-permute-done | bytes 262176 | tf_op jit(solution)/shard_map/ppermute | solution.py:315
  20.6 1.0 %shard_map.89 = bf16[512,256]{1,0:T(8,128)(2,1)} custom-call(f32[512,256]{1,0:T(8,128)S(1)} %shard_map.88.near_ref, bf16[1024,256]{1,0:T(8,128)(2,1)S(1)} %copy-done, bf16[512,256]{1,0:T(8,128)(2,1)S(1)} %collective-permute-done.9.rest_0_), custom_call_target="tpu_custom_call" | custom-call | tf_op jit(solution)/shard_map/pallas_call | solution.py:298
  (2 shorter events, 0.0 us)
Async XLA Ops:
  0.0 3.1 %copy-start.2 = (bf16[512,256]{1,0:T(8,128)(2,1)S(1)}, bf16[512,256]{1,0:T(8,128)(2,1)}, u32[]{:S(2)}) copy-start(bf16[512,256]{1,0:T(8,128)(2,1)} %v_ref.3) | copy-start | bytes 786436
  0.0 3.1 %copy-start.4 = (f32[16,256]{1,0:T(8,128)S(1)}, f32[16,256]{1,0:T(8,128)}, u32[]{:S(2)}) copy-start(f32[16,256]{1,0:T(8,128)} %rates_ref.3) | copy-start | bytes 49156
  0.0 3.1 %copy-start.5 = (f32[16,256]{1,0:T(8,128)S(1)}, f32[16,256]{1,0:T(8,128)}, u32[]{:S(2)}) copy-start(f32[16,256]{1,0:T(8,128)} %residue_ref.5) | copy-start | bytes 49156
  0.0 3.1 %copy-start.1 = (bf16[512,256]{1,0:T(8,128)(2,1)S(1)}, bf16[512,256]{1,0:T(8,128)(2,1)}, u32[]{:S(2)}) copy-start(bf16[512,256]{1,0:T(8,128)(2,1)} %k_ref.3) | copy-start | bytes 786436
  0.0 11.8 %collective-permute-start.3 = (bf16[512,256]{1,0:T(8,128)(2,1)}, bf16[512,256]{1,0:T(8,128)(2,1)S(1)}, u32[]{:S(2)}, u32[]{:S(2)}) collective-permute-start(bf16[512,256]{1,0:T(8,128)(2,1)} %q_ref.1), channel_id=1, source_target_pairs={{0,2},{1,3},{2,0},{3,1},{4,6},{5,7},{6,4},{7,5},{8,10},{9,11},{10,... | collective-permute-start | bytes 786440 | tf_op jit(solution)/shard_map/ppermute | solution.py:315
  5.0 5.7 %collective-permute-start = (f32[16,256]{1,0:T(8,128)S(1)}, f32[16,256]{1,0:T(8,128)S(1)}, u32[]{:S(2)}, u32[]{:S(2)}) collective-permute-start(f32[16,256]{1,0:T(8,128)S(1)} %get-tuple-element.21.total_in.total_ref), channel_id=1, source_target_pairs={{0,24},{4,28},{8,16},{12,20},{16,0},{20,4},{24,8},{28,12},{1,25},{... | collective-permute-start | bytes 49160 | tf_op jit(solution)/shard_map/ppermute | solution.py:330
  6.8 4.8 %collective-permute-start.1 = (f32[16,256]{1,0:T(8,128)S(1)}, f32[16,256]{1,0:T(8,128)S(1)}, u32[]{:S(2)}, u32[]{:S(2)}) collective-permute-start(f32[16,256]{1,0:T(8,128)S(1)} %get-tuple-element.21.total_in.total_ref), channel_id=1, source_target_pairs={{0,16},{4,20},{8,24},{12,28},{16,0},{20,4},{24,8},{28,12},{1,17},{... | collective-permute-start | bytes 49160 | tf_op jit(solution)/shard_map/ppermute | solution.py:330
  8.0 3.7 %collective-permute-start.2 = (f32[16,256]{1,0:T(8,128)S(1)}, f32[16,256]{1,0:T(8,128)S(1)}, u32[]{:S(2)}, u32[]{:S(2)}) collective-permute-start(f32[16,256]{1,0:T(8,128)S(1)} %get-tuple-element.21.total_in.total_ref), channel_id=1, source_target_pairs={{0,8},{4,12},{8,0},{12,4},{16,24},{20,28},{24,16},{28,20},{1,9},{5... | collective-permute-start | bytes 49160 | tf_op jit(solution)/shard_map/ppermute | solution.py:330
  9.7 8.5 %collective-permute-start.8 = (bf16[560,256]{1,0:T(8,128)(2,1)S(1)}, bf16[560,256]{1,0:T(8,128)(2,1)S(1)}, u32[]{:S(2)}, u32[]{:S(2)}) collective-permute-start(bf16[560,256]{1,0:T(8,128)(2,1)S(1)} %get-tuple-element.36), channel_id=1, source_target_pairs={{0,2},{1,3},{2,0},{3,1},{4,6},{5,7},{6,4},{7,5},{8,10},{9,11},{10,... | collective-permute-start | bytes 860168 | tf_op jit(solution)/shard_map/ppermute | solution.py:315
  11.8 3.9 %copy-start.3 = (bf16[512,256]{1,0:T(8,128)(2,1)S(1)}, bf16[512,256]{1,0:T(8,128)(2,1)}, u32[]{:S(2)}) copy-start(bf16[512,256]{1,0:T(8,128)(2,1)} %q_ref.1) | copy-start | bytes 786436
  11.8 3.8 %collective-permute-start.4 = (f32[16,256]{1,0:T(8,128)S(1)}, f32[16,256]{1,0:T(8,128)S(1)}, u32[]{:S(2)}, u32[]{:S(2)}) collective-permute-start(f32[16,256]{1,0:T(8,128)S(1)} %get-tuple-element.32), channel_id=1, source_target_pairs={{0,4},{4,0},{8,12},{12,8},{16,20},{20,16},{24,28},{28,24},{1,5},{5... | collective-permute-start | bytes 49160 | tf_op jit(solution)/shard_map/ppermute | solution.py:320
  13.4 4.7 %collective-permute-start.6 = (f32[16,256]{1,0:T(8,128)S(1)}, f32[16,256]{1,0:T(8,128)S(1)}, u32[]{:S(2)}, u32[]{:S(2)}) collective-permute-start(f32[16,256]{1,0:T(8,128)S(1)} %get-tuple-element.32), channel_id=1, source_target_pairs={{0,6},{1,7},{2,4},{3,5},{4,2},{5,3},{6,0},{7,1},{8,14},{9,15},{10,... | collective-permute-start | bytes 49160 | tf_op jit(solution)/shard_map/ppermute | solution.py:336
  14.3 3.9 %collective-permute-start.7 = (f32[16,256]{1,0:T(8,128)S(1)}, f32[16,256]{1,0:T(8,128)S(1)}, u32[]{:S(2)}, u32[]{:S(2)}) collective-permute-start(f32[16,256]{1,0:T(8,128)S(1)} %get-tuple-element.31.base_ref), channel_id=1, source_target_pairs={{0,2},{1,3},{2,0},{3,1},{4,6},{5,7},{6,4},{7,5},{8,10},{9,11},{10,... | collective-permute-start | bytes 49160 | tf_op jit(solution)/shard_map/ppermute | solution.py:315
  16.4 2.7 %copy-start = (bf16[1024,256]{1,0:T(8,128)(2,1)S(1)}, bf16[1024,256]{1,0:T(8,128)(2,1)}, u32[]{:S(2)}) copy-start(bf16[1024,256]{1,0:T(8,128)(2,1)} %weight_ref.3) | copy-start | bytes 1572868
  16.4 2.6 %collective-permute-start.5 = (bf16[512,256]{1,0:T(8,128)(2,1)S(1)}, bf16[512,256]{1,0:T(8,128)(2,1)S(1)}, u32[]{:S(2)}, u32[]{:S(2)}) collective-permute-start(bf16[512,256]{1,0:T(8,128)(2,1)S(1)} %shard_map.86.own_ref), channel_id=1, source_target_pairs={{0,1},{1,0},{2,3},{3,2},{4,5},{5,4},{6,7},{7,6},{8,9},{9,8},{10,11... | collective-permute-start | bytes 786440 | tf_op jit(solution)/shard_map/ppermute | solution.py:315
  18.9 0.7 %copy-start.6 = (f32[256]{0:T(256)S(1)}, f32[256]{0:T(256)}, u32[]{:S(2)}) copy-start(f32[256]{0:T(256)} %param.15) | copy-start | bytes 3076
  19.0 1.6 %collective-permute-start.9 = (bf16[512,256]{1,0:T(8,128)(2,1)S(1)}, bf16[512,256]{1,0:T(8,128)(2,1)S(1)}, u32[]{:S(2)}, u32[]{:S(2)}) collective-permute-start(bf16[512,256]{1,0:T(8,128)(2,1)S(1)} %shard_map.87.rest_0_), channel_id=1, source_target_pairs={{0,1},{1,0},{2,3},{3,2},{4,5},{5,4},{6,7},{7,6},{8,9},{9,8},{10,11... | collective-permute-start | bytes 786440 | tf_op jit(solution)/shard_map/ppermute | solution.py:315
